TPU v7x, 32 devices: a whole 2x2x4 slice. The times are simulated.
32 devices in a mesh: grp: 2 (over y), lon: 4 (over z), lat: 2 (over x), ta: 2 (over core).
Axes of the slice: x: 2, y: 2, z: 4, core: 2. Of those that a mesh axis runs over, the one named last changes fastest.
Arguments:
- swath: bfloat16 [1024, 128, 128], P(('grp', 'lon', 'lat'), 'ta'), parts along dimension 0, may hold values from -6 to 6
- obs_mask: int32 [1024, 128], P(('grp', 'lon', 'lat'), 'ta'), parts along dimension 0, may hold values 0 or 1
- target: int32 [1024], P(('grp', 'lon', 'lat')), parts along dimension 0, may hold values from 0 to 15
- send_list: int32 [16, 4, 32], P(('grp', 'lon', 'lat')), parts along dimension 0, may hold values from 0 to 63, as said below
- send_count: int32 [16, 4], P(('grp', 'lon', 'lat')), parts along dimension 0, may hold values from 0 to 32, as said below
- factor_space: float32 [96, 64, 512], P(None, ('grp', 'lat'), 'lon'), parts along dimension 1, may hold values from -0.6 to 0.6
- factor_time: float32 [256, 96], P(('grp', 'ta')), parts along dimension 0, may hold values from -0.625 to 0.625
Outputs:
- space_out: float32 [96, 64, 512], P(None, ('grp', 'lat'), 'lon'), parts along dimension 1
- time_out: float32 [256, 96], P(('grp', 'ta')), parts along dimension 0
There are 2 independent parts, one for each index of `grp`. A program takes and returns all parts, laid end to end along the dimension named above; each array names one. Nothing has to cross between parts.
Inputs may be any that keep to these rules, and one draw needn't show every extreme that they name: Entries k < send_count[g, d] of send_list[g, d] name slots of shard g; over all d every slot of the shard is named exactly once; other entries are 0. `send_count`: counts of one shard sum to 64; in each latitude band one owner receives 32 blocks from every shard of the band.
All inputs are finite; a program needn't handle non-finite values. No bound on the sum of `obs_mask` on one device may be relied on, other than what follows from the above.
Results may differ from a plain program's by a relative error of at most 0.007.
The roundings to bfloat16 on the way count: a program that leaves them out, or rounds other values in their place, can miss the bound.
Values may be sent and summed in bfloat16 or wider, within the bound.
No kernel may reach another device: no remote copies, remote signals or barrier semaphores. Data moves between devices by JAX's collectives and lax.ppermute only.
A program may use at most 64 MiB of HBM per device.

v0:
```python
import jax
import jax.numpy as jnp
from jax import lax
from jax.sharding import PartitionSpec as P

STEPS = 2


SMOOTH = 2.0
ETA_SPACE = 0.08
RIDGE = 1.0
EPSILON = 1e-06


def extended(value, sides, width, wrap):
    for axis, dim in sides:
        peers, length = (lax.axis_size(axis), value.shape[dim])
        up = [(i, (i + 1) % peers) for i in range(peers if wrap else peers - 1)]
        down = [(j, i) for i, j in up]
        last = lax.slice_in_dim(value, length - width, length, axis=dim)
        initial = lax.slice_in_dim(value, 0, width, axis=dim)
        before = lax.ppermute(last, axis, up)
        after = lax.ppermute(initial, axis, down)
        value = jnp.concatenate([before, value, after], axis=dim)
    return value


def laplace(surface):
    rows_ext = extended(surface.astype(jnp.bfloat16), (("lat", 1),), 1, False).astype(surface.dtype)
    cols_ext = extended(surface.astype(jnp.bfloat16), (("lon", 2),), 1, True).astype(surface.dtype)
    beside_all = rows_ext[:, 2:, :] + rows_ext[:, :-2, :] + cols_ext[:, :, 2:] + cols_ext[:, :, :-2]
    return 4.0 * surface - beside_all


def shards(swath, obs_mask, target, send_list, send_count, factor_space, factor_time):
    roster = send_list[0]
    tallies = send_count[0]
    width = roster.shape[1]
    filled = jnp.arange(width, dtype=jnp.int32)[None, :] < tallies[:, None]
    height = factor_space.shape[1]
    outgoing = swath[roster]
    weights_out = (obs_mask[roster] * filled[:, :, None].astype(jnp.int32)).astype(jnp.bfloat16)
    rows_out = target[roster]
    onehot_out = (
        (rows_out[:, :, None] == jnp.arange(height, dtype=jnp.int32)[None, None, :])
        & filled[:, :, None]
    ).astype(jnp.bfloat16)
    blocks_in, weights_in, onehot_in = (
        lax.all_to_all(outgoing, "lon", split_axis=0, concat_axis=0, tiled=True),
        lax.all_to_all(weights_out, "lon", split_axis=0, concat_axis=0, tiled=True),
        lax.all_to_all(onehot_out, "lon", split_axis=0, concat_axis=0, tiled=True),
    )
    received = blocks_in.shape[0] * blocks_in.shape[1]
    blocks_in = blocks_in.reshape(received, blocks_in.shape[2], blocks_in.shape[3])
    weights_in = weights_in.reshape(received, weights_in.shape[2]).astype(jnp.float32)
    onehot_in = onehot_in.reshape(received, height)
    n_lon = lax.axis_size("lon")
    n_lat = lax.axis_size("lat")
    n_ta = lax.axis_size("ta")
    cell_count = height * swath.shape[2] * n_lon * n_lat
    day_count = factor_time.shape[0] * n_ta
    spatial = factor_space
    packed = factor_space.astype(jnp.bfloat16)
    temporal = factor_time
    for sweep in range(STEPS):
        if sweep > 0:
            packed = spatial.astype(jnp.bfloat16)
        factor_rows = jnp.einsum(
            "bt,rtc->brc", onehot_in, packed, preferred_element_type=jnp.float32
        ).astype(jnp.bfloat16)
        time_bf = temporal.astype(jnp.bfloat16)
        predicted = jnp.einsum(
            "dr,brc->bdc", time_bf, factor_rows, preferred_element_type=jnp.float32
        )
        residual = (weights_in[:, :, None] * (predicted - blocks_in.astype(jnp.float32))).astype(
            jnp.bfloat16
        )
        block_grad = jnp.einsum(
            "dr,bdc->brc", time_bf, residual, preferred_element_type=jnp.float32
        )
        grad_high = block_grad.astype(jnp.bfloat16)
        grad_low = (block_grad - grad_high.astype(jnp.float32)).astype(jnp.bfloat16)
        local_space = jnp.einsum(
            "bt,brc->rtc", onehot_in, grad_high, preferred_element_type=jnp.float32
        )
        local_space = local_space + jnp.einsum(
            "bt,brc->rtc", onehot_in, grad_low, preferred_element_type=jnp.float32
        )
        local_time = jnp.einsum(
            "bdc,brc->dr", residual, factor_rows, preferred_element_type=jnp.float32
        )
        squares_rows = jnp.einsum(
            "brc,brc->br", factor_rows, factor_rows, preferred_element_type=jnp.float32
        )
        local_diag = jnp.einsum(
            "bd,br->dr", weights_in, squares_rows, precision=lax.Precision.HIGHEST
        )
        grad_time, grad_diag = lax.psum((local_time, local_diag), ("lon", "lat"))
        grad_space = lax.psum(local_space, "ta")
        space_new = spatial - ETA_SPACE * (grad_space + SMOOTH * laplace(spatial))
        time_new = temporal - grad_time / (grad_diag + RIDGE)
        part_space = jnp.sum(space_new * space_new, axis=(1, 2))
        part_time = jnp.sum(time_new * time_new, axis=0)
        space_sq = lax.psum(part_space, ("lon", "lat"))
        time_sq = lax.psum(part_time, "ta")
        rescale = ((time_sq / day_count + EPSILON) / (space_sq / cell_count + EPSILON)) ** 0.25
        spatial = space_new * rescale[:, None, None]
        temporal = time_new / rescale[None, :]
    return (spatial, temporal)


def solution(mesh):
    in_specs = (
        P(("grp", "lon", "lat"), "ta", None),
        P(("grp", "lon", "lat"), "ta"),
        P(("grp", "lon", "lat")),
        P(("grp", "lon", "lat"), None, None),
        P(("grp", "lon", "lat"), None),
        P(None, ("grp", "lat"), "lon"),
        P(("grp", "ta"), None),
    )
    out_specs = (P(None, ("grp", "lat"), "lon"), P(("grp", "ta"), None))
    return jax.shard_map(shards, mesh=mesh, in_specs=in_specs, out_specs=out_specs, check_vma=False)
```

profile of v0, /device:TPU:0, one launch (start us, length us, event | category | flops | bytes accessed | tf_op | source)
XLA Modules:
  0.0 266.7 jit_solution(12479847087037944260)
XLA Ops:
  11.1 6.3 %all-to-all-start.1 = ((bf16[4,2,256]{2,1,0:T(2,128)(2,1)}), bf16[4,2,256]{2,1,0:T(2,128)(2,1)S(1)}, u32[]{:S(2)}, u32[]{:S(2)}) async-start(bf16[4,2,256]{2,1,0:T(2,128)(2,1)} %reshape.138), calls=%async_computation.1 | async-start | bytes 8192 | tf_op jit(solution)/shard_map/all_to_all | solution.py:51
  19.7 3.4 %all-to-all-done.1 = bf16[4,2,256]{2,1,0:T(2,128)(2,1)S(1)} async-done(((bf16[4,2,256]{2,1,0:T(2,128)(2,1)}), bf16[4,2,256]{2,1,0:T(2,128)(2,1)S(1)}, u32[]{:S(2)}, u32[]{:S(2)}) %all-to-all-start.1) | async-done | bytes 4128 | tf_op jit(solution)/shard_map/all_to_all | solution.py:51
  23.0 3.3 %all-to-all-start = ((bf16[4,2,1024]{2,1,0:T(2,128)(2,1)}), bf16[4,2,1024]{2,1,0:T(2,128)(2,1)S(1)}, u32[]{:S(2)}, u32[]{:S(2)}) async-start(bf16[4,2,1024]{2,1,0:T(2,128)(2,1)} %reshape.140), calls=%async_computation | async-start | bytes 32768 | tf_op jit(solution)/shard_map/all_to_all | solution.py:50
  26.3 2.2 gather_fusion.2
  28.5 3.4 %all-to-all-done = bf16[4,2,1024]{2,1,0:T(2,128)(2,1)S(1)} async-done(((bf16[4,2,1024]{2,1,0:T(2,128)(2,1)}), bf16[4,2,1024]{2,1,0:T(2,128)(2,1)S(1)}, u32[]{:S(2)}, u32[]{:S(2)}) %all-to-all-start) | async-done | bytes 16416 | tf_op jit(solution)/shard_map/all_to_all | solution.py:50
  32.5 3.6 %all-to-all-start.2 = ((bf16[4,32,64,128]{3,2,1,0:T(8,128)(2,1)}), bf16[4,32,64,128]{3,2,1,0:T(8,128)(2,1)S(1)}, u32[]{:S(2)}, u32[]{:S(2)}) async-start(bf16[4,32,64,128]{3,2,1,0:T(8,128)(2,1)} %bitcast.72), calls=%async_computation.2 | async-start | bytes 4194304 | tf_op jit(solution)/shard_map/all_to_all | solution.py:49
  38.1 4.0 %collective-permute-start = (bf16[96,1,128]{2,1,0:T(2,128)(2,1)}, bf16[96,1,128]{2,1,0:T(2,128)(2,1)}, u32[]{:S(2)}, u32[]{:S(2)}) collective-permute-start(bf16[96,1,128]{2,1,0:T(2,128)(2,1)} %get-tuple-element.24), channel_id=1, source_target_pairs={{0,2},{1,3},{4,6},{5,7},{8,10},{9,11},{12,14},{13,15},{16,18},{17,... | collective-permute-start | bytes 73736 | tf_op jit(solution)/shard_map/ppermute | solution.py:22
  44.4 1.9 collective-permute-start.2
  46.4 1.9 collective-permute-start.3
  50.4 3.3 %fusion.2 = (f32[128,96]{0,1:T(8,128)}, bf16[128,96,128]{2,0,1:T(8,128)(2,1)}) fusion(bf16[128,16,1]{0,1,2:T(8,128)(2,1)S(1)} %reshape.128, bf16[96,16,128]{2,1,0:T(8,128)(2,1)S(1)} %convert_element_type.90), kind=kOutput, calls=%fused_computation.9 | convolution fusion | flops 56610816 | bytes 3592192 | tf_op jit(solution)/shard_map/bt,rtc->brc/dot_general | solution.py:68
  56.5 35.0 %all-to-all-done.2 = bf16[4,32,64,128]{3,2,1,0:T(8,128)(2,1)S(1)} async-done(((bf16[4,32,64,128]{3,2,1,0:T(8,128)(2,1)}), bf16[4,32,64,128]{3,2,1,0:T(8,128)(2,1)S(1)}, u32[]{:S(2)}, u32[]{:S(2)}) %all-to-all-start.2) | async-done | bytes 2097184 | tf_op jit(solution)/shard_map/all_to_all | solution.py:49
  91.5 5.0 %fusion.5 = bf16[128,64,128]{2,1,0:T(8,128)(2,1)S(1)} fusion(bf16[4,32,64,128]{3,2,1,0:T(8,128)(2,1)S(1)} %all-to-all-done.2, f32[128,64]{1,0:T(8,128)} %bitcast_convert_fusion.2, bf16[128,96,128]{2,0,1:T(8,128)(2,1)} %get-tuple-element.31, f32[64,96]{1,0:T(8,128)} %param.13), kind=kOutput, calls=%fused_computation.16 | convolution fusion | flops 205527040 | bytes 7397376 | tf_op jit(solution)/shard_map/dr,brc->bdc/dot_general | solution.py:72
  98.8 1.9 fusion.31
  101.0 2.9 %maximum_convert_fusion = f32[96,16,130]{2,1,0:T(8,128)} fusion(bf16[96,16,1]{2,1,0:T(8,128)(2,1)} %collective-permute-done.3, bf16[96,16,128]{2,1,0:T(8,128)(2,1)S(1)} %convert_element_type.90, bf16[96,16,1]{2,1,0:T(8,128)(2,1)} %collective-permute-done.2), kind=kLoop, calls=%fused_computation.59 | loop fusion | flops 1198080 | bytes 1198080 | tf_op jit(solution)/shard_map/convert_element_type | solution.py:30
  103.9 2.2 maximum_convert_fusion.2
  106.3 4.9 %fusion.40 = f32[64,96]{1,0:T(8,128)S(1)} fusion(bf16[128,64,128]{2,1,0:T(8,128)(2,1)} %copy-done.3, bf16[128,96,128]{2,0,1:T(8,128)(2,1)S(1)} %copy-done.1), kind=kOutput, calls=%fused_computation.41 | convolution fusion | flops 201326592 | bytes 5267456 | tf_op jit(solution)/shard_map/bdc,brc->dr/dot_general | solution.py:89
  111.2 10.7 %all-reduce.5.cloned.1.call-done = f32[96,16,128]{2,1,0:T(8,128)} async-done(((f32[96,16,128]{2,1,0:T(8,128)}), f32[96,16,128]{2,1,0:T(8,128)}) %all-reduce.5.cloned.1.call-update) | async-done | bytes 786448 | tf_op jit(solution)/shard_map/psum | solution.py:99
  121.9 5.1 %multiply_reduce_fusion.1 = (f32[96]{0:T(128)S(1)}, f32[96,16,128]{2,1,0:T(8,128)}) fusion(f32[96,16,128]{2,1,0:T(8,128)} %param.12, f32[96,16,128]{2,1,0:T(8,128)} %all-reduce.5.cloned.1.call-done, f32[96,16,130]{2,1,0:T(8,128)} %maximum_convert_fusion, f32[96,18,128]{2,1,0:T(8,128)} %maximum_convert_fusion.2), kind=kLoop, calls=%fused_computation.62 | loop fusion | flops 2162592 | bytes 5505408 | tf_op jit(solution)/shard_map/reduce_sum | solution.py:102
  127.0 38.2 %all-reduce.1 = (f32[96]{0:T(128)S(1)}, f32[64,96]{1,0:T(8,128)S(1)}, f32[64,96]{1,0:T(8,128)S(1)}) all-reduce(f32[96]{0:T(128)S(1)} %get-tuple-element.16, f32[64,96]{1,0:T(8,128)S(1)} %fusion.40, f32[64,96]{1,0:T(8,128)S(1)} %fusion.79), channel_id=1, replica_groups=mesh['grp'=2,'lon'=4,'lat'=2,'ta'=2] {'lon','lat'}, use_global_device_ids=true, to_apply=%region_6.0 | all-reduce | flops 12384 | bytes 99072 | tf_op jit(solution)/shard_map/psum | solution.py:104
  165.9 2.4 psum.73
  171.4 2.5 fusion
  174.0 1.9 collective-permute-start.4
  177.2 3.8 %collective-permute-start.7 = (bf16[96,16,1]{2,1,0:T(8,128)(2,1)}, bf16[96,16,1]{2,1,0:T(8,128)(2,1)}, u32[]{:S(2)}, u32[]{:S(2)}) collective-permute-start(bf16[96,16,1]{2,1,0:T(8,128)(2,1)} %get-tuple-element.23), channel_id=1, source_target_pairs={{4,0},{8,4},{12,8},{0,12},{5,1},{9,5},{13,9},{1,13},{6,2},{10,6},{... | collective-permute-start | bytes 9224 | tf_op jit(solution)/shard_map/ppermute | solution.py:23
  181.0 7.5 %fusion.7 = bf16[128,64,128]{2,1,0:T(8,128)(2,1)S(1)} fusion(bf16[4,32,64,128]{3,2,1,0:T(8,128)(2,1)S(1)} %all-to-all-done.2, f32[128,64]{1,0:T(8,128)S(1)} %copy-done.7, bf16[128,96,128]{2,0,1:T(8,128)(2,1)S(1)} %get-tuple-element.33, f32[64,96]{1,0:T(8,128)S(1)} %copy-done.8, f32[96]{0:T(128)S(1)} %fusion.67), kind=kOutput, calls=%fused_computation.18 | convolution fusion | flops 205533184 | bytes 7397760 | tf_op jit(solution)/shard_map/dr,brc->bdc/dot_general | solution.py:72
  190.8 1.9 fusion.37
  192.8 5.8 %fusion.43 = f32[64,96]{1,0:T(8,128)} fusion(bf16[128,64,128]{2,1,0:T(8,128)(2,1)S(1)} %copy-done.5, bf16[128,96,128]{2,0,1:T(8,128)(2,1)} %copy-done.2), kind=kOutput, calls=%fused_computation.42 | convolution fusion | flops 201326592 | bytes 5267456 | tf_op jit(solution)/shard_map/bdc,brc->dr/dot_general | solution.py:89
  198.8 2.7 %maximum_convert_fusion.1 = f32[96,16,130]{2,1,0:T(8,128)} fusion(bf16[96,16,1]{2,1,0:T(8,128)(2,1)} %collective-permute-done.7, bf16[96,16,128]{2,1,0:T(8,128)(2,1)S(1)} %multiply_convert_fusion, bf16[96,16,1]{2,1,0:T(8,128)(2,1)} %collective-permute-done.6), kind=kLoop, calls=%fused_computation.60 | loop fusion | flops 1198080 | bytes 1198080 | tf_op jit(solution)/shard_map/convert_element_type | solution.py:30
  202.7 9.3 %all-reduce.7.cloned.1.call-done = f32[96,16,128]{2,1,0:T(8,128)} async-done(((f32[96,16,128]{2,1,0:T(8,128)}), f32[96,16,128]{2,1,0:T(8,128)}) %all-reduce.7.cloned.1.call-update) | async-done | bytes 786448 | tf_op jit(solution)/shard_map/psum | solution.py:99
  212.0 4.3 %multiply_reduce_fusion = (f32[96]{0:T(128)S(1)}, f32[96,16,128]{2,1,0:T(8,128)}) fusion(f32[96,16,128]{2,1,0:T(8,128)} %all-reduce.7.cloned.1.call-done, f32[96,16,130]{2,1,0:T(8,128)} %maximum_convert_fusion.1, f32[96,18,128]{2,1,0:T(8,128)S(1)} %maximum_convert_fusion.3, f32[96,16,128]{2,1,0:T(8,128)S(1)} %copy-done.6, f32[96]{0:T(128)S(1)} %fusion.67), kind=kLoop, calls=%fused_computation.61 | loop fusion | flops 2359200 | bytes 5505792 | tf_op jit(solution)/shard_map/reduce_sum | solution.py:102
  216.3 38.2 %all-reduce = (f32[96]{0:T(128)S(1)}, f32[64,96]{1,0:T(8,128)S(1)}, f32[64,96]{1,0:T(8,128)S(1)}) all-reduce(f32[96]{0:T(128)S(1)} %get-tuple-element.10, f32[64,96]{1,0:T(8,128)S(1)} %copy-done.17, f32[64,96]{1,0:T(8,128)S(1)} %fusion.80), channel_id=1, replica_groups=mesh['grp'=2,'lon'=4,'lat'=2,'ta'=2] {'lon','lat'}, use_global_device_ids=true, to_apply=%region_13.0 | all-reduce | flops 12384 | bytes 99072 | tf_op jit(solution)/shard_map/psum | solution.py:104
  254.6 2.5 psum.78
  257.7 2.2 broadcast_multiply_fusion
  (87 shorter events, 28.3 us)
Async XLA Ops:
  7.2 19.1 %copy-start = (bf16[64,64,128]{2,1,0:T(8,128)(2,1)S(1)}, bf16[64,64,128]{2,1,0:T(8,128)(2,1)}, u32[]{:S(2)}) copy-start(bf16[64,64,128]{2,1,0:T(8,128)(2,1)} %param.7) | copy-start | bytes 3145732
  11.1 11.9 %all-to-all-start.1 = ((bf16[4,2,256]{2,1,0:T(2,128)(2,1)}), bf16[4,2,256]{2,1,0:T(2,128)(2,1)S(1)}, u32[]{:S(2)}, u32[]{:S(2)}) async-start(bf16[4,2,256]{2,1,0:T(2,128)(2,1)} %reshape.138), calls=%async_computation.1 | async-start | bytes 8192 | tf_op jit(solution)/shard_map/all_to_all | solution.py:51
  23.0 8.8 %copy-start.18 = (bf16[4,2,256]{2,1,0:T(2,128)(2,1)}, bf16[4,2,256]{2,1,0:T(2,128)(2,1)S(1)}, u32[]{:S(2)}) copy-start(bf16[4,2,256]{2,1,0:T(2,128)(2,1)S(1)} %all-to-all-done.1) | copy-start | bytes 12292
  23.0 8.8 %all-to-all-start = ((bf16[4,2,1024]{2,1,0:T(2,128)(2,1)}), bf16[4,2,1024]{2,1,0:T(2,128)(2,1)S(1)}, u32[]{:S(2)}, u32[]{:S(2)}) async-start(bf16[4,2,1024]{2,1,0:T(2,128)(2,1)} %reshape.140), calls=%async_computation | async-start | bytes 32768 | tf_op jit(solution)/shard_map/all_to_all | solution.py:50
  31.9 0.6 copy-start.16
  32.5 59.0 %all-to-all-start.2 = ((bf16[4,32,64,128]{3,2,1,0:T(8,128)(2,1)}), bf16[4,32,64,128]{3,2,1,0:T(8,128)(2,1)S(1)}, u32[]{:S(2)}, u32[]{:S(2)}) async-start(bf16[4,32,64,128]{3,2,1,0:T(8,128)(2,1)} %bitcast.72), calls=%async_computation.2 | async-start | bytes 4194304 | tf_op jit(solution)/shard_map/all_to_all | solution.py:49
  36.1 85.8 %all-reduce.5.cloned.1.call-start = ((), (), s32[]{:S(2)}) async-start(), calls=%async_computation.3 | async-start | bytes 1572864 | tf_op jit(solution)/shard_map/psum | solution.py:99
  38.1 65.8 %collective-permute-start = (bf16[96,1,128]{2,1,0:T(2,128)(2,1)}, bf16[96,1,128]{2,1,0:T(2,128)(2,1)}, u32[]{:S(2)}, u32[]{:S(2)}) collective-permute-start(bf16[96,1,128]{2,1,0:T(2,128)(2,1)} %get-tuple-element.24), channel_id=1, source_target_pairs={{0,2},{1,3},{4,6},{5,7},{8,10},{9,11},{12,14},{13,15},{16,18},{17,... | collective-permute-start | bytes 73736 | tf_op jit(solution)/shard_map/ppermute | solution.py:22
  42.1 61.8 %collective-permute-start.1 = (bf16[96,1,128]{2,1,0:T(2,128)(2,1)}, bf16[96,1,128]{2,1,0:T(2,128)(2,1)}, u32[]{:S(2)}, u32[]{:S(2)}) collective-permute-start(bf16[96,1,128]{2,1,0:T(2,128)(2,1)} %get-tuple-element.25), channel_id=1, source_target_pairs={{2,0},{3,1},{6,4},{7,5},{10,8},{11,9},{14,12},{15,13},{18,16},{19,... | collective-permute-start | bytes 73736 | tf_op jit(solution)/shard_map/ppermute | solution.py:23
  44.4 56.6 %collective-permute-start.2 = (bf16[96,16,1]{2,1,0:T(8,128)(2,1)}, bf16[96,16,1]{2,1,0:T(8,128)(2,1)}, u32[]{:S(2)}, u32[]{:S(2)}) collective-permute-start(bf16[96,16,1]{2,1,0:T(8,128)(2,1)} %get-tuple-element.26), channel_id=1, source_target_pairs={{0,4},{4,8},{8,12},{12,0},{1,5},{5,9},{9,13},{13,1},{2,6},{6,10},{... | collective-permute-start | bytes 9224 | tf_op jit(solution)/shard_map/ppermute | solution.py:22
  46.4 54.6 %collective-permute-start.3 = (bf16[96,16,1]{2,1,0:T(8,128)(2,1)}, bf16[96,16,1]{2,1,0:T(8,128)(2,1)}, u32[]{:S(2)}, u32[]{:S(2)}) collective-permute-start(bf16[96,16,1]{2,1,0:T(8,128)(2,1)} %get-tuple-element.27), channel_id=1, source_target_pairs={{4,0},{8,4},{12,8},{0,12},{5,1},{9,5},{13,9},{1,13},{6,2},{10,6},{... | collective-permute-start | bytes 9224 | tf_op jit(solution)/shard_map/ppermute | solution.py:23
  91.5 5.0 %copy-start.12 = (f32[64,96]{1,0:T(8,128)S(1)}, f32[64,96]{1,0:T(8,128)}, u32[]{:S(2)}) copy-start(f32[64,96]{1,0:T(8,128)} %param.13) | copy-start | bytes 73732
  96.5 1.4 copy-start.3
  100.7 111.3 %all-reduce.7.cloned.1.call-start = ((), (), s32[]{:S(2)}) async-start(), calls=%async_computation.4 | async-start | bytes 1572864 | tf_op jit(solution)/shard_map/psum | solution.py:99
  100.9 5.1 %copy-start.10 = (bf16[4,32,64]{2,1,0:T(8,128)(2,1)S(1)}, bf16[4,32,64]{2,1,0:T(8,128)(2,1)}, u32[]{:S(2)}) copy-start(bf16[4,32,64]{2,1,0:T(8,128)(2,1)} %reshape.141) | copy-start | bytes 49156
  101.0 5.1 %copy-start.14 = (f32[128,96]{0,1:T(8,128)S(1)}, f32[128,96]{0,1:T(8,128)}, u32[]{:S(2)}) copy-start(f32[128,96]{0,1:T(8,128)} %get-tuple-element.30) | copy-start | bytes 147460
  101.0 5.3 %copy-start.1 = (bf16[128,96,128]{2,0,1:T(8,128)(2,1)S(1)}, bf16[128,96,128]{2,0,1:T(8,128)(2,1)}, u32[]{:S(2)}) copy-start(bf16[128,96,128]{2,0,1:T(8,128)(2,1)} %get-tuple-element.31) | copy-start | bytes 9437188
  111.2 54.1 %copy-start.13 = (f32[64,96]{1,0:T(8,128)S(1)}, f32[64,96]{1,0:T(8,128)}, u32[]{:S(2)}) copy-start(f32[64,96]{1,0:T(8,128)} %param.13) | copy-start | bytes 73732
  168.4 12.7 %copy-start.7 = (f32[128,64]{1,0:T(8,128)S(1)}, f32[128,64]{1,0:T(8,128)}, u32[]{:S(2)}) copy-start(f32[128,64]{1,0:T(8,128)} %bitcast_convert_fusion.2) | copy-start | bytes 98308
  168.4 12.7 %copy-start.8 = (f32[64,96]{1,0:T(8,128)S(1)}, f32[64,96]{1,0:T(8,128)}, u32[]{:S(2)}) copy-start(f32[64,96]{1,0:T(8,128)} %get-tuple-element.15) | copy-start | bytes 73732
  174.0 7.1 %copy-start.2 = (bf16[128,96,128]{2,0,1:T(8,128)(2,1)}, bf16[128,96,128]{2,0,1:T(8,128)(2,1)S(1)}, u32[]{:S(2)}) copy-start(bf16[128,96,128]{2,0,1:T(8,128)(2,1)S(1)} %get-tuple-element.33) | copy-start | bytes 9437188
  174.0 27.6 %collective-permute-start.4 = (bf16[96,1,128]{2,1,0:T(2,128)(2,1)}, bf16[96,1,128]{2,1,0:T(2,128)(2,1)}, u32[]{:S(2)}, u32[]{:S(2)}) collective-permute-start(bf16[96,1,128]{2,1,0:T(2,128)(2,1)} %get-tuple-element.20), channel_id=1, source_target_pairs={{0,2},{1,3},{4,6},{5,7},{8,10},{9,11},{12,14},{13,15},{16,18},{17,... | collective-permute-start | bytes 73736 | tf_op jit(solution)/shard_map/ppermute | solution.py:22
  175.9 25.7 %collective-permute-start.5 = (bf16[96,1,128]{2,1,0:T(2,128)(2,1)}, bf16[96,1,128]{2,1,0:T(2,128)(2,1)}, u32[]{:S(2)}, u32[]{:S(2)}) collective-permute-start(bf16[96,1,128]{2,1,0:T(2,128)(2,1)} %get-tuple-element.21), channel_id=1, source_target_pairs={{2,0},{3,1},{6,4},{7,5},{10,8},{11,9},{14,12},{15,13},{18,16},{19,... | collective-permute-start | bytes 73736 | tf_op jit(solution)/shard_map/ppermute | solution.py:23
  177.1 21.6 %collective-permute-start.6 = (bf16[96,16,1]{2,1,0:T(8,128)(2,1)}, bf16[96,16,1]{2,1,0:T(8,128)(2,1)}, u32[]{:S(2)}, u32[]{:S(2)}) collective-permute-start(bf16[96,16,1]{2,1,0:T(8,128)(2,1)} %get-tuple-element.22), channel_id=1, source_target_pairs={{0,4},{4,8},{8,12},{12,0},{1,5},{5,9},{9,13},{13,1},{2,6},{6,10},{... | collective-permute-start | bytes 9224 | tf_op jit(solution)/shard_map/ppermute | solution.py:22
  177.2 21.6 %collective-permute-start.7 = (bf16[96,16,1]{2,1,0:T(8,128)(2,1)}, bf16[96,16,1]{2,1,0:T(8,128)(2,1)}, u32[]{:S(2)}, u32[]{:S(2)}) collective-permute-start(bf16[96,16,1]{2,1,0:T(8,128)(2,1)} %get-tuple-element.23), channel_id=1, source_target_pairs={{4,0},{8,4},{12,8},{0,12},{5,1},{9,5},{13,9},{1,13},{6,2},{10,6},{... | collective-permute-start | bytes 9224 | tf_op jit(solution)/shard_map/ppermute | solution.py:23
  188.5 1.4 copy-start.4
  190.8 1.9 copy-start.5
  192.8 5.8 %copy-start.11 = (bf16[4,32,64]{2,1,0:T(8,128)(2,1)S(1)}, bf16[4,32,64]{2,1,0:T(8,128)(2,1)}, u32[]{:S(2)}) copy-start(bf16[4,32,64]{2,1,0:T(8,128)(2,1)} %reshape.141) | copy-start | bytes 49156
  192.8 5.8 %copy-start.15 = (f32[128,96]{0,1:T(8,128)S(1)}, f32[128,96]{0,1:T(8,128)}, u32[]{:S(2)}) copy-start(f32[128,96]{0,1:T(8,128)} %get-tuple-element.32) | copy-start | bytes 147460
  198.5 13.4 %copy-start.6 = (f32[96,16,128]{2,1,0:T(8,128)S(1)}, f32[96,16,128]{2,1,0:T(8,128)}, u32[]{:S(2)}) copy-start(f32[96,16,128]{2,1,0:T(8,128)} %get-tuple-element.17) | copy-start | bytes 2359300
  202.7 13.6 %copy-start.17 = (f32[64,96]{1,0:T(8,128)S(1)}, f32[64,96]{1,0:T(8,128)}, u32[]{:S(2)}) copy-start(f32[64,96]{1,0:T(8,128)} %fusion.43) | copy-start | bytes 73732
  202.7 51.9 %copy-start.9 = (f32[64,96]{1,0:T(8,128)S(1)}, f32[64,96]{1,0:T(8,128)}, u32[]{:S(2)}) copy-start(f32[64,96]{1,0:T(8,128)} %get-tuple-element.15) | copy-start | bytes 73732
Sparse Core Ops, SparseCore 0:
  100.8 21.0 all-reduce.4
  192.9 19.0 all-reduce.6
where the time goes:
time: 268 us; the launch traced here: 267 us
  blocking collectives  81.4 us (30%)
  waiting for transfers between devices  61.8 us (23%)
  matrix products  37.1 us (14%)
  starting transfers between devices  29.6 us (11%)
  other arithmetic  27.3 us (10%)
  local copies, waits for them, and re-layouts  15.1 us (6%)
  between operations  14.4 us (5%)
    psum x2, blocking collectives, shards(): space_sq = lax.psum(part_space, ('lon', 'lat'))  76.5 us
    all_to_all x1, waiting for transfers between devices, shards(): lax.all_to_all(outgoing, 'lon', split_axis=0, concat_axis=0, tiled=True)  35 us
    psum x2, waiting for transfers between devices, shards(): grad_space = lax.psum(local_space, 'ta')  20 us
    dot_general x2, matrix products, shards(): jnp.einsum('dr,brc->bdc', time_bf, factor_rows, preferred_element_type=jn...  12.5 us
    dot_general x2, matrix products, shards(): jnp.einsum('bdc,brc->dr', residual, factor_rows, preferred_element_type=j...  10.6 us
    reduce_sum x2, other arithmetic, shards(): part_space = jnp.sum(space_new * space_new, axis=(1, 2))  9.43 us
    ppermute x4, starting transfers between devices, extended(): after = lax.ppermute(initial, axis, down)  8.26 us
    ppermute x4, starting transfers between devices, extended(): before = lax.ppermute(last, axis, up)  7.89 us
  transfers between devices with their start and end apart: 13, of which 5 were waited for; matrix products, arithmetic and copies ran while one was open for 21% of the time, Pallas kernels for 0%

commit v1 on v0

v1 whole, which is shorter than its diff:
```python
import functools

import jax
import jax.numpy as jnp
from jax import lax
from jax.experimental import pallas as pl
from jax.experimental.pallas import tpu as pltpu
from jax.sharding import PartitionSpec as P

SMOOTH = 2.0
ETA_SPACE = 0.08
RIDGE = 1.0
EPSILON = 1e-06

F32 = jnp.float32
BF16 = jnp.bfloat16
LANES = 128
TAIL = 16
COLS = 16
NORM = 8
VMEM_LIMIT = 56 * 1024 * 1024


def dot(a, b, contract):
    return lax.dot_general(a, b, ((contract[:1], contract[1:]), ((), ())), preferred_element_type=F32)


def route_kernel(n_lon, half, list_ref, count_ref, target_ref, swath_ref, mask_ref, *rest):
    outs, (place, total, seen) = rest[: 2 * n_lon], rest[2 * n_lon:]
    me, core = lax.axis_index("lon"), lax.axis_index("ta")
    slots, days, cells = swath_ref.shape

    def owner(d, carry):
        step = jnp.bitwise_xor(d, me)

        def entry(k, carry):
            slot = list_ref[0, d, k]
            row = target_ref[slot]
            far = jnp.bitwise_xor(lax.div(row, half), core)
            place[slot] = (far * n_lon + step) * half + lax.rem(row, half)
            return carry

        return lax.fori_loop(0, count_ref[0, d], entry, carry)

    lax.fori_loop(0, n_lon, owner, 0)
    total[...] = jnp.zeros(total.shape, F32)
    seen[...] = jnp.zeros(seen.shape, F32)
    mask = mask_ref[...].astype(F32)
    by_day = mask.T
    for slot in range(slots):
        at = place[slot]
        total[at] += swath_ref[slot].astype(F32) * by_day[:, slot:slot + 1]
        seen[pl.ds(at, 1), :days] += mask[slot:slot + 1, :]
    for piece, out in enumerate(outs):
        out[: half * days, :] = total[piece * half:(piece + 1) * half].reshape(half * days, cells).astype(BF16)
        out[half * days:, :] = seen[piece * half:piece * half + TAIL, :].astype(BF16)


def row_of(surface, row):
    return surface[:, row * LANES:(row + 1) * LANES]


def columns_as_rows(surface, half, flip, extra):
    rank = surface.shape[0]
    lane = lax.broadcasted_iota(jnp.int32, (rank, LANES), 1)
    block = jnp.zeros((rank, LANES), F32)
    for row in range(half):
        strip = row_of(surface, row)
        block = jnp.where(lane == row, strip[:, :1], block)
        block = jnp.where(lane == half + row, strip[:, LANES - 1:], block)
    if extra is not None:
        block = jnp.where(lane == COLS, extra, block)
    flip[...] = jnp.zeros(flip.shape, F32)
    flip[:rank, :] = block
    return flip[...].T[: COLS + NORM, :]


def rows_as_columns(rows, rank, flip):
    flip[...] = jnp.zeros(flip.shape, F32)
    flip[: rows.shape[0], :] = rows
    return flip[...].T[:rank, :]


def smoothed(surface, half, above, below, left_cols, right_cols):
    lane = lax.broadcasted_iota(jnp.int32, above.shape, 1)
    strips = []
    for row in range(half):
        here = row_of(surface, row)
        up = above if row == 0 else row_of(surface, row - 1)
        down = below if row == half - 1 else row_of(surface, row + 1)
        left = jnp.where(lane == 0, left_cols[:, half + row:half + row + 1], pltpu.roll(here, 1, 1))
        right = jnp.where(lane == LANES - 1, right_cols[:, row:row + 1], pltpu.roll(here, LANES - 1, 1))
        lap = 4.0 * here - (up + down + left + right)
        strips.append(here - (ETA_SPACE * SMOOTH) * lap)
    return strips


def prepare_kernel(half, space_ref, surface, edge_near, edge_far, cols, flip):
    core = lax.axis_index("ta")
    rank = surface.shape[0]
    height = space_ref.shape[0] // rank
    for row in range(half):
        surface[:, row * LANES:(row + 1) * LANES] = space_ref[pl.ds(core * half + row, rank, stride=height), :]
    edge_near[...] = space_ref[pl.ds(half - core, rank, stride=height), :]
    edge_far[...] = space_ref[pl.ds(core * (height - 1), rank, stride=height), :]
    cols[...] = columns_as_rows(surface[...], half, flip, None)


def pick(flag, a, b):
    return jnp.where(flag, a, b)


def model_kernel(half, surface, edge_near, edge_far, cols_a, cols_b, swap, time_own, time_other, base, predicted, packed, time_t, flip, days_all):
    core = lax.axis_index("ta")
    rank = surface.shape[0]
    days = time_own.shape[0]
    days_all[...] = jnp.zeros(days_all.shape, F32)
    days_all[:days, :rank] = time_own[...]
    days_all[days:, :rank] = time_other[...]
    time_full = days_all[...]
    time_t[...] = time_full.T[:rank, :]
    packed[...] = surface[...].astype(BF16)
    time_bf = time_full[:, :rank].astype(BF16)
    for at in range(0, half * LANES, 2 * LANES):
        predicted[:, at:at + 2 * LANES] = dot(time_bf, packed[:, at:at + 2 * LANES], (1, 0))
    above = pick(core == 0, edge_far[...], edge_near[...])
    below = pick(core == 0, edge_near[...], edge_far[...])
    odd = swap()
    left = rows_as_columns(pick(odd, cols_a[...], cols_b[...]), rank, flip)
    right = rows_as_columns(pick(odd, cols_b[...], cols_a[...]), rank, flip)
    for row, strip in enumerate(smoothed(surface[...], half, above, below, left, right)):
        base[:, row * LANES:(row + 1) * LANES] = strip


def gradients(half, base, predicted, packed, time_t, seen, summed, fresh, message, outgoing, edge_far, flip):
    core = lax.axis_index("ta")
    rank = time_t.shape[0]
    time_bf = time_t.astype(BF16)
    time_twice = jnp.concatenate([time_bf, time_bf], axis=1)
    seen_bf = seen.astype(BF16)
    width = 2 * LANES
    owner = lax.broadcasted_iota(jnp.int32, (TAIL, width), 0)
    lane = lax.broadcasted_iota(jnp.int32, (TAIL, width), 1)
    grad_time = jnp.zeros((rank, width), F32)
    grad_diag = jnp.zeros((rank, LANES), F32)
    norm = jnp.zeros((rank, 1), F32)
    for at in range(0, half * LANES, width):
        spread = (owner * LANES <= lane + at) & (lane + at < (owner + 1) * LANES)
        weight = dot(seen_bf, spread.astype(BF16), (0, 0))
        part = packed[:, at:at + width]
        residual = weight * predicted[:, at:at + width] - summed[:, at:at + width]
        high = residual.astype(BF16)
        low = (residual - high.astype(F32)).astype(BF16)
        both = jnp.concatenate([high, low], axis=0)
        grad_space = dot(time_twice, both, (1, 0))
        grad_time = grad_time + dot(part, both, (1, 1))
        new = base[:, at:at + width] - ETA_SPACE * grad_space
        fresh[:, at:at + width] = new
        norm = norm + jnp.sum(new * new, axis=1, keepdims=True)
        wide = part.astype(F32)
        for row in range(width // LANES):
            strip = row_of(wide, row)
            square = jnp.sum(strip * strip, axis=1, keepdims=True)
            grad_diag = grad_diag + square * seen[at // LANES + row:at // LANES + row + 1, :]
    grad_time = grad_time[:, :LANES] + grad_time[:, LANES:]
    message[:rank, :] = grad_time
    message[rank:2 * rank, :] = grad_diag
    last = columns_as_rows(fresh[...], half, flip, norm)
    message[2 * rank:, :] = last
    outgoing[:rank, :] = pltpu.roll(grad_time, LANES // 2, 1)
    outgoing[rank:2 * rank, :] = pltpu.roll(grad_diag, LANES // 2, 1)
    outgoing[2 * rank:2 * rank + COLS + NORM, :] = last
    first_row, last_row = fresh[:, :LANES], fresh[:, (half - 1) * LANES:]
    outgoing[2 * rank + COLS + NORM:, :] = pick(core == 0, last_row, first_row)
    edge_far[...] = pick(core == 0, first_row, last_row)


def first_kernel(half, n_lon, base, predicted, packed, time_t, *rest):
    near, far = rest[:n_lon], rest[n_lon:2 * n_lon]
    fresh, message, outgoing, edge_far, summed, seen, flip = rest[2 * n_lon:]
    days = (near[0].shape[0] - TAIL) // half
    for row in range(half):
        for first, parts in ((0, near), (days, far)):
            value = parts[0][row * days:(row + 1) * days, :].astype(F32)
            for piece in parts[1:]:
                value = value + piece[row * days:(row + 1) * days, :].astype(F32)
            summed[first:first + days, row * LANES:(row + 1) * LANES] = value

    def counts(parts):
        value = parts[0][half * days:, :].astype(F32)
        for piece in parts[1:]:
            value = value + piece[half * days:, :].astype(F32)
        return value

    seen[...] = counts(near) + pltpu.roll(counts(far), days, 1)
    gradients(half, base, predicted, packed, time_t[...], seen[...], summed, fresh, message, outgoing, edge_far, flip)


def settle(rank, day_count, cell_count, total, time_t):
    time_new = time_t - total[:rank, :] / (total[rank:2 * rank, :] + RIDGE)
    return time_new


def scaling(rank, day_count, cell_count, total, time_new, flip):
    space_sq = rows_as_columns(total[2 * rank + COLS:, :], rank, flip)[:, :1]
    square = time_new * time_new
    time_sq = 0.5 * jnp.sum(square + pltpu.roll(square, LANES // 2, 1), axis=1, keepdims=True)
    ratio = (time_sq / day_count + EPSILON) / (space_sq / cell_count + EPSILON)
    return jnp.sqrt(jnp.sqrt(ratio))


def total_of(parts):
    if len(parts) == 1:
        return parts[0][...]
    return (parts[0][...] + parts[1][...]) + (parts[2][...] + parts[3][...])


def second_kernel(half, counts, n_parts, swap, surface, time_t, summed, seen, edge_near, edge_far, *rest):
    parts, (cols_a, cols_b) = rest[:n_parts], rest[n_parts:n_parts + 2]
    fresh, time_out, message, outgoing, edge_out, flip, scaled, base, predicted, packed = rest[n_parts + 2:]
    core = lax.axis_index("ta")
    rank = surface.shape[0]
    total = total_of(parts)
    time_new = settle(rank, *counts, total, time_t[...])
    scale = scaling(rank, *counts, total, time_new, flip)
    time_now = time_new / scale
    time_out[...] = time_now
    scaled[...] = surface[...] * scale
    packed[...] = scaled[...].astype(BF16)
    time_bf = time_now.T.astype(BF16)
    for at in range(0, half * LANES, 2 * LANES):
        predicted[:, at:at + 2 * LANES] = dot(time_bf, packed[:, at:at + 2 * LANES], (1, 0))
    near, far = edge_near[...], edge_far[...]
    above = pick(core == 0, far, near) * scale
    below = pick(core == 0, near, far) * scale
    odd = swap()
    from_a, from_b = cols_a[2 * rank:2 * rank + COLS, :], cols_b[2 * rank:2 * rank + COLS, :]
    left = rows_as_columns(pick(odd, from_a, from_b), rank, flip) * scale
    right = rows_as_columns(pick(odd, from_b, from_a), rank, flip) * scale
    for row, strip in enumerate(smoothed(scaled[...], half, above, below, left, right)):
        base[:, row * LANES:(row + 1) * LANES] = strip
    gradients(half, base, predicted, packed, time_now, seen[...], summed, fresh, message, outgoing, edge_out, flip)


def last_kernel(half, counts, n_parts, surface, other, time_t, *rest):
    parts = rest[:n_parts]
    space_out, time_out, flip = rest[n_parts:]
    core = lax.axis_index("ta")
    rank = surface.shape[0]
    height = space_out.shape[0] // rank
    total = total_of(parts)
    time_new = settle(rank, *counts, total, time_t[...])
    scale = scaling(rank, *counts, total, time_new, flip)
    flip[...] = jnp.zeros(flip.shape, F32)
    flip[:rank, :] = time_new / scale
    time_out[...] = flip[...].T[: time_out.shape[0], :rank]
    for row in range(half):
        at = row * LANES
        space_out[pl.ds(core * half + row, rank, stride=height), :] = surface[:, at:at + LANES] * scale
        space_out[pl.ds((1 - core) * half + row, rank, stride=height), :] = other[:, at:at + LANES] * scale


def add_kernel(rank, mine, theirs, out):
    cols = slice(2 * rank, 2 * rank + COLS)
    out[: 2 * rank, :] = mine[: 2 * rank, :] + theirs[: 2 * rank, :]
    out[cols, :] = mine[cols, :]
    ends = slice(2 * rank + COLS, 2 * rank + COLS + NORM)
    out[ends, :] = mine[ends, :] + theirs[ends, :]


def shape(dims, dtype=F32):
    return jax.ShapeDtypeStruct(tuple(dims), dtype)


def call(kernel, out_shape, scratch=(), smem=0, flops=1_000_000):
    def run(*operands):
        return pl.pallas_call(
            kernel,
            out_shape=out_shape,
            in_specs=[pl.BlockSpec(memory_space=pltpu.SMEM)] * smem + [pl.BlockSpec(memory_space=pltpu.VMEM)] * (len(operands) - smem),
            out_specs=jax.tree.map(lambda _: pl.BlockSpec(memory_space=pltpu.VMEM), out_shape),
            scratch_shapes=list(scratch),
            compiler_params=pltpu.CompilerParams(vmem_limit_bytes=VMEM_LIMIT),
            cost_estimate=pl.CostEstimate(flops=flops, bytes_accessed=1_000_000, transcendentals=0),
        )(*operands)

    return run


def across(value, axis, step):
    peers = lax.axis_size(axis)
    return lax.ppermute(value, axis, [(i, i ^ step) for i in range(peers)])


def shards(swath, obs_mask, target, send_list, send_count, factor_space, factor_time):
    n_lon, n_lat, n_ta = (lax.axis_size(axis) for axis in ("lon", "lat", "ta"))
    slots, days, cells = swath.shape
    rank, height, _ = factor_space.shape
    half = height // n_ta
    wide = half * LANES
    counts = (float(days * n_ta), float(height * cells * n_lon * n_lat))
    message_rows = 2 * rank + COLS + NORM
    flip = pltpu.VMEM((LANES, LANES), F32)

    pieces = call(
        functools.partial(route_kernel, n_lon, half),
        [shape((half * days + TAIL, cells), BF16)] * (2 * n_lon),
        [pltpu.SMEM((slots,), jnp.int32), pltpu.VMEM((2 * n_lon * half, days, cells), F32), pltpu.VMEM((2 * n_lon * half + TAIL, LANES), F32)],
        smem=3,
    )(send_list, send_count, target, swath, obs_mask)
    near, far = pieces[:n_lon], pieces[n_lon:]
    order = sorted(range(1, n_lon), key=lambda step: (-((step + 1) // 2), step))
    near_in = {0: near[0]}
    for step in order:
        near_in[step] = across(near[step], "lon", step)
    far = [across(piece, "ta", 1) for piece in far]
    far_in = {0: far[0]}
    for step in order:
        far_in[step] = across(far[step], "lon", step)

    def bands(edge):
        there = [(2 * band + 1, 2 * band + 2) for band in range(n_lat - 1)]
        return lax.ppermute(edge, ("lat", "ta"), there + [(b, a) for a, b in there])

    paired = n_lon == 4

    def swap():
        return lax.rem(lax.axis_index("lon"), 2) == 1 if paired else jnp.bool_(True)

    def columns(value):
        if paired:
            return across(value, "lon", 1), across(value, "lon", 3)
        ring = [(i, (i + 1) % n_lon) for i in range(n_lon)]
        return lax.ppermute(value, "lon", ring), lax.ppermute(value, "lon", [(b, a) for a, b in ring])

    surface, edge_near, edge_far, cols = call(
        functools.partial(prepare_kernel, half),
        [shape((rank, wide)), shape((rank, LANES)), shape((rank, LANES)), shape((COLS + NORM, LANES))],
        [flip],
    )(factor_space.reshape(rank * height, cells))
    cols_a, cols_b = columns(cols)

    def model(*refs):
        model_kernel(half, *refs[:5], swap, *refs[5:])

    base, predicted, packed, time_t = call(
        model,
        [shape((rank, wide)), shape((2 * days, wide)), shape((rank, wide), BF16), shape((rank, LANES))],
        [flip, flip],
    )(surface, edge_near, bands(edge_far), cols_a, cols_b, factor_time, across(factor_time, "ta", 1))

    step_out = [shape((rank, wide)), shape((message_rows, LANES)), shape((message_rows + rank, LANES)), shape((rank, LANES))]
    surface, message, outgoing, edge_far, summed, seen = call(
        functools.partial(first_kernel, half, n_lon),
        step_out + [shape((2 * days, wide)), shape((TAIL, LANES))],
        [flip],
    )(base, predicted, packed, time_t, *[near_in[s] for s in range(n_lon)], *[far_in[s] for s in range(n_lon)])

    add = call(functools.partial(add_kernel, rank), shape((message_rows, LANES)))

    def gather(message, outgoing):
        incoming = across(outgoing, "ta", 1)
        total = add(message, incoming)
        step = 1
        while step < n_lat:
            total = add(total, across(total, "lat", step))
            step *= 2
        if paired:
            return incoming, [total] + [across(total, "lon", step) for step in (1, 2, 3)]
        step = 1
        own = total
        while step < n_lon:
            total = add(total, across(total, "lon", step))
            step *= 2
        return incoming, [total], own

    beside, *rest = gather(message, outgoing)
    parts = rest[0]
    if paired:
        cols_a, cols_b = parts[1], parts[3]
    else:
        cols_a, cols_b = columns(message)

    def second(*refs):
        second_kernel(half, counts, len(parts), swap, *refs)

    surface, time_t, message, outgoing, edge_far = call(
        second,
        [step_out[0], shape((rank, LANES))] + step_out[1:],
        [flip, pltpu.VMEM((rank, wide), F32), pltpu.VMEM((rank, wide), F32), pltpu.VMEM((2 * days, wide), F32), pltpu.VMEM((rank, wide), BF16)],
    )(surface, time_t, summed, seen, beside[message_rows:], bands(edge_far), *parts, cols_a, cols_b)

    other = across(surface, "ta", 1)
    parts = gather(message, outgoing)[1]
    space, time = call(
        functools.partial(last_kernel, half, counts, len(parts)),
        [shape((rank * height, cells)), shape(factor_time.shape)],
        [flip],
    )(surface, other, time_t, *parts)
    return space.reshape(rank, height, cells), time


def solution(mesh):
    in_specs = (
        P(("grp", "lon", "lat"), "ta", None),
        P(("grp", "lon", "lat"), "ta"),
        P(("grp", "lon", "lat")),
        P(("grp", "lon", "lat"), None, None),
        P(("grp", "lon", "lat"), None),
        P(None, ("grp", "lat"), "lon"),
        P(("grp", "ta"), None),
    )
    out_specs = (P(None, ("grp", "lat"), "lon"), P(("grp", "ta"), None))
    return jax.shard_map(shards, mesh=mesh, in_specs=in_specs, out_specs=out_specs, check_vma=False)
```

time: 268 us -> 105 us (0.39)
  blocking collectives: 81.4 us -> 0 us
  matrix products: 37.1 us -> 0 us
  other arithmetic: 27.3 us -> 0 us
  Pallas kernels: 0 us -> 26.2 us
  waiting for transfers between devices: 61.8 us -> 42.2 us
  between operations: 14.4 us -> 0.89 us
  local copies, waits for them, and re-layouts: 15.1 us -> 6.26 us
    psum x4 -> x0, blocking collectives: 81.4 us -> none  [the longest x2 76.5 us: shards(): space_sq = lax.psum(part_space, ('lon', 'lat'))]
    ppermute x8 -> x26, waiting for transfers between devices: 0.02 us -> 42.2 us  [the longest x24 42.2 us: across(): return lax.ppermute(value, axis, [(i, i ^ step) for i in range(peers)])]
    all_to_all x3 -> x0, waiting for transfers between devices: 41.7 us -> none  [the longest x1 35 us: shards(): lax.all_to_all(outgoing, 'lon', split_axis=0, concat_axis=0, tiled=True)]
    dot_general x14 -> x0, matrix products: 37.1 us -> none  [the longest x2 12.5 us: shards(): jnp.einsum('dr,brc->bdc', time_bf, factor_rows, preferred_element_type=jn...]
    pallas_call x0 -> x10, Pallas kernels: none -> 26.2 us  [run(): pl.pallas_call(kernel, out_shape=out_shape, in_specs=[pl.BlockSpec(memory...]
    psum x2 -> x0, waiting for transfers between devices: 20 us -> none  [shards(): grad_space = lax.psum(local_space, 'ta')]
    convert_element_type x9 -> x0, other arithmetic: 13.6 us -> none  [the longest x2 5.62 us: laplace(): extended(surface.astype(jnp.bfloat16), (('lon', 2),), 1, True)]
    all_to_all x3 -> x0, starting transfers between devices: 13.2 us -> none  [the longest x1 6.32 us: shards(): lax.all_to_all(onehot_out, 'lon', split_axis=0, concat_axis=0, tiled=True)]
  transfers between devices with their start and end apart: 13 -> 26, of which waited for: 5 -> 11; matrix products, arithmetic and copies ran while one was open for 21% -> 1% of each run, Pallas kernels for 0% -> 10%
where the time goes in v1:
time: 105 us; the launch traced here: 104 us
  waiting for transfers between devices  42.2 us (40%)
  starting transfers between devices  28.7 us (27%)
  Pallas kernels  26.2 us (25%)
  local copies, waits for them, and re-layouts  6.26 us (6%)
    ppermute x24, waiting for transfers between devices, across(): return lax.ppermute(value, axis, [(i, i ^ step) for i in range(peers)])  42.2 us
    ppermute x24, starting transfers between devices, across(): return lax.ppermute(value, axis, [(i, i ^ step) for i in range(peers)])  27.4 us
    pallas_call x10, Pallas kernels, run(): pl.pallas_call(kernel, out_shape=out_shape, in_specs=[pl.BlockSpec(memory...  26.2 us
    unnamed x50, local copies, waits for them, and re-layouts  4.85 us
  transfers between devices with their start and end apart: 26, of which 11 were waited for; matrix products, arithmetic and copies ran while one was open for 1% of the time, Pallas kernels for 10%

profile of v1, /device:TPU:0, one launch (start us, length us, event | category | flops | bytes accessed | tf_op | source)
XLA Modules:
  0.0 104.2 jit_solution(17316565139289835711)
XLA Ops:
  0.6 2.1 %shard_map.86 = (f32[96,1024]{1,0:T(8,128)}, f32[96,128]{1,0:T(8,128)}, f32[96,128]{1,0:T(8,128)}, f32[24,128]{1,0:T(8,128)}) custom-call(f32[1536,128]{1,0:T(8,128)} %bitcast.2), custom_call_target="tpu_custom_call" | custom-call | flops 1000000 | bytes 1000000 | tf_op jit(solution)/shard_map/pallas_call | solution.py:277
  3.4 4.4 %collective-permute-start.3 = (f32[64,96]{1,0:T(8,128)S(1)}, f32[64,96]{1,0:T(8,128)S(1)}, u32[]{:S(2)}, u32[]{:S(2)}) collective-permute-start(f32[64,96]{1,0:T(8,128)S(1)} %copy-done.20), channel_id=1, source_target_pairs={{0,1},{1,0},{2,3},{3,2},{4,5},{5,4},{6,7},{7,6},{8,9},{9,8},{10,11... | collective-permute-start | bytes 73736 | tf_op jit(solution)/shard_map/ppermute | solution.py:292
  7.8 3.6 %collective-permute-start.2 = (f32[24,128]{1,0:T(8,128)}, f32[24,128]{1,0:T(8,128)S(1)}, u32[]{:S(2)}, u32[]{:S(2)}) collective-permute-start(f32[24,128]{1,0:T(8,128)} %get-tuple-element.33), channel_id=1, source_target_pairs={{0,12},{4,8},{8,4},{12,0},{1,13},{5,9},{9,5},{13,1},{2,14},{6,10},... | collective-permute-start | bytes 36872 | tf_op jit(solution)/shard_map/ppermute | solution.py:292
  11.4 4.1 %shard_map.88 = (bf16[528,128]{1,0:T(8,128)(2,1)}, bf16[528,128]{1,0:T(8,128)(2,1)}, bf16[528,128]{1,0:T(8,128)(2,1)}, bf16[528,128]{1,0:T(8,128)(2,1)}, bf16[52...) custom-call(s32[1,4,32]{2,1,0:T(4,128)} %list_ref.1, ...), custom_call_target="tpu_custom_call" | custom-call | flops 1000000 | bytes 1000000 | tf_op jit(solution)/shard_map/pallas_call | solution.py:277
  15.5 2.0 %collective-permute-start.4 = (bf16[528,128]{1,0:T(8,128)(2,1)}, bf16[528,128]{1,0:T(8,128)(2,1)S(1)}, u32[]{:S(2)}, u32[]{:S(2)}) collective-permute-start(bf16[528,128]{1,0:T(8,128)(2,1)} %get-tuple-element.39), channel_id=1, source_target_pairs={{0,4},{4,0},{8,12},{12,8},{1,5},{5,1},{9,13},{13,9},{2,6},{6,2},{1... | collective-permute-start | bytes 405512 | tf_op jit(solution)/shard_map/ppermute | solution.py:292
  18.3 3.6 %collective-permute-done.4.rest_1_ = bf16[528,128]{1,0:T(8,128)(2,1)S(1)} collective-permute-done((bf16[528,128]{1,0:T(8,128)(2,1)}, bf16[528,128]{1,0:T(8,128)(2,1)S(1)}, u32[]{:S(2)}, u32[]{:S(2)}) %collective-permute-start.4) | collective-permute-done | bytes 135200 | tf_op jit(solution)/shard_map/ppermute | solution.py:292
  21.9 2.4 %collective-permute-start.6 = (bf16[528,128]{1,0:T(8,128)(2,1)}, bf16[528,128]{1,0:T(8,128)(2,1)S(1)}, u32[]{:S(2)}, u32[]{:S(2)}) collective-permute-start(bf16[528,128]{1,0:T(8,128)(2,1)} %get-tuple-element.41), channel_id=1, source_target_pairs={{0,12},{4,8},{8,4},{12,0},{1,13},{5,9},{9,5},{13,1},{2,14},{6,10},... | collective-permute-start | bytes 405512 | tf_op jit(solution)/shard_map/ppermute | solution.py:292
  24.3 5.6 %collective-permute-done.5.rest_2_ = bf16[528,128]{1,0:T(8,128)(2,1)S(1)} collective-permute-done((bf16[528,128]{1,0:T(8,128)(2,1)}, bf16[528,128]{1,0:T(8,128)(2,1)S(1)}, u32[]{:S(2)}, u32[]{:S(2)}) %collective-permute-start.5) | collective-permute-done | bytes 135200 | tf_op jit(solution)/shard_map/ppermute | solution.py:292
  30.2 4.3 %collective-permute-start.13 = (bf16[528,128]{1,0:T(8,128)(2,1)S(1)}, bf16[528,128]{1,0:T(8,128)(2,1)S(1)}, u32[]{:S(2)}, u32[]{:S(2)}) collective-permute-start(bf16[528,128]{1,0:T(8,128)(2,1)S(1)} %collective-permute-done.12), channel_id=1, source_target_pairs={{0,12},{4,8},{8,4},{12,0},{1,13},{5,9},{9,5},{13,1},{2,14},{6,10},... | collective-permute-start | bytes 405512 | tf_op jit(solution)/shard_map/ppermute | solution.py:292
  34.5 2.7 %shard_map.87 = (f32[96,1024]{1,0:T(8,128)}, f32[128,1024]{1,0:T(8,128)}, bf16[96,1024]{1,0:T(8,128)(2,1)}, f32[96,128]{1,0:T(8,128)}) custom-call(f32[96,1024]{1,0:T(8,128)} %get-tuple-element.30.refs_0_, f32[96,128]{1,0:T(8,128)} %get-tuple-element.31.refs_1_, f32[96,128]{1,0:T(8,128)} %copy-done.18, f32[24,128]{1,0:T(8,128)} %copy-done.23, ...), custom_call_target="tpu_custom_call" | custom-call | flops 1000000 | bytes 1000000 | tf_op jit(solution)/shard_map/pallas_call | solution.py:277
  37.2 6.1 %collective-permute-done.11.rest_6_ = bf16[528,128]{1,0:T(8,128)(2,1)S(1)} collective-permute-done((bf16[528,128]{1,0:T(8,128)(2,1)S(1)}, bf16[528,128]{1,0:T(8,128)(2,1)S(1)}, u32[]{:S(2)}, u32[]{:S(2)}) %collective-permute-start.11) | collective-permute-done | bytes 135200 | tf_op jit(solution)/shard_map/ppermute | solution.py:292
  44.0 3.8 %shard_map.89 = (f32[96,1024]{1,0:T(8,128)}, f32[216,128]{1,0:T(8,128)}, f32[312,128]{1,0:T(8,128)}, f32[96,128]{1,0:T(8,128)}, f32[128,1024]{1,0:T(8,128)}, /*index=5*/f32[16,128]{1,0:T(8,128)}) custom-call(f32[96,1024]{1,0:T(8,128)} %get-tuple-element.34.base, f32[128,1024]{1,0:T(8,128)} %get-tuple-element.35.predicted, ...), custom_call_target="tpu_custom_call" | custom-call | flops 1000000 | bytes 1000000 | tf_op jit(solution)/shard_map/pallas_call | solution.py:277
  47.8 1.6 %collective-permute-done.14.theirs = f32[312,128]{1,0:T(8,128)S(1)} collective-permute-done((f32[312,128]{1,0:T(8,128)}, f32[312,128]{1,0:T(8,128)S(1)}, u32[]{:S(2)}, u32[]{:S(2)}) %collective-permute-start.14) | collective-permute-done | bytes 159776 | tf_op jit(solution)/shard_map/ppermute | solution.py:292
  50.0 1.6 %shard_map.90.mine = f32[216,128]{1,0:T(8,128)} custom-call(f32[216,128]{1,0:T(8,128)} %get-tuple-element.51.mine, f32[312,128]{1,0:T(8,128)} %copy-done.3), custom_call_target="tpu_custom_call" | custom-call | flops 1000000 | bytes 1000000 | tf_op jit(solution)/shard_map/pallas_call | solution.py:277
  51.9 5.1 %collective-permute-done.16.theirs = f32[216,128]{1,0:T(8,128)S(1)} collective-permute-done((f32[216,128]{1,0:T(8,128)}, f32[216,128]{1,0:T(8,128)S(1)}, u32[]{:S(2)}, u32[]{:S(2)}) %collective-permute-start.16) | collective-permute-done | bytes 110624 | tf_op jit(solution)/shard_map/ppermute | solution.py:292
  57.6 1.6 %shard_map.91.refs_6_ = f32[216,128]{1,0:T(8,128)} custom-call(f32[216,128]{1,0:T(8,128)} %shard_map.90.mine, f32[216,128]{1,0:T(8,128)} %copy-done.15), custom_call_target="tpu_custom_call" | custom-call | flops 1000000 | bytes 1000000 | tf_op jit(solution)/shard_map/pallas_call | solution.py:277
  59.2 1.3 %collective-permute-start.19 = (f32[216,128]{1,0:T(8,128)}, f32[216,128]{1,0:T(8,128)S(1)}, u32[]{:S(2)}, u32[]{:S(2)}) collective-permute-start(f32[216,128]{1,0:T(8,128)} %shard_map.91.refs_6_), channel_id=1, source_target_pairs={{0,12},{4,8},{8,4},{12,0},{1,13},{5,9},{9,5},{13,1},{2,14},{6,10},... | collective-permute-start | bytes 331784 | tf_op jit(solution)/shard_map/ppermute | solution.py:292
  60.6 3.1 %collective-permute-start.18 = (f32[216,128]{1,0:T(8,128)}, f32[216,128]{1,0:T(8,128)S(1)}, u32[]{:S(2)}, u32[]{:S(2)}) collective-permute-start(f32[216,128]{1,0:T(8,128)} %shard_map.91.refs_6_), channel_id=1, source_target_pairs={{0,8},{4,12},{8,0},{12,4},{1,9},{5,13},{9,1},{13,5},{2,10},{6,14},... | collective-permute-start | bytes 331784 | tf_op jit(solution)/shard_map/ppermute | solution.py:292
  64.3 1.4 %slice.4.refs_4_ = f32[96,128]{1,0:T(8,128)} slice(f32[312,128]{1,0:T(8,128)} %copy-done.3), slice={[216:312], [0:128]} | slice | bytes 98304 | tf_op jit(solution)/shard_map/slice | solution.py:391
  65.7 1.6 %collective-permute-done.19.refs_9_.refs_11_ = f32[216,128]{1,0:T(8,128)S(1)} collective-permute-done((f32[216,128]{1,0:T(8,128)}, f32[216,128]{1,0:T(8,128)S(1)}, u32[]{:S(2)}, u32[]{:S(2)}) %collective-permute-start.19) | collective-permute-done | bytes 110624 | tf_op jit(solution)/shard_map/ppermute | solution.py:292
  67.3 5.3 %collective-permute-done.18.refs_8_ = f32[216,128]{1,0:T(8,128)S(1)} collective-permute-done((f32[216,128]{1,0:T(8,128)}, f32[216,128]{1,0:T(8,128)S(1)}, u32[]{:S(2)}, u32[]{:S(2)}) %collective-permute-start.18) | collective-permute-done | bytes 110624 | tf_op jit(solution)/shard_map/ppermute | solution.py:292
  73.3 4.2 %shard_map.92 = (f32[96,1024]{1,0:T(8,128)}, f32[96,128]{1,0:T(8,128)}, f32[216,128]{1,0:T(8,128)}, f32[312,128]{1,0:T(8,128)}, f32[96,128]{1,0:T(8,128)}) custom-call(f32[96,1024]{1,0:T(8,128)} %get-tuple-element.46.refs_0_, f32[96,128]{1,0:T(8,128)} %get-tuple-element.37.time_t.refs_1_, f32[128,1024]{1,0:T(8,128)} %get-tuple-element.47.refs_2_, ...), custom_call_target="tpu_custom_call" | custom-call | flops 1000000 | bytes 1000000 | tf_op jit(solution)/shard_map/pallas_call | solution.py:277
  78.0 1.7 %collective-permute-done.21.theirs = f32[312,128]{1,0:T(8,128)S(1)} collective-permute-done((f32[312,128]{1,0:T(8,128)}, f32[312,128]{1,0:T(8,128)S(1)}, u32[]{:S(2)}, u32[]{:S(2)}) %collective-permute-start.21) | collective-permute-done | bytes 159776 | tf_op jit(solution)/shard_map/ppermute | solution.py:292
  79.7 0.7 copy-done.4
  80.3 1.6 %shard_map.93.mine = f32[216,128]{1,0:T(8,128)} custom-call(f32[216,128]{1,0:T(8,128)} %get-tuple-element.54.mine, f32[312,128]{1,0:T(8,128)} %copy-done.4), custom_call_target="tpu_custom_call" | custom-call | flops 1000000 | bytes 1000000 | tf_op jit(solution)/shard_map/pallas_call | solution.py:277
  82.3 5.0 %collective-permute-done.22.theirs = f32[216,128]{1,0:T(8,128)S(1)} collective-permute-done((f32[216,128]{1,0:T(8,128)}, f32[216,128]{1,0:T(8,128)S(1)}, u32[]{:S(2)}, u32[]{:S(2)}) %collective-permute-start.22) | collective-permute-done | bytes 110624 | tf_op jit(solution)/shard_map/ppermute | solution.py:292
  87.9 1.6 %shard_map.94.rest_0_ = f32[216,128]{1,0:T(8,128)} custom-call(f32[216,128]{1,0:T(8,128)} %shard_map.93.mine, f32[216,128]{1,0:T(8,128)} %copy-done.16), custom_call_target="tpu_custom_call" | custom-call | flops 1000000 | bytes 1000000 | tf_op jit(solution)/shard_map/pallas_call | solution.py:277
  89.5 1.3 %collective-permute-start.25 = (f32[216,128]{1,0:T(8,128)}, f32[216,128]{1,0:T(8,128)S(1)}, u32[]{:S(2)}, u32[]{:S(2)}) collective-permute-start(f32[216,128]{1,0:T(8,128)} %shard_map.94.rest_0_), channel_id=1, source_target_pairs={{0,12},{4,8},{8,4},{12,0},{1,13},{5,9},{9,5},{13,1},{2,14},{6,10},... | collective-permute-start | bytes 331784 | tf_op jit(solution)/shard_map/ppermute | solution.py:292
  90.8 3.0 %collective-permute-start.23 = (f32[216,128]{1,0:T(8,128)}, f32[216,128]{1,0:T(8,128)S(1)}, u32[]{:S(2)}, u32[]{:S(2)}) collective-permute-start(f32[216,128]{1,0:T(8,128)} %shard_map.94.rest_0_), channel_id=1, source_target_pairs={{0,4},{4,0},{8,12},{12,8},{1,5},{5,1},{9,13},{13,9},{2,6},{6,2},{1... | collective-permute-start | bytes 331784 | tf_op jit(solution)/shard_map/ppermute | solution.py:292
  93.9 3.7 %collective-permute-done.25.rest_3_ = f32[216,128]{1,0:T(8,128)S(1)} collective-permute-done((f32[216,128]{1,0:T(8,128)}, f32[216,128]{1,0:T(8,128)S(1)}, u32[]{:S(2)}, u32[]{:S(2)}) %collective-permute-start.25) | collective-permute-done | bytes 110624 | tf_op jit(solution)/shard_map/ppermute | solution.py:292
  97.6 2.9 %collective-permute-done.24.rest_2_ = f32[216,128]{1,0:T(8,128)S(1)} collective-permute-done((f32[216,128]{1,0:T(8,128)}, f32[216,128]{1,0:T(8,128)S(1)}, u32[]{:S(2)}, u32[]{:S(2)}) %collective-permute-start.24) | collective-permute-done | bytes 110624 | tf_op jit(solution)/shard_map/ppermute | solution.py:292
  101.4 2.8 %shard_map.95 = (f32[1536,128]{1,0:T(8,128)}, f32[64,96]{1,0:T(8,128)}) custom-call(f32[96,1024]{1,0:T(8,128)} %get-tuple-element.52.surface, f32[96,1024]{1,0:T(8,128)} %copy-done.2, f32[96,128]{1,0:T(8,128)} %get-tuple-element.53.time_t, f32[216,128]{1,0:T(8,128)} %shard_map.94.rest_0_, f32[216,128]{1,0:T(8,128)} %copy-done.14, f32[216,128]{1,0:T(8,128)} %copy-done.13, ...), custom_call_target="tpu_custom_call" | custom-call | flops 1000000 | bytes 1000000 | tf_op jit(solution)/shard_map/pallas_call | solution.py:277
  (81 shorter events, 7.4 us)
Async XLA Ops:
  2.7 15.4 %collective-permute-start = (f32[96,128]{1,0:T(8,128)}, f32[96,128]{1,0:T(8,128)S(1)}, u32[]{:S(2)}, u32[]{:S(2)}) collective-permute-start(f32[96,128]{1,0:T(8,128)} %get-tuple-element.32), channel_id=1, source_target_pairs={{1,2},{2,1},{5,6},{6,5},{9,10},{10,9},{13,14},{14,13},{17,18},{18,... | collective-permute-start | bytes 147464 | tf_op jit(solution)/shard_map/ppermute | solution.py:323
  3.4 14.3 %collective-permute-start.3 = (f32[64,96]{1,0:T(8,128)S(1)}, f32[64,96]{1,0:T(8,128)S(1)}, u32[]{:S(2)}, u32[]{:S(2)}) collective-permute-start(f32[64,96]{1,0:T(8,128)S(1)} %copy-done.20), channel_id=1, source_target_pairs={{0,1},{1,0},{2,3},{3,2},{4,5},{5,4},{6,7},{7,6},{8,9},{9,8},{10,11... | collective-permute-start | bytes 73736 | tf_op jit(solution)/shard_map/ppermute | solution.py:292
  7.8 9.8 %collective-permute-start.2 = (f32[24,128]{1,0:T(8,128)}, f32[24,128]{1,0:T(8,128)S(1)}, u32[]{:S(2)}, u32[]{:S(2)}) collective-permute-start(f32[24,128]{1,0:T(8,128)} %get-tuple-element.33), channel_id=1, source_target_pairs={{0,12},{4,8},{8,4},{12,0},{1,13},{5,9},{9,5},{13,1},{2,14},{6,10},... | collective-permute-start | bytes 36872 | tf_op jit(solution)/shard_map/ppermute | solution.py:292
  11.4 6.2 %collective-permute-start.1 = (f32[24,128]{1,0:T(8,128)}, f32[24,128]{1,0:T(8,128)S(1)}, u32[]{:S(2)}, u32[]{:S(2)}) collective-permute-start(f32[24,128]{1,0:T(8,128)} %get-tuple-element.33), channel_id=1, source_target_pairs={{0,4},{4,0},{8,12},{12,8},{1,5},{5,1},{9,13},{13,9},{2,6},{6,2},{1... | collective-permute-start | bytes 36872 | tf_op jit(solution)/shard_map/ppermute | solution.py:292
  15.5 6.4 %collective-permute-start.4 = (bf16[528,128]{1,0:T(8,128)(2,1)}, bf16[528,128]{1,0:T(8,128)(2,1)S(1)}, u32[]{:S(2)}, u32[]{:S(2)}) collective-permute-start(bf16[528,128]{1,0:T(8,128)(2,1)} %get-tuple-element.39), channel_id=1, source_target_pairs={{0,4},{4,0},{8,12},{12,8},{1,5},{5,1},{9,13},{13,9},{2,6},{6,2},{1... | collective-permute-start | bytes 405512 | tf_op jit(solution)/shard_map/ppermute | solution.py:292
  17.6 16.9 %copy-start.22 = (f32[24,128]{1,0:T(8,128)}, f32[24,128]{1,0:T(8,128)S(1)}, u32[]{:S(2)}) copy-start(f32[24,128]{1,0:T(8,128)S(1)} %collective-permute-done.2.refs_4_) | copy-start | bytes 36868
  17.6 12.4 %collective-permute-start.5 = (bf16[528,128]{1,0:T(8,128)(2,1)}, bf16[528,128]{1,0:T(8,128)(2,1)S(1)}, u32[]{:S(2)}, u32[]{:S(2)}) collective-permute-start(bf16[528,128]{1,0:T(8,128)(2,1)} %get-tuple-element.40), channel_id=1, source_target_pairs={{0,8},{4,12},{8,0},{12,4},{1,9},{5,13},{9,1},{13,5},{2,10},{6,14},... | collective-permute-start | bytes 405512 | tf_op jit(solution)/shard_map/ppermute | solution.py:292
  17.6 16.9 %copy-start.23 = (f32[24,128]{1,0:T(8,128)}, f32[24,128]{1,0:T(8,128)S(1)}, u32[]{:S(2)}) copy-start(f32[24,128]{1,0:T(8,128)S(1)} %collective-permute-done.1.refs_3_) | copy-start | bytes 36868
  17.6 12.4 %collective-permute-start.8 = (bf16[528,128]{1,0:T(8,128)(2,1)}, bf16[528,128]{1,0:T(8,128)(2,1)S(1)}, u32[]{:S(2)}, u32[]{:S(2)}) collective-permute-start(bf16[528,128]{1,0:T(8,128)(2,1)} %get-tuple-element.43), channel_id=1, source_target_pairs={{0,1},{1,0},{2,3},{3,2},{4,5},{5,4},{6,7},{7,6},{8,9},{9,8},{10,11... | collective-permute-start | bytes 405512 | tf_op jit(solution)/shard_map/ppermute | solution.py:292
  17.7 16.8 %copy-start.21 = (f32[64,96]{1,0:T(8,128)}, f32[64,96]{1,0:T(8,128)S(1)}, u32[]{:S(2)}) copy-start(f32[64,96]{1,0:T(8,128)S(1)} %collective-permute-done.3.refs_6_) | copy-start | bytes 73732
  17.7 12.4 %collective-permute-start.10 = (bf16[528,128]{1,0:T(8,128)(2,1)}, bf16[528,128]{1,0:T(8,128)(2,1)S(1)}, u32[]{:S(2)}, u32[]{:S(2)}) collective-permute-start(bf16[528,128]{1,0:T(8,128)(2,1)} %get-tuple-element.44), channel_id=1, source_target_pairs={{0,1},{1,0},{2,3},{3,2},{4,5},{5,4},{6,7},{7,6},{8,9},{9,8},{10,11... | collective-permute-start | bytes 405512 | tf_op jit(solution)/shard_map/ppermute | solution.py:292
  18.2 16.3 %copy-start.18 = (f32[96,128]{1,0:T(8,128)}, f32[96,128]{1,0:T(8,128)S(1)}, u32[]{:S(2)}) copy-start(f32[96,128]{1,0:T(8,128)S(1)} %collective-permute-done.refs_2_) | copy-start | bytes 147460
  18.2 12.0 %collective-permute-start.12 = (bf16[528,128]{1,0:T(8,128)(2,1)}, bf16[528,128]{1,0:T(8,128)(2,1)S(1)}, u32[]{:S(2)}, u32[]{:S(2)}) collective-permute-start(bf16[528,128]{1,0:T(8,128)(2,1)} %get-tuple-element.45), channel_id=1, source_target_pairs={{0,1},{1,0},{2,3},{3,2},{4,5},{5,4},{6,7},{7,6},{8,9},{9,8},{10,11... | collective-permute-start | bytes 405512 | tf_op jit(solution)/shard_map/ppermute | solution.py:292
  21.9 15.2 %copy-start.5 = (bf16[528,128]{1,0:T(8,128)(2,1)}, bf16[528,128]{1,0:T(8,128)(2,1)S(1)}, u32[]{:S(2)}) copy-start(bf16[528,128]{1,0:T(8,128)(2,1)S(1)} %collective-permute-done.4.rest_1_) | copy-start | bytes 405508
  21.9 15.2 %collective-permute-start.6 = (bf16[528,128]{1,0:T(8,128)(2,1)}, bf16[528,128]{1,0:T(8,128)(2,1)S(1)}, u32[]{:S(2)}, u32[]{:S(2)}) collective-permute-start(bf16[528,128]{1,0:T(8,128)(2,1)} %get-tuple-element.41), channel_id=1, source_target_pairs={{0,12},{4,8},{8,4},{12,0},{1,13},{5,9},{9,5},{13,1},{2,14},{6,10},... | collective-permute-start | bytes 405512 | tf_op jit(solution)/shard_map/ppermute | solution.py:292
  30.0 7.2 %collective-permute-start.7 = (bf16[528,128]{1,0:T(8,128)(2,1)}, bf16[528,128]{1,0:T(8,128)(2,1)S(1)}, u32[]{:S(2)}, u32[]{:S(2)}) collective-permute-start(bf16[528,128]{1,0:T(8,128)(2,1)} %get-tuple-element.42), channel_id=1, source_target_pairs={{0,1},{1,0},{2,3},{3,2},{4,5},{5,4},{6,7},{7,6},{8,9},{9,8},{10,11... | collective-permute-start | bytes 405512 | tf_op jit(solution)/shard_map/ppermute | solution.py:292
  30.0 7.2 %collective-permute-start.9 = (bf16[528,128]{1,0:T(8,128)(2,1)S(1)}, bf16[528,128]{1,0:T(8,128)(2,1)S(1)}, u32[]{:S(2)}, u32[]{:S(2)}) collective-permute-start(bf16[528,128]{1,0:T(8,128)(2,1)S(1)} %collective-permute-done.8), channel_id=1, source_target_pairs={{0,4},{4,0},{8,12},{12,8},{1,5},{5,1},{9,13},{13,9},{2,6},{6,2},{1... | collective-permute-start | bytes 405512 | tf_op jit(solution)/shard_map/ppermute | solution.py:292
  30.1 13.2 %collective-permute-start.11 = (bf16[528,128]{1,0:T(8,128)(2,1)S(1)}, bf16[528,128]{1,0:T(8,128)(2,1)S(1)}, u32[]{:S(2)}, u32[]{:S(2)}) collective-permute-start(bf16[528,128]{1,0:T(8,128)(2,1)S(1)} %collective-permute-done.10), channel_id=1, source_target_pairs={{0,8},{4,12},{8,0},{12,4},{1,9},{5,13},{9,1},{13,5},{2,10},{6,14},... | collective-permute-start | bytes 405512 | tf_op jit(solution)/shard_map/ppermute | solution.py:292
  30.2 13.1 %collective-permute-start.13 = (bf16[528,128]{1,0:T(8,128)(2,1)S(1)}, bf16[528,128]{1,0:T(8,128)(2,1)S(1)}, u32[]{:S(2)}, u32[]{:S(2)}) collective-permute-start(bf16[528,128]{1,0:T(8,128)(2,1)S(1)} %collective-permute-done.12), channel_id=1, source_target_pairs={{0,12},{4,8},{8,4},{12,0},{1,13},{5,9},{9,5},{13,1},{2,14},{6,10},... | collective-permute-start | bytes 405512 | tf_op jit(solution)/shard_map/ppermute | solution.py:292
  47.8 1.6 %collective-permute-start.14 = (f32[312,128]{1,0:T(8,128)}, f32[312,128]{1,0:T(8,128)S(1)}, u32[]{:S(2)}, u32[]{:S(2)}) collective-permute-start(f32[312,128]{1,0:T(8,128)} %get-tuple-element.49), channel_id=1, source_target_pairs={{0,1},{1,0},{2,3},{3,2},{4,5},{5,4},{6,7},{7,6},{8,9},{9,8},{10,11... | collective-permute-start | bytes 479240 | tf_op jit(solution)/shard_map/ppermute | solution.py:292
  51.7 12.0 %copy-start.24 = (f32[96,128]{1,0:T(8,128)S(1)}, f32[96,128]{1,0:T(8,128)}, u32[]{:S(2)}) copy-start(f32[96,128]{1,0:T(8,128)} %get-tuple-element.50) | copy-start | bytes 147460
  51.7 5.3 %collective-permute-start.16 = (f32[216,128]{1,0:T(8,128)}, f32[216,128]{1,0:T(8,128)S(1)}, u32[]{:S(2)}, u32[]{:S(2)}) collective-permute-start(f32[216,128]{1,0:T(8,128)} %shard_map.90.mine), channel_id=1, source_target_pairs={{0,2},{2,0},{1,3},{3,1},{4,6},{6,4},{5,7},{7,5},{8,10},{10,8},{9,1... | collective-permute-start | bytes 331784 | tf_op jit(solution)/shard_map/ppermute | solution.py:292
  59.2 8.1 %collective-permute-start.19 = (f32[216,128]{1,0:T(8,128)}, f32[216,128]{1,0:T(8,128)S(1)}, u32[]{:S(2)}, u32[]{:S(2)}) collective-permute-start(f32[216,128]{1,0:T(8,128)} %shard_map.91.refs_6_), channel_id=1, source_target_pairs={{0,12},{4,8},{8,4},{12,0},{1,13},{5,9},{9,5},{13,1},{2,14},{6,10},... | collective-permute-start | bytes 331784 | tf_op jit(solution)/shard_map/ppermute | solution.py:292
  60.6 12.1 %collective-permute-start.18 = (f32[216,128]{1,0:T(8,128)}, f32[216,128]{1,0:T(8,128)S(1)}, u32[]{:S(2)}, u32[]{:S(2)}) collective-permute-start(f32[216,128]{1,0:T(8,128)} %shard_map.91.refs_6_), channel_id=1, source_target_pairs={{0,8},{4,12},{8,0},{12,4},{1,9},{5,13},{9,1},{13,5},{2,10},{6,14},... | collective-permute-start | bytes 331784 | tf_op jit(solution)/shard_map/ppermute | solution.py:292
  63.6 9.0 %collective-permute-start.17 = (f32[216,128]{1,0:T(8,128)}, f32[216,128]{1,0:T(8,128)S(1)}, u32[]{:S(2)}, u32[]{:S(2)}) collective-permute-start(f32[216,128]{1,0:T(8,128)} %shard_map.91.refs_6_), channel_id=1, source_target_pairs={{0,4},{4,0},{8,12},{12,8},{1,5},{5,1},{9,13},{13,9},{2,6},{6,2},{1... | collective-permute-start | bytes 331784 | tf_op jit(solution)/shard_map/ppermute | solution.py:292
  63.6 2.1 %collective-permute-start.15 = (f32[96,128]{1,0:T(8,128)S(1)}, f32[96,128]{1,0:T(8,128)S(1)}, u32[]{:S(2)}, u32[]{:S(2)}) collective-permute-start(f32[96,128]{1,0:T(8,128)S(1)} %copy-done.24), channel_id=1, source_target_pairs={{1,2},{2,1},{5,6},{6,5},{9,10},{10,9},{13,14},{14,13},{17,18},{18,... | collective-permute-start | bytes 147464 | tf_op jit(solution)/shard_map/ppermute | solution.py:323
  77.5 23.0 %collective-permute-start.20 = (f32[96,1024]{1,0:T(8,128)}, f32[96,1024]{1,0:T(8,128)S(1)}, u32[]{:S(2)}, u32[]{:S(2)}) collective-permute-start(f32[96,1024]{1,0:T(8,128)} %get-tuple-element.52.surface), channel_id=1, source_target_pairs={{0,1},{1,0},{2,3},{3,2},{4,5},{5,4},{6,7},{7,6},{8,9},{9,8},{10,11... | collective-permute-start | bytes 1179656 | tf_op jit(solution)/shard_map/ppermute | solution.py:292
  77.5 2.2 %collective-permute-start.21 = (f32[312,128]{1,0:T(8,128)}, f32[312,128]{1,0:T(8,128)S(1)}, u32[]{:S(2)}, u32[]{:S(2)}) collective-permute-start(f32[312,128]{1,0:T(8,128)} %get-tuple-element.55), channel_id=1, source_target_pairs={{0,1},{1,0},{2,3},{3,2},{4,5},{5,4},{6,7},{7,6},{8,9},{9,8},{10,11... | collective-permute-start | bytes 479240 | tf_op jit(solution)/shard_map/ppermute | solution.py:292
  81.9 5.3 %collective-permute-start.22 = (f32[216,128]{1,0:T(8,128)}, f32[216,128]{1,0:T(8,128)S(1)}, u32[]{:S(2)}, u32[]{:S(2)}) collective-permute-start(f32[216,128]{1,0:T(8,128)} %shard_map.93.mine), channel_id=1, source_target_pairs={{0,2},{2,0},{1,3},{3,1},{4,6},{6,4},{5,7},{7,5},{8,10},{10,8},{9,1... | collective-permute-start | bytes 331784 | tf_op jit(solution)/shard_map/ppermute | solution.py:292
  89.5 8.1 %collective-permute-start.25 = (f32[216,128]{1,0:T(8,128)}, f32[216,128]{1,0:T(8,128)S(1)}, u32[]{:S(2)}, u32[]{:S(2)}) collective-permute-start(f32[216,128]{1,0:T(8,128)} %shard_map.94.rest_0_), channel_id=1, source_target_pairs={{0,12},{4,8},{8,4},{12,0},{1,13},{5,9},{9,5},{13,1},{2,14},{6,10},... | collective-permute-start | bytes 331784 | tf_op jit(solution)/shard_map/ppermute | solution.py:292
  90.8 9.7 %collective-permute-start.24 = (f32[216,128]{1,0:T(8,128)}, f32[216,128]{1,0:T(8,128)S(1)}, u32[]{:S(2)}, u32[]{:S(2)}) collective-permute-start(f32[216,128]{1,0:T(8,128)} %shard_map.94.rest_0_), channel_id=1, source_target_pairs={{0,8},{4,12},{8,0},{12,4},{1,9},{5,13},{9,1},{13,5},{2,10},{6,14},... | collective-permute-start | bytes 331784 | tf_op jit(solution)/shard_map/ppermute | solution.py:292
  90.8 9.7 %collective-permute-start.23 = (f32[216,128]{1,0:T(8,128)}, f32[216,128]{1,0:T(8,128)S(1)}, u32[]{:S(2)}, u32[]{:S(2)}) collective-permute-start(f32[216,128]{1,0:T(8,128)} %shard_map.94.rest_0_), channel_id=1, source_target_pairs={{0,4},{4,0},{8,12},{12,8},{1,5},{5,1},{9,13},{13,9},{2,6},{6,2},{1... | collective-permute-start | bytes 331784 | tf_op jit(solution)/shard_map/ppermute | solution.py:292
  (19 other events, 50.9 us)

commit v2 on v1

--- a/solution.py
+++ b/solution.py
@@ -1,4 +1,5 @@
 import functools
+import math
 
 import jax
 import jax.numpy as jnp
@@ -18,7 +19,7 @@
 TAIL = 16
 COLS = 16
 NORM = 8
-VMEM_LIMIT = 56 * 1024 * 1024
+SPARE = 2 * 1024 * 1024
 
 
 def dot(a, b, contract):
@@ -95,7 +96,7 @@
     return strips
 
 
-def prepare_kernel(half, space_ref, surface, edge_near, edge_far, cols, flip):
+def prepare_kernel(half, space_ref, time_ref, after, surface, edge_near, edge_far, cols, time_own, flip):
     core = lax.axis_index("ta")
     rank = surface.shape[0]
     height = space_ref.shape[0] // rank
@@ -104,6 +105,7 @@
     edge_near[...] = space_ref[pl.ds(half - core, rank, stride=height), :]
     edge_far[...] = space_ref[pl.ds(core * (height - 1), rank, stride=height), :]
     cols[...] = columns_as_rows(surface[...], half, flip, None)
+    time_own[...] = time_ref[...]
 
 
 def pick(flag, a, b):
@@ -272,15 +274,22 @@
     return jax.ShapeDtypeStruct(tuple(dims), dtype)
 
 
-def call(kernel, out_shape, scratch=(), smem=0, flops=1_000_000):
+def padded(ref):
+    *outer, rows, lanes = (1, *ref.shape)
+    return math.prod(outer) * -(-rows // 16) * 16 * -(-lanes // LANES) * LANES * jnp.dtype(ref.dtype).itemsize
+
+
+def call(kernel, out_shape, scratch=(), smem=0, after=0, flops=1_000_000):
     def run(*operands):
+        vmem = [*operands[smem:len(operands) - after], *jax.tree.leaves(out_shape), *scratch]
+        specs = [pltpu.SMEM] * smem + [pltpu.VMEM] * (len(operands) - smem - after) + [pl.ANY] * after
         return pl.pallas_call(
             kernel,
             out_shape=out_shape,
-            in_specs=[pl.BlockSpec(memory_space=pltpu.SMEM)] * smem + [pl.BlockSpec(memory_space=pltpu.VMEM)] * (len(operands) - smem),
+            in_specs=[pl.BlockSpec(memory_space=space) for space in specs],
             out_specs=jax.tree.map(lambda _: pl.BlockSpec(memory_space=pltpu.VMEM), out_shape),
             scratch_shapes=list(scratch),
-            compiler_params=pltpu.CompilerParams(vmem_limit_bytes=VMEM_LIMIT),
+            compiler_params=pltpu.CompilerParams(vmem_limit_bytes=SPARE + sum(padded(ref) for ref in vmem if len(ref.shape) > 1)),
             cost_estimate=pl.CostEstimate(flops=flops, bytes_accessed=1_000_000, transcendentals=0),
         )(*operands)
 
@@ -288,8 +297,7 @@
 
 
 def across(value, axis, step):
-    peers = lax.axis_size(axis)
-    return lax.ppermute(value, axis, [(i, i ^ step) for i in range(peers)])
+    return lax.ppermute(value, axis, [(i, i ^ step) for i in range(lax.axis_size(axis))])
 
 
 def shards(swath, obs_mask, target, send_list, send_count, factor_space, factor_time):
@@ -309,14 +317,11 @@
         smem=3,
     )(send_list, send_count, target, swath, obs_mask)
     near, far = pieces[:n_lon], pieces[n_lon:]
-    order = sorted(range(1, n_lon), key=lambda step: (-((step + 1) // 2), step))
-    near_in = {0: near[0]}
-    for step in order:
-        near_in[step] = across(near[step], "lon", step)
-    far = [across(piece, "ta", 1) for piece in far]
-    far_in = {0: far[0]}
-    for step in order:
-        far_in[step] = across(far[step], "lon", step)
+    near_in, far_in = {0: near[0]}, {}
+    for step in (*range(n_lon // 2, n_lon), *range(n_lon // 2)):
+        if step:
+            near_in[step] = across(near[step], "lon", step)
+        far_in[step] = across(far[step], ("lon", "ta"), 2 * step + 1)
 
     def bands(edge):
         there = [(2 * band + 1, 2 * band + 2) for band in range(n_lat - 1)]
@@ -333,11 +338,12 @@
         ring = [(i, (i + 1) % n_lon) for i in range(n_lon)]
         return lax.ppermute(value, "lon", ring), lax.ppermute(value, "lon", [(b, a) for a, b in ring])
 
-    surface, edge_near, edge_far, cols = call(
+    surface, edge_near, edge_far, cols, time_own = call(
         functools.partial(prepare_kernel, half),
-        [shape((rank, wide)), shape((rank, LANES)), shape((rank, LANES)), shape((COLS + NORM, LANES))],
+        [shape((rank, wide)), shape((rank, LANES)), shape((rank, LANES)), shape((COLS + NORM, LANES)), shape(factor_time.shape)],
         [flip],
-    )(factor_space.reshape(rank * height, cells))
+        after=1,
+    )(factor_space.reshape(rank * height, cells), factor_time, near[0])
     cols_a, cols_b = columns(cols)
 
     def model(*refs):
@@ -347,7 +353,7 @@
         model,
         [shape((rank, wide)), shape((2 * days, wide)), shape((rank, wide), BF16), shape((rank, LANES))],
         [flip, flip],
-    )(surface, edge_near, bands(edge_far), cols_a, cols_b, factor_time, across(factor_time, "ta", 1))
+    )(surface, edge_near, bands(edge_far), cols_a, cols_b, time_own, across(time_own, "ta", 1))
 
     step_out = [shape((rank, wide)), shape((message_rows, LANES)), shape((message_rows + rank, LANES)), shape((rank, LANES))]
     surface, message, outgoing, edge_far, summed, seen = call(

time: 105 us -> 84.5 us (0.80)
  Pallas kernels: 26.2 us -> 9.07 us
  local copies, waits for them, and re-layouts: 6.26 us -> 3.98 us
    pallas_call x10, Pallas kernels: 26.2 us -> 9.07 us  [run(): pl.pallas_call(kernel, out_shape=out_shape, in_specs=[pl.BlockSpec(memory...]
    slice x1, local copies, waits for them, and re-layouts: 1.41 us -> 0.01 us  [shards(): beside[message_rows:]]
    unnamed x50 -> x14, local copies, waits for them, and re-layouts: 4.85 us -> 3.97 us
    ppermute x24 -> x21, starting transfers between devices: 27.4 us -> 26.7 us  [across(): lax.ppermute(value, axis, [(i, i ^ step) for i in range(lax.axis_size(axi...]
    ppermute x24 -> x21, waiting for transfers between devices: 42.2 us -> 42.4 us  [across(): lax.ppermute(value, axis, [(i, i ^ step) for i in range(lax.axis_size(axi...]
  transfers between devices with their start and end apart: 26 -> 23, of which waited for: 11 -> 13; matrix products, arithmetic and copies ran while one was open for 1% -> 0% of each run, Pallas kernels for 10% -> 1%
where the time goes in v2:
time: 84.5 us; the launch traced here: 84.2 us
  waiting for transfers between devices  42.4 us (50%)
  starting transfers between devices  28 us (33%)
  Pallas kernels  9.07 us (11%)
  local copies, waits for them, and re-layouts  3.98 us (5%)
    ppermute x21, waiting for transfers between devices, across(): lax.ppermute(value, axis, [(i, i ^ step) for i in range(lax.axis_size(axi...  42.4 us
    ppermute x21, starting transfers between devices, across(): lax.ppermute(value, axis, [(i, i ^ step) for i in range(lax.axis_size(axi...  26.7 us
    pallas_call x10, Pallas kernels, run(): pl.pallas_call(kernel, out_shape=out_shape, in_specs=[pl.BlockSpec(memory...  9.07 us
    unnamed x14, local copies, waits for them, and re-layouts  3.97 us
  transfers between devices with their start and end apart: 23, of which 13 were waited for; matrix products, arithmetic and copies ran while one was open for 0% of the time, Pallas kernels for 1%

profile of v2, /device:TPU:0, one launch (start us, length us, event | category | flops | bytes accessed | tf_op | source)
XLA Modules:
  0.0 84.2 jit_solution(1967500221942371326)
XLA Ops:
  0.6 1.2 %copy-done = bf16[64,64,128]{2,1,0:T(8,128)(2,1)S(1)} copy-done((bf16[64,64,128]{2,1,0:T(8,128)(2,1)S(1)}, bf16[64,64,128]{2,1,0:T(8,128)(2,1)}, u32[]{:S(2)}) %copy-start) | copy-done | bytes 1048600
  1.9 0.8 copy-done.2
  4.6 2.6 %shard_map.86 = (bf16[528,128]{1,0:T(8,128)(2,1)S(1)}, bf16[528,128]{1,0:T(8,128)(2,1)S(1)}, bf16[528,128]{1,0:T(8,128)(2,1)S(1)}, bf16[528,128]{1,0:T(8,128)(2,...) custom-call(s32[1,4,32]{2,1,0:T(4,128)S(1)} %copy-done.4, ...), custom_call_target="tpu_custom_call" | custom-call | flops 1000000 | bytes 1000000 | tf_op jit(solution)/shard_map/pallas_call | solution.py:286
  7.3 3.1 %collective-permute-start.4 = (bf16[528,128]{1,0:T(8,128)(2,1)S(1)}, bf16[528,128]{1,0:T(8,128)(2,1)S(1)}, u32[]{:S(2)}, u32[]{:S(2)}) collective-permute-start(bf16[528,128]{1,0:T(8,128)(2,1)S(1)} %get-tuple-element.41), channel_id=1, source_target_pairs={{0,4},{4,0},{8,12},{12,8},{1,5},{5,1},{9,13},{13,9},{2,6},{6,2},{1... | collective-permute-start | bytes 405512 | tf_op jit(solution)/shard_map/ppermute | solution.py:300
  10.4 2.6 %collective-permute-start.5 = (bf16[528,128]{1,0:T(8,128)(2,1)S(1)}, bf16[528,128]{1,0:T(8,128)(2,1)S(1)}, u32[]{:S(2)}, u32[]{:S(2)}) collective-permute-start(bf16[528,128]{1,0:T(8,128)(2,1)S(1)} %get-tuple-element.42), channel_id=1, source_target_pairs={{0,8},{4,12},{8,0},{12,4},{1,9},{5,13},{9,1},{13,5},{2,10},{6,14},... | collective-permute-start | bytes 405512 | tf_op jit(solution)/shard_map/ppermute | solution.py:300
  14.1 2.9 %collective-permute-start.3 = (f32[64,96]{1,0:T(8,128)S(1)}, f32[64,96]{1,0:T(8,128)S(1)}, u32[]{:S(2)}, u32[]{:S(2)}) collective-permute-start(f32[64,96]{1,0:T(8,128)S(1)} %get-tuple-element.36.refs_5_), channel_id=1, source_target_pairs={{0,1},{1,0},{2,3},{3,2},{4,5},{5,4},{6,7},{7,6},{8,9},{9,8},{10,11... | collective-permute-start | bytes 73736 | tf_op jit(solution)/shard_map/ppermute | solution.py:300
  17.0 2.6 %collective-permute-done.2.refs_4_ = f32[24,128]{1,0:T(8,128)S(1)} collective-permute-done((f32[24,128]{1,0:T(8,128)S(1)}, f32[24,128]{1,0:T(8,128)S(1)}, u32[]{:S(2)}, u32[]{:S(2)}) %collective-permute-start.2) | collective-permute-done | bytes 12320 | tf_op jit(solution)/shard_map/ppermute | solution.py:300
  19.9 3.3 %collective-permute-done.1.refs_3_ = f32[24,128]{1,0:T(8,128)S(1)} collective-permute-done((f32[24,128]{1,0:T(8,128)S(1)}, f32[24,128]{1,0:T(8,128)S(1)}, u32[]{:S(2)}, u32[]{:S(2)}) %collective-permute-start.1) | collective-permute-done | bytes 12320 | tf_op jit(solution)/shard_map/ppermute | solution.py:300
  23.3 1.2 %collective-permute-start.6 = (bf16[528,128]{1,0:T(8,128)(2,1)S(1)}, bf16[528,128]{1,0:T(8,128)(2,1)S(1)}, u32[]{:S(2)}, u32[]{:S(2)}) collective-permute-start(bf16[528,128]{1,0:T(8,128)(2,1)S(1)} %get-tuple-element.43), channel_id=1, source_target_pairs={{0,12},{4,8},{8,4},{12,0},{1,13},{5,9},{9,5},{13,1},{2,14},{6,10},... | collective-permute-start | bytes 405512 | tf_op jit(solution)/shard_map/ppermute | solution.py:300
  24.5 1.2 %collective-permute-start.8 = (bf16[528,128]{1,0:T(8,128)(2,1)S(1)}, bf16[528,128]{1,0:T(8,128)(2,1)S(1)}, u32[]{:S(2)}, u32[]{:S(2)}) collective-permute-start(bf16[528,128]{1,0:T(8,128)(2,1)S(1)} %get-tuple-element.45), channel_id=1, source_target_pairs={{0,5},{1,4},{4,1},{5,0},{8,13},{9,12},{12,9},{13,8},{2,7},{3,6},{6... | collective-permute-start | bytes 405512 | tf_op jit(solution)/shard_map/ppermute | solution.py:300
  25.7 1.9 %collective-permute-start.9 = (bf16[528,128]{1,0:T(8,128)(2,1)S(1)}, bf16[528,128]{1,0:T(8,128)(2,1)S(1)}, u32[]{:S(2)}, u32[]{:S(2)}) collective-permute-start(bf16[528,128]{1,0:T(8,128)(2,1)S(1)} %get-tuple-element.46), channel_id=1, source_target_pairs={{0,9},{1,8},{4,13},{5,12},{8,1},{9,0},{12,5},{13,4},{2,11},{3,10},... | collective-permute-start | bytes 405512 | tf_op jit(solution)/shard_map/ppermute | solution.py:300
  27.7 1.1 %collective-permute-start.10 = (bf16[528,128]{1,0:T(8,128)(2,1)S(1)}, bf16[528,128]{1,0:T(8,128)(2,1)S(1)}, u32[]{:S(2)}, u32[]{:S(2)}) collective-permute-start(bf16[528,128]{1,0:T(8,128)(2,1)S(1)} %get-tuple-element.47), channel_id=1, source_target_pairs={{0,13},{1,12},{4,9},{5,8},{8,5},{9,4},{12,1},{13,0},{2,15},{3,14},... | collective-permute-start | bytes 405512 | tf_op jit(solution)/shard_map/ppermute | solution.py:300
  29.4 2.1 %collective-permute-done.6.rest_3_ = bf16[528,128]{1,0:T(8,128)(2,1)S(1)} collective-permute-done((bf16[528,128]{1,0:T(8,128)(2,1)S(1)}, bf16[528,128]{1,0:T(8,128)(2,1)S(1)}, u32[]{:S(2)}, u32[]{:S(2)}) %collective-permute-start.6) | collective-permute-done | bytes 135200 | tf_op jit(solution)/shard_map/ppermute | solution.py:300
  31.5 3.5 %collective-permute-done.8.rest_5_ = bf16[528,128]{1,0:T(8,128)(2,1)S(1)} collective-permute-done((bf16[528,128]{1,0:T(8,128)(2,1)S(1)}, bf16[528,128]{1,0:T(8,128)(2,1)S(1)}, u32[]{:S(2)}, u32[]{:S(2)}) %collective-permute-start.8) | collective-permute-done | bytes 135200 | tf_op jit(solution)/shard_map/ppermute | solution.py:300
  35.0 5.2 %collective-permute-done.9.rest_6_ = bf16[528,128]{1,0:T(8,128)(2,1)S(1)} collective-permute-done((bf16[528,128]{1,0:T(8,128)(2,1)S(1)}, bf16[528,128]{1,0:T(8,128)(2,1)S(1)}, u32[]{:S(2)}, u32[]{:S(2)}) %collective-permute-start.9) | collective-permute-done | bytes 135200 | tf_op jit(solution)/shard_map/ppermute | solution.py:300
  40.2 1.5 %shard_map.89 = (f32[96,1024]{1,0:T(8,128)S(1)}, f32[216,128]{1,0:T(8,128)S(1)}, f32[312,128]{1,0:T(8,128)S(1)}, f32[96,128]{1,0:T(8,128)S(1)}, f32[128,1024]{1,0:T(8,128)S(1)}, /*index=5*/f32[16,128]{1,0:T(8,128)S(1)}) custom-call(f32[96,1024]{1,0:T(8,128)S(1)} %get-tuple-element.37.base, f32[128,1024]{1,0:T(8,128)S(1)} %get-tuple-element.38.predicted, ...), custom_call_target="tpu_custom_call" | custom-call | flops 1000000 | bytes 1000000 | tf_op jit(solution)/shard_map/pallas_call | solution.py:286
  42.4 1.0 %collective-permute-done.11.theirs = f32[312,128]{1,0:T(8,128)S(1)} collective-permute-done((f32[312,128]{1,0:T(8,128)S(1)}, f32[312,128]{1,0:T(8,128)S(1)}, u32[]{:S(2)}, u32[]{:S(2)}) %collective-permute-start.11) | collective-permute-done | bytes 159776 | tf_op jit(solution)/shard_map/ppermute | solution.py:300
  43.4 1.0 %collective-permute-start.13 = (f32[216,128]{1,0:T(8,128)S(1)}, f32[216,128]{1,0:T(8,128)S(1)}, u32[]{:S(2)}, u32[]{:S(2)}) collective-permute-start(f32[216,128]{1,0:T(8,128)S(1)} %shard_map.90.mine), channel_id=1, source_target_pairs={{0,2},{2,0},{1,3},{3,1},{4,6},{6,4},{5,7},{7,5},{8,10},{10,8},{9,1... | collective-permute-start | bytes 331784 | tf_op jit(solution)/shard_map/ppermute | solution.py:300
  44.4 4.4 %collective-permute-done.13.theirs = f32[216,128]{1,0:T(8,128)S(1)} collective-permute-done((f32[216,128]{1,0:T(8,128)S(1)}, f32[216,128]{1,0:T(8,128)S(1)}, u32[]{:S(2)}, u32[]{:S(2)}) %collective-permute-start.13) | collective-permute-done | bytes 110624 | tf_op jit(solution)/shard_map/ppermute | solution.py:300
  48.8 2.2 %collective-permute-start.16 = (f32[216,128]{1,0:T(8,128)S(1)}, f32[216,128]{1,0:T(8,128)S(1)}, u32[]{:S(2)}, u32[]{:S(2)}) collective-permute-start(f32[216,128]{1,0:T(8,128)S(1)} %shard_map.91.refs_6_), channel_id=1, source_target_pairs={{0,12},{4,8},{8,4},{12,0},{1,13},{5,9},{9,5},{13,1},{2,14},{6,10},... | collective-permute-start | bytes 331784 | tf_op jit(solution)/shard_map/ppermute | solution.py:300
  51.1 2.3 %collective-permute-start.15 = (f32[216,128]{1,0:T(8,128)S(1)}, f32[216,128]{1,0:T(8,128)S(1)}, u32[]{:S(2)}, u32[]{:S(2)}) collective-permute-start(f32[216,128]{1,0:T(8,128)S(1)} %shard_map.91.refs_6_), channel_id=1, source_target_pairs={{0,8},{4,12},{8,0},{12,4},{1,9},{5,13},{9,1},{13,5},{2,10},{6,14},... | collective-permute-start | bytes 331784 | tf_op jit(solution)/shard_map/ppermute | solution.py:300
  54.1 2.3 %collective-permute-done.16.refs_9_.refs_11_ = f32[216,128]{1,0:T(8,128)S(1)} collective-permute-done((f32[216,128]{1,0:T(8,128)S(1)}, f32[216,128]{1,0:T(8,128)S(1)}, u32[]{:S(2)}, u32[]{:S(2)}) %collective-permute-start.16) | collective-permute-done | bytes 110624 | tf_op jit(solution)/shard_map/ppermute | solution.py:300
  56.3 6.0 %collective-permute-done.15.refs_8_ = f32[216,128]{1,0:T(8,128)S(1)} collective-permute-done((f32[216,128]{1,0:T(8,128)S(1)}, f32[216,128]{1,0:T(8,128)S(1)}, u32[]{:S(2)}, u32[]{:S(2)}) %collective-permute-start.15) | collective-permute-done | bytes 110624 | tf_op jit(solution)/shard_map/ppermute | solution.py:300
  62.3 2.3 %shard_map.92 = (f32[96,1024]{1,0:T(8,128)S(1)}, f32[96,128]{1,0:T(8,128)S(1)}, f32[216,128]{1,0:T(8,128)S(1)}, f32[312,128]{1,0:T(8,128)S(1)}, f32[96,128]{1,0:T(8,128)}) custom-call(f32[96,1024]{1,0:T(8,128)S(1)} %get-tuple-element.48.refs_0_, f32[96,128]{1,0:T(8,128)S(1)} %get-tuple-element.40.time_t.refs_1_, f32[128,1024]{1,0:T(8,128)S(1)} %get-tuple-element.49.refs_2_, ...), custom_call_target="tpu_custom_call" | custom-call | flops 1000000 | bytes 1000000 | tf_op jit(solution)/shard_map/pallas_call | solution.py:286
  65.1 1.4 %collective-permute-done.18.theirs = f32[312,128]{1,0:T(8,128)S(1)} collective-permute-done((f32[312,128]{1,0:T(8,128)S(1)}, f32[312,128]{1,0:T(8,128)S(1)}, u32[]{:S(2)}, u32[]{:S(2)}) %collective-permute-start.18) | collective-permute-done | bytes 159776 | tf_op jit(solution)/shard_map/ppermute | solution.py:300
  66.6 1.0 %collective-permute-start.19 = (f32[216,128]{1,0:T(8,128)S(1)}, f32[216,128]{1,0:T(8,128)S(1)}, u32[]{:S(2)}, u32[]{:S(2)}) collective-permute-start(f32[216,128]{1,0:T(8,128)S(1)} %shard_map.93.mine), channel_id=1, source_target_pairs={{0,2},{2,0},{1,3},{3,1},{4,6},{6,4},{5,7},{7,5},{8,10},{10,8},{9,1... | collective-permute-start | bytes 331784 | tf_op jit(solution)/shard_map/ppermute | solution.py:300
  67.6 4.2 %collective-permute-done.19.theirs = f32[216,128]{1,0:T(8,128)S(1)} collective-permute-done((f32[216,128]{1,0:T(8,128)S(1)}, f32[216,128]{1,0:T(8,128)S(1)}, u32[]{:S(2)}, u32[]{:S(2)}) %collective-permute-start.19) | collective-permute-done | bytes 110624 | tf_op jit(solution)/shard_map/ppermute | solution.py:300
  71.8 2.1 %collective-permute-start.22 = (f32[216,128]{1,0:T(8,128)S(1)}, f32[216,128]{1,0:T(8,128)S(1)}, u32[]{:S(2)}, u32[]{:S(2)}) collective-permute-start(f32[216,128]{1,0:T(8,128)S(1)} %shard_map.94.rest_0_), channel_id=1, source_target_pairs={{0,12},{4,8},{8,4},{12,0},{1,13},{5,9},{9,5},{13,1},{2,14},{6,10},... | collective-permute-start | bytes 331784 | tf_op jit(solution)/shard_map/ppermute | solution.py:300
  73.9 2.4 %collective-permute-start.20 = (f32[216,128]{1,0:T(8,128)S(1)}, f32[216,128]{1,0:T(8,128)S(1)}, u32[]{:S(2)}, u32[]{:S(2)}) collective-permute-start(f32[216,128]{1,0:T(8,128)S(1)} %shard_map.94.rest_0_), channel_id=1, source_target_pairs={{0,4},{4,0},{8,12},{12,8},{1,5},{5,1},{9,13},{13,9},{2,6},{6,2},{1... | collective-permute-start | bytes 331784 | tf_op jit(solution)/shard_map/ppermute | solution.py:300
  76.2 3.5 %collective-permute-done.22.rest_3_ = f32[216,128]{1,0:T(8,128)S(1)} collective-permute-done((f32[216,128]{1,0:T(8,128)S(1)}, f32[216,128]{1,0:T(8,128)S(1)}, u32[]{:S(2)}, u32[]{:S(2)}) %collective-permute-start.22) | collective-permute-done | bytes 110624 | tf_op jit(solution)/shard_map/ppermute | solution.py:300
  79.7 2.9 %collective-permute-done.21.rest_2_ = f32[216,128]{1,0:T(8,128)S(1)} collective-permute-done((f32[216,128]{1,0:T(8,128)S(1)}, f32[216,128]{1,0:T(8,128)S(1)}, u32[]{:S(2)}, u32[]{:S(2)}) %collective-permute-start.21) | collective-permute-done | bytes 110624 | tf_op jit(solution)/shard_map/ppermute | solution.py:300
  82.7 1.5 %shard_map.95 = (f32[1536,128]{1,0:T(8,128)}, f32[64,96]{1,0:T(8,128)}) custom-call(f32[96,1024]{1,0:T(8,128)S(1)} %get-tuple-element.54.surface, f32[96,1024]{1,0:T(8,128)S(1)} %collective-permute-done.17.other, f32[96,128]{1,0:T(8,128)S(1)} %get-tuple-element.55.time_t, f32[216,128]{1,0:T(8,128)S(1)} %shard_map.94.rest_0_, ...), custom_call_target="tpu_custom_call" | custom-call | flops 1000000 | bytes 1000000 | tf_op jit(solution)/shard_map/pallas_call | solution.py:286
  (39 shorter events, 6.1 us)
Async XLA Ops:
  0.6 1.2 %copy-start = (bf16[64,64,128]{2,1,0:T(8,128)(2,1)S(1)}, bf16[64,64,128]{2,1,0:T(8,128)(2,1)}, u32[]{:S(2)}) copy-start(bf16[64,64,128]{2,1,0:T(8,128)(2,1)} %swath_ref.1) | copy-start | bytes 3145732
  1.9 0.8 copy-start.2
  2.6 0.7 copy-start.4
  3.3 0.7 copy-start.5
  4.0 0.7 copy-start.6
  4.6 8.3 %copy-start.1 = (f32[96,16,128]{2,1,0:T(8,128)S(1)}, f32[96,16,128]{2,1,0:T(8,128)}, u32[]{:S(2)}) copy-start(f32[96,16,128]{2,1,0:T(8,128)} %param.12) | copy-start | bytes 2359300
  4.6 8.3 %copy-start.3 = (f32[64,96]{1,0:T(8,128)S(1)}, f32[64,96]{1,0:T(8,128)}, u32[]{:S(2)}) copy-start(f32[64,96]{1,0:T(8,128)} %time_ref.1) | copy-start | bytes 73732
  7.3 18.5 %collective-permute-start.4 = (bf16[528,128]{1,0:T(8,128)(2,1)S(1)}, bf16[528,128]{1,0:T(8,128)(2,1)S(1)}, u32[]{:S(2)}, u32[]{:S(2)}) collective-permute-start(bf16[528,128]{1,0:T(8,128)(2,1)S(1)} %get-tuple-element.41), channel_id=1, source_target_pairs={{0,4},{4,0},{8,12},{12,8},{1,5},{5,1},{9,13},{13,9},{2,6},{6,2},{1... | collective-permute-start | bytes 405512 | tf_op jit(solution)/shard_map/ppermute | solution.py:300
  10.4 17.3 %collective-permute-start.5 = (bf16[528,128]{1,0:T(8,128)(2,1)S(1)}, bf16[528,128]{1,0:T(8,128)(2,1)S(1)}, u32[]{:S(2)}, u32[]{:S(2)}) collective-permute-start(bf16[528,128]{1,0:T(8,128)(2,1)S(1)} %get-tuple-element.42), channel_id=1, source_target_pairs={{0,8},{4,12},{8,0},{12,4},{1,9},{5,13},{9,1},{13,5},{2,10},{6,14},... | collective-permute-start | bytes 405512 | tf_op jit(solution)/shard_map/ppermute | solution.py:300
  13.3 11.2 %collective-permute-start = (f32[96,128]{1,0:T(8,128)S(1)}, f32[96,128]{1,0:T(8,128)S(1)}, u32[]{:S(2)}, u32[]{:S(2)}) collective-permute-start(f32[96,128]{1,0:T(8,128)S(1)} %get-tuple-element.34), channel_id=1, source_target_pairs={{1,2},{2,1},{5,6},{6,5},{9,10},{10,9},{13,14},{14,13},{17,18},{18,... | collective-permute-start | bytes 147464 | tf_op jit(solution)/shard_map/ppermute | solution.py:328
  14.0 5.6 %collective-permute-start.2 = (f32[24,128]{1,0:T(8,128)S(1)}, f32[24,128]{1,0:T(8,128)S(1)}, u32[]{:S(2)}, u32[]{:S(2)}) collective-permute-start(f32[24,128]{1,0:T(8,128)S(1)} %get-tuple-element.35), channel_id=1, source_target_pairs={{0,12},{4,8},{8,4},{12,0},{1,13},{5,9},{9,5},{13,1},{2,14},{6,10},... | collective-permute-start | bytes 36872 | tf_op jit(solution)/shard_map/ppermute | solution.py:300
  14.1 10.4 %collective-permute-start.3 = (f32[64,96]{1,0:T(8,128)S(1)}, f32[64,96]{1,0:T(8,128)S(1)}, u32[]{:S(2)}, u32[]{:S(2)}) collective-permute-start(f32[64,96]{1,0:T(8,128)S(1)} %get-tuple-element.36.refs_5_), channel_id=1, source_target_pairs={{0,1},{1,0},{2,3},{3,2},{4,5},{5,4},{6,7},{7,6},{8,9},{9,8},{10,11... | collective-permute-start | bytes 73736 | tf_op jit(solution)/shard_map/ppermute | solution.py:300
  19.6 3.7 %collective-permute-start.1 = (f32[24,128]{1,0:T(8,128)S(1)}, f32[24,128]{1,0:T(8,128)S(1)}, u32[]{:S(2)}, u32[]{:S(2)}) collective-permute-start(f32[24,128]{1,0:T(8,128)S(1)} %get-tuple-element.35), channel_id=1, source_target_pairs={{0,4},{4,0},{8,12},{12,8},{1,5},{5,1},{9,13},{13,9},{2,6},{6,2},{1... | collective-permute-start | bytes 36872 | tf_op jit(solution)/shard_map/ppermute | solution.py:300
  23.3 8.2 %collective-permute-start.6 = (bf16[528,128]{1,0:T(8,128)(2,1)S(1)}, bf16[528,128]{1,0:T(8,128)(2,1)S(1)}, u32[]{:S(2)}, u32[]{:S(2)}) collective-permute-start(bf16[528,128]{1,0:T(8,128)(2,1)S(1)} %get-tuple-element.43), channel_id=1, source_target_pairs={{0,12},{4,8},{8,4},{12,0},{1,13},{5,9},{9,5},{13,1},{2,14},{6,10},... | collective-permute-start | bytes 405512 | tf_op jit(solution)/shard_map/ppermute | solution.py:300
  24.5 7.0 %collective-permute-start.7 = (bf16[528,128]{1,0:T(8,128)(2,1)S(1)}, bf16[528,128]{1,0:T(8,128)(2,1)S(1)}, u32[]{:S(2)}, u32[]{:S(2)}) collective-permute-start(bf16[528,128]{1,0:T(8,128)(2,1)S(1)} %get-tuple-element.44), channel_id=1, source_target_pairs={{0,1},{1,0},{4,5},{5,4},{8,9},{9,8},{12,13},{13,12},{2,3},{3,2},{6... | collective-permute-start | bytes 405512 | tf_op jit(solution)/shard_map/ppermute | solution.py:300
  24.5 10.5 %collective-permute-start.8 = (bf16[528,128]{1,0:T(8,128)(2,1)S(1)}, bf16[528,128]{1,0:T(8,128)(2,1)S(1)}, u32[]{:S(2)}, u32[]{:S(2)}) collective-permute-start(bf16[528,128]{1,0:T(8,128)(2,1)S(1)} %get-tuple-element.45), channel_id=1, source_target_pairs={{0,5},{1,4},{4,1},{5,0},{8,13},{9,12},{12,9},{13,8},{2,7},{3,6},{6... | collective-permute-start | bytes 405512 | tf_op jit(solution)/shard_map/ppermute | solution.py:300
  25.7 14.5 %collective-permute-start.9 = (bf16[528,128]{1,0:T(8,128)(2,1)S(1)}, bf16[528,128]{1,0:T(8,128)(2,1)S(1)}, u32[]{:S(2)}, u32[]{:S(2)}) collective-permute-start(bf16[528,128]{1,0:T(8,128)(2,1)S(1)} %get-tuple-element.46), channel_id=1, source_target_pairs={{0,9},{1,8},{4,13},{5,12},{8,1},{9,0},{12,5},{13,4},{2,11},{3,10},... | collective-permute-start | bytes 405512 | tf_op jit(solution)/shard_map/ppermute | solution.py:300
  27.7 12.5 %collective-permute-start.10 = (bf16[528,128]{1,0:T(8,128)(2,1)S(1)}, bf16[528,128]{1,0:T(8,128)(2,1)S(1)}, u32[]{:S(2)}, u32[]{:S(2)}) collective-permute-start(bf16[528,128]{1,0:T(8,128)(2,1)S(1)} %get-tuple-element.47), channel_id=1, source_target_pairs={{0,13},{1,12},{4,9},{5,8},{8,5},{9,4},{12,1},{13,0},{2,15},{3,14},... | collective-permute-start | bytes 405512 | tf_op jit(solution)/shard_map/ppermute | solution.py:300
  41.7 1.7 %collective-permute-start.11 = (f32[312,128]{1,0:T(8,128)S(1)}, f32[312,128]{1,0:T(8,128)S(1)}, u32[]{:S(2)}, u32[]{:S(2)}) collective-permute-start(f32[312,128]{1,0:T(8,128)S(1)} %get-tuple-element.51), channel_id=1, source_target_pairs={{0,1},{1,0},{2,3},{3,2},{4,5},{5,4},{6,7},{7,6},{8,9},{9,8},{10,11... | collective-permute-start | bytes 479240 | tf_op jit(solution)/shard_map/ppermute | solution.py:300
  43.4 5.4 %collective-permute-start.13 = (f32[216,128]{1,0:T(8,128)S(1)}, f32[216,128]{1,0:T(8,128)S(1)}, u32[]{:S(2)}, u32[]{:S(2)}) collective-permute-start(f32[216,128]{1,0:T(8,128)S(1)} %shard_map.90.mine), channel_id=1, source_target_pairs={{0,2},{2,0},{1,3},{3,1},{4,6},{6,4},{5,7},{7,5},{8,10},{10,8},{9,1... | collective-permute-start | bytes 331784 | tf_op jit(solution)/shard_map/ppermute | solution.py:300
  48.8 7.5 %collective-permute-start.16 = (f32[216,128]{1,0:T(8,128)S(1)}, f32[216,128]{1,0:T(8,128)S(1)}, u32[]{:S(2)}, u32[]{:S(2)}) collective-permute-start(f32[216,128]{1,0:T(8,128)S(1)} %shard_map.91.refs_6_), channel_id=1, source_target_pairs={{0,12},{4,8},{8,4},{12,0},{1,13},{5,9},{9,5},{13,1},{2,14},{6,10},... | collective-permute-start | bytes 331784 | tf_op jit(solution)/shard_map/ppermute | solution.py:300
  51.1 11.2 %collective-permute-start.15 = (f32[216,128]{1,0:T(8,128)S(1)}, f32[216,128]{1,0:T(8,128)S(1)}, u32[]{:S(2)}, u32[]{:S(2)}) collective-permute-start(f32[216,128]{1,0:T(8,128)S(1)} %shard_map.91.refs_6_), channel_id=1, source_target_pairs={{0,8},{4,12},{8,0},{12,4},{1,9},{5,13},{9,1},{13,5},{2,10},{6,14},... | collective-permute-start | bytes 331784 | tf_op jit(solution)/shard_map/ppermute | solution.py:300
  53.4 8.9 %collective-permute-start.14 = (f32[216,128]{1,0:T(8,128)S(1)}, f32[216,128]{1,0:T(8,128)S(1)}, u32[]{:S(2)}, u32[]{:S(2)}) collective-permute-start(f32[216,128]{1,0:T(8,128)S(1)} %shard_map.91.refs_6_), channel_id=1, source_target_pairs={{0,4},{4,0},{8,12},{12,8},{1,5},{5,1},{9,13},{13,9},{2,6},{6,2},{1... | collective-permute-start | bytes 331784 | tf_op jit(solution)/shard_map/ppermute | solution.py:300
  53.4 0.7 collective-permute-start.12
  64.6 18.0 %collective-permute-start.17 = (f32[96,1024]{1,0:T(8,128)S(1)}, f32[96,1024]{1,0:T(8,128)S(1)}, u32[]{:S(2)}, u32[]{:S(2)}) collective-permute-start(f32[96,1024]{1,0:T(8,128)S(1)} %get-tuple-element.54.surface), channel_id=1, source_target_pairs={{0,1},{1,0},{2,3},{3,2},{4,5},{5,4},{6,7},{7,6},{8,9},{9,8},{10,11... | collective-permute-start | bytes 1179656 | tf_op jit(solution)/shard_map/ppermute | solution.py:300
  64.6 1.9 %collective-permute-start.18 = (f32[312,128]{1,0:T(8,128)S(1)}, f32[312,128]{1,0:T(8,128)S(1)}, u32[]{:S(2)}, u32[]{:S(2)}) collective-permute-start(f32[312,128]{1,0:T(8,128)S(1)} %get-tuple-element.57), channel_id=1, source_target_pairs={{0,1},{1,0},{2,3},{3,2},{4,5},{5,4},{6,7},{7,6},{8,9},{9,8},{10,11... | collective-permute-start | bytes 479240 | tf_op jit(solution)/shard_map/ppermute | solution.py:300
  66.6 5.2 %collective-permute-start.19 = (f32[216,128]{1,0:T(8,128)S(1)}, f32[216,128]{1,0:T(8,128)S(1)}, u32[]{:S(2)}, u32[]{:S(2)}) collective-permute-start(f32[216,128]{1,0:T(8,128)S(1)} %shard_map.93.mine), channel_id=1, source_target_pairs={{0,2},{2,0},{1,3},{3,1},{4,6},{6,4},{5,7},{7,5},{8,10},{10,8},{9,1... | collective-permute-start | bytes 331784 | tf_op jit(solution)/shard_map/ppermute | solution.py:300
  71.8 8.0 %collective-permute-start.22 = (f32[216,128]{1,0:T(8,128)S(1)}, f32[216,128]{1,0:T(8,128)S(1)}, u32[]{:S(2)}, u32[]{:S(2)}) collective-permute-start(f32[216,128]{1,0:T(8,128)S(1)} %shard_map.94.rest_0_), channel_id=1, source_target_pairs={{0,12},{4,8},{8,4},{12,0},{1,13},{5,9},{9,5},{13,1},{2,14},{6,10},... | collective-permute-start | bytes 331784 | tf_op jit(solution)/shard_map/ppermute | solution.py:300
  73.9 8.8 %collective-permute-start.21 = (f32[216,128]{1,0:T(8,128)S(1)}, f32[216,128]{1,0:T(8,128)S(1)}, u32[]{:S(2)}, u32[]{:S(2)}) collective-permute-start(f32[216,128]{1,0:T(8,128)S(1)} %shard_map.94.rest_0_), channel_id=1, source_target_pairs={{0,8},{4,12},{8,0},{12,4},{1,9},{5,13},{9,1},{13,5},{2,10},{6,14},... | collective-permute-start | bytes 331784 | tf_op jit(solution)/shard_map/ppermute | solution.py:300
  73.9 8.8 %collective-permute-start.20 = (f32[216,128]{1,0:T(8,128)S(1)}, f32[216,128]{1,0:T(8,128)S(1)}, u32[]{:S(2)}, u32[]{:S(2)}) collective-permute-start(f32[216,128]{1,0:T(8,128)S(1)} %shard_map.94.rest_0_), channel_id=1, source_target_pairs={{0,4},{4,0},{8,12},{12,8},{1,5},{5,1},{9,13},{13,9},{2,6},{6,2},{1... | collective-permute-start | bytes 331784 | tf_op jit(solution)/shard_map/ppermute | solution.py:300

commit v3 on v2

--- a/solution.py
+++ b/solution.py
@@ -20,16 +20,29 @@
 COLS = 16
 NORM = 8
 SPARE = 2 * 1024 * 1024
+SWATH_COPIES = 4
 
 
 def dot(a, b, contract):
     return lax.dot_general(a, b, ((contract[:1], contract[1:]), ((), ())), preferred_element_type=F32)
 
 
-def route_kernel(n_lon, half, list_ref, count_ref, target_ref, swath_ref, mask_ref, *rest):
-    outs, (place, total, seen) = rest[: 2 * n_lon], rest[2 * n_lon:]
+def route_kernel(half, sends, list_hbm, count_hbm, target_hbm, swath_hbm, mask_hbm, *rest):
+    outs, rest = rest[: len(sends)], rest[len(sends):]
+    list_ref, count_ref, target_ref, swath_ref, mask_ref, place, total, seen, arrived = rest
     me, core = lax.axis_index("lon"), lax.axis_index("ta")
+    n_lon = list_ref.shape[1]
     slots, days, cells = swath_ref.shape
+    chunk = slots // SWATH_COPIES
+    small = [(list_hbm, list_ref), (count_hbm, count_ref), (target_hbm, target_ref), (mask_hbm, mask_ref)]
+    large = [(swath_hbm.at[pl.ds(at, chunk)], swath_ref.at[pl.ds(at, chunk)]) for at in range(0, slots, chunk)]
+    copies = [pltpu.make_async_copy(src, dst, arrived.at[i]) for i, (src, dst) in enumerate(small + large)]
+    for copy in copies:
+        copy.start()
+    total[...] = jnp.zeros(total.shape, F32)
+    seen[...] = jnp.zeros(seen.shape, F32)
+    for copy in copies[: len(small)]:
+        copy.wait()
 
     def owner(d, carry):
         step = jnp.bitwise_xor(d, me)
@@ -44,36 +57,38 @@
         return lax.fori_loop(0, count_ref[0, d], entry, carry)
 
     lax.fori_loop(0, n_lon, owner, 0)
-    total[...] = jnp.zeros(total.shape, F32)
-    seen[...] = jnp.zeros(seen.shape, F32)
     mask = mask_ref[...].astype(F32)
     by_day = mask.T
     for slot in range(slots):
+        if slot % chunk == 0:
+            copies[len(small) + slot // chunk].wait()
         at = place[slot]
         total[at] += swath_ref[slot].astype(F32) * by_day[:, slot:slot + 1]
         seen[pl.ds(at, 1), :days] += mask[slot:slot + 1, :]
-    for piece, out in enumerate(outs):
-        out[: half * days, :] = total[piece * half:(piece + 1) * half].reshape(half * days, cells).astype(BF16)
-        out[half * days:, :] = seen[piece * half:piece * half + TAIL, :].astype(BF16)
+    for (side, step), out in zip(sends, outs):
+        at = (side * n_lon + step) * half
+        out[: half * days, :] = total[at:at + half].reshape(half * days, cells).astype(BF16)
+        out[half * days:, :] = seen[at:at + TAIL, :].astype(BF16)
 
 
 def row_of(surface, row):
     return surface[:, row * LANES:(row + 1) * LANES]
 
 
-def columns_as_rows(surface, half, flip, extra):
-    rank = surface.shape[0]
+def columns_as_rows(columns, flip):
+    rank = columns[0].shape[0]
     lane = lax.broadcasted_iota(jnp.int32, (rank, LANES), 1)
     block = jnp.zeros((rank, LANES), F32)
-    for row in range(half):
-        strip = row_of(surface, row)
-        block = jnp.where(lane == row, strip[:, :1], block)
-        block = jnp.where(lane == half + row, strip[:, LANES - 1:], block)
-    if extra is not None:
-        block = jnp.where(lane == COLS, extra, block)
+    for at, column in enumerate(columns):
+        block = jnp.where(lane == at, column, block)
     flip[...] = jnp.zeros(flip.shape, F32)
     flip[:rank, :] = block
-    return flip[...].T[: COLS + NORM, :]
+    return flip[...].T
+
+
+def border(surface, half):
+    strips = [row_of(surface, row) for row in range(half)]
+    return [strip[:, :1] for strip in strips] + [strip[:, LANES - 1:] for strip in strips]
 
 
 def rows_as_columns(rows, rank, flip):
@@ -104,7 +119,7 @@
         surface[:, row * LANES:(row + 1) * LANES] = space_ref[pl.ds(core * half + row, rank, stride=height), :]
     edge_near[...] = space_ref[pl.ds(half - core, rank, stride=height), :]
     edge_far[...] = space_ref[pl.ds(core * (height - 1), rank, stride=height), :]
-    cols[...] = columns_as_rows(surface[...], half, flip, None)
+    cols[...] = columns_as_rows(border(surface[...], half), flip)[:COLS, :]
     time_own[...] = time_ref[...]
 
 
@@ -134,8 +149,7 @@
         base[:, row * LANES:(row + 1) * LANES] = strip
 
 
-def gradients(half, base, predicted, packed, time_t, seen, summed, fresh, message, outgoing, edge_far, flip):
-    core = lax.axis_index("ta")
+def gradients(half, base, predicted, packed, time_t, seen, summed, fresh):
     rank = time_t.shape[0]
     time_bf = time_t.astype(BF16)
     time_twice = jnp.concatenate([time_bf, time_bf], axis=1)
@@ -164,17 +178,25 @@
             strip = row_of(wide, row)
             square = jnp.sum(strip * strip, axis=1, keepdims=True)
             grad_diag = grad_diag + square * seen[at // LANES + row:at // LANES + row + 1, :]
-    grad_time = grad_time[:, :LANES] + grad_time[:, LANES:]
+    return grad_time[:, :LANES] + grad_time[:, LANES:], grad_diag, norm
+
+
+def post(half, sums, fresh, message, outgoing, edge_far, flip):
+    grad_time, grad_diag, norm = sums
+    core = lax.axis_index("ta")
+    rank = norm.shape[0]
+    columns = [norm] if edge_far is None else [norm] + [norm] * (NORM - 1) + border(fresh[...], half)
+    last = columns_as_rows(columns, flip)[: message.shape[0] - 2 * rank, :]
     message[:rank, :] = grad_time
     message[rank:2 * rank, :] = grad_diag
-    last = columns_as_rows(fresh[...], half, flip, norm)
     message[2 * rank:, :] = last
     outgoing[:rank, :] = pltpu.roll(grad_time, LANES // 2, 1)
     outgoing[rank:2 * rank, :] = pltpu.roll(grad_diag, LANES // 2, 1)
-    outgoing[2 * rank:2 * rank + COLS + NORM, :] = last
-    first_row, last_row = fresh[:, :LANES], fresh[:, (half - 1) * LANES:]
-    outgoing[2 * rank + COLS + NORM:, :] = pick(core == 0, last_row, first_row)
-    edge_far[...] = pick(core == 0, first_row, last_row)
+    outgoing[2 * rank:2 * rank + NORM, :] = last[:NORM, :]
+    if edge_far is not None:
+        first_row, last_row = fresh[:, :LANES], fresh[:, (half - 1) * LANES:]
+        outgoing[2 * rank + NORM:, :] = pick(core == 0, last_row, first_row)
+        edge_far[...] = pick(core == 0, first_row, last_row)
 
 
 def first_kernel(half, n_lon, base, predicted, packed, time_t, *rest):
@@ -195,36 +217,33 @@
         return value
 
     seen[...] = counts(near) + pltpu.roll(counts(far), days, 1)
-    gradients(half, base, predicted, packed, time_t[...], seen[...], summed, fresh, message, outgoing, edge_far, flip)
-
-
-def settle(rank, day_count, cell_count, total, time_t):
+    sums = gradients(half, base, predicted, packed, time_t[...], seen[...], summed, fresh)
+    post(half, sums, fresh, message, outgoing, edge_far, flip)
+
+
+def settle(rank, counts, parts, time_t, flip):
+    day_count, cell_count = counts
+    total = parts[0][...].astype(F32)
+    if len(parts) > 1:
+        one, two, three = (part[...].astype(F32) for part in parts[1:])
+        total = (total + one) + (two + three)
     time_new = time_t - total[:rank, :] / (total[rank:2 * rank, :] + RIDGE)
-    return time_new
-
-
-def scaling(rank, day_count, cell_count, total, time_new, flip):
-    space_sq = rows_as_columns(total[2 * rank + COLS:, :], rank, flip)[:, :1]
+    norm = total[2 * rank:2 * rank + NORM, :]
+    if parts[0].dtype == BF16:
+        norm = norm + total[2 * rank + NORM:2 * rank + 2 * NORM, :]
+    space_sq = rows_as_columns(norm, rank, flip)[:, :1]
     square = time_new * time_new
     time_sq = 0.5 * jnp.sum(square + pltpu.roll(square, LANES // 2, 1), axis=1, keepdims=True)
     ratio = (time_sq / day_count + EPSILON) / (space_sq / cell_count + EPSILON)
-    return jnp.sqrt(jnp.sqrt(ratio))
-
-
-def total_of(parts):
-    if len(parts) == 1:
-        return parts[0][...]
-    return (parts[0][...] + parts[1][...]) + (parts[2][...] + parts[3][...])
+    return time_new, jnp.sqrt(jnp.sqrt(ratio))
 
 
 def second_kernel(half, counts, n_parts, swap, surface, time_t, summed, seen, edge_near, edge_far, *rest):
     parts, (cols_a, cols_b) = rest[:n_parts], rest[n_parts:n_parts + 2]
-    fresh, time_out, message, outgoing, edge_out, flip, scaled, base, predicted, packed = rest[n_parts + 2:]
+    fresh, time_out, message, outgoing, flip, scaled, base, predicted, packed = rest[n_parts + 2:]
     core = lax.axis_index("ta")
     rank = surface.shape[0]
-    total = total_of(parts)
-    time_new = settle(rank, *counts, total, time_t[...])
-    scale = scaling(rank, *counts, total, time_new, flip)
+    time_new, scale = settle(rank, counts, parts, time_t[...], flip)
     time_now = time_new / scale
     time_out[...] = time_now
     scaled[...] = surface[...] * scale
@@ -236,12 +255,13 @@
     above = pick(core == 0, far, near) * scale
     below = pick(core == 0, near, far) * scale
     odd = swap()
-    from_a, from_b = cols_a[2 * rank:2 * rank + COLS, :], cols_b[2 * rank:2 * rank + COLS, :]
+    from_a, from_b = cols_a[cols_a.shape[0] - COLS:, :], cols_b[cols_b.shape[0] - COLS:, :]
     left = rows_as_columns(pick(odd, from_a, from_b), rank, flip) * scale
     right = rows_as_columns(pick(odd, from_b, from_a), rank, flip) * scale
     for row, strip in enumerate(smoothed(scaled[...], half, above, below, left, right)):
         base[:, row * LANES:(row + 1) * LANES] = strip
-    gradients(half, base, predicted, packed, time_now, seen[...], summed, fresh, message, outgoing, edge_out, flip)
+    sums = gradients(half, base, predicted, packed, time_now, seen[...], summed, fresh)
+    post(half, sums, fresh, message, outgoing, None, flip)
 
 
 def last_kernel(half, counts, n_parts, surface, other, time_t, *rest):
@@ -250,9 +270,7 @@
     core = lax.axis_index("ta")
     rank = surface.shape[0]
     height = space_out.shape[0] // rank
-    total = total_of(parts)
-    time_new = settle(rank, *counts, total, time_t[...])
-    scale = scaling(rank, *counts, total, time_new, flip)
+    time_new, scale = settle(rank, counts, parts, time_t[...], flip)
     flip[...] = jnp.zeros(flip.shape, F32)
     flip[:rank, :] = time_new / scale
     time_out[...] = flip[...].T[: time_out.shape[0], :rank]
@@ -262,12 +280,30 @@
         space_out[pl.ds((1 - core) * half + row, rank, stride=height), :] = other[:, at:at + LANES] * scale
 
 
-def add_kernel(rank, mine, theirs, out):
-    cols = slice(2 * rank, 2 * rank + COLS)
-    out[: 2 * rank, :] = mine[: 2 * rank, :] + theirs[: 2 * rank, :]
-    out[cols, :] = mine[cols, :]
-    ends = slice(2 * rank + COLS, 2 * rank + COLS + NORM)
-    out[ends, :] = mine[ends, :] + theirs[ends, :]
+def core_kernel(rank, mine, theirs, edge_in, total, beside, edge_out):
+    rows = total.shape[0]
+    total[...] = mine[:rows, :] + theirs[:rows, :]
+    beside[...] = theirs[rows:, :]
+    edge_out[...] = edge_in[...]
+
+
+def add_kernel(mine, theirs, total):
+    rows = total.shape[0]
+    total[...] = mine[:rows, :] + theirs[:rows, :]
+
+
+def band_kernel(mine, theirs, message, after, total):
+    rows = mine.shape[0]
+    total[:rows, :] = mine[...] + theirs[...]
+    total[rows:, :] = message[rows:, :]
+
+
+def narrow_kernel(rank, mine, theirs, total):
+    value = mine[...] + theirs[...]
+    total[: 2 * rank, :] = value[: 2 * rank, :].astype(BF16)
+    norm = value[2 * rank:, :]
+    high = norm.astype(BF16).astype(F32)
+    total[2 * rank:, :] = jnp.concatenate([high, norm - high], axis=0).astype(BF16)
 
 
 def shape(dims, dtype=F32):
@@ -279,10 +315,10 @@
     return math.prod(outer) * -(-rows // 16) * 16 * -(-lanes // LANES) * LANES * jnp.dtype(ref.dtype).itemsize
 
 
-def call(kernel, out_shape, scratch=(), smem=0, after=0, flops=1_000_000):
+def call(kernel, out_shape, scratch=(), hbm=0, after=0, flops=1_000_000):
     def run(*operands):
-        vmem = [*operands[smem:len(operands) - after], *jax.tree.leaves(out_shape), *scratch]
-        specs = [pltpu.SMEM] * smem + [pltpu.VMEM] * (len(operands) - smem - after) + [pl.ANY] * after
+        vmem = [*operands[hbm:len(operands) - after], *jax.tree.leaves(out_shape), *scratch]
+        specs = [pltpu.HBM] * hbm + [pltpu.VMEM] * (len(operands) - hbm - after) + [pl.ANY] * after
         return pl.pallas_call(
             kernel,
             out_shape=out_shape,
@@ -307,21 +343,33 @@
     half = height // n_ta
     wide = half * LANES
     counts = (float(days * n_ta), float(height * cells * n_lon * n_lat))
-    message_rows = 2 * rank + COLS + NORM
+    sum_rows = 2 * rank + NORM
     flip = pltpu.VMEM((LANES, LANES), F32)
 
+    distant, close = range(n_lon // 2, n_lon), range(1, n_lon // 2)
+    sends = [(side, step) for steps in (distant, close) for side in (0, 1) for step in steps] + [(1, 0), (0, 0)]
     pieces = call(
-        functools.partial(route_kernel, n_lon, half),
-        [shape((half * days + TAIL, cells), BF16)] * (2 * n_lon),
-        [pltpu.SMEM((slots,), jnp.int32), pltpu.VMEM((2 * n_lon * half, days, cells), F32), pltpu.VMEM((2 * n_lon * half + TAIL, LANES), F32)],
-        smem=3,
+        functools.partial(route_kernel, half, sends),
+        [shape((half * days + TAIL, cells), BF16)] * len(sends),
+        [
+            pltpu.SMEM(send_list.shape, jnp.int32),
+            pltpu.SMEM(send_count.shape, jnp.int32),
+            pltpu.SMEM(target.shape, jnp.int32),
+            pltpu.VMEM(swath.shape, swath.dtype),
+            pltpu.VMEM(obs_mask.shape, jnp.int32),
+            pltpu.SMEM((slots,), jnp.int32),
+            pltpu.VMEM((2 * n_lon * half, days, cells), F32),
+            pltpu.VMEM((2 * n_lon * half + TAIL, LANES), F32),
+            pltpu.SemaphoreType.DMA((4 + SWATH_COPIES,)),
+        ],
+        hbm=5,
     )(send_list, send_count, target, swath, obs_mask)
-    near, far = pieces[:n_lon], pieces[n_lon:]
-    near_in, far_in = {0: near[0]}, {}
-    for step in (*range(n_lon // 2, n_lon), *range(n_lon // 2)):
-        if step:
-            near_in[step] = across(near[step], "lon", step)
-        far_in[step] = across(far[step], ("lon", "ta"), 2 * step + 1)
+    near_in, far_in = {}, {}
+    for (side, step), piece in zip(sends, pieces):
+        if side:
+            far_in[step] = across(piece, ("lon", "ta"), 2 * step + 1)
+        else:
+            near_in[step] = across(piece, "lon", step) if step else piece
 
     def bands(edge):
         there = [(2 * band + 1, 2 * band + 2) for band in range(n_lat - 1)]
@@ -340,10 +388,10 @@
 
     surface, edge_near, edge_far, cols, time_own = call(
         functools.partial(prepare_kernel, half),
-        [shape((rank, wide)), shape((rank, LANES)), shape((rank, LANES)), shape((COLS + NORM, LANES)), shape(factor_time.shape)],
+        [shape((rank, wide)), shape((rank, LANES)), shape((rank, LANES)), shape((COLS, LANES)), shape(factor_time.shape)],
         [flip],
         after=1,
-    )(factor_space.reshape(rank * height, cells), factor_time, near[0])
+    )(factor_space.reshape(rank * height, cells), factor_time, near_in[1])
     cols_a, cols_b = columns(cols)
 
     def model(*refs):
@@ -355,49 +403,57 @@
         [flip, flip],
     )(surface, edge_near, bands(edge_far), cols_a, cols_b, time_own, across(time_own, "ta", 1))
 
-    step_out = [shape((rank, wide)), shape((message_rows, LANES)), shape((message_rows + rank, LANES)), shape((rank, LANES))]
+    fresh = shape((rank, wide))
     surface, message, outgoing, edge_far, summed, seen = call(
         functools.partial(first_kernel, half, n_lon),
-        step_out + [shape((2 * days, wide)), shape((TAIL, LANES))],
+        [fresh, shape((sum_rows + COLS, LANES)), shape((sum_rows + rank, LANES)), shape((rank, LANES)), shape((2 * days, wide)), shape((TAIL, LANES))],
         [flip],
     )(base, predicted, packed, time_t, *[near_in[s] for s in range(n_lon)], *[far_in[s] for s in range(n_lon)])
 
-    add = call(functools.partial(add_kernel, rank), shape((message_rows, LANES)))
-
-    def gather(message, outgoing):
-        incoming = across(outgoing, "ta", 1)
-        total = add(message, incoming)
+    sums = shape((sum_rows, LANES))
+    add = call(add_kernel, sums)
+
+    def over_bands(total, last):
         step = 1
-        while step < n_lat:
+        while 2 * step < n_lat:
             total = add(total, across(total, "lat", step))
             step *= 2
+        return last(total, across(total, "lat", step))
+
+    def over_lon(total):
         if paired:
-            return incoming, [total] + [across(total, "lon", step) for step in (1, 2, 3)]
+            return [total] + [across(total, "lon", step) for step in (1, 2, 3)]
         step = 1
-        own = total
         while step < n_lon:
             total = add(total, across(total, "lon", step))
             step *= 2
-        return incoming, [total], own
-
-    beside, *rest = gather(message, outgoing)
-    parts = rest[0]
+        return [total]
+
+    total, edge_near, edge_far = call(
+        functools.partial(core_kernel, rank), [sums, shape((rank, LANES)), shape((rank, LANES))]
+    )(message, across(outgoing, "ta", 1), edge_far)
+    edge_far = bands(edge_far)
     if paired:
+        last = call(band_kernel, shape((sum_rows + COLS, LANES)), after=1)
+        parts = over_lon(over_bands(total, lambda mine, theirs: last(mine, theirs, message, edge_far)))
         cols_a, cols_b = parts[1], parts[3]
     else:
-        cols_a, cols_b = columns(message)
+        parts = over_lon(over_bands(total, add))
+        cols_a, cols_b = columns(message[sum_rows:])
 
     def second(*refs):
         second_kernel(half, counts, len(parts), swap, *refs)
 
-    surface, time_t, message, outgoing, edge_far = call(
+    surface, time_t, message, outgoing = call(
         second,
-        [step_out[0], shape((rank, LANES))] + step_out[1:],
+        [fresh, shape((rank, LANES)), sums, sums],
         [flip, pltpu.VMEM((rank, wide), F32), pltpu.VMEM((rank, wide), F32), pltpu.VMEM((2 * days, wide), F32), pltpu.VMEM((rank, wide), BF16)],
-    )(surface, time_t, summed, seen, beside[message_rows:], bands(edge_far), *parts, cols_a, cols_b)
-
+    )(surface, time_t, summed, seen, edge_near, edge_far, *parts, cols_a, cols_b)
+
+    total = add(message, across(outgoing, "ta", 1))
     other = across(surface, "ta", 1)
-    parts = gather(message, outgoing)[1]
+    narrow = call(functools.partial(narrow_kernel, rank), shape((sum_rows + NORM, LANES), BF16))
+    parts = over_lon(over_bands(total, narrow if paired else add))
     space, time = call(
         functools.partial(last_kernel, half, counts, len(parts)),
         [shape((rank * height, cells)), shape(factor_time.shape)],

time: 84.5 us -> 82 us (0.970)
  waiting for transfers between devices: 42.4 us -> 40.1 us
    ppermute x21, waiting for transfers between devices: 42.4 us -> 40.1 us  [across(): lax.ppermute(value, axis, [(i, i ^ step) for i in range(lax.axis_size(axi...]
  transfers between devices with their start and end apart: 23 -> 23, of which waited for: 13 -> 14; matrix products, arithmetic and copies ran while one was open for 0% -> 0% of each run, Pallas kernels for 1% -> 1%
where the time goes in v3:
time: 82 us; the launch traced here: 81.7 us
  waiting for transfers between devices  40.1 us (49%)
  starting transfers between devices  28.3 us (35%)
  Pallas kernels  8.6 us (10%)
  local copies, waits for them, and re-layouts  3.97 us (5%)
    ppermute x21, waiting for transfers between devices, across(): lax.ppermute(value, axis, [(i, i ^ step) for i in range(lax.axis_size(axi...  40.1 us
    ppermute x21, starting transfers between devices, across(): lax.ppermute(value, axis, [(i, i ^ step) for i in range(lax.axis_size(axi...  27 us
    pallas_call x10, Pallas kernels, run(): pl.pallas_call(kernel, out_shape=out_shape, in_specs=[pl.BlockSpec(memory...  8.6 us
    unnamed x14, local copies, waits for them, and re-layouts  3.97 us
  transfers between devices with their start and end apart: 23, of which 14 were waited for; matrix products, arithmetic and copies ran while one was open for 0% of the time, Pallas kernels for 1%

profile of v3, /device:TPU:0, one launch (start us, length us, event | category | flops | bytes accessed | tf_op | source)
XLA Modules:
  0.0 81.7 jit_solution(207816603647631509)
XLA Ops:
  0.6 1.2 %copy-done = bf16[64,64,128]{2,1,0:T(8,128)(2,1)S(1)} copy-done((bf16[64,64,128]{2,1,0:T(8,128)(2,1)S(1)}, bf16[64,64,128]{2,1,0:T(8,128)(2,1)}, u32[]{:S(2)}) %copy-start) | copy-done | bytes 1048600
  1.9 0.8 copy-done.2
  2.6 0.7 copy-done.4
  4.6 2.7 %shard_map.86 = (bf16[528,128]{1,0:T(8,128)(2,1)S(1)}, bf16[528,128]{1,0:T(8,128)(2,1)S(1)}, bf16[528,128]{1,0:T(8,128)(2,1)S(1)}, bf16[528,128]{1,0:T(8,128)(2,...) custom-call(s32[1,4,32]{2,1,0:T(4,128)S(1)} %copy-done.4, ...), custom_call_target="tpu_custom_call" | custom-call | flops 1000000 | bytes 1000000 | tf_op jit(solution)/shard_map/pallas_call | solution.py:322
  7.4 3.1 %collective-permute-start = (bf16[528,128]{1,0:T(8,128)(2,1)S(1)}, bf16[528,128]{1,0:T(8,128)(2,1)S(1)}, u32[]{:S(2)}, u32[]{:S(2)}) collective-permute-start(bf16[528,128]{1,0:T(8,128)(2,1)S(1)} %get-tuple-element.34), channel_id=1, source_target_pairs={{0,4},{4,0},{8,12},{12,8},{1,5},{5,1},{9,13},{13,9},{2,6},{6,2},{1... | collective-permute-start | bytes 405512 | tf_op jit(solution)/shard_map/ppermute | solution.py:336
  10.5 2.6 %collective-permute-start.5 = (bf16[528,128]{1,0:T(8,128)(2,1)S(1)}, bf16[528,128]{1,0:T(8,128)(2,1)S(1)}, u32[]{:S(2)}, u32[]{:S(2)}) collective-permute-start(bf16[528,128]{1,0:T(8,128)(2,1)S(1)} %get-tuple-element.45), channel_id=1, source_target_pairs={{0,8},{4,12},{8,0},{12,4},{1,9},{5,13},{9,1},{13,5},{2,10},{6,14},... | collective-permute-start | bytes 405512 | tf_op jit(solution)/shard_map/ppermute | solution.py:336
  13.0 3.0 %collective-permute-done.after.rest_1_ = bf16[528,128]{1,0:T(8,128)(2,1)S(1)} collective-permute-done((bf16[528,128]{1,0:T(8,128)(2,1)S(1)}, bf16[528,128]{1,0:T(8,128)(2,1)S(1)}, u32[]{:S(2)}, u32[]{:S(2)}) %collective-permute-start) | collective-permute-done | bytes 135200 | tf_op jit(solution)/shard_map/ppermute | solution.py:336
  17.1 3.2 %collective-permute-start.4 = (f32[64,96]{1,0:T(8,128)S(1)}, f32[64,96]{1,0:T(8,128)S(1)}, u32[]{:S(2)}, u32[]{:S(2)}) collective-permute-start(f32[64,96]{1,0:T(8,128)S(1)} %get-tuple-element.39.refs_5_), channel_id=1, source_target_pairs={{0,1},{1,0},{2,3},{3,2},{4,5},{5,4},{6,7},{7,6},{8,9},{9,8},{10,11... | collective-permute-start | bytes 73736 | tf_op jit(solution)/shard_map/ppermute | solution.py:336
  20.4 3.1 %collective-permute-start.3 = (f32[16,128]{1,0:T(8,128)S(1)}, f32[16,128]{1,0:T(8,128)S(1)}, u32[]{:S(2)}, u32[]{:S(2)}) collective-permute-start(f32[16,128]{1,0:T(8,128)S(1)} %get-tuple-element.38), channel_id=1, source_target_pairs={{0,12},{4,8},{8,4},{12,0},{1,13},{5,9},{9,5},{13,1},{2,14},{6,10},... | collective-permute-start | bytes 24584 | tf_op jit(solution)/shard_map/ppermute | solution.py:336
  23.5 0.7 collective-permute-start.6
  24.2 1.6 %collective-permute-done.3.refs_4_ = f32[16,128]{1,0:T(8,128)S(1)} collective-permute-done((f32[16,128]{1,0:T(8,128)S(1)}, f32[16,128]{1,0:T(8,128)S(1)}, u32[]{:S(2)}, u32[]{:S(2)}) %collective-permute-start.3) | collective-permute-done | bytes 8224 | tf_op jit(solution)/shard_map/ppermute | solution.py:336
  25.8 1.3 %collective-permute-done.2.refs_3_ = f32[16,128]{1,0:T(8,128)S(1)} collective-permute-done((f32[16,128]{1,0:T(8,128)S(1)}, f32[16,128]{1,0:T(8,128)S(1)}, u32[]{:S(2)}, u32[]{:S(2)}) %collective-permute-start.2) | collective-permute-done | bytes 8224 | tf_op jit(solution)/shard_map/ppermute | solution.py:336
  27.1 2.2 %collective-permute-start.9 = (bf16[528,128]{1,0:T(8,128)(2,1)S(1)}, bf16[528,128]{1,0:T(8,128)(2,1)S(1)}, u32[]{:S(2)}, u32[]{:S(2)}) collective-permute-start(bf16[528,128]{1,0:T(8,128)(2,1)S(1)} %get-tuple-element.49), channel_id=1, source_target_pairs={{0,9},{1,8},{4,13},{5,12},{8,1},{9,0},{12,5},{13,4},{2,11},{3,10},... | collective-permute-start | bytes 405512 | tf_op jit(solution)/shard_map/ppermute | solution.py:336
  29.3 0.7 collective-permute-start.10
  30.8 3.6 %collective-permute-done.8.rest_5_ = bf16[528,128]{1,0:T(8,128)(2,1)S(1)} collective-permute-done((bf16[528,128]{1,0:T(8,128)(2,1)S(1)}, bf16[528,128]{1,0:T(8,128)(2,1)S(1)}, u32[]{:S(2)}, u32[]{:S(2)}) %collective-permute-start.8) | collective-permute-done | bytes 135200 | tf_op jit(solution)/shard_map/ppermute | solution.py:336
  34.3 6.4 %collective-permute-done.9.rest_6_ = bf16[528,128]{1,0:T(8,128)(2,1)S(1)} collective-permute-done((bf16[528,128]{1,0:T(8,128)(2,1)S(1)}, bf16[528,128]{1,0:T(8,128)(2,1)S(1)}, u32[]{:S(2)}, u32[]{:S(2)}) %collective-permute-start.9) | collective-permute-done | bytes 135200 | tf_op jit(solution)/shard_map/ppermute | solution.py:336
  40.7 1.5 %shard_map.89 = (f32[96,1024]{1,0:T(8,128)S(1)}, f32[216,128]{1,0:T(8,128)S(1)}, f32[296,128]{1,0:T(8,128)S(1)}, f32[96,128]{1,0:T(8,128)S(1)}, f32[128,1024]{1,0:T(8,128)S(1)}, /*index=5*/f32[16,128]{1,0:T(8,128)S(1)}) custom-call(f32[96,1024]{1,0:T(8,128)S(1)} %get-tuple-element.40.base, f32[128,1024]{1,0:T(8,128)S(1)} %get-tuple-element.41.predicted, ...), custom_call_target="tpu_custom_call" | custom-call | flops 1000000 | bytes 1000000 | tf_op jit(solution)/shard_map/pallas_call | solution.py:322
  42.3 1.4 %collective-permute-start.11 = (f32[296,128]{1,0:T(8,128)S(1)}, f32[296,128]{1,0:T(8,128)S(1)}, u32[]{:S(2)}, u32[]{:S(2)}) collective-permute-start(f32[296,128]{1,0:T(8,128)S(1)} %get-tuple-element.55), channel_id=1, source_target_pairs={{0,1},{1,0},{2,3},{3,2},{4,5},{5,4},{6,7},{7,6},{8,9},{9,8},{10,11... | collective-permute-start | bytes 454664 | tf_op jit(solution)/shard_map/ppermute | solution.py:336
  43.6 1.0 %collective-permute-done.11.theirs = f32[296,128]{1,0:T(8,128)S(1)} collective-permute-done((f32[296,128]{1,0:T(8,128)S(1)}, f32[296,128]{1,0:T(8,128)S(1)}, u32[]{:S(2)}, u32[]{:S(2)}) %collective-permute-start.11) | collective-permute-done | bytes 151584 | tf_op jit(solution)/shard_map/ppermute | solution.py:336
  45.7 4.2 %collective-permute-done.13.theirs = f32[200,128]{1,0:T(8,128)S(1)} collective-permute-done((f32[200,128]{1,0:T(8,128)S(1)}, f32[200,128]{1,0:T(8,128)S(1)}, u32[]{:S(2)}, u32[]{:S(2)}) %collective-permute-start.13) | collective-permute-done | bytes 102432 | tf_op jit(solution)/shard_map/ppermute | solution.py:336
  49.9 0.8 %collective-permute-start.16 = (f32[216,128]{1,0:T(8,128)S(1)}, f32[216,128]{1,0:T(8,128)S(1)}, u32[]{:S(2)}, u32[]{:S(2)}) collective-permute-start(f32[216,128]{1,0:T(8,128)S(1)} %shard_map.91.refs_6_), channel_id=1, source_target_pairs={{0,12},{4,8},{8,4},{12,0},{1,13},{5,9},{9,5},{13,1},{2,14},{6,10},... | collective-permute-start | bytes 331784 | tf_op jit(solution)/shard_map/ppermute | solution.py:336
  50.8 3.4 %collective-permute-start.15 = (f32[216,128]{1,0:T(8,128)S(1)}, f32[216,128]{1,0:T(8,128)S(1)}, u32[]{:S(2)}, u32[]{:S(2)}) collective-permute-start(f32[216,128]{1,0:T(8,128)S(1)} %shard_map.91.refs_6_), channel_id=1, source_target_pairs={{0,8},{4,12},{8,0},{12,4},{1,9},{5,13},{9,1},{13,5},{2,10},{6,14},... | collective-permute-start | bytes 331784 | tf_op jit(solution)/shard_map/ppermute | solution.py:336
  54.4 3.4 %collective-permute-done.16.refs_9_.refs_11_ = f32[216,128]{1,0:T(8,128)S(1)} collective-permute-done((f32[216,128]{1,0:T(8,128)S(1)}, f32[216,128]{1,0:T(8,128)S(1)}, u32[]{:S(2)}, u32[]{:S(2)}) %collective-permute-start.16) | collective-permute-done | bytes 110624 | tf_op jit(solution)/shard_map/ppermute | solution.py:336
  57.8 6.7 %collective-permute-done.15.refs_8_ = f32[216,128]{1,0:T(8,128)S(1)} collective-permute-done((f32[216,128]{1,0:T(8,128)S(1)}, f32[216,128]{1,0:T(8,128)S(1)}, u32[]{:S(2)}, u32[]{:S(2)}) %collective-permute-start.15) | collective-permute-done | bytes 110624 | tf_op jit(solution)/shard_map/ppermute | solution.py:336
  64.5 1.7 %shard_map.92 = (f32[96,1024]{1,0:T(8,128)S(1)}, f32[96,128]{1,0:T(8,128)S(1)}, f32[200,128]{1,0:T(8,128)S(1)}, f32[200,128]{1,0:T(8,128)S(1)}) custom-call(f32[96,1024]{1,0:T(8,128)S(1)} %get-tuple-element.51.refs_0_, f32[96,128]{1,0:T(8,128)S(1)} %get-tuple-element.43.time_t.refs_1_, f32[128,1024]{1,0:T(8,128)S(1)} %get-tuple-element.52.refs_2_, ...), custom_call_target="tpu_custom_call" | custom-call | flops 1000000 | bytes 1000000 | tf_op jit(solution)/shard_map/pallas_call | solution.py:322
  66.8 1.4 %collective-permute-done.18.theirs = f32[200,128]{1,0:T(8,128)S(1)} collective-permute-done((f32[200,128]{1,0:T(8,128)S(1)}, f32[200,128]{1,0:T(8,128)S(1)}, u32[]{:S(2)}, u32[]{:S(2)}) %collective-permute-start.18) | collective-permute-done | bytes 102432 | tf_op jit(solution)/shard_map/ppermute | solution.py:336
  68.2 4.9 %collective-permute-done.19.theirs = f32[200,128]{1,0:T(8,128)S(1)} collective-permute-done((f32[200,128]{1,0:T(8,128)S(1)}, f32[200,128]{1,0:T(8,128)S(1)}, u32[]{:S(2)}, u32[]{:S(2)}) %collective-permute-start.19) | collective-permute-done | bytes 102432 | tf_op jit(solution)/shard_map/ppermute | solution.py:336
  73.2 0.8 %collective-permute-start.22 = (bf16[208,128]{1,0:T(8,128)(2,1)S(1)}, bf16[208,128]{1,0:T(8,128)(2,1)S(1)}, u32[]{:S(2)}, u32[]{:S(2)}) collective-permute-start(bf16[208,128]{1,0:T(8,128)(2,1)S(1)} %shard_map.94.rest_0_), channel_id=1, source_target_pairs={{0,12},{4,8},{8,4},{12,0},{1,13},{5,9},{9,5},{13,1},{2,14},{6,10},... | collective-permute-start | bytes 159752 | tf_op jit(solution)/shard_map/ppermute | solution.py:336
  74.0 3.6 %collective-permute-start.20 = (bf16[208,128]{1,0:T(8,128)(2,1)S(1)}, bf16[208,128]{1,0:T(8,128)(2,1)S(1)}, u32[]{:S(2)}, u32[]{:S(2)}) collective-permute-start(bf16[208,128]{1,0:T(8,128)(2,1)S(1)} %shard_map.94.rest_0_), channel_id=1, source_target_pairs={{0,4},{4,0},{8,12},{12,8},{1,5},{5,1},{9,13},{13,9},{2,6},{6,2},{1... | collective-permute-start | bytes 159752 | tf_op jit(solution)/shard_map/ppermute | solution.py:336
  77.6 1.8 %collective-permute-done.22.rest_3_ = bf16[208,128]{1,0:T(8,128)(2,1)S(1)} collective-permute-done((bf16[208,128]{1,0:T(8,128)(2,1)S(1)}, bf16[208,128]{1,0:T(8,128)(2,1)S(1)}, u32[]{:S(2)}, u32[]{:S(2)}) %collective-permute-start.22) | collective-permute-done | bytes 53280 | tf_op jit(solution)/shard_map/ppermute | solution.py:336
  79.4 0.8 collective-permute-done.21.rest_2_
  80.2 1.5 %shard_map.95 = (f32[1536,128]{1,0:T(8,128)}, f32[64,96]{1,0:T(8,128)}) custom-call(f32[96,1024]{1,0:T(8,128)S(1)} %get-tuple-element.60.surface, f32[96,1024]{1,0:T(8,128)S(1)} %collective-permute-done.17.other, f32[96,128]{1,0:T(8,128)S(1)} %get-tuple-element.61.time_t, bf16[208,128]{1,0:T(8,128)(2,1)S(1)} %shard_map.94.rest_0_, ...), custom_call_target="tpu_custom_call" | custom-call | flops 1000000 | bytes 1000000 | tf_op jit(solution)/shard_map/pallas_call | solution.py:322
  (38 shorter events, 5.1 us)
Async XLA Ops:
  0.6 1.2 %copy-start = (bf16[64,64,128]{2,1,0:T(8,128)(2,1)S(1)}, bf16[64,64,128]{2,1,0:T(8,128)(2,1)}, u32[]{:S(2)}) copy-start(bf16[64,64,128]{2,1,0:T(8,128)(2,1)} %swath_hbm.1) | copy-start | bytes 3145732
  1.9 0.8 copy-start.2
  2.6 0.7 copy-start.4
  3.3 0.7 copy-start.5
  4.0 0.7 copy-start.6
  4.6 11.4 %copy-start.1 = (f32[96,16,128]{2,1,0:T(8,128)S(1)}, f32[96,16,128]{2,1,0:T(8,128)}, u32[]{:S(2)}) copy-start(f32[96,16,128]{2,1,0:T(8,128)} %param.12) | copy-start | bytes 2359300
  4.6 11.4 %copy-start.3 = (f32[64,96]{1,0:T(8,128)S(1)}, f32[64,96]{1,0:T(8,128)}, u32[]{:S(2)}) copy-start(f32[64,96]{1,0:T(8,128)} %time_ref.1) | copy-start | bytes 73732
  7.4 8.7 %collective-permute-start = (bf16[528,128]{1,0:T(8,128)(2,1)S(1)}, bf16[528,128]{1,0:T(8,128)(2,1)S(1)}, u32[]{:S(2)}, u32[]{:S(2)}) collective-permute-start(bf16[528,128]{1,0:T(8,128)(2,1)S(1)} %get-tuple-element.34), channel_id=1, source_target_pairs={{0,4},{4,0},{8,12},{12,8},{1,5},{5,1},{9,13},{13,9},{2,6},{6,2},{1... | collective-permute-start | bytes 405512 | tf_op jit(solution)/shard_map/ppermute | solution.py:336
  10.5 13.0 %collective-permute-start.5 = (bf16[528,128]{1,0:T(8,128)(2,1)S(1)}, bf16[528,128]{1,0:T(8,128)(2,1)S(1)}, u32[]{:S(2)}, u32[]{:S(2)}) collective-permute-start(bf16[528,128]{1,0:T(8,128)(2,1)S(1)} %get-tuple-element.45), channel_id=1, source_target_pairs={{0,8},{4,12},{8,0},{12,4},{1,9},{5,13},{9,1},{13,5},{2,10},{6,14},... | collective-permute-start | bytes 405512 | tf_op jit(solution)/shard_map/ppermute | solution.py:336
  16.5 12.9 %collective-permute-start.1 = (f32[96,128]{1,0:T(8,128)S(1)}, f32[96,128]{1,0:T(8,128)S(1)}, u32[]{:S(2)}, u32[]{:S(2)}) collective-permute-start(f32[96,128]{1,0:T(8,128)S(1)} %get-tuple-element.37), channel_id=1, source_target_pairs={{1,2},{2,1},{5,6},{6,5},{9,10},{10,9},{13,14},{14,13},{17,18},{18,... | collective-permute-start | bytes 147464 | tf_op jit(solution)/shard_map/ppermute | solution.py:376
  17.1 10.0 %collective-permute-start.4 = (f32[64,96]{1,0:T(8,128)S(1)}, f32[64,96]{1,0:T(8,128)S(1)}, u32[]{:S(2)}, u32[]{:S(2)}) collective-permute-start(f32[64,96]{1,0:T(8,128)S(1)} %get-tuple-element.39.refs_5_), channel_id=1, source_target_pairs={{0,1},{1,0},{2,3},{3,2},{4,5},{5,4},{6,7},{7,6},{8,9},{9,8},{10,11... | collective-permute-start | bytes 73736 | tf_op jit(solution)/shard_map/ppermute | solution.py:336
  20.4 5.4 %collective-permute-start.3 = (f32[16,128]{1,0:T(8,128)S(1)}, f32[16,128]{1,0:T(8,128)S(1)}, u32[]{:S(2)}, u32[]{:S(2)}) collective-permute-start(f32[16,128]{1,0:T(8,128)S(1)} %get-tuple-element.38), channel_id=1, source_target_pairs={{0,12},{4,8},{8,4},{12,0},{1,13},{5,9},{9,5},{13,1},{2,14},{6,10},... | collective-permute-start | bytes 24584 | tf_op jit(solution)/shard_map/ppermute | solution.py:336
  23.5 3.7 %collective-permute-start.2 = (f32[16,128]{1,0:T(8,128)S(1)}, f32[16,128]{1,0:T(8,128)S(1)}, u32[]{:S(2)}, u32[]{:S(2)}) collective-permute-start(f32[16,128]{1,0:T(8,128)S(1)} %get-tuple-element.38), channel_id=1, source_target_pairs={{0,4},{4,0},{8,12},{12,8},{1,5},{5,1},{9,13},{13,9},{2,6},{6,2},{1... | collective-permute-start | bytes 24584 | tf_op jit(solution)/shard_map/ppermute | solution.py:336
  23.5 7.3 %collective-permute-start.6 = (bf16[528,128]{1,0:T(8,128)(2,1)S(1)}, bf16[528,128]{1,0:T(8,128)(2,1)S(1)}, u32[]{:S(2)}, u32[]{:S(2)}) collective-permute-start(bf16[528,128]{1,0:T(8,128)(2,1)S(1)} %get-tuple-element.46), channel_id=1, source_target_pairs={{0,12},{4,8},{8,4},{12,0},{1,13},{5,9},{9,5},{13,1},{2,14},{6,10},... | collective-permute-start | bytes 405512 | tf_op jit(solution)/shard_map/ppermute | solution.py:336
  25.8 5.0 %collective-permute-start.7 = (bf16[528,128]{1,0:T(8,128)(2,1)S(1)}, bf16[528,128]{1,0:T(8,128)(2,1)S(1)}, u32[]{:S(2)}, u32[]{:S(2)}) collective-permute-start(bf16[528,128]{1,0:T(8,128)(2,1)S(1)} %get-tuple-element.47), channel_id=1, source_target_pairs={{0,1},{1,0},{4,5},{5,4},{8,9},{9,8},{12,13},{13,12},{2,3},{3,2},{6... | collective-permute-start | bytes 405512 | tf_op jit(solution)/shard_map/ppermute | solution.py:336
  27.1 7.2 %collective-permute-start.8 = (bf16[528,128]{1,0:T(8,128)(2,1)S(1)}, bf16[528,128]{1,0:T(8,128)(2,1)S(1)}, u32[]{:S(2)}, u32[]{:S(2)}) collective-permute-start(bf16[528,128]{1,0:T(8,128)(2,1)S(1)} %get-tuple-element.48), channel_id=1, source_target_pairs={{0,5},{1,4},{4,1},{5,0},{8,13},{9,12},{12,9},{13,8},{2,7},{3,6},{6... | collective-permute-start | bytes 405512 | tf_op jit(solution)/shard_map/ppermute | solution.py:336
  27.1 13.6 %collective-permute-start.9 = (bf16[528,128]{1,0:T(8,128)(2,1)S(1)}, bf16[528,128]{1,0:T(8,128)(2,1)S(1)}, u32[]{:S(2)}, u32[]{:S(2)}) collective-permute-start(bf16[528,128]{1,0:T(8,128)(2,1)S(1)} %get-tuple-element.49), channel_id=1, source_target_pairs={{0,9},{1,8},{4,13},{5,12},{8,1},{9,0},{12,5},{13,4},{2,11},{3,10},... | collective-permute-start | bytes 405512 | tf_op jit(solution)/shard_map/ppermute | solution.py:336
  29.3 11.4 %collective-permute-start.10 = (bf16[528,128]{1,0:T(8,128)(2,1)S(1)}, bf16[528,128]{1,0:T(8,128)(2,1)S(1)}, u32[]{:S(2)}, u32[]{:S(2)}) collective-permute-start(bf16[528,128]{1,0:T(8,128)(2,1)S(1)} %get-tuple-element.50), channel_id=1, source_target_pairs={{0,13},{1,12},{4,9},{5,8},{8,5},{9,4},{12,1},{13,0},{2,15},{3,14},... | collective-permute-start | bytes 405512 | tf_op jit(solution)/shard_map/ppermute | solution.py:336
  42.3 2.4 %collective-permute-start.11 = (f32[296,128]{1,0:T(8,128)S(1)}, f32[296,128]{1,0:T(8,128)S(1)}, u32[]{:S(2)}, u32[]{:S(2)}) collective-permute-start(f32[296,128]{1,0:T(8,128)S(1)} %get-tuple-element.55), channel_id=1, source_target_pairs={{0,1},{1,0},{2,3},{3,2},{4,5},{5,4},{6,7},{7,6},{8,9},{9,8},{10,11... | collective-permute-start | bytes 454664 | tf_op jit(solution)/shard_map/ppermute | solution.py:336
  44.7 5.2 %collective-permute-start.13 = (f32[200,128]{1,0:T(8,128)S(1)}, f32[200,128]{1,0:T(8,128)S(1)}, u32[]{:S(2)}, u32[]{:S(2)}) collective-permute-start(f32[200,128]{1,0:T(8,128)S(1)} %get-tuple-element.59.mine), channel_id=1, source_target_pairs={{0,2},{2,0},{1,3},{3,1},{4,6},{6,4},{5,7},{7,5},{8,10},{10,8},{9,1... | collective-permute-start | bytes 307208 | tf_op jit(solution)/shard_map/ppermute | solution.py:336
  45.0 0.7 collective-permute-start.12
  49.9 7.9 %collective-permute-start.16 = (f32[216,128]{1,0:T(8,128)S(1)}, f32[216,128]{1,0:T(8,128)S(1)}, u32[]{:S(2)}, u32[]{:S(2)}) collective-permute-start(f32[216,128]{1,0:T(8,128)S(1)} %shard_map.91.refs_6_), channel_id=1, source_target_pairs={{0,12},{4,8},{8,4},{12,0},{1,13},{5,9},{9,5},{13,1},{2,14},{6,10},... | collective-permute-start | bytes 331784 | tf_op jit(solution)/shard_map/ppermute | solution.py:336
  50.8 13.8 %collective-permute-start.15 = (f32[216,128]{1,0:T(8,128)S(1)}, f32[216,128]{1,0:T(8,128)S(1)}, u32[]{:S(2)}, u32[]{:S(2)}) collective-permute-start(f32[216,128]{1,0:T(8,128)S(1)} %shard_map.91.refs_6_), channel_id=1, source_target_pairs={{0,8},{4,12},{8,0},{12,4},{1,9},{5,13},{9,1},{13,5},{2,10},{6,14},... | collective-permute-start | bytes 331784 | tf_op jit(solution)/shard_map/ppermute | solution.py:336
  54.1 10.4 %collective-permute-start.14 = (f32[216,128]{1,0:T(8,128)S(1)}, f32[216,128]{1,0:T(8,128)S(1)}, u32[]{:S(2)}, u32[]{:S(2)}) collective-permute-start(f32[216,128]{1,0:T(8,128)S(1)} %shard_map.91.refs_6_), channel_id=1, source_target_pairs={{0,4},{4,0},{8,12},{12,8},{1,5},{5,1},{9,13},{13,9},{2,6},{6,2},{1... | collective-permute-start | bytes 331784 | tf_op jit(solution)/shard_map/ppermute | solution.py:336
  66.2 14.0 %collective-permute-start.17 = (f32[96,1024]{1,0:T(8,128)S(1)}, f32[96,1024]{1,0:T(8,128)S(1)}, u32[]{:S(2)}, u32[]{:S(2)}) collective-permute-start(f32[96,1024]{1,0:T(8,128)S(1)} %get-tuple-element.60.surface), channel_id=1, source_target_pairs={{0,1},{1,0},{2,3},{3,2},{4,5},{5,4},{6,7},{7,6},{8,9},{9,8},{10,11... | collective-permute-start | bytes 1179656 | tf_op jit(solution)/shard_map/ppermute | solution.py:336
  66.4 1.8 %collective-permute-start.18 = (f32[200,128]{1,0:T(8,128)S(1)}, f32[200,128]{1,0:T(8,128)S(1)}, u32[]{:S(2)}, u32[]{:S(2)}) collective-permute-start(f32[200,128]{1,0:T(8,128)S(1)} %get-tuple-element.63), channel_id=1, source_target_pairs={{0,1},{1,0},{2,3},{3,2},{4,5},{5,4},{6,7},{7,6},{8,9},{9,8},{10,11... | collective-permute-start | bytes 307208 | tf_op jit(solution)/shard_map/ppermute | solution.py:336
  68.1 5.0 %collective-permute-start.19 = (f32[200,128]{1,0:T(8,128)S(1)}, f32[200,128]{1,0:T(8,128)S(1)}, u32[]{:S(2)}, u32[]{:S(2)}) collective-permute-start(f32[200,128]{1,0:T(8,128)S(1)} %shard_map.93.mine), channel_id=1, source_target_pairs={{0,2},{2,0},{1,3},{3,1},{4,6},{6,4},{5,7},{7,5},{8,10},{10,8},{9,1... | collective-permute-start | bytes 307208 | tf_op jit(solution)/shard_map/ppermute | solution.py:336
  73.2 6.2 %collective-permute-start.22 = (bf16[208,128]{1,0:T(8,128)(2,1)S(1)}, bf16[208,128]{1,0:T(8,128)(2,1)S(1)}, u32[]{:S(2)}, u32[]{:S(2)}) collective-permute-start(bf16[208,128]{1,0:T(8,128)(2,1)S(1)} %shard_map.94.rest_0_), channel_id=1, source_target_pairs={{0,12},{4,8},{8,4},{12,0},{1,13},{5,9},{9,5},{13,1},{2,14},{6,10},... | collective-permute-start | bytes 159752 | tf_op jit(solution)/shard_map/ppermute | solution.py:336
  74.0 6.2 %collective-permute-start.21 = (bf16[208,128]{1,0:T(8,128)(2,1)S(1)}, bf16[208,128]{1,0:T(8,128)(2,1)S(1)}, u32[]{:S(2)}, u32[]{:S(2)}) collective-permute-start(bf16[208,128]{1,0:T(8,128)(2,1)S(1)} %shard_map.94.rest_0_), channel_id=1, source_target_pairs={{0,8},{4,12},{8,0},{12,4},{1,9},{5,13},{9,1},{13,5},{2,10},{6,14},... | collective-permute-start | bytes 159752 | tf_op jit(solution)/shard_map/ppermute | solution.py:336
  74.0 6.2 %collective-permute-start.20 = (bf16[208,128]{1,0:T(8,128)(2,1)S(1)}, bf16[208,128]{1,0:T(8,128)(2,1)S(1)}, u32[]{:S(2)}, u32[]{:S(2)}) collective-permute-start(bf16[208,128]{1,0:T(8,128)(2,1)S(1)} %shard_map.94.rest_0_), channel_id=1, source_target_pairs={{0,4},{4,0},{8,12},{12,8},{1,5},{5,1},{9,13},{13,9},{2,6},{6,2},{1... | collective-permute-start | bytes 159752 | tf_op jit(solution)/shard_map/ppermute | solution.py:336

commit v4 on v3

--- a/solution.py
+++ b/solution.py
@@ -27,16 +27,18 @@
     return lax.dot_general(a, b, ((contract[:1], contract[1:]), ((), ())), preferred_element_type=F32)
 
 
-def route_kernel(half, sends, list_hbm, count_hbm, target_hbm, swath_hbm, mask_hbm, *rest):
+def route_kernel(half, sends, paired, list_hbm, count_hbm, target_hbm, swath_hbm, mask_hbm, space_hbm, time_hbm, *rest):
     outs, rest = rest[: len(sends)], rest[len(sends):]
-    list_ref, count_ref, target_ref, swath_ref, mask_ref, place, total, seen, arrived = rest
+    surface, edge_near, edge_far, cols, rest = *rest[:4], rest[4:]
+    list_ref, count_ref, target_ref, swath_ref, mask_ref, space_ref, time_ref, place, total, seen, flip, arrived = rest
     me, core = lax.axis_index("lon"), lax.axis_index("ta")
     n_lon = list_ref.shape[1]
     slots, days, cells = swath_ref.shape
     chunk = slots // SWATH_COPIES
     small = [(list_hbm, list_ref), (count_hbm, count_ref), (target_hbm, target_ref), (mask_hbm, mask_ref)]
     large = [(swath_hbm.at[pl.ds(at, chunk)], swath_ref.at[pl.ds(at, chunk)]) for at in range(0, slots, chunk)]
-    copies = [pltpu.make_async_copy(src, dst, arrived.at[i]) for i, (src, dst) in enumerate(small + large)]
+    model = [(space_hbm, space_ref), (time_hbm, time_ref)]
+    copies = [pltpu.make_async_copy(src, dst, arrived.at[i]) for i, (src, dst) in enumerate(small + large + model)]
     for copy in copies:
         copy.start()
     total[...] = jnp.zeros(total.shape, F32)
@@ -65,10 +67,29 @@
         at = place[slot]
         total[at] += swath_ref[slot].astype(F32) * by_day[:, slot:slot + 1]
         seen[pl.ds(at, 1), :days] += mask[slot:slot + 1, :]
+    for copy in copies[len(small) + len(large):]:
+        copy.wait()
+    rank = surface.shape[0]
+    height = space_ref.shape[0] // rank
+    for row in range(half):
+        surface[:, row * LANES:(row + 1) * LANES] = space_ref[pl.ds(core * half + row, rank, stride=height), :]
+    edge_near[...] = space_ref[pl.ds(half - core, rank, stride=height), :]
+    edge_far[...] = space_ref[pl.ds(core * (height - 1), rank, stride=height), :]
+    cols[...] = columns_as_rows(border(surface[...], half), flip)[:COLS, :]
     for (side, step), out in zip(sends, outs):
         at = (side * n_lon + step) * half
+        end = half * days + TAIL
         out[: half * days, :] = total[at:at + half].reshape(half * days, cells).astype(BF16)
-        out[half * days:, :] = seen[at:at + TAIL, :].astype(BF16)
+        out[half * days:end, :] = seen[at:at + TAIL, :].astype(BF16)
+        if (side, step) == (1, 0):
+            left = time_ref[...]
+            for part in range(end, end + 3 * days, days):
+                value = left.astype(BF16)
+                out[part:part + days, :] = jnp.zeros((days, LANES), BF16)
+                out[part:part + days, :rank] = value
+                left = left - value.astype(F32)
+        elif paired and side == 0 and step in (1, 3):
+            out[end:, :] = cols[...].astype(BF16)
 
 
 def row_of(surface, row):
@@ -111,41 +132,36 @@
     return strips
 
 
-def prepare_kernel(half, space_ref, time_ref, after, surface, edge_near, edge_far, cols, time_own, flip):
-    core = lax.axis_index("ta")
-    rank = surface.shape[0]
-    height = space_ref.shape[0] // rank
-    for row in range(half):
-        surface[:, row * LANES:(row + 1) * LANES] = space_ref[pl.ds(core * half + row, rank, stride=height), :]
-    edge_near[...] = space_ref[pl.ds(half - core, rank, stride=height), :]
-    edge_far[...] = space_ref[pl.ds(core * (height - 1), rank, stride=height), :]
-    cols[...] = columns_as_rows(border(surface[...], half), flip)[:COLS, :]
-    time_own[...] = time_ref[...]
-
-
 def pick(flag, a, b):
     return jnp.where(flag, a, b)
 
 
-def model_kernel(half, surface, edge_near, edge_far, cols_a, cols_b, swap, time_own, time_other, base, predicted, packed, time_t, flip, days_all):
-    core = lax.axis_index("ta")
+def model_kernel(half, surface, time_own, piece, predicted, packed, time_t, days_all):
     rank = surface.shape[0]
     days = time_own.shape[0]
+    at = half * days + TAIL
+    high, middle, low = (piece[first:first + days, :].astype(F32) for first in range(at, at + 3 * days, days))
     days_all[...] = jnp.zeros(days_all.shape, F32)
     days_all[:days, :rank] = time_own[...]
-    days_all[days:, :rank] = time_other[...]
+    days_all[days:, :] = (high + middle) + low
     time_full = days_all[...]
     time_t[...] = time_full.T[:rank, :]
     packed[...] = surface[...].astype(BF16)
     time_bf = time_full[:, :rank].astype(BF16)
     for at in range(0, half * LANES, 2 * LANES):
         predicted[:, at:at + 2 * LANES] = dot(time_bf, packed[:, at:at + 2 * LANES], (1, 0))
-    above = pick(core == 0, edge_far[...], edge_near[...])
-    below = pick(core == 0, edge_near[...], edge_far[...])
-    odd = swap()
-    left = rows_as_columns(pick(odd, cols_a[...], cols_b[...]), rank, flip)
-    right = rows_as_columns(pick(odd, cols_b[...], cols_a[...]), rank, flip)
-    for row, strip in enumerate(smoothed(surface[...], half, above, below, left, right)):
+
+
+def smooth(half, odd, surface, edge_near, edge_far, cols_a, cols_b, scale, base, flip):
+    core = lax.axis_index("ta")
+    rank = surface.shape[0]
+    above = pick(core == 0, edge_far, edge_near)
+    below = pick(core == 0, edge_near, edge_far)
+    left = rows_as_columns(pick(odd, cols_a, cols_b), rank, flip)
+    right = rows_as_columns(pick(odd, cols_b, cols_a), rank, flip)
+    if scale is not None:
+        above, below, left, right = above * scale, below * scale, left * scale, right * scale
+    for row, strip in enumerate(smoothed(surface, half, above, below, left, right)):
         base[:, row * LANES:(row + 1) * LANES] = strip
 
 
@@ -199,24 +215,29 @@
         edge_far[...] = pick(core == 0, first_row, last_row)
 
 
-def first_kernel(half, n_lon, base, predicted, packed, time_t, *rest):
-    near, far = rest[:n_lon], rest[n_lon:2 * n_lon]
-    fresh, message, outgoing, edge_far, summed, seen, flip = rest[2 * n_lon:]
-    days = (near[0].shape[0] - TAIL) // half
+def first_kernel(half, days, order, paired, swap, surface, edge_near, predicted, packed, time_t, *rest):
+    pieces, rest = dict(zip(order, rest)), rest[len(order):]
+    edge_far_in, rest = rest[0], rest[1:]
+    if paired:
+        at = half * days + TAIL
+        cols = [pieces[0, step][at:, :].astype(F32) for step in (1, 3)]
+    else:
+        cols, rest = [ref[...] for ref in rest[:2]], rest[2:]
+    fresh, message, outgoing, edge_far, summed, seen, flip, base = rest
+    smooth(half, swap(), surface[...], edge_near[...], edge_far_in[...], *cols, None, base, flip)
+    sides = [[pieces[key] for key in sorted(pieces) if key[0] == side] for side in (0, 1)]
+
+    def add_up(parts, rows):
+        value = parts[0][rows, :].astype(F32)
+        for piece in parts[1:]:
+            value = value + piece[rows, :].astype(F32)
+        return value
+
     for row in range(half):
-        for first, parts in ((0, near), (days, far)):
-            value = parts[0][row * days:(row + 1) * days, :].astype(F32)
-            for piece in parts[1:]:
-                value = value + piece[row * days:(row + 1) * days, :].astype(F32)
-            summed[first:first + days, row * LANES:(row + 1) * LANES] = value
-
-    def counts(parts):
-        value = parts[0][half * days:, :].astype(F32)
-        for piece in parts[1:]:
-            value = value + piece[half * days:, :].astype(F32)
-        return value
-
-    seen[...] = counts(near) + pltpu.roll(counts(far), days, 1)
+        for first, parts in zip((0, days), sides):
+            summed[first:first + days, row * LANES:(row + 1) * LANES] = add_up(parts, slice(row * days, (row + 1) * days))
+    near, far = (add_up(parts, slice(half * days, half * days + TAIL)) for parts in sides)
+    seen[...] = near + pltpu.roll(far, days, 1)
     sums = gradients(half, base, predicted, packed, time_t[...], seen[...], summed, fresh)
     post(half, sums, fresh, message, outgoing, edge_far, flip)
 
@@ -241,7 +262,6 @@
 def second_kernel(half, counts, n_parts, swap, surface, time_t, summed, seen, edge_near, edge_far, *rest):
     parts, (cols_a, cols_b) = rest[:n_parts], rest[n_parts:n_parts + 2]
     fresh, time_out, message, outgoing, flip, scaled, base, predicted, packed = rest[n_parts + 2:]
-    core = lax.axis_index("ta")
     rank = surface.shape[0]
     time_new, scale = settle(rank, counts, parts, time_t[...], flip)
     time_now = time_new / scale
@@ -251,15 +271,8 @@
     time_bf = time_now.T.astype(BF16)
     for at in range(0, half * LANES, 2 * LANES):
         predicted[:, at:at + 2 * LANES] = dot(time_bf, packed[:, at:at + 2 * LANES], (1, 0))
-    near, far = edge_near[...], edge_far[...]
-    above = pick(core == 0, far, near) * scale
-    below = pick(core == 0, near, far) * scale
-    odd = swap()
-    from_a, from_b = cols_a[cols_a.shape[0] - COLS:, :], cols_b[cols_b.shape[0] - COLS:, :]
-    left = rows_as_columns(pick(odd, from_a, from_b), rank, flip) * scale
-    right = rows_as_columns(pick(odd, from_b, from_a), rank, flip) * scale
-    for row, strip in enumerate(smoothed(scaled[...], half, above, below, left, right)):
-        base[:, row * LANES:(row + 1) * LANES] = strip
+    cols = [ref[ref.shape[0] - COLS:, :] for ref in (cols_a, cols_b)]
+    smooth(half, swap(), scaled[...], edge_near[...], edge_far[...], *cols, scale, base, flip)
     sums = gradients(half, base, predicted, packed, time_now, seen[...], summed, fresh)
     post(half, sums, fresh, message, outgoing, None, flip)
 
@@ -317,6 +330,7 @@
 
 def call(kernel, out_shape, scratch=(), hbm=0, after=0, flops=1_000_000):
     def run(*operands):
+        operands = [pltpu.with_memory_space_constraint(x, pltpu.HBM) if i < hbm else x for i, x in enumerate(operands)]
         vmem = [*operands[hbm:len(operands) - after], *jax.tree.leaves(out_shape), *scratch]
         specs = [pltpu.HBM] * hbm + [pltpu.VMEM] * (len(operands) - hbm - after) + [pl.ANY] * after
         return pl.pallas_call(
@@ -346,36 +360,44 @@
     sum_rows = 2 * rank + NORM
     flip = pltpu.VMEM((LANES, LANES), F32)
 
+    paired = n_lon == 4
+
     distant, close = range(n_lon // 2, n_lon), range(1, n_lon // 2)
-    sends = [(side, step) for steps in (distant, close) for side in (0, 1) for step in steps] + [(1, 0), (0, 0)]
-    pieces = call(
-        functools.partial(route_kernel, half, sends),
-        [shape((half * days + TAIL, cells), BF16)] * len(sends),
-        [
-            pltpu.SMEM(send_list.shape, jnp.int32),
-            pltpu.SMEM(send_count.shape, jnp.int32),
-            pltpu.SMEM(target.shape, jnp.int32),
-            pltpu.VMEM(swath.shape, swath.dtype),
-            pltpu.VMEM(obs_mask.shape, jnp.int32),
+    sends = [(0, step) for step in distant] + [(1, 0)] + [(1, step) for step in distant]
+    sends += [(side, step) for side in (0, 1) for step in close] + [(0, 0)]
+
+    def piece_rows(side, step):
+        more = 3 * days if (side, step) == (1, 0) else COLS if paired and side == 0 and step in (1, 3) else 0
+        return half * days + TAIL + more
+
+    operands = (send_list, send_count, target, swath, obs_mask, factor_space.reshape(rank * height, cells), factor_time)
+    *pieces, surface, edge_near, edge_far, cols = call(
+        functools.partial(route_kernel, half, sends, paired),
+        [shape((piece_rows(*key), cells), BF16) for key in sends]
+        + [shape((rank, wide)), shape((rank, LANES)), shape((rank, LANES)), shape((COLS, LANES))],
+        [pltpu.SMEM(ref.shape, jnp.int32) for ref in operands[:3]]
+        + [pltpu.VMEM(ref.shape, ref.dtype) for ref in operands[3:]]
+        + [
             pltpu.SMEM((slots,), jnp.int32),
             pltpu.VMEM((2 * n_lon * half, days, cells), F32),
             pltpu.VMEM((2 * n_lon * half + TAIL, LANES), F32),
-            pltpu.SemaphoreType.DMA((4 + SWATH_COPIES,)),
+            flip,
+            pltpu.SemaphoreType.DMA((len(operands) - 1 + SWATH_COPIES,)),
         ],
-        hbm=5,
-    )(send_list, send_count, target, swath, obs_mask)
-    near_in, far_in = {}, {}
-    for (side, step), piece in zip(sends, pieces):
+        hbm=len(operands),
+    )(*operands)
+
+    def arrived(key, piece):
+        side, step = key
         if side:
-            far_in[step] = across(piece, ("lon", "ta"), 2 * step + 1)
-        else:
-            near_in[step] = across(piece, "lon", step) if step else piece
+            return across(piece, ("lon", "ta"), 2 * step + 1)
+        return across(piece, "lon", step) if step else piece
+
+    pieces = {key: arrived(key, piece) for key, piece in zip(sends, pieces)}
 
     def bands(edge):
         there = [(2 * band + 1, 2 * band + 2) for band in range(n_lat - 1)]
         return lax.ppermute(edge, ("lat", "ta"), there + [(b, a) for a, b in there])
-
-    paired = n_lon == 4
 
     def swap():
         return lax.rem(lax.axis_index("lon"), 2) == 1 if paired else jnp.bool_(True)
@@ -386,29 +408,18 @@
         ring = [(i, (i + 1) % n_lon) for i in range(n_lon)]
         return lax.ppermute(value, "lon", ring), lax.ppermute(value, "lon", [(b, a) for a, b in ring])
 
-    surface, edge_near, edge_far, cols, time_own = call(
-        functools.partial(prepare_kernel, half),
-        [shape((rank, wide)), shape((rank, LANES)), shape((rank, LANES)), shape((COLS, LANES)), shape(factor_time.shape)],
+    predicted, packed, time_t = call(
+        functools.partial(model_kernel, half),
+        [shape((2 * days, wide)), shape((rank, wide), BF16), shape((rank, LANES))],
         [flip],
-        after=1,
-    )(factor_space.reshape(rank * height, cells), factor_time, near_in[1])
-    cols_a, cols_b = columns(cols)
-
-    def model(*refs):
-        model_kernel(half, *refs[:5], swap, *refs[5:])
-
-    base, predicted, packed, time_t = call(
-        model,
-        [shape((rank, wide)), shape((2 * days, wide)), shape((rank, wide), BF16), shape((rank, LANES))],
-        [flip, flip],
-    )(surface, edge_near, bands(edge_far), cols_a, cols_b, time_own, across(time_own, "ta", 1))
+    )(surface, factor_time, pieces[1, 0])
 
     fresh = shape((rank, wide))
     surface, message, outgoing, edge_far, summed, seen = call(
-        functools.partial(first_kernel, half, n_lon),
+        functools.partial(first_kernel, half, days, sends, paired, swap),
         [fresh, shape((sum_rows + COLS, LANES)), shape((sum_rows + rank, LANES)), shape((rank, LANES)), shape((2 * days, wide)), shape((TAIL, LANES))],
-        [flip],
-    )(base, predicted, packed, time_t, *[near_in[s] for s in range(n_lon)], *[far_in[s] for s in range(n_lon)])
+        [flip, pltpu.VMEM((rank, wide), F32)],
+    )(surface, edge_near, predicted, packed, time_t, *[pieces[key] for key in sends], bands(edge_far), *(() if paired else columns(cols)))
 
     sums = shape((sum_rows, LANES))
     add = call(add_kernel, sums)

time: 82 us -> 73.6 us (0.90)
  waiting for transfers between devices: 40.1 us -> 34.8 us
  local copies, waits for them, and re-layouts: 3.97 us -> 0.01 us
    ppermute x21 -> x18, waiting for transfers between devices: 40.1 us -> 34.8 us  [across(): lax.ppermute(value, axis, [(i, i ^ step) for i in range(lax.axis_size(axi...]
    unnamed x14 -> x2, local copies, waits for them, and re-layouts: 3.97 us -> 0.01 us
    ppermute x21 -> x18, starting transfers between devices: 27 us -> 27.5 us  [across(): lax.ppermute(value, axis, [(i, i ^ step) for i in range(lax.axis_size(axi...]
    pallas_call x10 -> x9, Pallas kernels: 8.6 us -> 9.05 us  [run(): pl.pallas_call(kernel, out_shape=out_shape, in_specs=[pl.BlockSpec(memory...]
  transfers between devices with their start and end apart: 23 -> 20, of which waited for: 14 -> 12; matrix products, arithmetic and copies ran while one was open for 0% -> 0% of each run, Pallas kernels for 1% -> 0%
where the time goes in v4:
time: 73.6 us; the launch traced here: 73.4 us
  waiting for transfers between devices  34.8 us (47%)
  starting transfers between devices  28.8 us (39%)
  Pallas kernels  9.05 us (12%)
    ppermute x18, waiting for transfers between devices, across(): lax.ppermute(value, axis, [(i, i ^ step) for i in range(lax.axis_size(axi...  34.8 us
    ppermute x18, starting transfers between devices, across(): lax.ppermute(value, axis, [(i, i ^ step) for i in range(lax.axis_size(axi...  27.5 us
    pallas_call x9, Pallas kernels, run(): pl.pallas_call(kernel, out_shape=out_shape, in_specs=[pl.BlockSpec(memory...  9.05 us
  transfers between devices with their start and end apart: 20, of which 12 were waited for; matrix products, arithmetic and copies ran while one was open for 0% of the time, Pallas kernels for 0%

profile of v4, /device:TPU:0, one launch (start us, length us, event | category | flops | bytes accessed | tf_op | source)
XLA Modules:
  0.0 73.4 jit_solution(18114236658081395231)
XLA Ops:
  0.6 3.9 %shard_map.86 = (bf16[528,128]{1,0:T(8,128)(2,1)S(1)}, bf16[544,128]{1,0:T(8,128)(2,1)S(1)}, bf16[720,128]{1,0:T(8,128)(2,1)S(1)}, bf16[528,128]{1,0:T(8,128)(2,...) custom-call(s32[1,4,32]{2,1,0:T(4,128)} %list_hbm.1, ...), custom_call_target="tpu_custom_call" | custom-call | flops 1000000 | bytes 1000000 | tf_op jit(solution)/shard_map/pallas_call | solution.py:336
  4.6 0.5 collective-permute-start
  5.1 3.7 %collective-permute-start.1 = (bf16[528,128]{1,0:T(8,128)(2,1)S(1)}, bf16[528,128]{1,0:T(8,128)(2,1)S(1)}, u32[]{:S(2)}, u32[]{:S(2)}) collective-permute-start(bf16[528,128]{1,0:T(8,128)(2,1)S(1)} %get-tuple-element.37), channel_id=1, source_target_pairs={{0,8},{4,12},{8,0},{12,4},{1,9},{5,13},{9,1},{13,5},{2,10},{6,14},... | collective-permute-start | bytes 405512 | tf_op jit(solution)/shard_map/ppermute | solution.py:350
  8.7 0.7 collective-permute-start.7
  9.4 1.4 %collective-permute-start.2 = (bf16[544,128]{1,0:T(8,128)(2,1)S(1)}, bf16[544,128]{1,0:T(8,128)(2,1)S(1)}, u32[]{:S(2)}, u32[]{:S(2)}) collective-permute-start(bf16[544,128]{1,0:T(8,128)(2,1)S(1)} %get-tuple-element.38), channel_id=1, source_target_pairs={{0,12},{4,8},{8,4},{12,0},{1,13},{5,9},{9,5},{13,1},{2,14},{6,10},... | collective-permute-start | bytes 417800 | tf_op jit(solution)/shard_map/ppermute | solution.py:350
  10.8 0.3 collective-permute-start.5
  11.1 4.6 %collective-permute-start.3 = (bf16[528,128]{1,0:T(8,128)(2,1)S(1)}, bf16[528,128]{1,0:T(8,128)(2,1)S(1)}, u32[]{:S(2)}, u32[]{:S(2)}) collective-permute-start(bf16[528,128]{1,0:T(8,128)(2,1)S(1)} %get-tuple-element.39), channel_id=1, source_target_pairs={{0,9},{1,8},{4,13},{5,12},{8,1},{9,0},{12,5},{13,4},{2,11},{3,10},... | collective-permute-start | bytes 405512 | tf_op jit(solution)/shard_map/ppermute | solution.py:350
  15.7 2.7 %collective-permute-done.1.rest_0_ = bf16[528,128]{1,0:T(8,128)(2,1)S(1)} collective-permute-done((bf16[528,128]{1,0:T(8,128)(2,1)S(1)}, bf16[528,128]{1,0:T(8,128)(2,1)S(1)}, u32[]{:S(2)}, u32[]{:S(2)}) %collective-permute-start.1) | collective-permute-done | bytes 135200 | tf_op jit(solution)/shard_map/ppermute | solution.py:350
  18.4 4.8 %collective-permute-start.4 = (bf16[528,128]{1,0:T(8,128)(2,1)S(1)}, bf16[528,128]{1,0:T(8,128)(2,1)S(1)}, u32[]{:S(2)}, u32[]{:S(2)}) collective-permute-start(bf16[528,128]{1,0:T(8,128)(2,1)S(1)} %get-tuple-element.40), channel_id=1, source_target_pairs={{0,13},{1,12},{4,9},{5,8},{8,5},{9,4},{12,1},{13,0},{2,15},{3,14},... | collective-permute-start | bytes 405512 | tf_op jit(solution)/shard_map/ppermute | solution.py:350
  23.3 0.2 shard_map.87
  23.5 6.8 %collective-permute-done.3.rest_3_ = bf16[528,128]{1,0:T(8,128)(2,1)S(1)} collective-permute-done((bf16[528,128]{1,0:T(8,128)(2,1)S(1)}, bf16[528,128]{1,0:T(8,128)(2,1)S(1)}, u32[]{:S(2)}, u32[]{:S(2)}) %collective-permute-start.3) | collective-permute-done | bytes 135200 | tf_op jit(solution)/shard_map/ppermute | solution.py:350
  30.3 2.8 %collective-permute-done.6.rest_6_ = bf16[528,128]{1,0:T(8,128)(2,1)S(1)} collective-permute-done((bf16[528,128]{1,0:T(8,128)(2,1)S(1)}, bf16[528,128]{1,0:T(8,128)(2,1)S(1)}, u32[]{:S(2)}, u32[]{:S(2)}) %collective-permute-start.6) | collective-permute-done | bytes 135200 | tf_op jit(solution)/shard_map/ppermute | solution.py:350
  33.2 1.6 %shard_map.88 = (f32[96,1024]{1,0:T(8,128)S(1)}, f32[216,128]{1,0:T(8,128)S(1)}, f32[296,128]{1,0:T(8,128)S(1)}, f32[96,128]{1,0:T(8,128)S(1)}, f32[128,1024]{1,0:T(8,128)S(1)}, /*index=5*/f32[16,128]{1,0:T(8,128)S(1)}) custom-call(f32[96,1024]{1,0:T(8,128)S(1)} %get-tuple-element.31.surface, f32[96,128]{1,0:T(8,128)S(1)} %get-tuple-element.32.edge_near, ...), custom_call_target="tpu_custom_call" | custom-call | flops 1000000 | bytes 1000000 | tf_op jit(solution)/shard_map/pallas_call | solution.py:336
  34.9 1.3 %collective-permute-done.8.theirs = f32[296,128]{1,0:T(8,128)S(1)} collective-permute-done((f32[296,128]{1,0:T(8,128)S(1)}, f32[296,128]{1,0:T(8,128)S(1)}, u32[]{:S(2)}, u32[]{:S(2)}) %collective-permute-start.8) | collective-permute-done | bytes 151584 | tf_op jit(solution)/shard_map/ppermute | solution.py:350
  36.2 1.5 %collective-permute-start.10 = (f32[200,128]{1,0:T(8,128)S(1)}, f32[200,128]{1,0:T(8,128)S(1)}, u32[]{:S(2)}, u32[]{:S(2)}) collective-permute-start(f32[200,128]{1,0:T(8,128)S(1)} %get-tuple-element.53.mine), channel_id=1, source_target_pairs={{0,2},{2,0},{1,3},{3,1},{4,6},{6,4},{5,7},{7,5},{8,10},{10,8},{9,1... | collective-permute-start | bytes 307208 | tf_op jit(solution)/shard_map/ppermute | solution.py:350
  37.7 0.7 collective-permute-start.9
  38.4 2.9 %collective-permute-done.10.theirs = f32[200,128]{1,0:T(8,128)S(1)} collective-permute-done((f32[200,128]{1,0:T(8,128)S(1)}, f32[200,128]{1,0:T(8,128)S(1)}, u32[]{:S(2)}, u32[]{:S(2)}) %collective-permute-start.10) | collective-permute-done | bytes 102432 | tf_op jit(solution)/shard_map/ppermute | solution.py:350
  41.2 2.2 %collective-permute-start.13 = (f32[216,128]{1,0:T(8,128)S(1)}, f32[216,128]{1,0:T(8,128)S(1)}, u32[]{:S(2)}, u32[]{:S(2)}) collective-permute-start(f32[216,128]{1,0:T(8,128)S(1)} %shard_map.90.refs_6_), channel_id=1, source_target_pairs={{0,12},{4,8},{8,4},{12,0},{1,13},{5,9},{9,5},{13,1},{2,14},{6,10},... | collective-permute-start | bytes 331784 | tf_op jit(solution)/shard_map/ppermute | solution.py:350
  43.5 0.9 %collective-permute-start.12 = (f32[216,128]{1,0:T(8,128)S(1)}, f32[216,128]{1,0:T(8,128)S(1)}, u32[]{:S(2)}, u32[]{:S(2)}) collective-permute-start(f32[216,128]{1,0:T(8,128)S(1)} %shard_map.90.refs_6_), channel_id=1, source_target_pairs={{0,8},{4,12},{8,0},{12,4},{1,9},{5,13},{9,1},{13,5},{2,10},{6,14},... | collective-permute-start | bytes 331784 | tf_op jit(solution)/shard_map/ppermute | solution.py:350
  44.3 1.4 %collective-permute-start.11 = (f32[216,128]{1,0:T(8,128)S(1)}, f32[216,128]{1,0:T(8,128)S(1)}, u32[]{:S(2)}, u32[]{:S(2)}) collective-permute-start(f32[216,128]{1,0:T(8,128)S(1)} %shard_map.90.refs_6_), channel_id=1, source_target_pairs={{0,4},{4,0},{8,12},{12,8},{1,5},{5,1},{9,13},{13,9},{2,6},{6,2},{1... | collective-permute-start | bytes 331784 | tf_op jit(solution)/shard_map/ppermute | solution.py:350
  45.7 2.8 %collective-permute-done.13.refs_9_.refs_11_ = f32[216,128]{1,0:T(8,128)S(1)} collective-permute-done((f32[216,128]{1,0:T(8,128)S(1)}, f32[216,128]{1,0:T(8,128)S(1)}, u32[]{:S(2)}, u32[]{:S(2)}) %collective-permute-start.13) | collective-permute-done | bytes 110624 | tf_op jit(solution)/shard_map/ppermute | solution.py:350
  48.4 5.8 %collective-permute-done.12.refs_8_ = f32[216,128]{1,0:T(8,128)S(1)} collective-permute-done((f32[216,128]{1,0:T(8,128)S(1)}, f32[216,128]{1,0:T(8,128)S(1)}, u32[]{:S(2)}, u32[]{:S(2)}) %collective-permute-start.12) | collective-permute-done | bytes 110624 | tf_op jit(solution)/shard_map/ppermute | solution.py:350
  54.3 1.7 %shard_map.91 = (f32[96,1024]{1,0:T(8,128)S(1)}, f32[96,128]{1,0:T(8,128)S(1)}, f32[200,128]{1,0:T(8,128)S(1)}, f32[200,128]{1,0:T(8,128)S(1)}) custom-call(f32[96,1024]{1,0:T(8,128)S(1)} %get-tuple-element.45.refs_0_, f32[96,128]{1,0:T(8,128)S(1)} %get-tuple-element.36.time_t.refs_1_, f32[128,1024]{1,0:T(8,128)S(1)} %get-tuple-element.46.refs_2_, ...), custom_call_target="tpu_custom_call" | custom-call | flops 1000000 | bytes 1000000 | tf_op jit(solution)/shard_map/pallas_call | solution.py:336
  56.0 0.9 %collective-permute-start.14 = (f32[96,1024]{1,0:T(8,128)S(1)}, f32[96,1024]{1,0:T(8,128)S(1)}, u32[]{:S(2)}, u32[]{:S(2)}) collective-permute-start(f32[96,1024]{1,0:T(8,128)S(1)} %get-tuple-element.54.surface), channel_id=1, source_target_pairs={{0,1},{1,0},{2,3},{3,2},{4,5},{5,4},{6,7},{7,6},{8,9},{9,8},{10,11... | collective-permute-start | bytes 1179656 | tf_op jit(solution)/shard_map/ppermute | solution.py:350
  56.9 1.4 %collective-permute-done.15.theirs = f32[200,128]{1,0:T(8,128)S(1)} collective-permute-done((f32[200,128]{1,0:T(8,128)S(1)}, f32[200,128]{1,0:T(8,128)S(1)}, u32[]{:S(2)}, u32[]{:S(2)}) %collective-permute-start.15) | collective-permute-done | bytes 102432 | tf_op jit(solution)/shard_map/ppermute | solution.py:350
  58.3 0.7 collective-permute-start.16
  59.1 4.5 %collective-permute-done.16.theirs = f32[200,128]{1,0:T(8,128)S(1)} collective-permute-done((f32[200,128]{1,0:T(8,128)S(1)}, f32[200,128]{1,0:T(8,128)S(1)}, u32[]{:S(2)}, u32[]{:S(2)}) %collective-permute-start.16) | collective-permute-done | bytes 102432 | tf_op jit(solution)/shard_map/ppermute | solution.py:350
  63.6 3.1 %collective-permute-start.19 = (bf16[208,128]{1,0:T(8,128)(2,1)S(1)}, bf16[208,128]{1,0:T(8,128)(2,1)S(1)}, u32[]{:S(2)}, u32[]{:S(2)}) collective-permute-start(bf16[208,128]{1,0:T(8,128)(2,1)S(1)} %shard_map.93.rest_0_), channel_id=1, source_target_pairs={{0,12},{4,8},{8,4},{12,0},{1,13},{5,9},{9,5},{13,1},{2,14},{6,10},... | collective-permute-start | bytes 159752 | tf_op jit(solution)/shard_map/ppermute | solution.py:350
  66.7 1.4 %collective-permute-start.17 = (bf16[208,128]{1,0:T(8,128)(2,1)S(1)}, bf16[208,128]{1,0:T(8,128)(2,1)S(1)}, u32[]{:S(2)}, u32[]{:S(2)}) collective-permute-start(bf16[208,128]{1,0:T(8,128)(2,1)S(1)} %shard_map.93.rest_0_), channel_id=1, source_target_pairs={{0,4},{4,0},{8,12},{12,8},{1,5},{5,1},{9,13},{13,9},{2,6},{6,2},{1... | collective-permute-start | bytes 159752 | tf_op jit(solution)/shard_map/ppermute | solution.py:350
  68.0 1.6 %collective-permute-done.19.rest_3_ = bf16[208,128]{1,0:T(8,128)(2,1)S(1)} collective-permute-done((bf16[208,128]{1,0:T(8,128)(2,1)S(1)}, bf16[208,128]{1,0:T(8,128)(2,1)S(1)}, u32[]{:S(2)}, u32[]{:S(2)}) %collective-permute-start.19) | collective-permute-done | bytes 53280 | tf_op jit(solution)/shard_map/ppermute | solution.py:350
  69.6 2.1 %collective-permute-done.18.rest_2_ = bf16[208,128]{1,0:T(8,128)(2,1)S(1)} collective-permute-done((bf16[208,128]{1,0:T(8,128)(2,1)S(1)}, bf16[208,128]{1,0:T(8,128)(2,1)S(1)}, u32[]{:S(2)}, u32[]{:S(2)}) %collective-permute-start.18) | collective-permute-done | bytes 53280 | tf_op jit(solution)/shard_map/ppermute | solution.py:350
  71.9 1.5 %shard_map.94 = (f32[1536,128]{1,0:T(8,128)}, f32[64,96]{1,0:T(8,128)}) custom-call(f32[96,1024]{1,0:T(8,128)S(1)} %get-tuple-element.54.surface, f32[96,1024]{1,0:T(8,128)S(1)} %collective-permute-done.14.other, f32[96,128]{1,0:T(8,128)S(1)} %get-tuple-element.55.time_t, bf16[208,128]{1,0:T(8,128)(2,1)S(1)} %shard_map.93.rest_0_, ...), custom_call_target="tpu_custom_call" | custom-call | flops 1000000 | bytes 1000000 | tf_op jit(solution)/shard_map/pallas_call | solution.py:336
  (19 shorter events, 0.4 us)
Async XLA Ops:
  0.6 22.6 %copy-start = (f32[64,96]{1,0:T(8,128)S(1)}, f32[64,96]{1,0:T(8,128)}, u32[]{:S(2)}) copy-start(f32[64,96]{1,0:T(8,128)} %time_own.1) | copy-start | bytes 73732
  4.6 18.7 %collective-permute-start = (bf16[720,128]{1,0:T(8,128)(2,1)S(1)}, bf16[720,128]{1,0:T(8,128)(2,1)S(1)}, u32[]{:S(2)}, u32[]{:S(2)}) collective-permute-start(bf16[720,128]{1,0:T(8,128)(2,1)S(1)} %get-tuple-element.33), channel_id=1, source_target_pairs={{0,1},{1,0},{4,5},{5,4},{8,9},{9,8},{12,13},{13,12},{2,3},{3,2},{6... | collective-permute-start | bytes 552968 | tf_op jit(solution)/shard_map/ppermute | solution.py:350
  5.1 13.4 %collective-permute-start.1 = (bf16[528,128]{1,0:T(8,128)(2,1)S(1)}, bf16[528,128]{1,0:T(8,128)(2,1)S(1)}, u32[]{:S(2)}, u32[]{:S(2)}) collective-permute-start(bf16[528,128]{1,0:T(8,128)(2,1)S(1)} %get-tuple-element.37), channel_id=1, source_target_pairs={{0,8},{4,12},{8,0},{12,4},{1,9},{5,13},{9,1},{13,5},{2,10},{6,14},... | collective-permute-start | bytes 405512 | tf_op jit(solution)/shard_map/ppermute | solution.py:350
  8.7 2.4 %collective-permute-start.7 = (f32[96,128]{1,0:T(8,128)S(1)}, f32[96,128]{1,0:T(8,128)S(1)}, u32[]{:S(2)}, u32[]{:S(2)}) collective-permute-start(f32[96,128]{1,0:T(8,128)S(1)} %get-tuple-element.44), channel_id=1, source_target_pairs={{1,2},{2,1},{5,6},{6,5},{9,10},{10,9},{13,14},{14,13},{17,18},{18,... | collective-permute-start | bytes 147464 | tf_op jit(solution)/shard_map/ppermute | solution.py:400
  9.4 23.7 %collective-permute-start.2 = (bf16[544,128]{1,0:T(8,128)(2,1)S(1)}, bf16[544,128]{1,0:T(8,128)(2,1)S(1)}, u32[]{:S(2)}, u32[]{:S(2)}) collective-permute-start(bf16[544,128]{1,0:T(8,128)(2,1)S(1)} %get-tuple-element.38), channel_id=1, source_target_pairs={{0,12},{4,8},{8,4},{12,0},{1,13},{5,9},{9,5},{13,1},{2,14},{6,10},... | collective-permute-start | bytes 417800 | tf_op jit(solution)/shard_map/ppermute | solution.py:350
  10.8 22.3 %collective-permute-start.5 = (bf16[544,128]{1,0:T(8,128)(2,1)S(1)}, bf16[544,128]{1,0:T(8,128)(2,1)S(1)}, u32[]{:S(2)}, u32[]{:S(2)}) collective-permute-start(bf16[544,128]{1,0:T(8,128)(2,1)S(1)} %get-tuple-element.41), channel_id=1, source_target_pairs={{0,4},{4,0},{8,12},{12,8},{1,5},{5,1},{9,13},{13,9},{2,6},{6,2},{1... | collective-permute-start | bytes 417800 | tf_op jit(solution)/shard_map/ppermute | solution.py:350
  11.1 19.2 %collective-permute-start.3 = (bf16[528,128]{1,0:T(8,128)(2,1)S(1)}, bf16[528,128]{1,0:T(8,128)(2,1)S(1)}, u32[]{:S(2)}, u32[]{:S(2)}) collective-permute-start(bf16[528,128]{1,0:T(8,128)(2,1)S(1)} %get-tuple-element.39), channel_id=1, source_target_pairs={{0,9},{1,8},{4,13},{5,12},{8,1},{9,0},{12,5},{13,4},{2,11},{3,10},... | collective-permute-start | bytes 405512 | tf_op jit(solution)/shard_map/ppermute | solution.py:350
  18.4 11.9 %collective-permute-start.4 = (bf16[528,128]{1,0:T(8,128)(2,1)S(1)}, bf16[528,128]{1,0:T(8,128)(2,1)S(1)}, u32[]{:S(2)}, u32[]{:S(2)}) collective-permute-start(bf16[528,128]{1,0:T(8,128)(2,1)S(1)} %get-tuple-element.40), channel_id=1, source_target_pairs={{0,13},{1,12},{4,9},{5,8},{8,5},{9,4},{12,1},{13,0},{2,15},{3,14},... | collective-permute-start | bytes 405512 | tf_op jit(solution)/shard_map/ppermute | solution.py:350
  23.2 9.9 %collective-permute-start.6 = (bf16[528,128]{1,0:T(8,128)(2,1)S(1)}, bf16[528,128]{1,0:T(8,128)(2,1)S(1)}, u32[]{:S(2)}, u32[]{:S(2)}) collective-permute-start(bf16[528,128]{1,0:T(8,128)(2,1)S(1)} %get-tuple-element.42), channel_id=1, source_target_pairs={{0,5},{1,4},{4,1},{5,0},{8,13},{9,12},{12,9},{13,8},{2,7},{3,6},{6... | collective-permute-start | bytes 405512 | tf_op jit(solution)/shard_map/ppermute | solution.py:350
  34.8 1.4 %collective-permute-start.8 = (f32[296,128]{1,0:T(8,128)S(1)}, f32[296,128]{1,0:T(8,128)S(1)}, u32[]{:S(2)}, u32[]{:S(2)}) collective-permute-start(f32[296,128]{1,0:T(8,128)S(1)} %get-tuple-element.49), channel_id=1, source_target_pairs={{0,1},{1,0},{2,3},{3,2},{4,5},{5,4},{6,7},{7,6},{8,9},{9,8},{10,11... | collective-permute-start | bytes 454664 | tf_op jit(solution)/shard_map/ppermute | solution.py:350
  36.2 5.0 %collective-permute-start.10 = (f32[200,128]{1,0:T(8,128)S(1)}, f32[200,128]{1,0:T(8,128)S(1)}, u32[]{:S(2)}, u32[]{:S(2)}) collective-permute-start(f32[200,128]{1,0:T(8,128)S(1)} %get-tuple-element.53.mine), channel_id=1, source_target_pairs={{0,2},{2,0},{1,3},{3,1},{4,6},{6,4},{5,7},{7,5},{8,10},{10,8},{9,1... | collective-permute-start | bytes 307208 | tf_op jit(solution)/shard_map/ppermute | solution.py:350
  37.7 0.7 collective-permute-start.9
  41.2 7.2 %collective-permute-start.13 = (f32[216,128]{1,0:T(8,128)S(1)}, f32[216,128]{1,0:T(8,128)S(1)}, u32[]{:S(2)}, u32[]{:S(2)}) collective-permute-start(f32[216,128]{1,0:T(8,128)S(1)} %shard_map.90.refs_6_), channel_id=1, source_target_pairs={{0,12},{4,8},{8,4},{12,0},{1,13},{5,9},{9,5},{13,1},{2,14},{6,10},... | collective-permute-start | bytes 331784 | tf_op jit(solution)/shard_map/ppermute | solution.py:350
  43.5 10.8 %collective-permute-start.12 = (f32[216,128]{1,0:T(8,128)S(1)}, f32[216,128]{1,0:T(8,128)S(1)}, u32[]{:S(2)}, u32[]{:S(2)}) collective-permute-start(f32[216,128]{1,0:T(8,128)S(1)} %shard_map.90.refs_6_), channel_id=1, source_target_pairs={{0,8},{4,12},{8,0},{12,4},{1,9},{5,13},{9,1},{13,5},{2,10},{6,14},... | collective-permute-start | bytes 331784 | tf_op jit(solution)/shard_map/ppermute | solution.py:350
  44.3 9.9 %collective-permute-start.11 = (f32[216,128]{1,0:T(8,128)S(1)}, f32[216,128]{1,0:T(8,128)S(1)}, u32[]{:S(2)}, u32[]{:S(2)}) collective-permute-start(f32[216,128]{1,0:T(8,128)S(1)} %shard_map.90.refs_6_), channel_id=1, source_target_pairs={{0,4},{4,0},{8,12},{12,8},{1,5},{5,1},{9,13},{13,9},{2,6},{6,2},{1... | collective-permute-start | bytes 331784 | tf_op jit(solution)/shard_map/ppermute | solution.py:350
  56.0 15.9 %collective-permute-start.14 = (f32[96,1024]{1,0:T(8,128)S(1)}, f32[96,1024]{1,0:T(8,128)S(1)}, u32[]{:S(2)}, u32[]{:S(2)}) collective-permute-start(f32[96,1024]{1,0:T(8,128)S(1)} %get-tuple-element.54.surface), channel_id=1, source_target_pairs={{0,1},{1,0},{2,3},{3,2},{4,5},{5,4},{6,7},{7,6},{8,9},{9,8},{10,11... | collective-permute-start | bytes 1179656 | tf_op jit(solution)/shard_map/ppermute | solution.py:350
  56.8 1.5 %collective-permute-start.15 = (f32[200,128]{1,0:T(8,128)S(1)}, f32[200,128]{1,0:T(8,128)S(1)}, u32[]{:S(2)}, u32[]{:S(2)}) collective-permute-start(f32[200,128]{1,0:T(8,128)S(1)} %get-tuple-element.57), channel_id=1, source_target_pairs={{0,1},{1,0},{2,3},{3,2},{4,5},{5,4},{6,7},{7,6},{8,9},{9,8},{10,11... | collective-permute-start | bytes 307208 | tf_op jit(solution)/shard_map/ppermute | solution.py:350
  58.3 5.2 %collective-permute-start.16 = (f32[200,128]{1,0:T(8,128)S(1)}, f32[200,128]{1,0:T(8,128)S(1)}, u32[]{:S(2)}, u32[]{:S(2)}) collective-permute-start(f32[200,128]{1,0:T(8,128)S(1)} %shard_map.92.mine), channel_id=1, source_target_pairs={{0,2},{2,0},{1,3},{3,1},{4,6},{6,4},{5,7},{7,5},{8,10},{10,8},{9,1... | collective-permute-start | bytes 307208 | tf_op jit(solution)/shard_map/ppermute | solution.py:350
  63.6 6.0 %collective-permute-start.19 = (bf16[208,128]{1,0:T(8,128)(2,1)S(1)}, bf16[208,128]{1,0:T(8,128)(2,1)S(1)}, u32[]{:S(2)}, u32[]{:S(2)}) collective-permute-start(bf16[208,128]{1,0:T(8,128)(2,1)S(1)} %shard_map.93.rest_0_), channel_id=1, source_target_pairs={{0,12},{4,8},{8,4},{12,0},{1,13},{5,9},{9,5},{13,1},{2,14},{6,10},... | collective-permute-start | bytes 159752 | tf_op jit(solution)/shard_map/ppermute | solution.py:350
  66.7 5.1 %collective-permute-start.18 = (bf16[208,128]{1,0:T(8,128)(2,1)S(1)}, bf16[208,128]{1,0:T(8,128)(2,1)S(1)}, u32[]{:S(2)}, u32[]{:S(2)}) collective-permute-start(bf16[208,128]{1,0:T(8,128)(2,1)S(1)} %shard_map.93.rest_0_), channel_id=1, source_target_pairs={{0,8},{4,12},{8,0},{12,4},{1,9},{5,13},{9,1},{13,5},{2,10},{6,14},... | collective-permute-start | bytes 159752 | tf_op jit(solution)/shard_map/ppermute | solution.py:350
  66.7 5.2 %collective-permute-start.17 = (bf16[208,128]{1,0:T(8,128)(2,1)S(1)}, bf16[208,128]{1,0:T(8,128)(2,1)S(1)}, u32[]{:S(2)}, u32[]{:S(2)}) collective-permute-start(bf16[208,128]{1,0:T(8,128)(2,1)S(1)} %shard_map.93.rest_0_), channel_id=1, source_target_pairs={{0,4},{4,0},{8,12},{12,8},{1,5},{5,1},{9,13},{13,9},{2,6},{6,2},{1... | collective-permute-start | bytes 159752 | tf_op jit(solution)/shard_map/ppermute | solution.py:350

commit v5 on v4

--- a/solution.py
+++ b/solution.py
@@ -300,6 +300,10 @@
     edge_out[...] = edge_in[...]
 
 
+def merge_kernel(mine, theirs, out):
+    out[...] = (mine[...].astype(F32) + theirs[...].astype(F32)).astype(BF16)
+
+
 def add_kernel(mine, theirs, total):
     rows = total.shape[0]
     total[...] = mine[:rows, :] + theirs[:rows, :]
@@ -363,7 +367,7 @@
     paired = n_lon == 4
 
     distant, close = range(n_lon // 2, n_lon), range(1, n_lon // 2)
-    sends = [(0, step) for step in distant] + [(1, 0)] + [(1, step) for step in distant]
+    sends = [(1, step) for step in reversed(distant)] + [(0, step) for step in distant] + [(1, 0)]
     sends += [(side, step) for side in (0, 1) for step in close] + [(0, 0)]
 
     def piece_rows(side, step):
@@ -393,7 +397,12 @@
             return across(piece, ("lon", "ta"), 2 * step + 1)
         return across(piece, "lon", step) if step else piece
 
-    pieces = {key: arrived(key, piece) for key, piece in zip(sends, pieces)}
+    pieces = dict(zip(sends, pieces))
+    if paired:
+        passing = across(pieces.pop((1, 3)), "lon", 1)
+        pieces[1, 2] = call(merge_kernel, shape(passing.shape, BF16))(pieces[1, 2], passing)
+    pieces = {key: arrived(key, piece) for key, piece in pieces.items()}
+    order = list(pieces)
 
     def bands(edge):
         there = [(2 * band + 1, 2 * band + 2) for band in range(n_lat - 1)]
@@ -416,10 +425,10 @@
 
     fresh = shape((rank, wide))
     surface, message, outgoing, edge_far, summed, seen = call(
-        functools.partial(first_kernel, half, days, sends, paired, swap),
+        functools.partial(first_kernel, half, days, order, paired, swap),
         [fresh, shape((sum_rows + COLS, LANES)), shape((sum_rows + rank, LANES)), shape((rank, LANES)), shape((2 * days, wide)), shape((TAIL, LANES))],
         [flip, pltpu.VMEM((rank, wide), F32)],
-    )(surface, edge_near, predicted, packed, time_t, *[pieces[key] for key in sends], bands(edge_far), *(() if paired else columns(cols)))
+    )(surface, edge_near, predicted, packed, time_t, *[pieces[key] for key in order], bands(edge_far), *(() if paired else columns(cols)))
 
     sums = shape((sum_rows, LANES))
     add = call(add_kernel, sums)

time: 73.6 us -> 69.3 us (0.942)
  starting transfers between devices: 28.8 us -> 23.4 us
    ppermute x18, starting transfers between devices: 27.5 us -> 22.1 us  [across(): lax.ppermute(value, axis, [(i, i ^ step) for i in range(lax.axis_size(axi...]
    pallas_call x9 -> x10, Pallas kernels: 9.05 us -> 9.07 us  [run(): pl.pallas_call(kernel, out_shape=out_shape, in_specs=[pl.BlockSpec(memory...]
where the time goes in v5:
time: 69.3 us; the launch traced here: 69.1 us
  waiting for transfers between devices  35.5 us (51%)
  starting transfers between devices  23.4 us (34%)
  Pallas kernels  9.07 us (13%)
  between operations  0.72 us (1%)
    ppermute x18, waiting for transfers between devices, across(): lax.ppermute(value, axis, [(i, i ^ step) for i in range(lax.axis_size(axi...  35.5 us
    ppermute x18, starting transfers between devices, across(): lax.ppermute(value, axis, [(i, i ^ step) for i in range(lax.axis_size(axi...  22.1 us
    pallas_call x10, Pallas kernels, run(): pl.pallas_call(kernel, out_shape=out_shape, in_specs=[pl.BlockSpec(memory...  9.07 us
  transfers between devices with their start and end apart: 20, of which 12 were waited for; matrix products, arithmetic and copies ran while one was open for 0% of the time, Pallas kernels for 0%

profile of v5, /device:TPU:0, one launch (start us, length us, event | category | flops | bytes accessed | tf_op | source)
XLA Modules:
  0.0 69.1 jit_solution(15173409556518584345)
XLA Ops:
  0.6 3.9 %shard_map.86 = (bf16[528,128]{1,0:T(8,128)(2,1)S(1)}, bf16[528,128]{1,0:T(8,128)(2,1)S(1)}, bf16[528,128]{1,0:T(8,128)(2,1)S(1)}, bf16[544,128]{1,0:T(8,128)(2,...) custom-call(s32[1,4,32]{2,1,0:T(4,128)} %list_hbm.1, ...), custom_call_target="tpu_custom_call" | custom-call | flops 1000000 | bytes 1000000 | tf_op jit(solution)/shard_map/pallas_call | solution.py:340
  4.5 0.5 collective-permute-start
  5.1 2.7 %collective-permute-start.1 = (bf16[528,128]{1,0:T(8,128)(2,1)S(1)}, bf16[528,128]{1,0:T(8,128)(2,1)S(1)}, u32[]{:S(2)}, u32[]{:S(2)}) collective-permute-start(bf16[528,128]{1,0:T(8,128)(2,1)S(1)} %get-tuple-element.38), channel_id=1, source_target_pairs={{0,4},{4,0},{8,12},{12,8},{1,5},{5,1},{9,13},{13,9},{2,6},{6,2},{1... | collective-permute-start | bytes 405512 | tf_op jit(solution)/shard_map/ppermute | solution.py:354
  7.7 0.7 collective-permute-start.7
  8.4 2.5 %collective-permute-start.4 = (bf16[544,128]{1,0:T(8,128)(2,1)S(1)}, bf16[544,128]{1,0:T(8,128)(2,1)S(1)}, u32[]{:S(2)}, u32[]{:S(2)}) collective-permute-start(bf16[544,128]{1,0:T(8,128)(2,1)S(1)} %get-tuple-element.40), channel_id=1, source_target_pairs={{0,12},{4,8},{8,4},{12,0},{1,13},{5,9},{9,5},{13,1},{2,14},{6,10},... | collective-permute-start | bytes 417800 | tf_op jit(solution)/shard_map/ppermute | solution.py:354
  10.9 0.7 collective-permute-start.5
  11.6 1.2 %collective-permute-start.3 = (bf16[528,128]{1,0:T(8,128)(2,1)S(1)}, bf16[528,128]{1,0:T(8,128)(2,1)S(1)}, u32[]{:S(2)}, u32[]{:S(2)}) collective-permute-start(bf16[528,128]{1,0:T(8,128)(2,1)S(1)} %get-tuple-element.39), channel_id=1, source_target_pairs={{0,8},{4,12},{8,0},{12,4},{1,9},{5,13},{9,1},{13,5},{2,10},{6,14},... | collective-permute-start | bytes 405512 | tf_op jit(solution)/shard_map/ppermute | solution.py:354
  12.8 3.1 %collective-permute-start.6 = (bf16[528,128]{1,0:T(8,128)(2,1)S(1)}, bf16[528,128]{1,0:T(8,128)(2,1)S(1)}, u32[]{:S(2)}, u32[]{:S(2)}) collective-permute-start(bf16[528,128]{1,0:T(8,128)(2,1)S(1)} %get-tuple-element.42), channel_id=1, source_target_pairs={{0,5},{1,4},{4,1},{5,0},{8,13},{9,12},{12,9},{13,8},{2,7},{3,6},{6... | collective-permute-start | bytes 405512 | tf_op jit(solution)/shard_map/ppermute | solution.py:354
  16.0 0.3 collective-permute-start.2
  16.3 0.4 copy-done
  16.9 4.8 %collective-permute-done.3.rest_1_ = bf16[528,128]{1,0:T(8,128)(2,1)S(1)} collective-permute-done((bf16[528,128]{1,0:T(8,128)(2,1)S(1)}, bf16[528,128]{1,0:T(8,128)(2,1)S(1)}, u32[]{:S(2)}, u32[]{:S(2)}) %collective-permute-start.3) | collective-permute-done | bytes 135200 | tf_op jit(solution)/shard_map/ppermute | solution.py:354
  21.8 5.6 %collective-permute-done.6.rest_5_ = bf16[528,128]{1,0:T(8,128)(2,1)S(1)} collective-permute-done((bf16[528,128]{1,0:T(8,128)(2,1)S(1)}, bf16[528,128]{1,0:T(8,128)(2,1)S(1)}, u32[]{:S(2)}, u32[]{:S(2)}) %collective-permute-start.6) | collective-permute-done | bytes 135200 | tf_op jit(solution)/shard_map/ppermute | solution.py:354
  27.4 2.8 %collective-permute-done.2.rest_0_ = bf16[528,128]{1,0:T(8,128)(2,1)S(1)} collective-permute-done((bf16[528,128]{1,0:T(8,128)(2,1)S(1)}, bf16[528,128]{1,0:T(8,128)(2,1)S(1)}, u32[]{:S(2)}, u32[]{:S(2)}) %collective-permute-start.2) | collective-permute-done | bytes 135200 | tf_op jit(solution)/shard_map/ppermute | solution.py:354
  30.2 1.6 %shard_map.89 = (f32[96,1024]{1,0:T(8,128)S(1)}, f32[216,128]{1,0:T(8,128)S(1)}, f32[296,128]{1,0:T(8,128)S(1)}, f32[96,128]{1,0:T(8,128)S(1)}, f32[128,1024]{1,0:T(8,128)S(1)}, /*index=5*/f32[16,128]{1,0:T(8,128)S(1)}) custom-call(f32[96,1024]{1,0:T(8,128)S(1)} %get-tuple-element.31.surface, f32[96,128]{1,0:T(8,128)S(1)} %get-tuple-element.32.edge_near, ...), custom_call_target="tpu_custom_call" | custom-call | flops 1000000 | bytes 1000000 | tf_op jit(solution)/shard_map/pallas_call | solution.py:340
  31.8 1.4 %collective-permute-done.8.theirs = f32[296,128]{1,0:T(8,128)S(1)} collective-permute-done((f32[296,128]{1,0:T(8,128)S(1)}, f32[296,128]{1,0:T(8,128)S(1)}, u32[]{:S(2)}, u32[]{:S(2)}) %collective-permute-start.8) | collective-permute-done | bytes 151584 | tf_op jit(solution)/shard_map/ppermute | solution.py:354
  33.2 0.8 %collective-permute-start.10 = (f32[200,128]{1,0:T(8,128)S(1)}, f32[200,128]{1,0:T(8,128)S(1)}, u32[]{:S(2)}, u32[]{:S(2)}) collective-permute-start(f32[200,128]{1,0:T(8,128)S(1)} %get-tuple-element.53.mine), channel_id=1, source_target_pairs={{0,2},{2,0},{1,3},{3,1},{4,6},{6,4},{5,7},{7,5},{8,10},{10,8},{9,1... | collective-permute-start | bytes 307208 | tf_op jit(solution)/shard_map/ppermute | solution.py:354
  34.0 0.7 collective-permute-start.9
  34.7 3.5 %collective-permute-done.10.theirs = f32[200,128]{1,0:T(8,128)S(1)} collective-permute-done((f32[200,128]{1,0:T(8,128)S(1)}, f32[200,128]{1,0:T(8,128)S(1)}, u32[]{:S(2)}, u32[]{:S(2)}) %collective-permute-start.10) | collective-permute-done | bytes 102432 | tf_op jit(solution)/shard_map/ppermute | solution.py:354
  38.2 2.9 %collective-permute-start.13 = (f32[216,128]{1,0:T(8,128)S(1)}, f32[216,128]{1,0:T(8,128)S(1)}, u32[]{:S(2)}, u32[]{:S(2)}) collective-permute-start(f32[216,128]{1,0:T(8,128)S(1)} %shard_map.91.refs_6_), channel_id=1, source_target_pairs={{0,12},{4,8},{8,4},{12,0},{1,13},{5,9},{9,5},{13,1},{2,14},{6,10},... | collective-permute-start | bytes 331784 | tf_op jit(solution)/shard_map/ppermute | solution.py:354
  41.2 1.5 %collective-permute-start.11 = (f32[216,128]{1,0:T(8,128)S(1)}, f32[216,128]{1,0:T(8,128)S(1)}, u32[]{:S(2)}, u32[]{:S(2)}) collective-permute-start(f32[216,128]{1,0:T(8,128)S(1)} %shard_map.91.refs_6_), channel_id=1, source_target_pairs={{0,4},{4,0},{8,12},{12,8},{1,5},{5,1},{9,13},{13,9},{2,6},{6,2},{1... | collective-permute-start | bytes 331784 | tf_op jit(solution)/shard_map/ppermute | solution.py:354
  42.7 3.2 %collective-permute-done.13.refs_9_.refs_11_ = f32[216,128]{1,0:T(8,128)S(1)} collective-permute-done((f32[216,128]{1,0:T(8,128)S(1)}, f32[216,128]{1,0:T(8,128)S(1)}, u32[]{:S(2)}, u32[]{:S(2)}) %collective-permute-start.13) | collective-permute-done | bytes 110624 | tf_op jit(solution)/shard_map/ppermute | solution.py:354
  45.9 4.9 %collective-permute-done.12.refs_8_ = f32[216,128]{1,0:T(8,128)S(1)} collective-permute-done((f32[216,128]{1,0:T(8,128)S(1)}, f32[216,128]{1,0:T(8,128)S(1)}, u32[]{:S(2)}, u32[]{:S(2)}) %collective-permute-start.12) | collective-permute-done | bytes 110624 | tf_op jit(solution)/shard_map/ppermute | solution.py:354
  50.8 1.7 %shard_map.92 = (f32[96,1024]{1,0:T(8,128)S(1)}, f32[96,128]{1,0:T(8,128)S(1)}, f32[200,128]{1,0:T(8,128)S(1)}, f32[200,128]{1,0:T(8,128)S(1)}) custom-call(f32[96,1024]{1,0:T(8,128)S(1)} %get-tuple-element.45.refs_0_, f32[96,128]{1,0:T(8,128)S(1)} %get-tuple-element.36.time_t.refs_1_, f32[128,1024]{1,0:T(8,128)S(1)} %get-tuple-element.46.refs_2_, ...), custom_call_target="tpu_custom_call" | custom-call | flops 1000000 | bytes 1000000 | tf_op jit(solution)/shard_map/pallas_call | solution.py:340
  52.7 0.4 collective-permute-start.15
  53.1 1.4 %collective-permute-done.15.theirs = f32[200,128]{1,0:T(8,128)S(1)} collective-permute-done((f32[200,128]{1,0:T(8,128)S(1)}, f32[200,128]{1,0:T(8,128)S(1)}, u32[]{:S(2)}, u32[]{:S(2)}) %collective-permute-start.15) | collective-permute-done | bytes 102432 | tf_op jit(solution)/shard_map/ppermute | solution.py:354
  54.5 0.7 %collective-permute-start.16 = (f32[200,128]{1,0:T(8,128)S(1)}, f32[200,128]{1,0:T(8,128)S(1)}, u32[]{:S(2)}, u32[]{:S(2)}) collective-permute-start(f32[200,128]{1,0:T(8,128)S(1)} %shard_map.93.mine), channel_id=1, source_target_pairs={{0,2},{2,0},{1,3},{3,1},{4,6},{6,4},{5,7},{7,5},{8,10},{10,8},{9,1... | collective-permute-start | bytes 307208 | tf_op jit(solution)/shard_map/ppermute | solution.py:354
  55.2 4.3 %collective-permute-done.16.theirs = f32[200,128]{1,0:T(8,128)S(1)} collective-permute-done((f32[200,128]{1,0:T(8,128)S(1)}, f32[200,128]{1,0:T(8,128)S(1)}, u32[]{:S(2)}, u32[]{:S(2)}) %collective-permute-start.16) | collective-permute-done | bytes 102432 | tf_op jit(solution)/shard_map/ppermute | solution.py:354
  59.5 2.8 %collective-permute-start.19 = (bf16[208,128]{1,0:T(8,128)(2,1)S(1)}, bf16[208,128]{1,0:T(8,128)(2,1)S(1)}, u32[]{:S(2)}, u32[]{:S(2)}) collective-permute-start(bf16[208,128]{1,0:T(8,128)(2,1)S(1)} %shard_map.94.rest_0_), channel_id=1, source_target_pairs={{0,12},{4,8},{8,4},{12,0},{1,13},{5,9},{9,5},{13,1},{2,14},{6,10},... | collective-permute-start | bytes 159752 | tf_op jit(solution)/shard_map/ppermute | solution.py:354
  62.3 1.6 %collective-permute-start.17 = (bf16[208,128]{1,0:T(8,128)(2,1)S(1)}, bf16[208,128]{1,0:T(8,128)(2,1)S(1)}, u32[]{:S(2)}, u32[]{:S(2)}) collective-permute-start(bf16[208,128]{1,0:T(8,128)(2,1)S(1)} %shard_map.94.rest_0_), channel_id=1, source_target_pairs={{0,4},{4,0},{8,12},{12,8},{1,5},{5,1},{9,13},{13,9},{2,6},{6,2},{1... | collective-permute-start | bytes 159752 | tf_op jit(solution)/shard_map/ppermute | solution.py:354
  63.9 1.5 %collective-permute-done.19.rest_3_ = bf16[208,128]{1,0:T(8,128)(2,1)S(1)} collective-permute-done((bf16[208,128]{1,0:T(8,128)(2,1)S(1)}, bf16[208,128]{1,0:T(8,128)(2,1)S(1)}, u32[]{:S(2)}, u32[]{:S(2)}) %collective-permute-start.19) | collective-permute-done | bytes 53280 | tf_op jit(solution)/shard_map/ppermute | solution.py:354
  65.5 1.9 %collective-permute-done.18.rest_2_ = bf16[208,128]{1,0:T(8,128)(2,1)S(1)} collective-permute-done((bf16[208,128]{1,0:T(8,128)(2,1)S(1)}, bf16[208,128]{1,0:T(8,128)(2,1)S(1)}, u32[]{:S(2)}, u32[]{:S(2)}) %collective-permute-start.18) | collective-permute-done | bytes 53280 | tf_op jit(solution)/shard_map/ppermute | solution.py:354
  67.6 1.5 %shard_map.95 = (f32[1536,128]{1,0:T(8,128)}, f32[64,96]{1,0:T(8,128)}) custom-call(f32[96,1024]{1,0:T(8,128)S(1)} %get-tuple-element.54.surface, f32[96,1024]{1,0:T(8,128)S(1)} %collective-permute-done.14.other, f32[96,128]{1,0:T(8,128)S(1)} %get-tuple-element.55.time_t, bf16[208,128]{1,0:T(8,128)(2,1)S(1)} %shard_map.94.rest_0_, ...), custom_call_target="tpu_custom_call" | custom-call | flops 1000000 | bytes 1000000 | tf_op jit(solution)/shard_map/pallas_call | solution.py:340
  (20 shorter events, 0.7 us)
Async XLA Ops:
  4.5 11.4 %collective-permute-start = (bf16[720,128]{1,0:T(8,128)(2,1)S(1)}, bf16[720,128]{1,0:T(8,128)(2,1)S(1)}, u32[]{:S(2)}, u32[]{:S(2)}) collective-permute-start(bf16[720,128]{1,0:T(8,128)(2,1)S(1)} %get-tuple-element.33), channel_id=1, source_target_pairs={{0,1},{1,0},{4,5},{5,4},{8,9},{9,8},{12,13},{13,12},{2,3},{3,2},{6... | collective-permute-start | bytes 552968 | tf_op jit(solution)/shard_map/ppermute | solution.py:354
  5.1 7.8 %collective-permute-start.1 = (bf16[528,128]{1,0:T(8,128)(2,1)S(1)}, bf16[528,128]{1,0:T(8,128)(2,1)S(1)}, u32[]{:S(2)}, u32[]{:S(2)}) collective-permute-start(bf16[528,128]{1,0:T(8,128)(2,1)S(1)} %get-tuple-element.38), channel_id=1, source_target_pairs={{0,4},{4,0},{8,12},{12,8},{1,5},{5,1},{9,13},{13,9},{2,6},{6,2},{1... | collective-permute-start | bytes 405512 | tf_op jit(solution)/shard_map/ppermute | solution.py:354
  7.7 3.9 %collective-permute-start.7 = (f32[96,128]{1,0:T(8,128)S(1)}, f32[96,128]{1,0:T(8,128)S(1)}, u32[]{:S(2)}, u32[]{:S(2)}) collective-permute-start(f32[96,128]{1,0:T(8,128)S(1)} %get-tuple-element.44), channel_id=1, source_target_pairs={{1,2},{2,1},{5,6},{6,5},{9,10},{10,9},{13,14},{14,13},{17,18},{18,... | collective-permute-start | bytes 147464 | tf_op jit(solution)/shard_map/ppermute | solution.py:409
  8.4 19.0 %collective-permute-start.4 = (bf16[544,128]{1,0:T(8,128)(2,1)S(1)}, bf16[544,128]{1,0:T(8,128)(2,1)S(1)}, u32[]{:S(2)}, u32[]{:S(2)}) collective-permute-start(bf16[544,128]{1,0:T(8,128)(2,1)S(1)} %get-tuple-element.40), channel_id=1, source_target_pairs={{0,12},{4,8},{8,4},{12,0},{1,13},{5,9},{9,5},{13,1},{2,14},{6,10},... | collective-permute-start | bytes 417800 | tf_op jit(solution)/shard_map/ppermute | solution.py:354
  10.9 16.4 %collective-permute-start.5 = (bf16[544,128]{1,0:T(8,128)(2,1)S(1)}, bf16[544,128]{1,0:T(8,128)(2,1)S(1)}, u32[]{:S(2)}, u32[]{:S(2)}) collective-permute-start(bf16[544,128]{1,0:T(8,128)(2,1)S(1)} %get-tuple-element.41), channel_id=1, source_target_pairs={{0,4},{4,0},{8,12},{12,8},{1,5},{5,1},{9,13},{13,9},{2,6},{6,2},{1... | collective-permute-start | bytes 417800 | tf_op jit(solution)/shard_map/ppermute | solution.py:354
  11.6 10.2 %collective-permute-start.3 = (bf16[528,128]{1,0:T(8,128)(2,1)S(1)}, bf16[528,128]{1,0:T(8,128)(2,1)S(1)}, u32[]{:S(2)}, u32[]{:S(2)}) collective-permute-start(bf16[528,128]{1,0:T(8,128)(2,1)S(1)} %get-tuple-element.39), channel_id=1, source_target_pairs={{0,8},{4,12},{8,0},{12,4},{1,9},{5,13},{9,1},{13,5},{2,10},{6,14},... | collective-permute-start | bytes 405512 | tf_op jit(solution)/shard_map/ppermute | solution.py:354
  12.8 14.5 %collective-permute-start.6 = (bf16[528,128]{1,0:T(8,128)(2,1)S(1)}, bf16[528,128]{1,0:T(8,128)(2,1)S(1)}, u32[]{:S(2)}, u32[]{:S(2)}) collective-permute-start(bf16[528,128]{1,0:T(8,128)(2,1)S(1)} %get-tuple-element.42), channel_id=1, source_target_pairs={{0,5},{1,4},{4,1},{5,0},{8,13},{9,12},{12,9},{13,8},{2,7},{3,6},{6... | collective-permute-start | bytes 405512 | tf_op jit(solution)/shard_map/ppermute | solution.py:354
  15.9 0.8 %copy-start = (f32[64,96]{1,0:T(8,128)S(1)}, f32[64,96]{1,0:T(8,128)}, u32[]{:S(2)}) copy-start(f32[64,96]{1,0:T(8,128)} %time_own.1) | copy-start | bytes 73732
  16.0 14.2 %collective-permute-start.2 = (bf16[528,128]{1,0:T(8,128)(2,1)S(1)}, bf16[528,128]{1,0:T(8,128)(2,1)S(1)}, u32[]{:S(2)}, u32[]{:S(2)}) collective-permute-start(bf16[528,128]{1,0:T(8,128)(2,1)S(1)} %shard_map.88), channel_id=1, source_target_pairs={{0,9},{1,8},{4,13},{5,12},{8,1},{9,0},{12,5},{13,4},{2,11},{3,10},... | collective-permute-start | bytes 405512 | tf_op jit(solution)/shard_map/ppermute | solution.py:354
  31.8 1.4 %collective-permute-start.8 = (f32[296,128]{1,0:T(8,128)S(1)}, f32[296,128]{1,0:T(8,128)S(1)}, u32[]{:S(2)}, u32[]{:S(2)}) collective-permute-start(f32[296,128]{1,0:T(8,128)S(1)} %get-tuple-element.49), channel_id=1, source_target_pairs={{0,1},{1,0},{2,3},{3,2},{4,5},{5,4},{6,7},{7,6},{8,9},{9,8},{10,11... | collective-permute-start | bytes 454664 | tf_op jit(solution)/shard_map/ppermute | solution.py:354
  33.2 5.0 %collective-permute-start.10 = (f32[200,128]{1,0:T(8,128)S(1)}, f32[200,128]{1,0:T(8,128)S(1)}, u32[]{:S(2)}, u32[]{:S(2)}) collective-permute-start(f32[200,128]{1,0:T(8,128)S(1)} %get-tuple-element.53.mine), channel_id=1, source_target_pairs={{0,2},{2,0},{1,3},{3,1},{4,6},{6,4},{5,7},{7,5},{8,10},{10,8},{9,1... | collective-permute-start | bytes 307208 | tf_op jit(solution)/shard_map/ppermute | solution.py:354
  34.0 0.7 collective-permute-start.9
  38.2 7.7 %collective-permute-start.13 = (f32[216,128]{1,0:T(8,128)S(1)}, f32[216,128]{1,0:T(8,128)S(1)}, u32[]{:S(2)}, u32[]{:S(2)}) collective-permute-start(f32[216,128]{1,0:T(8,128)S(1)} %shard_map.91.refs_6_), channel_id=1, source_target_pairs={{0,12},{4,8},{8,4},{12,0},{1,13},{5,9},{9,5},{13,1},{2,14},{6,10},... | collective-permute-start | bytes 331784 | tf_op jit(solution)/shard_map/ppermute | solution.py:354
  41.2 9.6 %collective-permute-start.12 = (f32[216,128]{1,0:T(8,128)S(1)}, f32[216,128]{1,0:T(8,128)S(1)}, u32[]{:S(2)}, u32[]{:S(2)}) collective-permute-start(f32[216,128]{1,0:T(8,128)S(1)} %shard_map.91.refs_6_), channel_id=1, source_target_pairs={{0,8},{4,12},{8,0},{12,4},{1,9},{5,13},{9,1},{13,5},{2,10},{6,14},... | collective-permute-start | bytes 331784 | tf_op jit(solution)/shard_map/ppermute | solution.py:354
  41.2 9.6 %collective-permute-start.11 = (f32[216,128]{1,0:T(8,128)S(1)}, f32[216,128]{1,0:T(8,128)S(1)}, u32[]{:S(2)}, u32[]{:S(2)}) collective-permute-start(f32[216,128]{1,0:T(8,128)S(1)} %shard_map.91.refs_6_), channel_id=1, source_target_pairs={{0,4},{4,0},{8,12},{12,8},{1,5},{5,1},{9,13},{13,9},{2,6},{6,2},{1... | collective-permute-start | bytes 331784 | tf_op jit(solution)/shard_map/ppermute | solution.py:354
  52.5 15.1 %collective-permute-start.14 = (f32[96,1024]{1,0:T(8,128)S(1)}, f32[96,1024]{1,0:T(8,128)S(1)}, u32[]{:S(2)}, u32[]{:S(2)}) collective-permute-start(f32[96,1024]{1,0:T(8,128)S(1)} %get-tuple-element.54.surface), channel_id=1, source_target_pairs={{0,1},{1,0},{2,3},{3,2},{4,5},{5,4},{6,7},{7,6},{8,9},{9,8},{10,11... | collective-permute-start | bytes 1179656 | tf_op jit(solution)/shard_map/ppermute | solution.py:354
  52.7 1.8 %collective-permute-start.15 = (f32[200,128]{1,0:T(8,128)S(1)}, f32[200,128]{1,0:T(8,128)S(1)}, u32[]{:S(2)}, u32[]{:S(2)}) collective-permute-start(f32[200,128]{1,0:T(8,128)S(1)} %get-tuple-element.57), channel_id=1, source_target_pairs={{0,1},{1,0},{2,3},{3,2},{4,5},{5,4},{6,7},{7,6},{8,9},{9,8},{10,11... | collective-permute-start | bytes 307208 | tf_op jit(solution)/shard_map/ppermute | solution.py:354
  54.5 5.0 %collective-permute-start.16 = (f32[200,128]{1,0:T(8,128)S(1)}, f32[200,128]{1,0:T(8,128)S(1)}, u32[]{:S(2)}, u32[]{:S(2)}) collective-permute-start(f32[200,128]{1,0:T(8,128)S(1)} %shard_map.93.mine), channel_id=1, source_target_pairs={{0,2},{2,0},{1,3},{3,1},{4,6},{6,4},{5,7},{7,5},{8,10},{10,8},{9,1... | collective-permute-start | bytes 307208 | tf_op jit(solution)/shard_map/ppermute | solution.py:354
  59.5 6.0 %collective-permute-start.19 = (bf16[208,128]{1,0:T(8,128)(2,1)S(1)}, bf16[208,128]{1,0:T(8,128)(2,1)S(1)}, u32[]{:S(2)}, u32[]{:S(2)}) collective-permute-start(bf16[208,128]{1,0:T(8,128)(2,1)S(1)} %shard_map.94.rest_0_), channel_id=1, source_target_pairs={{0,12},{4,8},{8,4},{12,0},{1,13},{5,9},{9,5},{13,1},{2,14},{6,10},... | collective-permute-start | bytes 159752 | tf_op jit(solution)/shard_map/ppermute | solution.py:354
  62.3 5.1 %collective-permute-start.18 = (bf16[208,128]{1,0:T(8,128)(2,1)S(1)}, bf16[208,128]{1,0:T(8,128)(2,1)S(1)}, u32[]{:S(2)}, u32[]{:S(2)}) collective-permute-start(bf16[208,128]{1,0:T(8,128)(2,1)S(1)} %shard_map.94.rest_0_), channel_id=1, source_target_pairs={{0,8},{4,12},{8,0},{12,4},{1,9},{5,13},{9,1},{13,5},{2,10},{6,14},... | collective-permute-start | bytes 159752 | tf_op jit(solution)/shard_map/ppermute | solution.py:354
  62.3 5.3 %collective-permute-start.17 = (bf16[208,128]{1,0:T(8,128)(2,1)S(1)}, bf16[208,128]{1,0:T(8,128)(2,1)S(1)}, u32[]{:S(2)}, u32[]{:S(2)}) collective-permute-start(bf16[208,128]{1,0:T(8,128)(2,1)S(1)} %shard_map.94.rest_0_), channel_id=1, source_target_pairs={{0,4},{4,0},{8,12},{12,8},{1,5},{5,1},{9,13},{13,9},{2,6},{6,2},{1... | collective-permute-start | bytes 159752 | tf_op jit(solution)/shard_map/ppermute | solution.py:354

commit v6 on v5

--- a/solution.py
+++ b/solution.py
@@ -197,22 +197,32 @@
     return grad_time[:, :LANES] + grad_time[:, LANES:], grad_diag, norm
 
 
-def post(half, sums, fresh, message, outgoing, edge_far, flip):
+def post_own(half, sums, fresh, message, outgoing, edge_far, flip):
     grad_time, grad_diag, norm = sums
     core = lax.axis_index("ta")
     rank = norm.shape[0]
-    columns = [norm] if edge_far is None else [norm] + [norm] * (NORM - 1) + border(fresh[...], half)
-    last = columns_as_rows(columns, flip)[: message.shape[0] - 2 * rank, :]
+    days = LANES // 2
+    own = lax.broadcasted_iota(jnp.int32, grad_time.shape, 1) < days
+    last = columns_as_rows([norm] * NORM + border(fresh[...], half), flip)
+    message[:rank, :] = jnp.where(own, grad_time, pltpu.roll(grad_diag, days, 1))
+    message[rank:, :] = last[: NORM + COLS, :]
+    outgoing[:rank, :] = jnp.where(own, pltpu.roll(grad_time, days, 1), grad_diag)
+    outgoing[rank:rank + NORM, :] = last[:NORM, :]
+    first_row, last_row = fresh[:, :LANES], fresh[:, (half - 1) * LANES:]
+    outgoing[rank + NORM:, :] = pick(core == 0, last_row, first_row)
+    edge_far[...] = pick(core == 0, first_row, last_row)
+
+
+def post_all(sums, message, outgoing, flip):
+    grad_time, grad_diag, norm = sums
+    rank = norm.shape[0]
+    last = columns_as_rows([norm], flip)[:NORM, :]
     message[:rank, :] = grad_time
     message[rank:2 * rank, :] = grad_diag
     message[2 * rank:, :] = last
     outgoing[:rank, :] = pltpu.roll(grad_time, LANES // 2, 1)
     outgoing[rank:2 * rank, :] = pltpu.roll(grad_diag, LANES // 2, 1)
-    outgoing[2 * rank:2 * rank + NORM, :] = last[:NORM, :]
-    if edge_far is not None:
-        first_row, last_row = fresh[:, :LANES], fresh[:, (half - 1) * LANES:]
-        outgoing[2 * rank + NORM:, :] = pick(core == 0, last_row, first_row)
-        edge_far[...] = pick(core == 0, first_row, last_row)
+    outgoing[2 * rank:, :] = last
 
 
 def first_kernel(half, days, order, paired, swap, surface, edge_near, predicted, packed, time_t, *rest):
@@ -239,31 +249,42 @@
     near, far = (add_up(parts, slice(half * days, half * days + TAIL)) for parts in sides)
     seen[...] = near + pltpu.roll(far, days, 1)
     sums = gradients(half, base, predicted, packed, time_t[...], seen[...], summed, fresh)
-    post(half, sums, fresh, message, outgoing, edge_far, flip)
-
-
-def settle(rank, counts, parts, time_t, flip):
-    day_count, cell_count = counts
+    post_own(half, sums, fresh, message, outgoing, edge_far, flip)
+
+
+def total_of(parts):
     total = parts[0][...].astype(F32)
     if len(parts) > 1:
         one, two, three = (part[...].astype(F32) for part in parts[1:])
         total = (total + one) + (two + three)
-    time_new = time_t - total[:rank, :] / (total[rank:2 * rank, :] + RIDGE)
-    norm = total[2 * rank:2 * rank + NORM, :]
-    if parts[0].dtype == BF16:
-        norm = norm + total[2 * rank + NORM:2 * rank + 2 * NORM, :]
-    space_sq = rows_as_columns(norm, rank, flip)[:, :1]
+    return total
+
+
+def own_kernel(n_parts, time_t, *rest):
+    parts, (time_own, norm) = rest[:n_parts], rest[n_parts:]
+    rank = time_t.shape[0]
+    days = LANES // 2
+    total = total_of(parts)
+    block = total[:rank, :]
+    own = lax.broadcasted_iota(jnp.int32, block.shape, 1) < days
+    time_own[...] = jnp.where(own, time_t[...] - block / (pltpu.roll(block, days, 1) + RIDGE), 0.0)
+    norm[...] = total[rank:rank + NORM, :]
+
+
+def rescaling(counts, norm, time_new, flip):
+    day_count, cell_count = counts
+    space_sq = rows_as_columns(norm, time_new.shape[0], flip)[:, :1]
     square = time_new * time_new
     time_sq = 0.5 * jnp.sum(square + pltpu.roll(square, LANES // 2, 1), axis=1, keepdims=True)
     ratio = (time_sq / day_count + EPSILON) / (space_sq / cell_count + EPSILON)
-    return time_new, jnp.sqrt(jnp.sqrt(ratio))
-
-
-def second_kernel(half, counts, n_parts, swap, surface, time_t, summed, seen, edge_near, edge_far, *rest):
-    parts, (cols_a, cols_b) = rest[:n_parts], rest[n_parts:n_parts + 2]
-    fresh, time_out, message, outgoing, flip, scaled, base, predicted, packed = rest[n_parts + 2:]
+    return jnp.sqrt(jnp.sqrt(ratio))
+
+
+def second_kernel(half, counts, swap, surface, time_own, time_other, norm, summed, seen, edge_near, edge_far, cols_a, cols_b, *rest):
+    fresh, time_out, message, outgoing, flip, scaled, base, predicted, packed = rest
     rank = surface.shape[0]
-    time_new, scale = settle(rank, counts, parts, time_t[...], flip)
+    time_new = time_own[...] + pltpu.roll(time_other[...], LANES // 2, 1)
+    scale = rescaling(counts, norm[...], time_new, flip)
     time_now = time_new / scale
     time_out[...] = time_now
     scaled[...] = surface[...] * scale
@@ -274,7 +295,7 @@
     cols = [ref[ref.shape[0] - COLS:, :] for ref in (cols_a, cols_b)]
     smooth(half, swap(), scaled[...], edge_near[...], edge_far[...], *cols, scale, base, flip)
     sums = gradients(half, base, predicted, packed, time_now, seen[...], summed, fresh)
-    post(half, sums, fresh, message, outgoing, None, flip)
+    post_all(sums, message, outgoing, flip)
 
 
 def last_kernel(half, counts, n_parts, surface, other, time_t, *rest):
@@ -283,7 +304,12 @@
     core = lax.axis_index("ta")
     rank = surface.shape[0]
     height = space_out.shape[0] // rank
-    time_new, scale = settle(rank, counts, parts, time_t[...], flip)
+    total = total_of(parts)
+    time_new = time_t[...] - total[:rank, :] / (total[rank:2 * rank, :] + RIDGE)
+    norm = total[2 * rank:2 * rank + NORM, :]
+    if parts[0].dtype == BF16:
+        norm = norm + total[2 * rank + NORM:, :]
+    scale = rescaling(counts, norm, time_new, flip)
     flip[...] = jnp.zeros(flip.shape, F32)
     flip[:rank, :] = time_new / scale
     time_out[...] = flip[...].T[: time_out.shape[0], :rank]
@@ -293,11 +319,10 @@
         space_out[pl.ds((1 - core) * half + row, rank, stride=height), :] = other[:, at:at + LANES] * scale
 
 
-def core_kernel(rank, mine, theirs, edge_in, total, beside, edge_out):
+def core_kernel(mine, theirs, total, beside):
     rows = total.shape[0]
     total[...] = mine[:rows, :] + theirs[:rows, :]
     beside[...] = theirs[rows:, :]
-    edge_out[...] = edge_in[...]
 
 
 def merge_kernel(mine, theirs, out):
@@ -309,7 +334,7 @@
     total[...] = mine[:rows, :] + theirs[:rows, :]
 
 
-def band_kernel(mine, theirs, message, after, total):
+def band_kernel(mine, theirs, message, total):
     rows = mine.shape[0]
     total[:rows, :] = mine[...] + theirs[...]
     total[rows:, :] = message[rows:, :]
@@ -361,7 +386,7 @@
     half = height // n_ta
     wide = half * LANES
     counts = (float(days * n_ta), float(height * cells * n_lon * n_lat))
-    sum_rows = 2 * rank + NORM
+    own_rows, sum_rows = rank + NORM, 2 * rank + NORM
     flip = pltpu.VMEM((LANES, LANES), F32)
 
     paired = n_lon == 4
@@ -423,15 +448,15 @@
         [flip],
     )(surface, factor_time, pieces[1, 0])
 
-    fresh = shape((rank, wide))
+    fresh, edge = shape((rank, wide)), shape((rank, LANES))
     surface, message, outgoing, edge_far, summed, seen = call(
         functools.partial(first_kernel, half, days, order, paired, swap),
-        [fresh, shape((sum_rows + COLS, LANES)), shape((sum_rows + rank, LANES)), shape((rank, LANES)), shape((2 * days, wide)), shape((TAIL, LANES))],
+        [fresh, shape((own_rows + COLS, LANES)), shape((own_rows + rank, LANES)), edge, shape((2 * days, wide)), shape((TAIL, LANES))],
         [flip, pltpu.VMEM((rank, wide), F32)],
     )(surface, edge_near, predicted, packed, time_t, *[pieces[key] for key in order], bands(edge_far), *(() if paired else columns(cols)))
 
-    sums = shape((sum_rows, LANES))
-    add = call(add_kernel, sums)
+    def add(mine, theirs):
+        return call(add_kernel, shape(theirs.shape))(mine, theirs)
 
     def over_bands(total, last):
         step = 1
@@ -449,26 +474,21 @@
             step *= 2
         return [total]
 
-    total, edge_near, edge_far = call(
-        functools.partial(core_kernel, rank), [sums, shape((rank, LANES)), shape((rank, LANES))]
-    )(message, across(outgoing, "ta", 1), edge_far)
-    edge_far = bands(edge_far)
+    total, edge_near = call(core_kernel, [shape((own_rows, LANES)), edge])(message, across(outgoing, "ta", 1))
     if paired:
-        last = call(band_kernel, shape((sum_rows + COLS, LANES)), after=1)
-        parts = over_lon(over_bands(total, lambda mine, theirs: last(mine, theirs, message, edge_far)))
-        cols_a, cols_b = parts[1], parts[3]
+        last = call(band_kernel, shape(message.shape))
+        parts = over_lon(over_bands(total, lambda mine, theirs: last(mine, theirs, message)))
+        cols = parts[1], parts[3]
     else:
         parts = over_lon(over_bands(total, add))
-        cols_a, cols_b = columns(message[sum_rows:])
-
-    def second(*refs):
-        second_kernel(half, counts, len(parts), swap, *refs)
+        cols = columns(message[own_rows:])
+    time_own, norm = call(functools.partial(own_kernel, len(parts)), [edge, shape((NORM, LANES))])(time_t, *parts)
 
     surface, time_t, message, outgoing = call(
-        second,
-        [fresh, shape((rank, LANES)), sums, sums],
+        functools.partial(second_kernel, half, counts, swap),
+        [fresh, edge, shape((sum_rows, LANES)), shape((sum_rows, LANES))],
         [flip, pltpu.VMEM((rank, wide), F32), pltpu.VMEM((rank, wide), F32), pltpu.VMEM((2 * days, wide), F32), pltpu.VMEM((rank, wide), BF16)],
-    )(surface, time_t, summed, seen, edge_near, edge_far, *parts, cols_a, cols_b)
+    )(surface, time_own, across(time_own, "ta", 1), norm, summed, seen, edge_near, bands(edge_far), *cols)
 
     total = add(message, across(outgoing, "ta", 1))
     other = across(surface, "ta", 1)

time: 69.3 us -> 65.1 us (0.939)
  waiting for transfers between devices: 35.5 us -> 30.6 us
    ppermute x18 -> x19, waiting for transfers between devices: 35.5 us -> 30.6 us  [across(): lax.ppermute(value, axis, [(i, i ^ step) for i in range(lax.axis_size(axi...]
    ppermute x18 -> x19, starting transfers between devices: 22.1 us -> 22.5 us  [across(): lax.ppermute(value, axis, [(i, i ^ step) for i in range(lax.axis_size(axi...]
    pallas_call x10 -> x11, Pallas kernels: 9.07 us -> 9.2 us  [run(): pl.pallas_call(kernel, out_shape=out_shape, in_specs=[pl.BlockSpec(memory...]
  transfers between devices with their start and end apart: 20 -> 21, of which waited for: 12 -> 12; matrix products, arithmetic and copies ran while one was open for 0% -> 0% of each run, Pallas kernels for 0% -> 1%
where the time goes in v6:
time: 65.1 us; the launch traced here: 64.8 us
  waiting for transfers between devices  30.6 us (47%)
  starting transfers between devices  23.8 us (37%)
  Pallas kernels  9.2 us (14%)
  between operations  0.73 us (1%)
    ppermute x19, waiting for transfers between devices, across(): lax.ppermute(value, axis, [(i, i ^ step) for i in range(lax.axis_size(axi...  30.6 us
    ppermute x19, starting transfers between devices, across(): lax.ppermute(value, axis, [(i, i ^ step) for i in range(lax.axis_size(axi...  22.5 us
    pallas_call x11, Pallas kernels, run(): pl.pallas_call(kernel, out_shape=out_shape, in_specs=[pl.BlockSpec(memory...  9.2 us
    ppermute x2, starting transfers between devices, bands(): return lax.ppermute(edge, ('lat', 'ta'), there + [(b, a) for a, b in there])  1.3 us
  transfers between devices with their start and end apart: 21, of which 12 were waited for; matrix products, arithmetic and copies ran while one was open for 0% of the time, Pallas kernels for 1%

profile of v6, /device:TPU:0, one launch (start us, length us, event | category | flops | bytes accessed | tf_op | source)
XLA Modules:
  0.0 64.8 jit_solution(1734434537059864115)
XLA Ops:
  0.6 3.9 %shard_map.86 = (bf16[528,128]{1,0:T(8,128)(2,1)S(1)}, bf16[528,128]{1,0:T(8,128)(2,1)S(1)}, bf16[528,128]{1,0:T(8,128)(2,1)S(1)}, bf16[544,128]{1,0:T(8,128)(2,...) custom-call(s32[1,4,32]{2,1,0:T(4,128)} %list_hbm.1, ...), custom_call_target="tpu_custom_call" | custom-call | flops 1000000 | bytes 1000000 | tf_op jit(solution)/shard_map/pallas_call | solution.py:365
  4.5 0.5 collective-permute-start
  5.1 2.7 %collective-permute-start.1 = (bf16[528,128]{1,0:T(8,128)(2,1)S(1)}, bf16[528,128]{1,0:T(8,128)(2,1)S(1)}, u32[]{:S(2)}, u32[]{:S(2)}) collective-permute-start(bf16[528,128]{1,0:T(8,128)(2,1)S(1)} %get-tuple-element.39), channel_id=1, source_target_pairs={{0,4},{4,0},{8,12},{12,8},{1,5},{5,1},{9,13},{13,9},{2,6},{6,2},{1... | collective-permute-start | bytes 405512 | tf_op jit(solution)/shard_map/ppermute | solution.py:379
  7.7 0.7 %collective-permute-start.7 = (f32[96,128]{1,0:T(8,128)S(1)}, f32[96,128]{1,0:T(8,128)S(1)}, u32[]{:S(2)}, u32[]{:S(2)}) collective-permute-start(f32[96,128]{1,0:T(8,128)S(1)} %get-tuple-element.45), channel_id=1, source_target_pairs={{1,2},{2,1},{5,6},{6,5},{9,10},{10,9},{13,14},{14,13},{17,18},{18,... | collective-permute-start | bytes 147464 | tf_op jit(solution)/shard_map/ppermute | solution.py:434
  8.4 2.5 %collective-permute-start.4 = (bf16[544,128]{1,0:T(8,128)(2,1)S(1)}, bf16[544,128]{1,0:T(8,128)(2,1)S(1)}, u32[]{:S(2)}, u32[]{:S(2)}) collective-permute-start(bf16[544,128]{1,0:T(8,128)(2,1)S(1)} %get-tuple-element.41), channel_id=1, source_target_pairs={{0,12},{4,8},{8,4},{12,0},{1,13},{5,9},{9,5},{13,1},{2,14},{6,10},... | collective-permute-start | bytes 417800 | tf_op jit(solution)/shard_map/ppermute | solution.py:379
  10.9 0.7 %collective-permute-start.5 = (bf16[544,128]{1,0:T(8,128)(2,1)S(1)}, bf16[544,128]{1,0:T(8,128)(2,1)S(1)}, u32[]{:S(2)}, u32[]{:S(2)}) collective-permute-start(bf16[544,128]{1,0:T(8,128)(2,1)S(1)} %get-tuple-element.42), channel_id=1, source_target_pairs={{0,4},{4,0},{8,12},{12,8},{1,5},{5,1},{9,13},{13,9},{2,6},{6,2},{1... | collective-permute-start | bytes 417800 | tf_op jit(solution)/shard_map/ppermute | solution.py:379
  11.6 1.2 %collective-permute-start.3 = (bf16[528,128]{1,0:T(8,128)(2,1)S(1)}, bf16[528,128]{1,0:T(8,128)(2,1)S(1)}, u32[]{:S(2)}, u32[]{:S(2)}) collective-permute-start(bf16[528,128]{1,0:T(8,128)(2,1)S(1)} %get-tuple-element.40), channel_id=1, source_target_pairs={{0,8},{4,12},{8,0},{12,4},{1,9},{5,13},{9,1},{13,5},{2,10},{6,14},... | collective-permute-start | bytes 405512 | tf_op jit(solution)/shard_map/ppermute | solution.py:379
  12.8 3.1 %collective-permute-start.6 = (bf16[528,128]{1,0:T(8,128)(2,1)S(1)}, bf16[528,128]{1,0:T(8,128)(2,1)S(1)}, u32[]{:S(2)}, u32[]{:S(2)}) collective-permute-start(bf16[528,128]{1,0:T(8,128)(2,1)S(1)} %get-tuple-element.43), channel_id=1, source_target_pairs={{0,5},{1,4},{4,1},{5,0},{8,13},{9,12},{12,9},{13,8},{2,7},{3,6},{6... | collective-permute-start | bytes 405512 | tf_op jit(solution)/shard_map/ppermute | solution.py:379
  16.3 0.4 copy-done
  16.9 4.9 %collective-permute-done.3.rest_1_ = bf16[528,128]{1,0:T(8,128)(2,1)S(1)} collective-permute-done((bf16[528,128]{1,0:T(8,128)(2,1)S(1)}, bf16[528,128]{1,0:T(8,128)(2,1)S(1)}, u32[]{:S(2)}, u32[]{:S(2)}) %collective-permute-start.3) | collective-permute-done | bytes 135200 | tf_op jit(solution)/shard_map/ppermute | solution.py:379
  21.8 5.6 %collective-permute-done.6.rest_5_ = bf16[528,128]{1,0:T(8,128)(2,1)S(1)} collective-permute-done((bf16[528,128]{1,0:T(8,128)(2,1)S(1)}, bf16[528,128]{1,0:T(8,128)(2,1)S(1)}, u32[]{:S(2)}, u32[]{:S(2)}) %collective-permute-start.6) | collective-permute-done | bytes 135200 | tf_op jit(solution)/shard_map/ppermute | solution.py:379
  27.4 2.8 %collective-permute-done.2.rest_0_ = bf16[528,128]{1,0:T(8,128)(2,1)S(1)} collective-permute-done((bf16[528,128]{1,0:T(8,128)(2,1)S(1)}, bf16[528,128]{1,0:T(8,128)(2,1)S(1)}, u32[]{:S(2)}, u32[]{:S(2)}) %collective-permute-start.2) | collective-permute-done | bytes 135200 | tf_op jit(solution)/shard_map/ppermute | solution.py:379
  30.2 1.6 %shard_map.89 = (f32[96,1024]{1,0:T(8,128)S(1)}, f32[120,128]{1,0:T(8,128)S(1)}, f32[200,128]{1,0:T(8,128)S(1)}, f32[96,128]{1,0:T(8,128)S(1)}, f32[128,1024]{1,0:T(8,128)S(1)}, /*index=5*/f32[16,128]{1,0:T(8,128)S(1)}) custom-call(f32[96,1024]{1,0:T(8,128)S(1)} %get-tuple-element.32.surface, f32[96,128]{1,0:T(8,128)S(1)} %get-tuple-element.33.edge_near, ...), custom_call_target="tpu_custom_call" | custom-call | flops 1000000 | bytes 1000000 | tf_op jit(solution)/shard_map/pallas_call | solution.py:365
  31.8 1.3 %collective-permute-done.8.theirs = f32[200,128]{1,0:T(8,128)S(1)} collective-permute-done((f32[200,128]{1,0:T(8,128)S(1)}, f32[200,128]{1,0:T(8,128)S(1)}, u32[]{:S(2)}, u32[]{:S(2)}) %collective-permute-start.8) | collective-permute-done | bytes 102432 | tf_op jit(solution)/shard_map/ppermute | solution.py:379
  33.2 0.8 %collective-permute-start.9 = (f32[104,128]{1,0:T(8,128)S(1)}, f32[104,128]{1,0:T(8,128)S(1)}, u32[]{:S(2)}, u32[]{:S(2)}) collective-permute-start(f32[104,128]{1,0:T(8,128)S(1)} %get-tuple-element.49.mine), channel_id=1, source_target_pairs={{0,2},{2,0},{1,3},{3,1},{4,6},{6,4},{5,7},{7,5},{8,10},{10,8},{9,1... | collective-permute-start | bytes 159752 | tf_op jit(solution)/shard_map/ppermute | solution.py:379
  34.0 3.4 %collective-permute-done.9.theirs = f32[104,128]{1,0:T(8,128)S(1)} collective-permute-done((f32[104,128]{1,0:T(8,128)S(1)}, f32[104,128]{1,0:T(8,128)S(1)}, u32[]{:S(2)}, u32[]{:S(2)}) %collective-permute-start.9) | collective-permute-done | bytes 53280 | tf_op jit(solution)/shard_map/ppermute | solution.py:379
  37.4 2.9 %collective-permute-start.12 = (f32[120,128]{1,0:T(8,128)S(1)}, f32[120,128]{1,0:T(8,128)S(1)}, u32[]{:S(2)}, u32[]{:S(2)}) collective-permute-start(f32[120,128]{1,0:T(8,128)S(1)} %shard_map.91.rest_0_), channel_id=1, source_target_pairs={{0,12},{4,8},{8,4},{12,0},{1,13},{5,9},{9,5},{13,1},{2,14},{6,10},... | collective-permute-start | bytes 184328 | tf_op jit(solution)/shard_map/ppermute | solution.py:379
  40.3 1.5 %collective-permute-start.10 = (f32[120,128]{1,0:T(8,128)S(1)}, f32[120,128]{1,0:T(8,128)S(1)}, u32[]{:S(2)}, u32[]{:S(2)}) collective-permute-start(f32[120,128]{1,0:T(8,128)S(1)} %shard_map.91.rest_0_), channel_id=1, source_target_pairs={{0,4},{4,0},{8,12},{12,8},{1,5},{5,1},{9,13},{13,9},{2,6},{6,2},{1... | collective-permute-start | bytes 184328 | tf_op jit(solution)/shard_map/ppermute | solution.py:379
  41.8 0.7 %collective-permute-start.14 = (f32[96,128]{1,0:T(8,128)S(1)}, f32[96,128]{1,0:T(8,128)S(1)}, u32[]{:S(2)}, u32[]{:S(2)}) collective-permute-start(f32[96,128]{1,0:T(8,128)S(1)} %get-tuple-element.55), channel_id=1, source_target_pairs={{1,2},{2,1},{5,6},{6,5},{9,10},{10,9},{13,14},{14,13},{17,18},{18,... | collective-permute-start | bytes 147464 | tf_op jit(solution)/shard_map/ppermute | solution.py:434
  42.5 1.1 %collective-permute-done.12.rest_3_.cols_b = f32[120,128]{1,0:T(8,128)S(1)} collective-permute-done((f32[120,128]{1,0:T(8,128)S(1)}, f32[120,128]{1,0:T(8,128)S(1)}, u32[]{:S(2)}, u32[]{:S(2)}) %collective-permute-start.12) | collective-permute-done | bytes 61472 | tf_op jit(solution)/shard_map/ppermute | solution.py:379
  43.5 1.9 %collective-permute-done.11.rest_2_ = f32[120,128]{1,0:T(8,128)S(1)} collective-permute-done((f32[120,128]{1,0:T(8,128)S(1)}, f32[120,128]{1,0:T(8,128)S(1)}, u32[]{:S(2)}, u32[]{:S(2)}) %collective-permute-start.11) | collective-permute-done | bytes 61472 | tf_op jit(solution)/shard_map/ppermute | solution.py:379
  45.7 1.2 %collective-permute-done.13.time_other = f32[96,128]{1,0:T(8,128)S(1)} collective-permute-done((f32[96,128]{1,0:T(8,128)S(1)}, f32[96,128]{1,0:T(8,128)S(1)}, u32[]{:S(2)}, u32[]{:S(2)}) %collective-permute-start.13) | collective-permute-done | bytes 49184 | tf_op jit(solution)/shard_map/ppermute | solution.py:379
  46.9 1.8 %shard_map.93 = (f32[96,1024]{1,0:T(8,128)S(1)}, f32[96,128]{1,0:T(8,128)S(1)}, f32[200,128]{1,0:T(8,128)S(1)}, f32[200,128]{1,0:T(8,128)S(1)}) custom-call(f32[96,1024]{1,0:T(8,128)S(1)} %get-tuple-element.46.surface, f32[96,128]{1,0:T(8,128)S(1)} %get-tuple-element.50.time_own, f32[96,128]{1,0:T(8,128)S(1)} %collective-permute-done.13.time_other, ...), custom_call_target="tpu_custom_call" | custom-call | flops 1000000 | bytes 1000000 | tf_op jit(solution)/shard_map/pallas_call | solution.py:365
  48.8 0.4 collective-permute-start.16
  49.2 1.4 %collective-permute-done.16.theirs = f32[200,128]{1,0:T(8,128)S(1)} collective-permute-done((f32[200,128]{1,0:T(8,128)S(1)}, f32[200,128]{1,0:T(8,128)S(1)}, u32[]{:S(2)}, u32[]{:S(2)}) %collective-permute-start.16) | collective-permute-done | bytes 102432 | tf_op jit(solution)/shard_map/ppermute | solution.py:379
  50.6 1.1 %collective-permute-start.17 = (f32[200,128]{1,0:T(8,128)S(1)}, f32[200,128]{1,0:T(8,128)S(1)}, u32[]{:S(2)}, u32[]{:S(2)}) collective-permute-start(f32[200,128]{1,0:T(8,128)S(1)} %shard_map.94.mine), channel_id=1, source_target_pairs={{0,2},{2,0},{1,3},{3,1},{4,6},{6,4},{5,7},{7,5},{8,10},{10,8},{9,1... | collective-permute-start | bytes 307208 | tf_op jit(solution)/shard_map/ppermute | solution.py:379
  51.7 3.9 %collective-permute-done.17.theirs = f32[200,128]{1,0:T(8,128)S(1)} collective-permute-done((f32[200,128]{1,0:T(8,128)S(1)}, f32[200,128]{1,0:T(8,128)S(1)}, u32[]{:S(2)}, u32[]{:S(2)}) %collective-permute-start.17) | collective-permute-done | bytes 102432 | tf_op jit(solution)/shard_map/ppermute | solution.py:379
  55.6 2.3 %collective-permute-start.20 = (bf16[208,128]{1,0:T(8,128)(2,1)S(1)}, bf16[208,128]{1,0:T(8,128)(2,1)S(1)}, u32[]{:S(2)}, u32[]{:S(2)}) collective-permute-start(bf16[208,128]{1,0:T(8,128)(2,1)S(1)} %shard_map.95.rest_0_), channel_id=1, source_target_pairs={{0,12},{4,8},{8,4},{12,0},{1,13},{5,9},{9,5},{13,1},{2,14},{6,10},... | collective-permute-start | bytes 159752 | tf_op jit(solution)/shard_map/ppermute | solution.py:379
  57.9 2.2 %collective-permute-start.18 = (bf16[208,128]{1,0:T(8,128)(2,1)S(1)}, bf16[208,128]{1,0:T(8,128)(2,1)S(1)}, u32[]{:S(2)}, u32[]{:S(2)}) collective-permute-start(bf16[208,128]{1,0:T(8,128)(2,1)S(1)} %shard_map.95.rest_0_), channel_id=1, source_target_pairs={{0,4},{4,0},{8,12},{12,8},{1,5},{5,1},{9,13},{13,9},{2,6},{6,2},{1... | collective-permute-start | bytes 159752 | tf_op jit(solution)/shard_map/ppermute | solution.py:379
  60.1 1.5 %collective-permute-done.20.rest_3_ = bf16[208,128]{1,0:T(8,128)(2,1)S(1)} collective-permute-done((bf16[208,128]{1,0:T(8,128)(2,1)S(1)}, bf16[208,128]{1,0:T(8,128)(2,1)S(1)}, u32[]{:S(2)}, u32[]{:S(2)}) %collective-permute-start.20) | collective-permute-done | bytes 53280 | tf_op jit(solution)/shard_map/ppermute | solution.py:379
  61.6 1.7 %collective-permute-done.19.rest_2_ = bf16[208,128]{1,0:T(8,128)(2,1)S(1)} collective-permute-done((bf16[208,128]{1,0:T(8,128)(2,1)S(1)}, bf16[208,128]{1,0:T(8,128)(2,1)S(1)}, u32[]{:S(2)}, u32[]{:S(2)}) %collective-permute-start.19) | collective-permute-done | bytes 53280 | tf_op jit(solution)/shard_map/ppermute | solution.py:379
  63.3 1.5 %shard_map.96 = (f32[1536,128]{1,0:T(8,128)}, f32[64,96]{1,0:T(8,128)}) custom-call(f32[96,1024]{1,0:T(8,128)S(1)} %get-tuple-element.56.surface, f32[96,1024]{1,0:T(8,128)S(1)} %collective-permute-done.15.other, f32[96,128]{1,0:T(8,128)S(1)} %get-tuple-element.57.time_t, bf16[208,128]{1,0:T(8,128)(2,1)S(1)} %shard_map.95.rest_0_, ...), custom_call_target="tpu_custom_call" | custom-call | flops 1000000 | bytes 1000000 | tf_op jit(solution)/shard_map/pallas_call | solution.py:365
  (23 shorter events, 1.0 us)
Async XLA Ops:
  4.5 11.4 %collective-permute-start = (bf16[720,128]{1,0:T(8,128)(2,1)S(1)}, bf16[720,128]{1,0:T(8,128)(2,1)S(1)}, u32[]{:S(2)}, u32[]{:S(2)}) collective-permute-start(bf16[720,128]{1,0:T(8,128)(2,1)S(1)} %get-tuple-element.34), channel_id=1, source_target_pairs={{0,1},{1,0},{4,5},{5,4},{8,9},{9,8},{12,13},{13,12},{2,3},{3,2},{6... | collective-permute-start | bytes 552968 | tf_op jit(solution)/shard_map/ppermute | solution.py:379
  5.1 7.8 %collective-permute-start.1 = (bf16[528,128]{1,0:T(8,128)(2,1)S(1)}, bf16[528,128]{1,0:T(8,128)(2,1)S(1)}, u32[]{:S(2)}, u32[]{:S(2)}) collective-permute-start(bf16[528,128]{1,0:T(8,128)(2,1)S(1)} %get-tuple-element.39), channel_id=1, source_target_pairs={{0,4},{4,0},{8,12},{12,8},{1,5},{5,1},{9,13},{13,9},{2,6},{6,2},{1... | collective-permute-start | bytes 405512 | tf_op jit(solution)/shard_map/ppermute | solution.py:379
  7.7 3.9 %collective-permute-start.7 = (f32[96,128]{1,0:T(8,128)S(1)}, f32[96,128]{1,0:T(8,128)S(1)}, u32[]{:S(2)}, u32[]{:S(2)}) collective-permute-start(f32[96,128]{1,0:T(8,128)S(1)} %get-tuple-element.45), channel_id=1, source_target_pairs={{1,2},{2,1},{5,6},{6,5},{9,10},{10,9},{13,14},{14,13},{17,18},{18,... | collective-permute-start | bytes 147464 | tf_op jit(solution)/shard_map/ppermute | solution.py:434
  8.4 19.0 %collective-permute-start.4 = (bf16[544,128]{1,0:T(8,128)(2,1)S(1)}, bf16[544,128]{1,0:T(8,128)(2,1)S(1)}, u32[]{:S(2)}, u32[]{:S(2)}) collective-permute-start(bf16[544,128]{1,0:T(8,128)(2,1)S(1)} %get-tuple-element.41), channel_id=1, source_target_pairs={{0,12},{4,8},{8,4},{12,0},{1,13},{5,9},{9,5},{13,1},{2,14},{6,10},... | collective-permute-start | bytes 417800 | tf_op jit(solution)/shard_map/ppermute | solution.py:379
  10.9 16.4 %collective-permute-start.5 = (bf16[544,128]{1,0:T(8,128)(2,1)S(1)}, bf16[544,128]{1,0:T(8,128)(2,1)S(1)}, u32[]{:S(2)}, u32[]{:S(2)}) collective-permute-start(bf16[544,128]{1,0:T(8,128)(2,1)S(1)} %get-tuple-element.42), channel_id=1, source_target_pairs={{0,4},{4,0},{8,12},{12,8},{1,5},{5,1},{9,13},{13,9},{2,6},{6,2},{1... | collective-permute-start | bytes 417800 | tf_op jit(solution)/shard_map/ppermute | solution.py:379
  11.6 10.2 %collective-permute-start.3 = (bf16[528,128]{1,0:T(8,128)(2,1)S(1)}, bf16[528,128]{1,0:T(8,128)(2,1)S(1)}, u32[]{:S(2)}, u32[]{:S(2)}) collective-permute-start(bf16[528,128]{1,0:T(8,128)(2,1)S(1)} %get-tuple-element.40), channel_id=1, source_target_pairs={{0,8},{4,12},{8,0},{12,4},{1,9},{5,13},{9,1},{13,5},{2,10},{6,14},... | collective-permute-start | bytes 405512 | tf_op jit(solution)/shard_map/ppermute | solution.py:379
  12.8 14.5 %collective-permute-start.6 = (bf16[528,128]{1,0:T(8,128)(2,1)S(1)}, bf16[528,128]{1,0:T(8,128)(2,1)S(1)}, u32[]{:S(2)}, u32[]{:S(2)}) collective-permute-start(bf16[528,128]{1,0:T(8,128)(2,1)S(1)} %get-tuple-element.43), channel_id=1, source_target_pairs={{0,5},{1,4},{4,1},{5,0},{8,13},{9,12},{12,9},{13,8},{2,7},{3,6},{6... | collective-permute-start | bytes 405512 | tf_op jit(solution)/shard_map/ppermute | solution.py:379
  15.9 0.8 %copy-start = (f32[64,96]{1,0:T(8,128)S(1)}, f32[64,96]{1,0:T(8,128)}, u32[]{:S(2)}) copy-start(f32[64,96]{1,0:T(8,128)} %time_own.1) | copy-start | bytes 73732
  16.0 14.2 %collective-permute-start.2 = (bf16[528,128]{1,0:T(8,128)(2,1)S(1)}, bf16[528,128]{1,0:T(8,128)(2,1)S(1)}, u32[]{:S(2)}, u32[]{:S(2)}) collective-permute-start(bf16[528,128]{1,0:T(8,128)(2,1)S(1)} %shard_map.88), channel_id=1, source_target_pairs={{0,9},{1,8},{4,13},{5,12},{8,1},{9,0},{12,5},{13,4},{2,11},{3,10},... | collective-permute-start | bytes 405512 | tf_op jit(solution)/shard_map/ppermute | solution.py:379
  31.8 1.3 %collective-permute-start.8 = (f32[200,128]{1,0:T(8,128)S(1)}, f32[200,128]{1,0:T(8,128)S(1)}, u32[]{:S(2)}, u32[]{:S(2)}) collective-permute-start(f32[200,128]{1,0:T(8,128)S(1)} %get-tuple-element.48), channel_id=1, source_target_pairs={{0,1},{1,0},{2,3},{3,2},{4,5},{5,4},{6,7},{7,6},{8,9},{9,8},{10,11... | collective-permute-start | bytes 307208 | tf_op jit(solution)/shard_map/ppermute | solution.py:379
  33.2 4.2 %collective-permute-start.9 = (f32[104,128]{1,0:T(8,128)S(1)}, f32[104,128]{1,0:T(8,128)S(1)}, u32[]{:S(2)}, u32[]{:S(2)}) collective-permute-start(f32[104,128]{1,0:T(8,128)S(1)} %get-tuple-element.49.mine), channel_id=1, source_target_pairs={{0,2},{2,0},{1,3},{3,1},{4,6},{6,4},{5,7},{7,5},{8,10},{10,8},{9,1... | collective-permute-start | bytes 159752 | tf_op jit(solution)/shard_map/ppermute | solution.py:379
  37.4 6.2 %collective-permute-start.12 = (f32[120,128]{1,0:T(8,128)S(1)}, f32[120,128]{1,0:T(8,128)S(1)}, u32[]{:S(2)}, u32[]{:S(2)}) collective-permute-start(f32[120,128]{1,0:T(8,128)S(1)} %shard_map.91.rest_0_), channel_id=1, source_target_pairs={{0,12},{4,8},{8,4},{12,0},{1,13},{5,9},{9,5},{13,1},{2,14},{6,10},... | collective-permute-start | bytes 184328 | tf_op jit(solution)/shard_map/ppermute | solution.py:379
  40.3 5.2 %collective-permute-start.11 = (f32[120,128]{1,0:T(8,128)S(1)}, f32[120,128]{1,0:T(8,128)S(1)}, u32[]{:S(2)}, u32[]{:S(2)}) collective-permute-start(f32[120,128]{1,0:T(8,128)S(1)} %shard_map.91.rest_0_), channel_id=1, source_target_pairs={{0,8},{4,12},{8,0},{12,4},{1,9},{5,13},{9,1},{13,5},{2,10},{6,14},... | collective-permute-start | bytes 184328 | tf_op jit(solution)/shard_map/ppermute | solution.py:379
  40.3 5.2 %collective-permute-start.10 = (f32[120,128]{1,0:T(8,128)S(1)}, f32[120,128]{1,0:T(8,128)S(1)}, u32[]{:S(2)}, u32[]{:S(2)}) collective-permute-start(f32[120,128]{1,0:T(8,128)S(1)} %shard_map.91.rest_0_), channel_id=1, source_target_pairs={{0,4},{4,0},{8,12},{12,8},{1,5},{5,1},{9,13},{13,9},{2,6},{6,2},{1... | collective-permute-start | bytes 184328 | tf_op jit(solution)/shard_map/ppermute | solution.py:379
  41.8 3.9 %collective-permute-start.14 = (f32[96,128]{1,0:T(8,128)S(1)}, f32[96,128]{1,0:T(8,128)S(1)}, u32[]{:S(2)}, u32[]{:S(2)}) collective-permute-start(f32[96,128]{1,0:T(8,128)S(1)} %get-tuple-element.55), channel_id=1, source_target_pairs={{1,2},{2,1},{5,6},{6,5},{9,10},{10,9},{13,14},{14,13},{17,18},{18,... | collective-permute-start | bytes 147464 | tf_op jit(solution)/shard_map/ppermute | solution.py:434
  45.6 1.3 %collective-permute-start.13 = (f32[96,128]{1,0:T(8,128)S(1)}, f32[96,128]{1,0:T(8,128)S(1)}, u32[]{:S(2)}, u32[]{:S(2)}) collective-permute-start(f32[96,128]{1,0:T(8,128)S(1)} %get-tuple-element.50.time_own), channel_id=1, source_target_pairs={{0,1},{1,0},{2,3},{3,2},{4,5},{5,4},{6,7},{7,6},{8,9},{9,8},{10,11... | collective-permute-start | bytes 147464 | tf_op jit(solution)/shard_map/ppermute | solution.py:379
  48.6 14.7 %collective-permute-start.15 = (f32[96,1024]{1,0:T(8,128)S(1)}, f32[96,1024]{1,0:T(8,128)S(1)}, u32[]{:S(2)}, u32[]{:S(2)}) collective-permute-start(f32[96,1024]{1,0:T(8,128)S(1)} %get-tuple-element.56.surface), channel_id=1, source_target_pairs={{0,1},{1,0},{2,3},{3,2},{4,5},{5,4},{6,7},{7,6},{8,9},{9,8},{10,11... | collective-permute-start | bytes 1179656 | tf_op jit(solution)/shard_map/ppermute | solution.py:379
  48.8 1.7 %collective-permute-start.16 = (f32[200,128]{1,0:T(8,128)S(1)}, f32[200,128]{1,0:T(8,128)S(1)}, u32[]{:S(2)}, u32[]{:S(2)}) collective-permute-start(f32[200,128]{1,0:T(8,128)S(1)} %get-tuple-element.59), channel_id=1, source_target_pairs={{0,1},{1,0},{2,3},{3,2},{4,5},{5,4},{6,7},{7,6},{8,9},{9,8},{10,11... | collective-permute-start | bytes 307208 | tf_op jit(solution)/shard_map/ppermute | solution.py:379
  50.6 5.0 %collective-permute-start.17 = (f32[200,128]{1,0:T(8,128)S(1)}, f32[200,128]{1,0:T(8,128)S(1)}, u32[]{:S(2)}, u32[]{:S(2)}) collective-permute-start(f32[200,128]{1,0:T(8,128)S(1)} %shard_map.94.mine), channel_id=1, source_target_pairs={{0,2},{2,0},{1,3},{3,1},{4,6},{6,4},{5,7},{7,5},{8,10},{10,8},{9,1... | collective-permute-start | bytes 307208 | tf_op jit(solution)/shard_map/ppermute | solution.py:379
  55.6 6.0 %collective-permute-start.20 = (bf16[208,128]{1,0:T(8,128)(2,1)S(1)}, bf16[208,128]{1,0:T(8,128)(2,1)S(1)}, u32[]{:S(2)}, u32[]{:S(2)}) collective-permute-start(bf16[208,128]{1,0:T(8,128)(2,1)S(1)} %shard_map.95.rest_0_), channel_id=1, source_target_pairs={{0,12},{4,8},{8,4},{12,0},{1,13},{5,9},{9,5},{13,1},{2,14},{6,10},... | collective-permute-start | bytes 159752 | tf_op jit(solution)/shard_map/ppermute | solution.py:379
  57.9 5.4 %collective-permute-start.19 = (bf16[208,128]{1,0:T(8,128)(2,1)S(1)}, bf16[208,128]{1,0:T(8,128)(2,1)S(1)}, u32[]{:S(2)}, u32[]{:S(2)}) collective-permute-start(bf16[208,128]{1,0:T(8,128)(2,1)S(1)} %shard_map.95.rest_0_), channel_id=1, source_target_pairs={{0,8},{4,12},{8,0},{12,4},{1,9},{5,13},{9,1},{13,5},{2,10},{6,14},... | collective-permute-start | bytes 159752 | tf_op jit(solution)/shard_map/ppermute | solution.py:379
  57.9 5.4 %collective-permute-start.18 = (bf16[208,128]{1,0:T(8,128)(2,1)S(1)}, bf16[208,128]{1,0:T(8,128)(2,1)S(1)}, u32[]{:S(2)}, u32[]{:S(2)}) collective-permute-start(bf16[208,128]{1,0:T(8,128)(2,1)S(1)} %shard_map.95.rest_0_), channel_id=1, source_target_pairs={{0,4},{4,0},{8,12},{12,8},{1,5},{5,1},{9,13},{13,9},{2,6},{6,2},{1... | collective-permute-start | bytes 159752 | tf_op jit(solution)/shard_map/ppermute | solution.py:379

commit v7 on v6

--- a/solution.py
+++ b/solution.py
@@ -325,7 +325,8 @@
     beside[...] = theirs[rows:, :]
 
 
-def merge_kernel(mine, theirs, out):
+def merge_kernel(mine, theirs, edge_in, out, edge_out):
+    edge_out[...] = edge_in[...]
     out[...] = (mine[...].astype(F32) + theirs[...].astype(F32)).astype(BF16)
 
 
@@ -425,7 +426,8 @@
     pieces = dict(zip(sends, pieces))
     if paired:
         passing = across(pieces.pop((1, 3)), "lon", 1)
-        pieces[1, 2] = call(merge_kernel, shape(passing.shape, BF16))(pieces[1, 2], passing)
+        outs = [shape(passing.shape, BF16), shape(edge_far.shape)]
+        pieces[1, 2], edge_far = call(merge_kernel, outs)(pieces[1, 2], passing, edge_far)
     pieces = {key: arrived(key, piece) for key, piece in pieces.items()}
     order = list(pieces)
 

time: 65.1 us -> 63.2 us (0.971)
  starting transfers between devices: 23.8 us -> 21 us
  waiting for transfers between devices: 30.6 us -> 32.1 us
    ppermute x19, starting transfers between devices: 22.5 us -> 19.7 us  [across(): lax.ppermute(value, axis, [(i, i ^ step) for i in range(lax.axis_size(axi...]
    ppermute x19, waiting for transfers between devices: 30.6 us -> 32.1 us  [across(): lax.ppermute(value, axis, [(i, i ^ step) for i in range(lax.axis_size(axi...]
  transfers between devices with their start and end apart: 21 -> 21, of which waited for: 12 -> 13; matrix products, arithmetic and copies ran while one was open for 0% -> 0% of each run, Pallas kernels for 1% -> 1%
where the time goes in v7:
time: 63.2 us; the launch traced here: 63 us
  waiting for transfers between devices  32.1 us (51%)
  starting transfers between devices  21 us (33%)
  Pallas kernels  9.2 us (15%)
  between operations  0.74 us (1%)
    ppermute x19, waiting for transfers between devices, across(): lax.ppermute(value, axis, [(i, i ^ step) for i in range(lax.axis_size(axi...  32.1 us
    ppermute x19, starting transfers between devices, across(): lax.ppermute(value, axis, [(i, i ^ step) for i in range(lax.axis_size(axi...  19.7 us
    pallas_call x11, Pallas kernels, run(): pl.pallas_call(kernel, out_shape=out_shape, in_specs=[pl.BlockSpec(memory...  9.2 us
    ppermute x2, starting transfers between devices, bands(): return lax.ppermute(edge, ('lat', 'ta'), there + [(b, a) for a, b in there])  1.31 us
  transfers between devices with their start and end apart: 21, of which 13 were waited for; matrix products, arithmetic and copies ran while one was open for 0% of the time, Pallas kernels for 1%

profile of v7, /device:TPU:0, one launch (start us, length us, event | category | flops | bytes accessed | tf_op | source)
XLA Modules:
  0.0 63.0 jit_solution(7699277713446790906)
XLA Ops:
  0.6 3.9 %shard_map.86 = (bf16[528,128]{1,0:T(8,128)(2,1)S(1)}, bf16[528,128]{1,0:T(8,128)(2,1)S(1)}, bf16[528,128]{1,0:T(8,128)(2,1)S(1)}, bf16[544,128]{1,0:T(8,128)(2,...) custom-call(s32[1,4,32]{2,1,0:T(4,128)} %list_hbm.1, ...), custom_call_target="tpu_custom_call" | custom-call | flops 1000000 | bytes 1000000 | tf_op jit(solution)/shard_map/pallas_call | solution.py:366
  4.5 3.1 %collective-permute-start.1 = (bf16[528,128]{1,0:T(8,128)(2,1)S(1)}, bf16[528,128]{1,0:T(8,128)(2,1)S(1)}, u32[]{:S(2)}, u32[]{:S(2)}) collective-permute-start(bf16[528,128]{1,0:T(8,128)(2,1)S(1)} %get-tuple-element.41), channel_id=1, source_target_pairs={{0,4},{4,0},{8,12},{12,8},{1,5},{5,1},{9,13},{13,9},{2,6},{6,2},{1... | collective-permute-start | bytes 405512 | tf_op jit(solution)/shard_map/ppermute | solution.py:380
  7.6 2.6 %collective-permute-start.3 = (bf16[528,128]{1,0:T(8,128)(2,1)S(1)}, bf16[528,128]{1,0:T(8,128)(2,1)S(1)}, u32[]{:S(2)}, u32[]{:S(2)}) collective-permute-start(bf16[528,128]{1,0:T(8,128)(2,1)S(1)} %get-tuple-element.44), channel_id=1, source_target_pairs={{0,8},{4,12},{8,0},{12,4},{1,9},{5,13},{9,1},{13,5},{2,10},{6,14},... | collective-permute-start | bytes 405512 | tf_op jit(solution)/shard_map/ppermute | solution.py:380
  10.2 0.9 %collective-permute-start.5 = (bf16[544,128]{1,0:T(8,128)(2,1)S(1)}, bf16[544,128]{1,0:T(8,128)(2,1)S(1)}, u32[]{:S(2)}, u32[]{:S(2)}) collective-permute-start(bf16[544,128]{1,0:T(8,128)(2,1)S(1)} %get-tuple-element.46), channel_id=1, source_target_pairs={{0,4},{4,0},{8,12},{12,8},{1,5},{5,1},{9,13},{13,9},{2,6},{6,2},{1... | collective-permute-start | bytes 417800 | tf_op jit(solution)/shard_map/ppermute | solution.py:380
  11.1 2.1 %collective-permute-done.1.theirs = bf16[528,128]{1,0:T(8,128)(2,1)S(1)} collective-permute-done((bf16[528,128]{1,0:T(8,128)(2,1)S(1)}, bf16[528,128]{1,0:T(8,128)(2,1)S(1)}, u32[]{:S(2)}, u32[]{:S(2)}) %collective-permute-start.1) | collective-permute-done | bytes 135200 | tf_op jit(solution)/shard_map/ppermute | solution.py:380
  13.3 7.0 %collective-permute-done.3.rest_1_ = bf16[528,128]{1,0:T(8,128)(2,1)S(1)} collective-permute-done((bf16[528,128]{1,0:T(8,128)(2,1)S(1)}, bf16[528,128]{1,0:T(8,128)(2,1)S(1)}, u32[]{:S(2)}, u32[]{:S(2)}) %collective-permute-start.3) | collective-permute-done | bytes 135200 | tf_op jit(solution)/shard_map/ppermute | solution.py:380
  20.3 0.7 %collective-permute-start.7 = (f32[96,128]{1,0:T(8,128)S(1)}, f32[96,128]{1,0:T(8,128)S(1)}, u32[]{:S(2)}, u32[]{:S(2)}) collective-permute-start(f32[96,128]{1,0:T(8,128)S(1)} %get-tuple-element.49), channel_id=1, source_target_pairs={{1,2},{2,1},{5,6},{6,5},{9,10},{10,9},{13,14},{14,13},{17,18},{18,... | collective-permute-start | bytes 147464 | tf_op jit(solution)/shard_map/ppermute | solution.py:436
  20.9 0.2 shard_map.87
  21.2 3.0 %collective-permute-done.6.rest_5_ = bf16[528,128]{1,0:T(8,128)(2,1)S(1)} collective-permute-done((bf16[528,128]{1,0:T(8,128)(2,1)S(1)}, bf16[528,128]{1,0:T(8,128)(2,1)S(1)}, u32[]{:S(2)}, u32[]{:S(2)}) %collective-permute-start.6) | collective-permute-done | bytes 135200 | tf_op jit(solution)/shard_map/ppermute | solution.py:380
  24.2 4.3 %collective-permute-done.2.rest_0_ = bf16[528,128]{1,0:T(8,128)(2,1)S(1)} collective-permute-done((bf16[528,128]{1,0:T(8,128)(2,1)S(1)}, bf16[528,128]{1,0:T(8,128)(2,1)S(1)}, u32[]{:S(2)}, u32[]{:S(2)}) %collective-permute-start.2) | collective-permute-done | bytes 135200 | tf_op jit(solution)/shard_map/ppermute | solution.py:380
  28.5 1.6 %shard_map.89 = (f32[96,1024]{1,0:T(8,128)S(1)}, f32[120,128]{1,0:T(8,128)S(1)}, f32[200,128]{1,0:T(8,128)S(1)}, f32[96,128]{1,0:T(8,128)S(1)}, f32[128,1024]{1,0:T(8,128)S(1)}, /*index=5*/f32[16,128]{1,0:T(8,128)S(1)}) custom-call(f32[96,1024]{1,0:T(8,128)S(1)} %get-tuple-element.34.surface, f32[96,128]{1,0:T(8,128)S(1)} %get-tuple-element.35.edge_near, ...), custom_call_target="tpu_custom_call" | custom-call | flops 1000000 | bytes 1000000 | tf_op jit(solution)/shard_map/pallas_call | solution.py:366
  30.1 1.3 %collective-permute-done.8.theirs = f32[200,128]{1,0:T(8,128)S(1)} collective-permute-done((f32[200,128]{1,0:T(8,128)S(1)}, f32[200,128]{1,0:T(8,128)S(1)}, u32[]{:S(2)}, u32[]{:S(2)}) %collective-permute-start.8) | collective-permute-done | bytes 102432 | tf_op jit(solution)/shard_map/ppermute | solution.py:380
  31.4 1.6 %collective-permute-start.9 = (f32[104,128]{1,0:T(8,128)S(1)}, f32[104,128]{1,0:T(8,128)S(1)}, u32[]{:S(2)}, u32[]{:S(2)}) collective-permute-start(f32[104,128]{1,0:T(8,128)S(1)} %get-tuple-element.53.mine), channel_id=1, source_target_pairs={{0,2},{2,0},{1,3},{3,1},{4,6},{6,4},{5,7},{7,5},{8,10},{10,8},{9,1... | collective-permute-start | bytes 159752 | tf_op jit(solution)/shard_map/ppermute | solution.py:380
  33.0 2.6 %collective-permute-done.9.theirs = f32[104,128]{1,0:T(8,128)S(1)} collective-permute-done((f32[104,128]{1,0:T(8,128)S(1)}, f32[104,128]{1,0:T(8,128)S(1)}, u32[]{:S(2)}, u32[]{:S(2)}) %collective-permute-start.9) | collective-permute-done | bytes 53280 | tf_op jit(solution)/shard_map/ppermute | solution.py:380
  35.6 2.4 %collective-permute-start.12 = (f32[120,128]{1,0:T(8,128)S(1)}, f32[120,128]{1,0:T(8,128)S(1)}, u32[]{:S(2)}, u32[]{:S(2)}) collective-permute-start(f32[120,128]{1,0:T(8,128)S(1)} %shard_map.91.rest_0_), channel_id=1, source_target_pairs={{0,12},{4,8},{8,4},{12,0},{1,13},{5,9},{9,5},{13,1},{2,14},{6,10},... | collective-permute-start | bytes 184328 | tf_op jit(solution)/shard_map/ppermute | solution.py:380
  38.1 2.0 %collective-permute-start.10 = (f32[120,128]{1,0:T(8,128)S(1)}, f32[120,128]{1,0:T(8,128)S(1)}, u32[]{:S(2)}, u32[]{:S(2)}) collective-permute-start(f32[120,128]{1,0:T(8,128)S(1)} %shard_map.91.rest_0_), channel_id=1, source_target_pairs={{0,4},{4,0},{8,12},{12,8},{1,5},{5,1},{9,13},{13,9},{2,6},{6,2},{1... | collective-permute-start | bytes 184328 | tf_op jit(solution)/shard_map/ppermute | solution.py:380
  40.1 0.7 %collective-permute-start.14 = (f32[96,128]{1,0:T(8,128)S(1)}, f32[96,128]{1,0:T(8,128)S(1)}, u32[]{:S(2)}, u32[]{:S(2)}) collective-permute-start(f32[96,128]{1,0:T(8,128)S(1)} %get-tuple-element.59), channel_id=1, source_target_pairs={{1,2},{2,1},{5,6},{6,5},{9,10},{10,9},{13,14},{14,13},{17,18},{18,... | collective-permute-start | bytes 147464 | tf_op jit(solution)/shard_map/ppermute | solution.py:436
  40.8 1.3 %collective-permute-done.12.rest_3_.cols_b = f32[120,128]{1,0:T(8,128)S(1)} collective-permute-done((f32[120,128]{1,0:T(8,128)S(1)}, f32[120,128]{1,0:T(8,128)S(1)}, u32[]{:S(2)}, u32[]{:S(2)}) %collective-permute-start.12) | collective-permute-done | bytes 61472 | tf_op jit(solution)/shard_map/ppermute | solution.py:380
  42.1 1.6 %collective-permute-done.11.rest_2_ = f32[120,128]{1,0:T(8,128)S(1)} collective-permute-done((f32[120,128]{1,0:T(8,128)S(1)}, f32[120,128]{1,0:T(8,128)S(1)}, u32[]{:S(2)}, u32[]{:S(2)}) %collective-permute-start.11) | collective-permute-done | bytes 61472 | tf_op jit(solution)/shard_map/ppermute | solution.py:380
  43.7 0.1 shard_map.92
  43.9 1.2 %collective-permute-done.13.time_other = f32[96,128]{1,0:T(8,128)S(1)} collective-permute-done((f32[96,128]{1,0:T(8,128)S(1)}, f32[96,128]{1,0:T(8,128)S(1)}, u32[]{:S(2)}, u32[]{:S(2)}) %collective-permute-start.13) | collective-permute-done | bytes 49184 | tf_op jit(solution)/shard_map/ppermute | solution.py:380
  45.1 1.7 %shard_map.93 = (f32[96,1024]{1,0:T(8,128)S(1)}, f32[96,128]{1,0:T(8,128)S(1)}, f32[200,128]{1,0:T(8,128)S(1)}, f32[200,128]{1,0:T(8,128)S(1)}) custom-call(f32[96,1024]{1,0:T(8,128)S(1)} %get-tuple-element.50.surface, f32[96,128]{1,0:T(8,128)S(1)} %get-tuple-element.54.time_own, f32[96,128]{1,0:T(8,128)S(1)} %collective-permute-done.13.time_other, ...), custom_call_target="tpu_custom_call" | custom-call | flops 1000000 | bytes 1000000 | tf_op jit(solution)/shard_map/pallas_call | solution.py:366
  46.9 0.3 collective-permute-start.15
  47.2 0.3 collective-permute-start.16
  47.4 1.4 %collective-permute-done.16.theirs = f32[200,128]{1,0:T(8,128)S(1)} collective-permute-done((f32[200,128]{1,0:T(8,128)S(1)}, f32[200,128]{1,0:T(8,128)S(1)}, u32[]{:S(2)}, u32[]{:S(2)}) %collective-permute-start.16) | collective-permute-done | bytes 102432 | tf_op jit(solution)/shard_map/ppermute | solution.py:380
  48.8 1.9 %collective-permute-start.17 = (f32[200,128]{1,0:T(8,128)S(1)}, f32[200,128]{1,0:T(8,128)S(1)}, u32[]{:S(2)}, u32[]{:S(2)}) collective-permute-start(f32[200,128]{1,0:T(8,128)S(1)} %shard_map.94.mine), channel_id=1, source_target_pairs={{0,2},{2,0},{1,3},{3,1},{4,6},{6,4},{5,7},{7,5},{8,10},{10,8},{9,1... | collective-permute-start | bytes 307208 | tf_op jit(solution)/shard_map/ppermute | solution.py:380
  50.7 3.2 %collective-permute-done.17.theirs = f32[200,128]{1,0:T(8,128)S(1)} collective-permute-done((f32[200,128]{1,0:T(8,128)S(1)}, f32[200,128]{1,0:T(8,128)S(1)}, u32[]{:S(2)}, u32[]{:S(2)}) %collective-permute-start.17) | collective-permute-done | bytes 102432 | tf_op jit(solution)/shard_map/ppermute | solution.py:380
  54.0 2.4 %collective-permute-start.20 = (bf16[208,128]{1,0:T(8,128)(2,1)S(1)}, bf16[208,128]{1,0:T(8,128)(2,1)S(1)}, u32[]{:S(2)}, u32[]{:S(2)}) collective-permute-start(bf16[208,128]{1,0:T(8,128)(2,1)S(1)} %shard_map.95.rest_0_), channel_id=1, source_target_pairs={{0,12},{4,8},{8,4},{12,0},{1,13},{5,9},{9,5},{13,1},{2,14},{6,10},... | collective-permute-start | bytes 159752 | tf_op jit(solution)/shard_map/ppermute | solution.py:380
  56.4 2.0 %collective-permute-start.18 = (bf16[208,128]{1,0:T(8,128)(2,1)S(1)}, bf16[208,128]{1,0:T(8,128)(2,1)S(1)}, u32[]{:S(2)}, u32[]{:S(2)}) collective-permute-start(bf16[208,128]{1,0:T(8,128)(2,1)S(1)} %shard_map.95.rest_0_), channel_id=1, source_target_pairs={{0,4},{4,0},{8,12},{12,8},{1,5},{5,1},{9,13},{13,9},{2,6},{6,2},{1... | collective-permute-start | bytes 159752 | tf_op jit(solution)/shard_map/ppermute | solution.py:380
  58.4 1.5 %collective-permute-done.20.rest_3_ = bf16[208,128]{1,0:T(8,128)(2,1)S(1)} collective-permute-done((bf16[208,128]{1,0:T(8,128)(2,1)S(1)}, bf16[208,128]{1,0:T(8,128)(2,1)S(1)}, u32[]{:S(2)}, u32[]{:S(2)}) %collective-permute-start.20) | collective-permute-done | bytes 53280 | tf_op jit(solution)/shard_map/ppermute | solution.py:380
  59.9 1.5 %collective-permute-done.19.rest_2_ = bf16[208,128]{1,0:T(8,128)(2,1)S(1)} collective-permute-done((bf16[208,128]{1,0:T(8,128)(2,1)S(1)}, bf16[208,128]{1,0:T(8,128)(2,1)S(1)}, u32[]{:S(2)}, u32[]{:S(2)}) %collective-permute-start.19) | collective-permute-done | bytes 53280 | tf_op jit(solution)/shard_map/ppermute | solution.py:380
  61.5 1.5 %shard_map.96 = (f32[1536,128]{1,0:T(8,128)}, f32[64,96]{1,0:T(8,128)}) custom-call(f32[96,1024]{1,0:T(8,128)S(1)} %get-tuple-element.60.surface, f32[96,1024]{1,0:T(8,128)S(1)} %collective-permute-done.15.other, f32[96,128]{1,0:T(8,128)S(1)} %get-tuple-element.61.time_t, bf16[208,128]{1,0:T(8,128)(2,1)S(1)} %shard_map.95.rest_0_, ...), custom_call_target="tpu_custom_call" | custom-call | flops 1000000 | bytes 1000000 | tf_op jit(solution)/shard_map/pallas_call | solution.py:366
  (23 shorter events, 0.3 us)
Async XLA Ops:
  4.5 8.7 %collective-permute-start.1 = (bf16[528,128]{1,0:T(8,128)(2,1)S(1)}, bf16[528,128]{1,0:T(8,128)(2,1)S(1)}, u32[]{:S(2)}, u32[]{:S(2)}) collective-permute-start(bf16[528,128]{1,0:T(8,128)(2,1)S(1)} %get-tuple-element.41), channel_id=1, source_target_pairs={{0,4},{4,0},{8,12},{12,8},{1,5},{5,1},{9,13},{13,9},{2,6},{6,2},{1... | collective-permute-start | bytes 405512 | tf_op jit(solution)/shard_map/ppermute | solution.py:380
  7.6 12.6 %collective-permute-start.3 = (bf16[528,128]{1,0:T(8,128)(2,1)S(1)}, bf16[528,128]{1,0:T(8,128)(2,1)S(1)}, u32[]{:S(2)}, u32[]{:S(2)}) collective-permute-start(bf16[528,128]{1,0:T(8,128)(2,1)S(1)} %get-tuple-element.44), channel_id=1, source_target_pairs={{0,8},{4,12},{8,0},{12,4},{1,9},{5,13},{9,1},{13,5},{2,10},{6,14},... | collective-permute-start | bytes 405512 | tf_op jit(solution)/shard_map/ppermute | solution.py:380
  10.2 10.0 %collective-permute-start = (bf16[720,128]{1,0:T(8,128)(2,1)S(1)}, bf16[720,128]{1,0:T(8,128)(2,1)S(1)}, u32[]{:S(2)}, u32[]{:S(2)}) collective-permute-start(bf16[720,128]{1,0:T(8,128)(2,1)S(1)} %get-tuple-element.36), channel_id=1, source_target_pairs={{0,1},{1,0},{4,5},{5,4},{8,9},{9,8},{12,13},{13,12},{2,3},{3,2},{6... | collective-permute-start | bytes 552968 | tf_op jit(solution)/shard_map/ppermute | solution.py:380
  10.2 13.9 %collective-permute-start.4 = (bf16[544,128]{1,0:T(8,128)(2,1)S(1)}, bf16[544,128]{1,0:T(8,128)(2,1)S(1)}, u32[]{:S(2)}, u32[]{:S(2)}) collective-permute-start(bf16[544,128]{1,0:T(8,128)(2,1)S(1)} %get-tuple-element.45), channel_id=1, source_target_pairs={{0,12},{4,8},{8,4},{12,0},{1,13},{5,9},{9,5},{13,1},{2,14},{6,10},... | collective-permute-start | bytes 417800 | tf_op jit(solution)/shard_map/ppermute | solution.py:380
  10.2 13.9 %collective-permute-start.5 = (bf16[544,128]{1,0:T(8,128)(2,1)S(1)}, bf16[544,128]{1,0:T(8,128)(2,1)S(1)}, u32[]{:S(2)}, u32[]{:S(2)}) collective-permute-start(bf16[544,128]{1,0:T(8,128)(2,1)S(1)} %get-tuple-element.46), channel_id=1, source_target_pairs={{0,4},{4,0},{8,12},{12,8},{1,5},{5,1},{9,13},{13,9},{2,6},{6,2},{1... | collective-permute-start | bytes 417800 | tf_op jit(solution)/shard_map/ppermute | solution.py:380
  13.2 10.9 %collective-permute-start.6 = (bf16[528,128]{1,0:T(8,128)(2,1)S(1)}, bf16[528,128]{1,0:T(8,128)(2,1)S(1)}, u32[]{:S(2)}, u32[]{:S(2)}) collective-permute-start(bf16[528,128]{1,0:T(8,128)(2,1)S(1)} %get-tuple-element.47), channel_id=1, source_target_pairs={{0,5},{1,4},{4,1},{5,0},{8,13},{9,12},{12,9},{13,8},{2,7},{3,6},{6... | collective-permute-start | bytes 405512 | tf_op jit(solution)/shard_map/ppermute | solution.py:380
  13.2 7.7 %copy-start = (f32[64,96]{1,0:T(8,128)S(1)}, f32[64,96]{1,0:T(8,128)}, u32[]{:S(2)}) copy-start(f32[64,96]{1,0:T(8,128)} %time_own.1) | copy-start | bytes 73732
  20.3 8.2 %collective-permute-start.2 = (bf16[528,128]{1,0:T(8,128)(2,1)S(1)}, bf16[528,128]{1,0:T(8,128)(2,1)S(1)}, u32[]{:S(2)}, u32[]{:S(2)}) collective-permute-start(bf16[528,128]{1,0:T(8,128)(2,1)S(1)} %get-tuple-element.43), channel_id=1, source_target_pairs={{0,9},{1,8},{4,13},{5,12},{8,1},{9,0},{12,5},{13,4},{2,11},{3,10},... | collective-permute-start | bytes 405512 | tf_op jit(solution)/shard_map/ppermute | solution.py:380
  20.3 3.9 %collective-permute-start.7 = (f32[96,128]{1,0:T(8,128)S(1)}, f32[96,128]{1,0:T(8,128)S(1)}, u32[]{:S(2)}, u32[]{:S(2)}) collective-permute-start(f32[96,128]{1,0:T(8,128)S(1)} %get-tuple-element.49), channel_id=1, source_target_pairs={{1,2},{2,1},{5,6},{6,5},{9,10},{10,9},{13,14},{14,13},{17,18},{18,... | collective-permute-start | bytes 147464 | tf_op jit(solution)/shard_map/ppermute | solution.py:436
  30.1 1.3 %collective-permute-start.8 = (f32[200,128]{1,0:T(8,128)S(1)}, f32[200,128]{1,0:T(8,128)S(1)}, u32[]{:S(2)}, u32[]{:S(2)}) collective-permute-start(f32[200,128]{1,0:T(8,128)S(1)} %get-tuple-element.52), channel_id=1, source_target_pairs={{0,1},{1,0},{2,3},{3,2},{4,5},{5,4},{6,7},{7,6},{8,9},{9,8},{10,11... | collective-permute-start | bytes 307208 | tf_op jit(solution)/shard_map/ppermute | solution.py:380
  31.4 4.2 %collective-permute-start.9 = (f32[104,128]{1,0:T(8,128)S(1)}, f32[104,128]{1,0:T(8,128)S(1)}, u32[]{:S(2)}, u32[]{:S(2)}) collective-permute-start(f32[104,128]{1,0:T(8,128)S(1)} %get-tuple-element.53.mine), channel_id=1, source_target_pairs={{0,2},{2,0},{1,3},{3,1},{4,6},{6,4},{5,7},{7,5},{8,10},{10,8},{9,1... | collective-permute-start | bytes 159752 | tf_op jit(solution)/shard_map/ppermute | solution.py:380
  35.6 6.5 %collective-permute-start.12 = (f32[120,128]{1,0:T(8,128)S(1)}, f32[120,128]{1,0:T(8,128)S(1)}, u32[]{:S(2)}, u32[]{:S(2)}) collective-permute-start(f32[120,128]{1,0:T(8,128)S(1)} %shard_map.91.rest_0_), channel_id=1, source_target_pairs={{0,12},{4,8},{8,4},{12,0},{1,13},{5,9},{9,5},{13,1},{2,14},{6,10},... | collective-permute-start | bytes 184328 | tf_op jit(solution)/shard_map/ppermute | solution.py:380
  38.1 5.6 %collective-permute-start.11 = (f32[120,128]{1,0:T(8,128)S(1)}, f32[120,128]{1,0:T(8,128)S(1)}, u32[]{:S(2)}, u32[]{:S(2)}) collective-permute-start(f32[120,128]{1,0:T(8,128)S(1)} %shard_map.91.rest_0_), channel_id=1, source_target_pairs={{0,8},{4,12},{8,0},{12,4},{1,9},{5,13},{9,1},{13,5},{2,10},{6,14},... | collective-permute-start | bytes 184328 | tf_op jit(solution)/shard_map/ppermute | solution.py:380
  38.1 5.6 %collective-permute-start.10 = (f32[120,128]{1,0:T(8,128)S(1)}, f32[120,128]{1,0:T(8,128)S(1)}, u32[]{:S(2)}, u32[]{:S(2)}) collective-permute-start(f32[120,128]{1,0:T(8,128)S(1)} %shard_map.91.rest_0_), channel_id=1, source_target_pairs={{0,4},{4,0},{8,12},{12,8},{1,5},{5,1},{9,13},{13,9},{2,6},{6,2},{1... | collective-permute-start | bytes 184328 | tf_op jit(solution)/shard_map/ppermute | solution.py:380
  40.1 3.8 %collective-permute-start.14 = (f32[96,128]{1,0:T(8,128)S(1)}, f32[96,128]{1,0:T(8,128)S(1)}, u32[]{:S(2)}, u32[]{:S(2)}) collective-permute-start(f32[96,128]{1,0:T(8,128)S(1)} %get-tuple-element.59), channel_id=1, source_target_pairs={{1,2},{2,1},{5,6},{6,5},{9,10},{10,9},{13,14},{14,13},{17,18},{18,... | collective-permute-start | bytes 147464 | tf_op jit(solution)/shard_map/ppermute | solution.py:436
  43.8 1.3 %collective-permute-start.13 = (f32[96,128]{1,0:T(8,128)S(1)}, f32[96,128]{1,0:T(8,128)S(1)}, u32[]{:S(2)}, u32[]{:S(2)}) collective-permute-start(f32[96,128]{1,0:T(8,128)S(1)} %get-tuple-element.54.time_own), channel_id=1, source_target_pairs={{0,1},{1,0},{2,3},{3,2},{4,5},{5,4},{6,7},{7,6},{8,9},{9,8},{10,11... | collective-permute-start | bytes 147464 | tf_op jit(solution)/shard_map/ppermute | solution.py:380
  46.9 14.6 %collective-permute-start.15 = (f32[96,1024]{1,0:T(8,128)S(1)}, f32[96,1024]{1,0:T(8,128)S(1)}, u32[]{:S(2)}, u32[]{:S(2)}) collective-permute-start(f32[96,1024]{1,0:T(8,128)S(1)} %get-tuple-element.60.surface), channel_id=1, source_target_pairs={{0,1},{1,0},{2,3},{3,2},{4,5},{5,4},{6,7},{7,6},{8,9},{9,8},{10,11... | collective-permute-start | bytes 1179656 | tf_op jit(solution)/shard_map/ppermute | solution.py:380
  47.2 1.6 %collective-permute-start.16 = (f32[200,128]{1,0:T(8,128)S(1)}, f32[200,128]{1,0:T(8,128)S(1)}, u32[]{:S(2)}, u32[]{:S(2)}) collective-permute-start(f32[200,128]{1,0:T(8,128)S(1)} %get-tuple-element.63), channel_id=1, source_target_pairs={{0,1},{1,0},{2,3},{3,2},{4,5},{5,4},{6,7},{7,6},{8,9},{9,8},{10,11... | collective-permute-start | bytes 307208 | tf_op jit(solution)/shard_map/ppermute | solution.py:380
  48.8 5.1 %collective-permute-start.17 = (f32[200,128]{1,0:T(8,128)S(1)}, f32[200,128]{1,0:T(8,128)S(1)}, u32[]{:S(2)}, u32[]{:S(2)}) collective-permute-start(f32[200,128]{1,0:T(8,128)S(1)} %shard_map.94.mine), channel_id=1, source_target_pairs={{0,2},{2,0},{1,3},{3,1},{4,6},{6,4},{5,7},{7,5},{8,10},{10,8},{9,1... | collective-permute-start | bytes 307208 | tf_op jit(solution)/shard_map/ppermute | solution.py:380
  54.0 6.0 %collective-permute-start.20 = (bf16[208,128]{1,0:T(8,128)(2,1)S(1)}, bf16[208,128]{1,0:T(8,128)(2,1)S(1)}, u32[]{:S(2)}, u32[]{:S(2)}) collective-permute-start(bf16[208,128]{1,0:T(8,128)(2,1)S(1)} %shard_map.95.rest_0_), channel_id=1, source_target_pairs={{0,12},{4,8},{8,4},{12,0},{1,13},{5,9},{9,5},{13,1},{2,14},{6,10},... | collective-permute-start | bytes 159752 | tf_op jit(solution)/shard_map/ppermute | solution.py:380
  56.4 5.1 %collective-permute-start.19 = (bf16[208,128]{1,0:T(8,128)(2,1)S(1)}, bf16[208,128]{1,0:T(8,128)(2,1)S(1)}, u32[]{:S(2)}, u32[]{:S(2)}) collective-permute-start(bf16[208,128]{1,0:T(8,128)(2,1)S(1)} %shard_map.95.rest_0_), channel_id=1, source_target_pairs={{0,8},{4,12},{8,0},{12,4},{1,9},{5,13},{9,1},{13,5},{2,10},{6,14},... | collective-permute-start | bytes 159752 | tf_op jit(solution)/shard_map/ppermute | solution.py:380
  56.4 5.1 %collective-permute-start.18 = (bf16[208,128]{1,0:T(8,128)(2,1)S(1)}, bf16[208,128]{1,0:T(8,128)(2,1)S(1)}, u32[]{:S(2)}, u32[]{:S(2)}) collective-permute-start(bf16[208,128]{1,0:T(8,128)(2,1)S(1)} %shard_map.95.rest_0_), channel_id=1, source_target_pairs={{0,4},{4,0},{8,12},{12,8},{1,5},{5,1},{9,13},{13,9},{2,6},{6,2},{1... | collective-permute-start | bytes 159752 | tf_op jit(solution)/shard_map/ppermute | solution.py:380

commit v8 on v7

--- a/solution.py
+++ b/solution.py
@@ -325,7 +325,8 @@
     beside[...] = theirs[rows:, :]
 
 
-def merge_kernel(mine, theirs, edge_in, out, edge_out):
+def merge_kernel(mine, theirs, piece_in, edge_in, out, piece_out, edge_out):
+    piece_out[...] = piece_in[...]
     edge_out[...] = edge_in[...]
     out[...] = (mine[...].astype(F32) + theirs[...].astype(F32)).astype(BF16)
 
@@ -426,8 +427,8 @@
     pieces = dict(zip(sends, pieces))
     if paired:
         passing = across(pieces.pop((1, 3)), "lon", 1)
-        outs = [shape(passing.shape, BF16), shape(edge_far.shape)]
-        pieces[1, 2], edge_far = call(merge_kernel, outs)(pieces[1, 2], passing, edge_far)
+        outs = [shape(passing.shape, BF16), shape(passing.shape, BF16), shape(edge_far.shape)]
+        pieces[1, 2], pieces[1, 1], edge_far = call(merge_kernel, outs)(pieces[1, 2], passing, pieces[1, 1], edge_far)
     pieces = {key: arrived(key, piece) for key, piece in pieces.items()}
     order = list(pieces)
 

time: 63.2 us -> 62.7 us (level)
  waiting for transfers between devices: 32.1 us -> 29.8 us
  starting transfers between devices: 21 us -> 22.8 us
    ppermute x19, waiting for transfers between devices: 32.1 us -> 29.8 us  [across(): lax.ppermute(value, axis, [(i, i ^ step) for i in range(lax.axis_size(axi...]
    ppermute x19, starting transfers between devices: 19.7 us -> 21.5 us  [across(): lax.ppermute(value, axis, [(i, i ^ step) for i in range(lax.axis_size(axi...]
  transfers between devices with their start and end apart: 21 -> 21, of which waited for: 13 -> 12; matrix products, arithmetic and copies ran while one was open for 0% -> 0% of each run, Pallas kernels for 1% -> 1%
where the time goes in v8:
time: 62.7 us; the launch traced here: 62.5 us
  waiting for transfers between devices  29.8 us (48%)
  starting transfers between devices  22.8 us (36%)
  Pallas kernels  9.21 us (15%)
  between operations  0.73 us (1%)
    ppermute x19, waiting for transfers between devices, across(): lax.ppermute(value, axis, [(i, i ^ step) for i in range(lax.axis_size(axi...  29.8 us
    ppermute x19, starting transfers between devices, across(): lax.ppermute(value, axis, [(i, i ^ step) for i in range(lax.axis_size(axi...  21.5 us
    pallas_call x11, Pallas kernels, run(): pl.pallas_call(kernel, out_shape=out_shape, in_specs=[pl.BlockSpec(memory...  9.21 us
    ppermute x2, starting transfers between devices, bands(): return lax.ppermute(edge, ('lat', 'ta'), there + [(b, a) for a, b in there])  1.31 us
  transfers between devices with their start and end apart: 21, of which 12 were waited for; matrix products, arithmetic and copies ran while one was open for 0% of the time, Pallas kernels for 1%

profile of v8, /device:TPU:0, one launch (start us, length us, event | category | flops | bytes accessed | tf_op | source)
XLA Modules:
  0.0 62.5 jit_solution(14591242122427505924)
XLA Ops:
  0.6 3.9 %shard_map.86 = (bf16[528,128]{1,0:T(8,128)(2,1)S(1)}, bf16[528,128]{1,0:T(8,128)(2,1)S(1)}, bf16[528,128]{1,0:T(8,128)(2,1)S(1)}, bf16[544,128]{1,0:T(8,128)(2,...) custom-call(s32[1,4,32]{2,1,0:T(4,128)} %list_hbm.1, ...), custom_call_target="tpu_custom_call" | custom-call | flops 1000000 | bytes 1000000 | tf_op jit(solution)/shard_map/pallas_call | solution.py:367
  4.5 3.1 %collective-permute-start.1 = (bf16[528,128]{1,0:T(8,128)(2,1)S(1)}, bf16[528,128]{1,0:T(8,128)(2,1)S(1)}, u32[]{:S(2)}, u32[]{:S(2)}) collective-permute-start(bf16[528,128]{1,0:T(8,128)(2,1)S(1)} %get-tuple-element.42), channel_id=1, source_target_pairs={{0,4},{4,0},{8,12},{12,8},{1,5},{5,1},{9,13},{13,9},{2,6},{6,2},{1... | collective-permute-start | bytes 405512 | tf_op jit(solution)/shard_map/ppermute | solution.py:381
  7.6 2.6 %collective-permute-start.3 = (bf16[528,128]{1,0:T(8,128)(2,1)S(1)}, bf16[528,128]{1,0:T(8,128)(2,1)S(1)}, u32[]{:S(2)}, u32[]{:S(2)}) collective-permute-start(bf16[528,128]{1,0:T(8,128)(2,1)S(1)} %get-tuple-element.46), channel_id=1, source_target_pairs={{0,8},{4,12},{8,0},{12,4},{1,9},{5,13},{9,1},{13,5},{2,10},{6,14},... | collective-permute-start | bytes 405512 | tf_op jit(solution)/shard_map/ppermute | solution.py:381
  10.2 0.9 %collective-permute-start.5 = (bf16[544,128]{1,0:T(8,128)(2,1)S(1)}, bf16[544,128]{1,0:T(8,128)(2,1)S(1)}, u32[]{:S(2)}, u32[]{:S(2)}) collective-permute-start(bf16[544,128]{1,0:T(8,128)(2,1)S(1)} %get-tuple-element.48), channel_id=1, source_target_pairs={{0,4},{4,0},{8,12},{12,8},{1,5},{5,1},{9,13},{13,9},{2,6},{6,2},{1... | collective-permute-start | bytes 417800 | tf_op jit(solution)/shard_map/ppermute | solution.py:381
  11.1 2.1 %collective-permute-done.1.theirs = bf16[528,128]{1,0:T(8,128)(2,1)S(1)} collective-permute-done((bf16[528,128]{1,0:T(8,128)(2,1)S(1)}, bf16[528,128]{1,0:T(8,128)(2,1)S(1)}, u32[]{:S(2)}, u32[]{:S(2)}) %collective-permute-start.1) | collective-permute-done | bytes 135200 | tf_op jit(solution)/shard_map/ppermute | solution.py:381
  13.3 1.0 %collective-permute-start.2 = (bf16[528,128]{1,0:T(8,128)(2,1)S(1)}, bf16[528,128]{1,0:T(8,128)(2,1)S(1)}, u32[]{:S(2)}, u32[]{:S(2)}) collective-permute-start(bf16[528,128]{1,0:T(8,128)(2,1)S(1)} %get-tuple-element.45), channel_id=1, source_target_pairs={{0,9},{1,8},{4,13},{5,12},{8,1},{9,0},{12,5},{13,4},{2,11},{3,10},... | collective-permute-start | bytes 405512 | tf_op jit(solution)/shard_map/ppermute | solution.py:381
  14.3 6.0 %collective-permute-done.3.rest_1_ = bf16[528,128]{1,0:T(8,128)(2,1)S(1)} collective-permute-done((bf16[528,128]{1,0:T(8,128)(2,1)S(1)}, bf16[528,128]{1,0:T(8,128)(2,1)S(1)}, u32[]{:S(2)}, u32[]{:S(2)}) %collective-permute-start.3) | collective-permute-done | bytes 135200 | tf_op jit(solution)/shard_map/ppermute | solution.py:381
  20.3 0.7 %collective-permute-start.7 = (f32[96,128]{1,0:T(8,128)S(1)}, f32[96,128]{1,0:T(8,128)S(1)}, u32[]{:S(2)}, u32[]{:S(2)}) collective-permute-start(f32[96,128]{1,0:T(8,128)S(1)} %get-tuple-element.51), channel_id=1, source_target_pairs={{1,2},{2,1},{5,6},{6,5},{9,10},{10,9},{13,14},{14,13},{17,18},{18,... | collective-permute-start | bytes 147464 | tf_op jit(solution)/shard_map/ppermute | solution.py:437
  20.9 0.2 shard_map.87
  21.2 6.2 %collective-permute-done.2.rest_0_ = bf16[528,128]{1,0:T(8,128)(2,1)S(1)} collective-permute-done((bf16[528,128]{1,0:T(8,128)(2,1)S(1)}, bf16[528,128]{1,0:T(8,128)(2,1)S(1)}, u32[]{:S(2)}, u32[]{:S(2)}) %collective-permute-start.2) | collective-permute-done | bytes 135200 | tf_op jit(solution)/shard_map/ppermute | solution.py:381
  27.4 1.6 %shard_map.89 = (f32[96,1024]{1,0:T(8,128)S(1)}, f32[120,128]{1,0:T(8,128)S(1)}, f32[200,128]{1,0:T(8,128)S(1)}, f32[96,128]{1,0:T(8,128)S(1)}, f32[128,1024]{1,0:T(8,128)S(1)}, /*index=5*/f32[16,128]{1,0:T(8,128)S(1)}) custom-call(f32[96,1024]{1,0:T(8,128)S(1)} %get-tuple-element.35.surface, f32[96,128]{1,0:T(8,128)S(1)} %get-tuple-element.36.edge_near, ...), custom_call_target="tpu_custom_call" | custom-call | flops 1000000 | bytes 1000000 | tf_op jit(solution)/shard_map/pallas_call | solution.py:367
  29.0 0.7 %collective-permute-start.8 = (f32[200,128]{1,0:T(8,128)S(1)}, f32[200,128]{1,0:T(8,128)S(1)}, u32[]{:S(2)}, u32[]{:S(2)}) collective-permute-start(f32[200,128]{1,0:T(8,128)S(1)} %get-tuple-element.54), channel_id=1, source_target_pairs={{0,1},{1,0},{2,3},{3,2},{4,5},{5,4},{6,7},{7,6},{8,9},{9,8},{10,11... | collective-permute-start | bytes 307208 | tf_op jit(solution)/shard_map/ppermute | solution.py:381
  29.8 0.9 %collective-permute-done.8.theirs = f32[200,128]{1,0:T(8,128)S(1)} collective-permute-done((f32[200,128]{1,0:T(8,128)S(1)}, f32[200,128]{1,0:T(8,128)S(1)}, u32[]{:S(2)}, u32[]{:S(2)}) %collective-permute-start.8) | collective-permute-done | bytes 102432 | tf_op jit(solution)/shard_map/ppermute | solution.py:381
  30.7 1.6 %collective-permute-start.9 = (f32[104,128]{1,0:T(8,128)S(1)}, f32[104,128]{1,0:T(8,128)S(1)}, u32[]{:S(2)}, u32[]{:S(2)}) collective-permute-start(f32[104,128]{1,0:T(8,128)S(1)} %get-tuple-element.55.mine), channel_id=1, source_target_pairs={{0,2},{2,0},{1,3},{3,1},{4,6},{6,4},{5,7},{7,5},{8,10},{10,8},{9,1... | collective-permute-start | bytes 159752 | tf_op jit(solution)/shard_map/ppermute | solution.py:381
  32.3 2.6 %collective-permute-done.9.theirs = f32[104,128]{1,0:T(8,128)S(1)} collective-permute-done((f32[104,128]{1,0:T(8,128)S(1)}, f32[104,128]{1,0:T(8,128)S(1)}, u32[]{:S(2)}, u32[]{:S(2)}) %collective-permute-start.9) | collective-permute-done | bytes 53280 | tf_op jit(solution)/shard_map/ppermute | solution.py:381
  35.0 2.6 %collective-permute-start.12 = (f32[120,128]{1,0:T(8,128)S(1)}, f32[120,128]{1,0:T(8,128)S(1)}, u32[]{:S(2)}, u32[]{:S(2)}) collective-permute-start(f32[120,128]{1,0:T(8,128)S(1)} %shard_map.91.rest_0_), channel_id=1, source_target_pairs={{0,12},{4,8},{8,4},{12,0},{1,13},{5,9},{9,5},{13,1},{2,14},{6,10},... | collective-permute-start | bytes 184328 | tf_op jit(solution)/shard_map/ppermute | solution.py:381
  37.6 1.8 %collective-permute-start.10 = (f32[120,128]{1,0:T(8,128)S(1)}, f32[120,128]{1,0:T(8,128)S(1)}, u32[]{:S(2)}, u32[]{:S(2)}) collective-permute-start(f32[120,128]{1,0:T(8,128)S(1)} %shard_map.91.rest_0_), channel_id=1, source_target_pairs={{0,4},{4,0},{8,12},{12,8},{1,5},{5,1},{9,13},{13,9},{2,6},{6,2},{1... | collective-permute-start | bytes 184328 | tf_op jit(solution)/shard_map/ppermute | solution.py:381
  39.4 0.7 %collective-permute-start.14 = (f32[96,128]{1,0:T(8,128)S(1)}, f32[96,128]{1,0:T(8,128)S(1)}, u32[]{:S(2)}, u32[]{:S(2)}) collective-permute-start(f32[96,128]{1,0:T(8,128)S(1)} %get-tuple-element.61), channel_id=1, source_target_pairs={{1,2},{2,1},{5,6},{6,5},{9,10},{10,9},{13,14},{14,13},{17,18},{18,... | collective-permute-start | bytes 147464 | tf_op jit(solution)/shard_map/ppermute | solution.py:437
  40.1 1.0 %collective-permute-done.12.rest_3_.cols_b = f32[120,128]{1,0:T(8,128)S(1)} collective-permute-done((f32[120,128]{1,0:T(8,128)S(1)}, f32[120,128]{1,0:T(8,128)S(1)}, u32[]{:S(2)}, u32[]{:S(2)}) %collective-permute-start.12) | collective-permute-done | bytes 61472 | tf_op jit(solution)/shard_map/ppermute | solution.py:381
  41.0 1.9 %collective-permute-done.11.rest_2_ = f32[120,128]{1,0:T(8,128)S(1)} collective-permute-done((f32[120,128]{1,0:T(8,128)S(1)}, f32[120,128]{1,0:T(8,128)S(1)}, u32[]{:S(2)}, u32[]{:S(2)}) %collective-permute-start.11) | collective-permute-done | bytes 61472 | tf_op jit(solution)/shard_map/ppermute | solution.py:381
  43.1 1.2 %collective-permute-done.13.time_other = f32[96,128]{1,0:T(8,128)S(1)} collective-permute-done((f32[96,128]{1,0:T(8,128)S(1)}, f32[96,128]{1,0:T(8,128)S(1)}, u32[]{:S(2)}, u32[]{:S(2)}) %collective-permute-start.13) | collective-permute-done | bytes 49184 | tf_op jit(solution)/shard_map/ppermute | solution.py:381
  44.3 1.7 %shard_map.93 = (f32[96,1024]{1,0:T(8,128)S(1)}, f32[96,128]{1,0:T(8,128)S(1)}, f32[200,128]{1,0:T(8,128)S(1)}, f32[200,128]{1,0:T(8,128)S(1)}) custom-call(f32[96,1024]{1,0:T(8,128)S(1)} %get-tuple-element.52.surface, f32[96,128]{1,0:T(8,128)S(1)} %get-tuple-element.56.time_own, f32[96,128]{1,0:T(8,128)S(1)} %collective-permute-done.13.time_other, ...), custom_call_target="tpu_custom_call" | custom-call | flops 1000000 | bytes 1000000 | tf_op jit(solution)/shard_map/pallas_call | solution.py:367
  46.1 0.4 collective-permute-start.15
  46.5 0.2 collective-permute-start.16
  46.7 1.4 %collective-permute-done.16.theirs = f32[200,128]{1,0:T(8,128)S(1)} collective-permute-done((f32[200,128]{1,0:T(8,128)S(1)}, f32[200,128]{1,0:T(8,128)S(1)}, u32[]{:S(2)}, u32[]{:S(2)}) %collective-permute-start.16) | collective-permute-done | bytes 102432 | tf_op jit(solution)/shard_map/ppermute | solution.py:381
  48.0 2.0 %collective-permute-start.17 = (f32[200,128]{1,0:T(8,128)S(1)}, f32[200,128]{1,0:T(8,128)S(1)}, u32[]{:S(2)}, u32[]{:S(2)}) collective-permute-start(f32[200,128]{1,0:T(8,128)S(1)} %shard_map.94.mine), channel_id=1, source_target_pairs={{0,2},{2,0},{1,3},{3,1},{4,6},{6,4},{5,7},{7,5},{8,10},{10,8},{9,1... | collective-permute-start | bytes 307208 | tf_op jit(solution)/shard_map/ppermute | solution.py:381
  50.1 3.2 %collective-permute-done.17.theirs = f32[200,128]{1,0:T(8,128)S(1)} collective-permute-done((f32[200,128]{1,0:T(8,128)S(1)}, f32[200,128]{1,0:T(8,128)S(1)}, u32[]{:S(2)}, u32[]{:S(2)}) %collective-permute-start.17) | collective-permute-done | bytes 102432 | tf_op jit(solution)/shard_map/ppermute | solution.py:381
  53.3 2.7 %collective-permute-start.20 = (bf16[208,128]{1,0:T(8,128)(2,1)S(1)}, bf16[208,128]{1,0:T(8,128)(2,1)S(1)}, u32[]{:S(2)}, u32[]{:S(2)}) collective-permute-start(bf16[208,128]{1,0:T(8,128)(2,1)S(1)} %shard_map.95.rest_0_), channel_id=1, source_target_pairs={{0,12},{4,8},{8,4},{12,0},{1,13},{5,9},{9,5},{13,1},{2,14},{6,10},... | collective-permute-start | bytes 159752 | tf_op jit(solution)/shard_map/ppermute | solution.py:381
  56.0 1.8 %collective-permute-start.18 = (bf16[208,128]{1,0:T(8,128)(2,1)S(1)}, bf16[208,128]{1,0:T(8,128)(2,1)S(1)}, u32[]{:S(2)}, u32[]{:S(2)}) collective-permute-start(bf16[208,128]{1,0:T(8,128)(2,1)S(1)} %shard_map.95.rest_0_), channel_id=1, source_target_pairs={{0,4},{4,0},{8,12},{12,8},{1,5},{5,1},{9,13},{13,9},{2,6},{6,2},{1... | collective-permute-start | bytes 159752 | tf_op jit(solution)/shard_map/ppermute | solution.py:381
  57.7 1.5 %collective-permute-done.20.rest_3_ = bf16[208,128]{1,0:T(8,128)(2,1)S(1)} collective-permute-done((bf16[208,128]{1,0:T(8,128)(2,1)S(1)}, bf16[208,128]{1,0:T(8,128)(2,1)S(1)}, u32[]{:S(2)}, u32[]{:S(2)}) %collective-permute-start.20) | collective-permute-done | bytes 53280 | tf_op jit(solution)/shard_map/ppermute | solution.py:381
  59.3 1.7 %collective-permute-done.19.rest_2_ = bf16[208,128]{1,0:T(8,128)(2,1)S(1)} collective-permute-done((bf16[208,128]{1,0:T(8,128)(2,1)S(1)}, bf16[208,128]{1,0:T(8,128)(2,1)S(1)}, u32[]{:S(2)}, u32[]{:S(2)}) %collective-permute-start.19) | collective-permute-done | bytes 53280 | tf_op jit(solution)/shard_map/ppermute | solution.py:381
  61.0 1.5 %shard_map.96 = (f32[1536,128]{1,0:T(8,128)}, f32[64,96]{1,0:T(8,128)}) custom-call(f32[96,1024]{1,0:T(8,128)S(1)} %get-tuple-element.62.surface, f32[96,1024]{1,0:T(8,128)S(1)} %collective-permute-done.15.other, f32[96,128]{1,0:T(8,128)S(1)} %get-tuple-element.63.time_t, bf16[208,128]{1,0:T(8,128)(2,1)S(1)} %shard_map.95.rest_0_, ...), custom_call_target="tpu_custom_call" | custom-call | flops 1000000 | bytes 1000000 | tf_op jit(solution)/shard_map/pallas_call | solution.py:367
  (23 shorter events, 0.3 us)
Async XLA Ops:
  4.5 8.7 %collective-permute-start.1 = (bf16[528,128]{1,0:T(8,128)(2,1)S(1)}, bf16[528,128]{1,0:T(8,128)(2,1)S(1)}, u32[]{:S(2)}, u32[]{:S(2)}) collective-permute-start(bf16[528,128]{1,0:T(8,128)(2,1)S(1)} %get-tuple-element.42), channel_id=1, source_target_pairs={{0,4},{4,0},{8,12},{12,8},{1,5},{5,1},{9,13},{13,9},{2,6},{6,2},{1... | collective-permute-start | bytes 405512 | tf_op jit(solution)/shard_map/ppermute | solution.py:381
  7.6 12.6 %collective-permute-start.3 = (bf16[528,128]{1,0:T(8,128)(2,1)S(1)}, bf16[528,128]{1,0:T(8,128)(2,1)S(1)}, u32[]{:S(2)}, u32[]{:S(2)}) collective-permute-start(bf16[528,128]{1,0:T(8,128)(2,1)S(1)} %get-tuple-element.46), channel_id=1, source_target_pairs={{0,8},{4,12},{8,0},{12,4},{1,9},{5,13},{9,1},{13,5},{2,10},{6,14},... | collective-permute-start | bytes 405512 | tf_op jit(solution)/shard_map/ppermute | solution.py:381
  10.2 10.0 %collective-permute-start = (bf16[720,128]{1,0:T(8,128)(2,1)S(1)}, bf16[720,128]{1,0:T(8,128)(2,1)S(1)}, u32[]{:S(2)}, u32[]{:S(2)}) collective-permute-start(bf16[720,128]{1,0:T(8,128)(2,1)S(1)} %get-tuple-element.37), channel_id=1, source_target_pairs={{0,1},{1,0},{4,5},{5,4},{8,9},{9,8},{12,13},{13,12},{2,3},{3,2},{6... | collective-permute-start | bytes 552968 | tf_op jit(solution)/shard_map/ppermute | solution.py:381
  10.2 10.9 %collective-permute-start.4 = (bf16[544,128]{1,0:T(8,128)(2,1)S(1)}, bf16[544,128]{1,0:T(8,128)(2,1)S(1)}, u32[]{:S(2)}, u32[]{:S(2)}) collective-permute-start(bf16[544,128]{1,0:T(8,128)(2,1)S(1)} %get-tuple-element.47), channel_id=1, source_target_pairs={{0,12},{4,8},{8,4},{12,0},{1,13},{5,9},{9,5},{13,1},{2,14},{6,10},... | collective-permute-start | bytes 417800 | tf_op jit(solution)/shard_map/ppermute | solution.py:381
  10.2 10.9 %collective-permute-start.5 = (bf16[544,128]{1,0:T(8,128)(2,1)S(1)}, bf16[544,128]{1,0:T(8,128)(2,1)S(1)}, u32[]{:S(2)}, u32[]{:S(2)}) collective-permute-start(bf16[544,128]{1,0:T(8,128)(2,1)S(1)} %get-tuple-element.48), channel_id=1, source_target_pairs={{0,4},{4,0},{8,12},{12,8},{1,5},{5,1},{9,13},{13,9},{2,6},{6,2},{1... | collective-permute-start | bytes 417800 | tf_op jit(solution)/shard_map/ppermute | solution.py:381
  13.2 7.7 %copy-start = (f32[64,96]{1,0:T(8,128)S(1)}, f32[64,96]{1,0:T(8,128)}, u32[]{:S(2)}) copy-start(f32[64,96]{1,0:T(8,128)} %time_own.1) | copy-start | bytes 73732
  13.3 14.1 %collective-permute-start.2 = (bf16[528,128]{1,0:T(8,128)(2,1)S(1)}, bf16[528,128]{1,0:T(8,128)(2,1)S(1)}, u32[]{:S(2)}, u32[]{:S(2)}) collective-permute-start(bf16[528,128]{1,0:T(8,128)(2,1)S(1)} %get-tuple-element.45), channel_id=1, source_target_pairs={{0,9},{1,8},{4,13},{5,12},{8,1},{9,0},{12,5},{13,4},{2,11},{3,10},... | collective-permute-start | bytes 405512 | tf_op jit(solution)/shard_map/ppermute | solution.py:381
  20.3 7.2 %collective-permute-start.6 = (bf16[528,128]{1,0:T(8,128)(2,1)S(1)}, bf16[528,128]{1,0:T(8,128)(2,1)S(1)}, u32[]{:S(2)}, u32[]{:S(2)}) collective-permute-start(bf16[528,128]{1,0:T(8,128)(2,1)S(1)} %get-tuple-element.49), channel_id=1, source_target_pairs={{0,5},{1,4},{4,1},{5,0},{8,13},{9,12},{12,9},{13,8},{2,7},{3,6},{6... | collective-permute-start | bytes 405512 | tf_op jit(solution)/shard_map/ppermute | solution.py:381
  20.3 0.9 %collective-permute-start.7 = (f32[96,128]{1,0:T(8,128)S(1)}, f32[96,128]{1,0:T(8,128)S(1)}, u32[]{:S(2)}, u32[]{:S(2)}) collective-permute-start(f32[96,128]{1,0:T(8,128)S(1)} %get-tuple-element.51), channel_id=1, source_target_pairs={{1,2},{2,1},{5,6},{6,5},{9,10},{10,9},{13,14},{14,13},{17,18},{18,... | collective-permute-start | bytes 147464 | tf_op jit(solution)/shard_map/ppermute | solution.py:437
  29.0 1.7 %collective-permute-start.8 = (f32[200,128]{1,0:T(8,128)S(1)}, f32[200,128]{1,0:T(8,128)S(1)}, u32[]{:S(2)}, u32[]{:S(2)}) collective-permute-start(f32[200,128]{1,0:T(8,128)S(1)} %get-tuple-element.54), channel_id=1, source_target_pairs={{0,1},{1,0},{2,3},{3,2},{4,5},{5,4},{6,7},{7,6},{8,9},{9,8},{10,11... | collective-permute-start | bytes 307208 | tf_op jit(solution)/shard_map/ppermute | solution.py:381
  30.7 4.2 %collective-permute-start.9 = (f32[104,128]{1,0:T(8,128)S(1)}, f32[104,128]{1,0:T(8,128)S(1)}, u32[]{:S(2)}, u32[]{:S(2)}) collective-permute-start(f32[104,128]{1,0:T(8,128)S(1)} %get-tuple-element.55.mine), channel_id=1, source_target_pairs={{0,2},{2,0},{1,3},{3,1},{4,6},{6,4},{5,7},{7,5},{8,10},{10,8},{9,1... | collective-permute-start | bytes 159752 | tf_op jit(solution)/shard_map/ppermute | solution.py:381
  35.0 6.1 %collective-permute-start.12 = (f32[120,128]{1,0:T(8,128)S(1)}, f32[120,128]{1,0:T(8,128)S(1)}, u32[]{:S(2)}, u32[]{:S(2)}) collective-permute-start(f32[120,128]{1,0:T(8,128)S(1)} %shard_map.91.rest_0_), channel_id=1, source_target_pairs={{0,12},{4,8},{8,4},{12,0},{1,13},{5,9},{9,5},{13,1},{2,14},{6,10},... | collective-permute-start | bytes 184328 | tf_op jit(solution)/shard_map/ppermute | solution.py:381
  37.6 5.4 %collective-permute-start.11 = (f32[120,128]{1,0:T(8,128)S(1)}, f32[120,128]{1,0:T(8,128)S(1)}, u32[]{:S(2)}, u32[]{:S(2)}) collective-permute-start(f32[120,128]{1,0:T(8,128)S(1)} %shard_map.91.rest_0_), channel_id=1, source_target_pairs={{0,8},{4,12},{8,0},{12,4},{1,9},{5,13},{9,1},{13,5},{2,10},{6,14},... | collective-permute-start | bytes 184328 | tf_op jit(solution)/shard_map/ppermute | solution.py:381
  37.6 5.4 %collective-permute-start.10 = (f32[120,128]{1,0:T(8,128)S(1)}, f32[120,128]{1,0:T(8,128)S(1)}, u32[]{:S(2)}, u32[]{:S(2)}) collective-permute-start(f32[120,128]{1,0:T(8,128)S(1)} %shard_map.91.rest_0_), channel_id=1, source_target_pairs={{0,4},{4,0},{8,12},{12,8},{1,5},{5,1},{9,13},{13,9},{2,6},{6,2},{1... | collective-permute-start | bytes 184328 | tf_op jit(solution)/shard_map/ppermute | solution.py:381
  39.4 3.7 %collective-permute-start.14 = (f32[96,128]{1,0:T(8,128)S(1)}, f32[96,128]{1,0:T(8,128)S(1)}, u32[]{:S(2)}, u32[]{:S(2)}) collective-permute-start(f32[96,128]{1,0:T(8,128)S(1)} %get-tuple-element.61), channel_id=1, source_target_pairs={{1,2},{2,1},{5,6},{6,5},{9,10},{10,9},{13,14},{14,13},{17,18},{18,... | collective-permute-start | bytes 147464 | tf_op jit(solution)/shard_map/ppermute | solution.py:437
  43.0 1.3 %collective-permute-start.13 = (f32[96,128]{1,0:T(8,128)S(1)}, f32[96,128]{1,0:T(8,128)S(1)}, u32[]{:S(2)}, u32[]{:S(2)}) collective-permute-start(f32[96,128]{1,0:T(8,128)S(1)} %get-tuple-element.56.time_own), channel_id=1, source_target_pairs={{0,1},{1,0},{2,3},{3,2},{4,5},{5,4},{6,7},{7,6},{8,9},{9,8},{10,11... | collective-permute-start | bytes 147464 | tf_op jit(solution)/shard_map/ppermute | solution.py:381
  46.1 14.9 %collective-permute-start.15 = (f32[96,1024]{1,0:T(8,128)S(1)}, f32[96,1024]{1,0:T(8,128)S(1)}, u32[]{:S(2)}, u32[]{:S(2)}) collective-permute-start(f32[96,1024]{1,0:T(8,128)S(1)} %get-tuple-element.62.surface), channel_id=1, source_target_pairs={{0,1},{1,0},{2,3},{3,2},{4,5},{5,4},{6,7},{7,6},{8,9},{9,8},{10,11... | collective-permute-start | bytes 1179656 | tf_op jit(solution)/shard_map/ppermute | solution.py:381
  46.5 1.5 %collective-permute-start.16 = (f32[200,128]{1,0:T(8,128)S(1)}, f32[200,128]{1,0:T(8,128)S(1)}, u32[]{:S(2)}, u32[]{:S(2)}) collective-permute-start(f32[200,128]{1,0:T(8,128)S(1)} %get-tuple-element.65), channel_id=1, source_target_pairs={{0,1},{1,0},{2,3},{3,2},{4,5},{5,4},{6,7},{7,6},{8,9},{9,8},{10,11... | collective-permute-start | bytes 307208 | tf_op jit(solution)/shard_map/ppermute | solution.py:381
  48.0 5.2 %collective-permute-start.17 = (f32[200,128]{1,0:T(8,128)S(1)}, f32[200,128]{1,0:T(8,128)S(1)}, u32[]{:S(2)}, u32[]{:S(2)}) collective-permute-start(f32[200,128]{1,0:T(8,128)S(1)} %shard_map.94.mine), channel_id=1, source_target_pairs={{0,2},{2,0},{1,3},{3,1},{4,6},{6,4},{5,7},{7,5},{8,10},{10,8},{9,1... | collective-permute-start | bytes 307208 | tf_op jit(solution)/shard_map/ppermute | solution.py:381
  53.3 6.0 %collective-permute-start.20 = (bf16[208,128]{1,0:T(8,128)(2,1)S(1)}, bf16[208,128]{1,0:T(8,128)(2,1)S(1)}, u32[]{:S(2)}, u32[]{:S(2)}) collective-permute-start(bf16[208,128]{1,0:T(8,128)(2,1)S(1)} %shard_map.95.rest_0_), channel_id=1, source_target_pairs={{0,12},{4,8},{8,4},{12,0},{1,13},{5,9},{9,5},{13,1},{2,14},{6,10},... | collective-permute-start | bytes 159752 | tf_op jit(solution)/shard_map/ppermute | solution.py:381
  56.0 5.0 %collective-permute-start.19 = (bf16[208,128]{1,0:T(8,128)(2,1)S(1)}, bf16[208,128]{1,0:T(8,128)(2,1)S(1)}, u32[]{:S(2)}, u32[]{:S(2)}) collective-permute-start(bf16[208,128]{1,0:T(8,128)(2,1)S(1)} %shard_map.95.rest_0_), channel_id=1, source_target_pairs={{0,8},{4,12},{8,0},{12,4},{1,9},{5,13},{9,1},{13,5},{2,10},{6,14},... | collective-permute-start | bytes 159752 | tf_op jit(solution)/shard_map/ppermute | solution.py:381
  56.0 5.0 %collective-permute-start.18 = (bf16[208,128]{1,0:T(8,128)(2,1)S(1)}, bf16[208,128]{1,0:T(8,128)(2,1)S(1)}, u32[]{:S(2)}, u32[]{:S(2)}) collective-permute-start(bf16[208,128]{1,0:T(8,128)(2,1)S(1)} %shard_map.95.rest_0_), channel_id=1, source_target_pairs={{0,4},{4,0},{8,12},{12,8},{1,5},{5,1},{9,13},{13,9},{2,6},{6,2},{1... | collective-permute-start | bytes 159752 | tf_op jit(solution)/shard_map/ppermute | solution.py:381

commit v9 on v8

--- a/solution.py
+++ b/solution.py
@@ -197,7 +197,7 @@
     return grad_time[:, :LANES] + grad_time[:, LANES:], grad_diag, norm
 
 
-def post_own(half, sums, fresh, message, outgoing, edge_far, flip):
+def post_own(half, sums, fresh, message, crossing, outgoing, edge_far, flip):
     grad_time, grad_diag, norm = sums
     core = lax.axis_index("ta")
     rank = norm.shape[0]
@@ -206,23 +206,32 @@
     last = columns_as_rows([norm] * NORM + border(fresh[...], half), flip)
     message[:rank, :] = jnp.where(own, grad_time, pltpu.roll(grad_diag, days, 1))
     message[rank:, :] = last[: NORM + COLS, :]
-    outgoing[:rank, :] = jnp.where(own, pltpu.roll(grad_time, days, 1), grad_diag)
-    outgoing[rank:rank + NORM, :] = last[:NORM, :]
+    for out in (crossing, outgoing):
+        out[:rank, :] = jnp.where(own, pltpu.roll(grad_time, days, 1), grad_diag)
+        out[rank:rank + NORM, :] = last[:NORM, :]
     first_row, last_row = fresh[:, :LANES], fresh[:, (half - 1) * LANES:]
     outgoing[rank + NORM:, :] = pick(core == 0, last_row, first_row)
     edge_far[...] = pick(core == 0, first_row, last_row)
+
+
+def narrow(value, rank):
+    high = value[2 * rank:, :].astype(BF16)
+    low = (value[2 * rank:, :] - high.astype(F32)).astype(BF16)
+    return value[: 2 * rank, :].astype(BF16), jnp.concatenate([high.astype(F32), low.astype(F32)], axis=0).astype(BF16)
+
+
+def widened(value, rank):
+    value = value.astype(F32)
+    return jnp.concatenate([value[: 2 * rank, :], value[2 * rank:2 * rank + NORM, :] + value[2 * rank + NORM:, :]], axis=0)
 
 
 def post_all(sums, message, outgoing, flip):
     grad_time, grad_diag, norm = sums
     rank = norm.shape[0]
     last = columns_as_rows([norm], flip)[:NORM, :]
-    message[:rank, :] = grad_time
-    message[rank:2 * rank, :] = grad_diag
-    message[2 * rank:, :] = last
-    outgoing[:rank, :] = pltpu.roll(grad_time, LANES // 2, 1)
-    outgoing[rank:2 * rank, :] = pltpu.roll(grad_diag, LANES // 2, 1)
-    outgoing[2 * rank:, :] = last
+    for out, shift in ((message, 0), (outgoing, LANES // 2)):
+        parts = [pltpu.roll(part, shift, 1) if shift else part for part in (grad_time, grad_diag)]
+        out[: 2 * rank, :], out[2 * rank:, :] = narrow(jnp.concatenate([*parts, last], axis=0), rank)
 
 
 def first_kernel(half, days, order, paired, swap, surface, edge_near, predicted, packed, time_t, *rest):
@@ -233,7 +242,7 @@
         cols = [pieces[0, step][at:, :].astype(F32) for step in (1, 3)]
     else:
         cols, rest = [ref[...] for ref in rest[:2]], rest[2:]
-    fresh, message, outgoing, edge_far, summed, seen, flip, base = rest
+    fresh, message, crossing, outgoing, edge_far, summed, seen, flip, base = rest
     smooth(half, swap(), surface[...], edge_near[...], edge_far_in[...], *cols, None, base, flip)
     sides = [[pieces[key] for key in sorted(pieces) if key[0] == side] for side in (0, 1)]
 
@@ -249,7 +258,7 @@
     near, far = (add_up(parts, slice(half * days, half * days + TAIL)) for parts in sides)
     seen[...] = near + pltpu.roll(far, days, 1)
     sums = gradients(half, base, predicted, packed, time_t[...], seen[...], summed, fresh)
-    post_own(half, sums, fresh, message, outgoing, edge_far, flip)
+    post_own(half, sums, fresh, message, crossing, outgoing, edge_far, flip)
 
 
 def total_of(parts):
@@ -305,11 +314,10 @@
     rank = surface.shape[0]
     height = space_out.shape[0] // rank
     total = total_of(parts)
+    if parts[0].dtype == BF16:
+        total = widened(total, rank)
     time_new = time_t[...] - total[:rank, :] / (total[rank:2 * rank, :] + RIDGE)
-    norm = total[2 * rank:2 * rank + NORM, :]
-    if parts[0].dtype == BF16:
-        norm = norm + total[2 * rank + NORM:, :]
-    scale = rescaling(counts, norm, time_new, flip)
+    scale = rescaling(counts, total[2 * rank:, :], time_new, flip)
     flip[...] = jnp.zeros(flip.shape, F32)
     flip[:rank, :] = time_new / scale
     time_out[...] = flip[...].T[: time_out.shape[0], :rank]
@@ -319,12 +327,6 @@
         space_out[pl.ds((1 - core) * half + row, rank, stride=height), :] = other[:, at:at + LANES] * scale
 
 
-def core_kernel(mine, theirs, total, beside):
-    rows = total.shape[0]
-    total[...] = mine[:rows, :] + theirs[:rows, :]
-    beside[...] = theirs[rows:, :]
-
-
 def merge_kernel(mine, theirs, piece_in, edge_in, out, piece_out, edge_out):
     piece_out[...] = piece_in[...]
     edge_out[...] = edge_in[...]
@@ -332,22 +334,23 @@
 
 
 def add_kernel(mine, theirs, total):
-    rows = total.shape[0]
-    total[...] = mine[:rows, :] + theirs[:rows, :]
-
-
-def band_kernel(mine, theirs, message, total):
-    rows = mine.shape[0]
-    total[:rows, :] = mine[...] + theirs[...]
-    total[rows:, :] = message[rows:, :]
-
-
-def narrow_kernel(rank, mine, theirs, total):
-    value = mine[...] + theirs[...]
-    total[: 2 * rank, :] = value[: 2 * rank, :].astype(BF16)
-    norm = value[2 * rank:, :]
-    high = norm.astype(BF16).astype(F32)
-    total[2 * rank:, :] = jnp.concatenate([high, norm - high], axis=0).astype(BF16)
+    total[...] = mine[...] + theirs[...]
+
+
+def own_sum_kernel(mine, core, band, both, total, beside):
+    rows = both.shape[0]
+    total[:rows, :] = (mine[:rows, :] + core[:rows, :]) + (band[:rows, :] + both[...])
+    total[rows:, :] = mine[rows:, :]
+    beside[...] = core[rows:, :]
+
+
+def all_sum_kernel(rank, mine, core, band, both, total):
+    one, two, three, four = (widened(part[...], rank) for part in (mine, core, band, both))
+    value = (one + two) + (three + four)
+    if total.dtype == BF16:
+        total[: 2 * rank, :], total[2 * rank:, :] = narrow(value, rank)
+    else:
+        total[...] = value
 
 
 def shape(dims, dtype=F32):
@@ -452,51 +455,46 @@
     )(surface, factor_time, pieces[1, 0])
 
     fresh, edge = shape((rank, wide)), shape((rank, LANES))
-    surface, message, outgoing, edge_far, summed, seen = call(
+    surface, message, crossing, outgoing, edge_far, summed, seen = call(
         functools.partial(first_kernel, half, days, order, paired, swap),
-        [fresh, shape((own_rows + COLS, LANES)), shape((own_rows + rank, LANES)), edge, shape((2 * days, wide)), shape((TAIL, LANES))],
+        [fresh, shape((own_rows + COLS, LANES)), shape((own_rows, LANES)), shape((own_rows + rank, LANES)), edge, shape((2 * days, wide)), shape((TAIL, LANES))],
         [flip, pltpu.VMEM((rank, wide), F32)],
     )(surface, edge_near, predicted, packed, time_t, *[pieces[key] for key in order], bands(edge_far), *(() if paired else columns(cols)))
 
+    narrowed = shape((sum_rows + NORM, LANES), BF16)
+
     def add(mine, theirs):
-        return call(add_kernel, shape(theirs.shape))(mine, theirs)
-
-    def over_bands(total, last):
-        step = 1
-        while 2 * step < n_lat:
-            total = add(total, across(total, "lat", step))
+        return call(add_kernel, shape(mine.shape))(mine, theirs)
+
+    def doubled(total, axis, step):
+        while step < lax.axis_size(axis):
+            total = add(total, across(total, axis, step))
             step *= 2
-        return last(total, across(total, "lat", step))
+        return total
 
     def over_lon(total):
         if paired:
             return [total] + [across(total, "lon", step) for step in (1, 2, 3)]
-        step = 1
-        while step < n_lon:
-            total = add(total, across(total, "lon", step))
-            step *= 2
-        return [total]
-
-    total, edge_near = call(core_kernel, [shape((own_rows, LANES)), edge])(message, across(outgoing, "ta", 1))
-    if paired:
-        last = call(band_kernel, shape(message.shape))
-        parts = over_lon(over_bands(total, lambda mine, theirs: last(mine, theirs, message)))
-        cols = parts[1], parts[3]
-    else:
-        parts = over_lon(over_bands(total, add))
-        cols = columns(message[own_rows:])
+        return [doubled(total, "lon", 1)]
+
+    def around(mine, core, both):
+        return mine, across(core, "ta", 1), across(mine, "lat", 1), across(both, ("lat", "ta"), 3)
+
+    total, edge_near = call(own_sum_kernel, [shape(message.shape), edge])(*around(message, outgoing, crossing))
+    parts = over_lon(doubled(total, "lat", 2))
+    cols = (parts[1], parts[3]) if paired else columns(message[own_rows:])
     time_own, norm = call(functools.partial(own_kernel, len(parts)), [edge, shape((NORM, LANES))])(time_t, *parts)
 
     surface, time_t, message, outgoing = call(
         functools.partial(second_kernel, half, counts, swap),
-        [fresh, edge, shape((sum_rows, LANES)), shape((sum_rows, LANES))],
+        [fresh, edge, narrowed, narrowed],
         [flip, pltpu.VMEM((rank, wide), F32), pltpu.VMEM((rank, wide), F32), pltpu.VMEM((2 * days, wide), F32), pltpu.VMEM((rank, wide), BF16)],
     )(surface, time_own, across(time_own, "ta", 1), norm, summed, seen, edge_near, bands(edge_far), *cols)
 
-    total = add(message, across(outgoing, "ta", 1))
     other = across(surface, "ta", 1)
-    narrow = call(functools.partial(narrow_kernel, rank), shape((sum_rows + NORM, LANES), BF16))
-    parts = over_lon(over_bands(total, narrow if paired else add))
+    total = narrowed if paired and n_lat == 2 else shape((sum_rows, LANES))
+    total = call(functools.partial(all_sum_kernel, rank), total)(*around(message, outgoing, outgoing))
+    parts = over_lon(doubled(total, "lat", 2))
     space, time = call(
         functools.partial(last_kernel, half, counts, len(parts)),
         [shape((rank * height, cells)), shape(factor_time.shape)],

time: 62.7 us -> 62 us (0.989)
    ppermute x19 -> x21, waiting for transfers between devices: 29.8 us -> 29.4 us  [across(): lax.ppermute(value, axis, [(i, i ^ step) for i in range(lax.axis_size(axi...]
    ppermute x19 -> x21, starting transfers between devices: 21.5 us -> 21.2 us  [across(): lax.ppermute(value, axis, [(i, i ^ step) for i in range(lax.axis_size(axi...]
    pallas_call x11 -> x9, Pallas kernels: 9.21 us -> 9.21 us  [run(): pl.pallas_call(kernel, out_shape=out_shape, in_specs=[pl.BlockSpec(memory...]
  transfers between devices with their start and end apart: 21 -> 23, of which waited for: 12 -> 11; matrix products, arithmetic and copies ran while one was open for 0% -> 0% of each run, Pallas kernels for 1% -> 1%
where the time goes in v9:
time: 62 us; the launch traced here: 61.8 us
  waiting for transfers between devices  29.4 us (47%)
  starting transfers between devices  22.5 us (36%)
  Pallas kernels  9.21 us (15%)
  between operations  0.74 us (1%)
    ppermute x21, waiting for transfers between devices, across(): lax.ppermute(value, axis, [(i, i ^ step) for i in range(lax.axis_size(axi...  29.4 us
    ppermute x21, starting transfers between devices, across(): lax.ppermute(value, axis, [(i, i ^ step) for i in range(lax.axis_size(axi...  21.2 us
    pallas_call x9, Pallas kernels, run(): pl.pallas_call(kernel, out_shape=out_shape, in_specs=[pl.BlockSpec(memory...  9.21 us
    ppermute x2, starting transfers between devices, bands(): return lax.ppermute(edge, ('lat', 'ta'), there + [(b, a) for a, b in there])  1.31 us
  transfers between devices with their start and end apart: 23, of which 11 were waited for; matrix products, arithmetic and copies ran while one was open for 0% of the time, Pallas kernels for 1%

profile of v9, /device:TPU:0, one launch (start us, length us, event | category | flops | bytes accessed | tf_op | source)
XLA Modules:
  0.0 61.8 jit_solution(2923092988928993380)
XLA Ops:
  0.6 3.9 %shard_map.86 = (bf16[528,128]{1,0:T(8,128)(2,1)S(1)}, bf16[528,128]{1,0:T(8,128)(2,1)S(1)}, bf16[528,128]{1,0:T(8,128)(2,1)S(1)}, bf16[544,128]{1,0:T(8,128)(2,...) custom-call(s32[1,4,32]{2,1,0:T(4,128)} %list_hbm.1, ...), custom_call_target="tpu_custom_call" | custom-call | flops 1000000 | bytes 1000000 | tf_op jit(solution)/shard_map/pallas_call | solution.py:370
  4.5 3.1 %collective-permute-start.1 = (bf16[528,128]{1,0:T(8,128)(2,1)S(1)}, bf16[528,128]{1,0:T(8,128)(2,1)S(1)}, u32[]{:S(2)}, u32[]{:S(2)}) collective-permute-start(bf16[528,128]{1,0:T(8,128)(2,1)S(1)} %get-tuple-element.43), channel_id=1, source_target_pairs={{0,4},{4,0},{8,12},{12,8},{1,5},{5,1},{9,13},{13,9},{2,6},{6,2},{1... | collective-permute-start | bytes 405512 | tf_op jit(solution)/shard_map/ppermute | solution.py:384
  7.6 2.6 %collective-permute-start.3 = (bf16[528,128]{1,0:T(8,128)(2,1)S(1)}, bf16[528,128]{1,0:T(8,128)(2,1)S(1)}, u32[]{:S(2)}, u32[]{:S(2)}) collective-permute-start(bf16[528,128]{1,0:T(8,128)(2,1)S(1)} %get-tuple-element.47), channel_id=1, source_target_pairs={{0,8},{4,12},{8,0},{12,4},{1,9},{5,13},{9,1},{13,5},{2,10},{6,14},... | collective-permute-start | bytes 405512 | tf_op jit(solution)/shard_map/ppermute | solution.py:384
  10.2 0.9 %collective-permute-start.5 = (bf16[544,128]{1,0:T(8,128)(2,1)S(1)}, bf16[544,128]{1,0:T(8,128)(2,1)S(1)}, u32[]{:S(2)}, u32[]{:S(2)}) collective-permute-start(bf16[544,128]{1,0:T(8,128)(2,1)S(1)} %get-tuple-element.49), channel_id=1, source_target_pairs={{0,4},{4,0},{8,12},{12,8},{1,5},{5,1},{9,13},{13,9},{2,6},{6,2},{1... | collective-permute-start | bytes 417800 | tf_op jit(solution)/shard_map/ppermute | solution.py:384
  11.1 2.1 %collective-permute-done.1.theirs = bf16[528,128]{1,0:T(8,128)(2,1)S(1)} collective-permute-done((bf16[528,128]{1,0:T(8,128)(2,1)S(1)}, bf16[528,128]{1,0:T(8,128)(2,1)S(1)}, u32[]{:S(2)}, u32[]{:S(2)}) %collective-permute-start.1) | collective-permute-done | bytes 135200 | tf_op jit(solution)/shard_map/ppermute | solution.py:384
  13.3 1.0 %collective-permute-start.2 = (bf16[528,128]{1,0:T(8,128)(2,1)S(1)}, bf16[528,128]{1,0:T(8,128)(2,1)S(1)}, u32[]{:S(2)}, u32[]{:S(2)}) collective-permute-start(bf16[528,128]{1,0:T(8,128)(2,1)S(1)} %get-tuple-element.46), channel_id=1, source_target_pairs={{0,9},{1,8},{4,13},{5,12},{8,1},{9,0},{12,5},{13,4},{2,11},{3,10},... | collective-permute-start | bytes 405512 | tf_op jit(solution)/shard_map/ppermute | solution.py:384
  14.3 6.0 %collective-permute-done.3.rest_1_ = bf16[528,128]{1,0:T(8,128)(2,1)S(1)} collective-permute-done((bf16[528,128]{1,0:T(8,128)(2,1)S(1)}, bf16[528,128]{1,0:T(8,128)(2,1)S(1)}, u32[]{:S(2)}, u32[]{:S(2)}) %collective-permute-start.3) | collective-permute-done | bytes 135200 | tf_op jit(solution)/shard_map/ppermute | solution.py:384
  20.3 0.7 %collective-permute-start.7 = (f32[96,128]{1,0:T(8,128)S(1)}, f32[96,128]{1,0:T(8,128)S(1)}, u32[]{:S(2)}, u32[]{:S(2)}) collective-permute-start(f32[96,128]{1,0:T(8,128)S(1)} %get-tuple-element.52), channel_id=1, source_target_pairs={{1,2},{2,1},{5,6},{6,5},{9,10},{10,9},{13,14},{14,13},{17,18},{18,... | collective-permute-start | bytes 147464 | tf_op jit(solution)/shard_map/ppermute | solution.py:440
  21.0 0.2 shard_map.87
  21.2 6.2 %collective-permute-done.2.rest_0_ = bf16[528,128]{1,0:T(8,128)(2,1)S(1)} collective-permute-done((bf16[528,128]{1,0:T(8,128)(2,1)S(1)}, bf16[528,128]{1,0:T(8,128)(2,1)S(1)}, u32[]{:S(2)}, u32[]{:S(2)}) %collective-permute-start.2) | collective-permute-done | bytes 135200 | tf_op jit(solution)/shard_map/ppermute | solution.py:384
  27.4 1.6 %shard_map.89 = (f32[96,1024]{1,0:T(8,128)S(1)}, f32[120,128]{1,0:T(8,128)S(1)}, f32[104,128]{1,0:T(8,128)S(1)}, f32[200,128]{1,0:T(8,128)S(1)}, f32[96,128]{1,0...) custom-call(f32[96,1024]{1,0:T(8,128)S(1)} %get-tuple-element.36.surface, ...), custom_call_target="tpu_custom_call" | custom-call | flops 1000000 | bytes 1000000 | tf_op jit(solution)/shard_map/pallas_call | solution.py:370
  29.0 0.7 %collective-permute-start.8 = (f32[200,128]{1,0:T(8,128)S(1)}, f32[200,128]{1,0:T(8,128)S(1)}, u32[]{:S(2)}, u32[]{:S(2)}) collective-permute-start(f32[200,128]{1,0:T(8,128)S(1)} %get-tuple-element.55), channel_id=1, source_target_pairs={{0,1},{1,0},{2,3},{3,2},{4,5},{5,4},{6,7},{7,6},{8,9},{9,8},{10,11... | collective-permute-start | bytes 307208 | tf_op jit(solution)/shard_map/ppermute | solution.py:384
  29.8 1.5 %collective-permute-start.9 = (f32[120,128]{1,0:T(8,128)S(1)}, f32[120,128]{1,0:T(8,128)S(1)}, u32[]{:S(2)}, u32[]{:S(2)}) collective-permute-start(f32[120,128]{1,0:T(8,128)S(1)} %get-tuple-element.54.mine), channel_id=1, source_target_pairs={{0,2},{2,0},{1,3},{3,1},{4,6},{6,4},{5,7},{7,5},{8,10},{10,8},{9,1... | collective-permute-start | bytes 184328 | tf_op jit(solution)/shard_map/ppermute | solution.py:384
  31.3 4.1 %collective-permute-done.10.both = f32[104,128]{1,0:T(8,128)S(1)} collective-permute-done((f32[104,128]{1,0:T(8,128)S(1)}, f32[104,128]{1,0:T(8,128)S(1)}, u32[]{:S(2)}, u32[]{:S(2)}) %collective-permute-start.10) | collective-permute-done | bytes 53280 | tf_op jit(solution)/shard_map/ppermute | solution.py:384
  35.4 2.6 %collective-permute-start.13 = (f32[120,128]{1,0:T(8,128)S(1)}, f32[120,128]{1,0:T(8,128)S(1)}, u32[]{:S(2)}, u32[]{:S(2)}) collective-permute-start(f32[120,128]{1,0:T(8,128)S(1)} %get-tuple-element.57.rest_0_), channel_id=1, source_target_pairs={{0,12},{4,8},{8,4},{12,0},{1,13},{5,9},{9,5},{13,1},{2,14},{6,10},... | collective-permute-start | bytes 184328 | tf_op jit(solution)/shard_map/ppermute | solution.py:384
  38.0 1.8 %collective-permute-start.11 = (f32[120,128]{1,0:T(8,128)S(1)}, f32[120,128]{1,0:T(8,128)S(1)}, u32[]{:S(2)}, u32[]{:S(2)}) collective-permute-start(f32[120,128]{1,0:T(8,128)S(1)} %get-tuple-element.57.rest_0_), channel_id=1, source_target_pairs={{0,4},{4,0},{8,12},{12,8},{1,5},{5,1},{9,13},{13,9},{2,6},{6,2},{1... | collective-permute-start | bytes 184328 | tf_op jit(solution)/shard_map/ppermute | solution.py:384
  39.9 0.7 %collective-permute-start.15 = (f32[96,128]{1,0:T(8,128)S(1)}, f32[96,128]{1,0:T(8,128)S(1)}, u32[]{:S(2)}, u32[]{:S(2)}) collective-permute-start(f32[96,128]{1,0:T(8,128)S(1)} %get-tuple-element.63), channel_id=1, source_target_pairs={{1,2},{2,1},{5,6},{6,5},{9,10},{10,9},{13,14},{14,13},{17,18},{18,... | collective-permute-start | bytes 147464 | tf_op jit(solution)/shard_map/ppermute | solution.py:440
  40.5 1.5 %collective-permute-done.13.rest_3_.cols_b = f32[120,128]{1,0:T(8,128)S(1)} collective-permute-done((f32[120,128]{1,0:T(8,128)S(1)}, f32[120,128]{1,0:T(8,128)S(1)}, u32[]{:S(2)}, u32[]{:S(2)}) %collective-permute-start.13) | collective-permute-done | bytes 61472 | tf_op jit(solution)/shard_map/ppermute | solution.py:384
  42.0 1.9 %collective-permute-done.12.rest_2_ = f32[120,128]{1,0:T(8,128)S(1)} collective-permute-done((f32[120,128]{1,0:T(8,128)S(1)}, f32[120,128]{1,0:T(8,128)S(1)}, u32[]{:S(2)}, u32[]{:S(2)}) %collective-permute-start.12) | collective-permute-done | bytes 61472 | tf_op jit(solution)/shard_map/ppermute | solution.py:384
  44.1 1.2 %collective-permute-done.14.time_other = f32[96,128]{1,0:T(8,128)S(1)} collective-permute-done((f32[96,128]{1,0:T(8,128)S(1)}, f32[96,128]{1,0:T(8,128)S(1)}, u32[]{:S(2)}, u32[]{:S(2)}) %collective-permute-start.14) | collective-permute-done | bytes 49184 | tf_op jit(solution)/shard_map/ppermute | solution.py:384
  45.3 1.7 %shard_map.92 = (f32[96,1024]{1,0:T(8,128)S(1)}, f32[96,128]{1,0:T(8,128)S(1)}, bf16[208,128]{1,0:T(8,128)(2,1)S(1)}, bf16[208,128]{1,0:T(8,128)(2,1)S(1)}) custom-call(f32[96,1024]{1,0:T(8,128)S(1)} %get-tuple-element.53.surface, f32[96,128]{1,0:T(8,128)S(1)} %get-tuple-element.58.time_own, f32[96,128]{1,0:T(8,128)S(1)} %collective-permute-done.14.time_other, ...), custom_call_target="tpu_custom_call" | custom-call | flops 1000000 | bytes 1000000 | tf_op jit(solution)/shard_map/pallas_call | solution.py:370
  47.0 0.2 collective-permute-start.16
  47.2 1.0 %collective-permute-start.18 = (bf16[208,128]{1,0:T(8,128)(2,1)S(1)}, bf16[208,128]{1,0:T(8,128)(2,1)S(1)}, u32[]{:S(2)}, u32[]{:S(2)}) collective-permute-start(bf16[208,128]{1,0:T(8,128)(2,1)S(1)} %get-tuple-element.66.mine), channel_id=1, source_target_pairs={{0,2},{2,0},{1,3},{3,1},{4,6},{6,4},{5,7},{7,5},{8,10},{10,8},{9,1... | collective-permute-start | bytes 159752 | tf_op jit(solution)/shard_map/ppermute | solution.py:384
  48.2 0.7 %collective-permute-start.19 = (bf16[208,128]{1,0:T(8,128)(2,1)S(1)}, bf16[208,128]{1,0:T(8,128)(2,1)S(1)}, u32[]{:S(2)}, u32[]{:S(2)}) collective-permute-start(bf16[208,128]{1,0:T(8,128)(2,1)S(1)} %get-tuple-element.67), channel_id=1, source_target_pairs={{0,3},{1,2},{2,1},{3,0},{4,7},{5,6},{6,5},{7,4},{8,11},{9,10},{10,... | collective-permute-start | bytes 159752 | tf_op jit(solution)/shard_map/ppermute | solution.py:384
  48.9 0.4 collective-permute-start.17
  49.4 2.2 %collective-permute-done.18.band = bf16[208,128]{1,0:T(8,128)(2,1)S(1)} collective-permute-done((bf16[208,128]{1,0:T(8,128)(2,1)S(1)}, bf16[208,128]{1,0:T(8,128)(2,1)S(1)}, u32[]{:S(2)}, u32[]{:S(2)}) %collective-permute-start.18) | collective-permute-done | bytes 53280 | tf_op jit(solution)/shard_map/ppermute | solution.py:384
  51.6 0.6 %collective-permute-done.19.both = bf16[208,128]{1,0:T(8,128)(2,1)S(1)} collective-permute-done((bf16[208,128]{1,0:T(8,128)(2,1)S(1)}, bf16[208,128]{1,0:T(8,128)(2,1)S(1)}, u32[]{:S(2)}, u32[]{:S(2)}) %collective-permute-start.19) | collective-permute-done | bytes 53280 | tf_op jit(solution)/shard_map/ppermute | solution.py:384
  52.3 2.6 %collective-permute-start.22 = (bf16[208,128]{1,0:T(8,128)(2,1)S(1)}, bf16[208,128]{1,0:T(8,128)(2,1)S(1)}, u32[]{:S(2)}, u32[]{:S(2)}) collective-permute-start(bf16[208,128]{1,0:T(8,128)(2,1)S(1)} %shard_map.93.rest_0_), channel_id=1, source_target_pairs={{0,12},{4,8},{8,4},{12,0},{1,13},{5,9},{9,5},{13,1},{2,14},{6,10},... | collective-permute-start | bytes 159752 | tf_op jit(solution)/shard_map/ppermute | solution.py:384
  54.9 1.8 %collective-permute-start.20 = (bf16[208,128]{1,0:T(8,128)(2,1)S(1)}, bf16[208,128]{1,0:T(8,128)(2,1)S(1)}, u32[]{:S(2)}, u32[]{:S(2)}) collective-permute-start(bf16[208,128]{1,0:T(8,128)(2,1)S(1)} %shard_map.93.rest_0_), channel_id=1, source_target_pairs={{0,4},{4,0},{8,12},{12,8},{1,5},{5,1},{9,13},{13,9},{2,6},{6,2},{1... | collective-permute-start | bytes 159752 | tf_op jit(solution)/shard_map/ppermute | solution.py:384
  56.8 1.9 %collective-permute-done.22.rest_3_ = bf16[208,128]{1,0:T(8,128)(2,1)S(1)} collective-permute-done((bf16[208,128]{1,0:T(8,128)(2,1)S(1)}, bf16[208,128]{1,0:T(8,128)(2,1)S(1)}, u32[]{:S(2)}, u32[]{:S(2)}) %collective-permute-start.22) | collective-permute-done | bytes 53280 | tf_op jit(solution)/shard_map/ppermute | solution.py:384
  58.6 1.7 %collective-permute-done.21.rest_2_ = bf16[208,128]{1,0:T(8,128)(2,1)S(1)} collective-permute-done((bf16[208,128]{1,0:T(8,128)(2,1)S(1)}, bf16[208,128]{1,0:T(8,128)(2,1)S(1)}, u32[]{:S(2)}, u32[]{:S(2)}) %collective-permute-start.21) | collective-permute-done | bytes 53280 | tf_op jit(solution)/shard_map/ppermute | solution.py:384
  60.3 1.5 %shard_map.94 = (f32[1536,128]{1,0:T(8,128)}, f32[64,96]{1,0:T(8,128)}) custom-call(f32[96,1024]{1,0:T(8,128)S(1)} %get-tuple-element.64.surface, f32[96,1024]{1,0:T(8,128)S(1)} %collective-permute-done.16.other, f32[96,128]{1,0:T(8,128)S(1)} %get-tuple-element.65.time_t, bf16[208,128]{1,0:T(8,128)(2,1)S(1)} %shard_map.93.rest_0_, ...), custom_call_target="tpu_custom_call" | custom-call | flops 1000000 | bytes 1000000 | tf_op jit(solution)/shard_map/pallas_call | solution.py:370
  (25 shorter events, 0.3 us)
Async XLA Ops:
  4.5 8.7 %collective-permute-start.1 = (bf16[528,128]{1,0:T(8,128)(2,1)S(1)}, bf16[528,128]{1,0:T(8,128)(2,1)S(1)}, u32[]{:S(2)}, u32[]{:S(2)}) collective-permute-start(bf16[528,128]{1,0:T(8,128)(2,1)S(1)} %get-tuple-element.43), channel_id=1, source_target_pairs={{0,4},{4,0},{8,12},{12,8},{1,5},{5,1},{9,13},{13,9},{2,6},{6,2},{1... | collective-permute-start | bytes 405512 | tf_op jit(solution)/shard_map/ppermute | solution.py:384
  7.6 12.7 %collective-permute-start.3 = (bf16[528,128]{1,0:T(8,128)(2,1)S(1)}, bf16[528,128]{1,0:T(8,128)(2,1)S(1)}, u32[]{:S(2)}, u32[]{:S(2)}) collective-permute-start(bf16[528,128]{1,0:T(8,128)(2,1)S(1)} %get-tuple-element.47), channel_id=1, source_target_pairs={{0,8},{4,12},{8,0},{12,4},{1,9},{5,13},{9,1},{13,5},{2,10},{6,14},... | collective-permute-start | bytes 405512 | tf_op jit(solution)/shard_map/ppermute | solution.py:384
  10.2 10.1 %collective-permute-start = (bf16[720,128]{1,0:T(8,128)(2,1)S(1)}, bf16[720,128]{1,0:T(8,128)(2,1)S(1)}, u32[]{:S(2)}, u32[]{:S(2)}) collective-permute-start(bf16[720,128]{1,0:T(8,128)(2,1)S(1)} %get-tuple-element.38), channel_id=1, source_target_pairs={{0,1},{1,0},{4,5},{5,4},{8,9},{9,8},{12,13},{13,12},{2,3},{3,2},{6... | collective-permute-start | bytes 552968 | tf_op jit(solution)/shard_map/ppermute | solution.py:384
  10.2 11.0 %collective-permute-start.4 = (bf16[544,128]{1,0:T(8,128)(2,1)S(1)}, bf16[544,128]{1,0:T(8,128)(2,1)S(1)}, u32[]{:S(2)}, u32[]{:S(2)}) collective-permute-start(bf16[544,128]{1,0:T(8,128)(2,1)S(1)} %get-tuple-element.48), channel_id=1, source_target_pairs={{0,12},{4,8},{8,4},{12,0},{1,13},{5,9},{9,5},{13,1},{2,14},{6,10},... | collective-permute-start | bytes 417800 | tf_op jit(solution)/shard_map/ppermute | solution.py:384
  10.2 11.0 %collective-permute-start.5 = (bf16[544,128]{1,0:T(8,128)(2,1)S(1)}, bf16[544,128]{1,0:T(8,128)(2,1)S(1)}, u32[]{:S(2)}, u32[]{:S(2)}) collective-permute-start(bf16[544,128]{1,0:T(8,128)(2,1)S(1)} %get-tuple-element.49), channel_id=1, source_target_pairs={{0,4},{4,0},{8,12},{12,8},{1,5},{5,1},{9,13},{13,9},{2,6},{6,2},{1... | collective-permute-start | bytes 417800 | tf_op jit(solution)/shard_map/ppermute | solution.py:384
  13.2 7.7 %copy-start = (f32[64,96]{1,0:T(8,128)S(1)}, f32[64,96]{1,0:T(8,128)}, u32[]{:S(2)}) copy-start(f32[64,96]{1,0:T(8,128)} %time_own.1) | copy-start | bytes 73732
  13.3 14.1 %collective-permute-start.2 = (bf16[528,128]{1,0:T(8,128)(2,1)S(1)}, bf16[528,128]{1,0:T(8,128)(2,1)S(1)}, u32[]{:S(2)}, u32[]{:S(2)}) collective-permute-start(bf16[528,128]{1,0:T(8,128)(2,1)S(1)} %get-tuple-element.46), channel_id=1, source_target_pairs={{0,9},{1,8},{4,13},{5,12},{8,1},{9,0},{12,5},{13,4},{2,11},{3,10},... | collective-permute-start | bytes 405512 | tf_op jit(solution)/shard_map/ppermute | solution.py:384
  20.3 7.1 %collective-permute-start.6 = (bf16[528,128]{1,0:T(8,128)(2,1)S(1)}, bf16[528,128]{1,0:T(8,128)(2,1)S(1)}, u32[]{:S(2)}, u32[]{:S(2)}) collective-permute-start(bf16[528,128]{1,0:T(8,128)(2,1)S(1)} %get-tuple-element.50), channel_id=1, source_target_pairs={{0,5},{1,4},{4,1},{5,0},{8,13},{9,12},{12,9},{13,8},{2,7},{3,6},{6... | collective-permute-start | bytes 405512 | tf_op jit(solution)/shard_map/ppermute | solution.py:384
  20.3 0.9 %collective-permute-start.7 = (f32[96,128]{1,0:T(8,128)S(1)}, f32[96,128]{1,0:T(8,128)S(1)}, u32[]{:S(2)}, u32[]{:S(2)}) collective-permute-start(f32[96,128]{1,0:T(8,128)S(1)} %get-tuple-element.52), channel_id=1, source_target_pairs={{1,2},{2,1},{5,6},{6,5},{9,10},{10,9},{13,14},{14,13},{17,18},{18,... | collective-permute-start | bytes 147464 | tf_op jit(solution)/shard_map/ppermute | solution.py:440
  29.0 6.4 %collective-permute-start.8 = (f32[200,128]{1,0:T(8,128)S(1)}, f32[200,128]{1,0:T(8,128)S(1)}, u32[]{:S(2)}, u32[]{:S(2)}) collective-permute-start(f32[200,128]{1,0:T(8,128)S(1)} %get-tuple-element.55), channel_id=1, source_target_pairs={{0,1},{1,0},{2,3},{3,2},{4,5},{5,4},{6,7},{7,6},{8,9},{9,8},{10,11... | collective-permute-start | bytes 307208 | tf_op jit(solution)/shard_map/ppermute | solution.py:384
  29.8 5.6 %collective-permute-start.9 = (f32[120,128]{1,0:T(8,128)S(1)}, f32[120,128]{1,0:T(8,128)S(1)}, u32[]{:S(2)}, u32[]{:S(2)}) collective-permute-start(f32[120,128]{1,0:T(8,128)S(1)} %get-tuple-element.54.mine), channel_id=1, source_target_pairs={{0,2},{2,0},{1,3},{3,1},{4,6},{6,4},{5,7},{7,5},{8,10},{10,8},{9,1... | collective-permute-start | bytes 184328 | tf_op jit(solution)/shard_map/ppermute | solution.py:384
  31.3 4.1 %collective-permute-start.10 = (f32[104,128]{1,0:T(8,128)S(1)}, f32[104,128]{1,0:T(8,128)S(1)}, u32[]{:S(2)}, u32[]{:S(2)}) collective-permute-start(f32[104,128]{1,0:T(8,128)S(1)} %get-tuple-element.56), channel_id=1, source_target_pairs={{0,3},{1,2},{2,1},{3,0},{4,7},{5,6},{6,5},{7,4},{8,11},{9,10},{10,... | collective-permute-start | bytes 159752 | tf_op jit(solution)/shard_map/ppermute | solution.py:384
  35.4 6.6 %collective-permute-start.13 = (f32[120,128]{1,0:T(8,128)S(1)}, f32[120,128]{1,0:T(8,128)S(1)}, u32[]{:S(2)}, u32[]{:S(2)}) collective-permute-start(f32[120,128]{1,0:T(8,128)S(1)} %get-tuple-element.57.rest_0_), channel_id=1, source_target_pairs={{0,12},{4,8},{8,4},{12,0},{1,13},{5,9},{9,5},{13,1},{2,14},{6,10},... | collective-permute-start | bytes 184328 | tf_op jit(solution)/shard_map/ppermute | solution.py:384
  38.0 5.9 %collective-permute-start.12 = (f32[120,128]{1,0:T(8,128)S(1)}, f32[120,128]{1,0:T(8,128)S(1)}, u32[]{:S(2)}, u32[]{:S(2)}) collective-permute-start(f32[120,128]{1,0:T(8,128)S(1)} %get-tuple-element.57.rest_0_), channel_id=1, source_target_pairs={{0,8},{4,12},{8,0},{12,4},{1,9},{5,13},{9,1},{13,5},{2,10},{6,14},... | collective-permute-start | bytes 184328 | tf_op jit(solution)/shard_map/ppermute | solution.py:384
  38.0 5.9 %collective-permute-start.11 = (f32[120,128]{1,0:T(8,128)S(1)}, f32[120,128]{1,0:T(8,128)S(1)}, u32[]{:S(2)}, u32[]{:S(2)}) collective-permute-start(f32[120,128]{1,0:T(8,128)S(1)} %get-tuple-element.57.rest_0_), channel_id=1, source_target_pairs={{0,4},{4,0},{8,12},{12,8},{1,5},{5,1},{9,13},{13,9},{2,6},{6,2},{1... | collective-permute-start | bytes 184328 | tf_op jit(solution)/shard_map/ppermute | solution.py:384
  39.9 4.2 %collective-permute-start.15 = (f32[96,128]{1,0:T(8,128)S(1)}, f32[96,128]{1,0:T(8,128)S(1)}, u32[]{:S(2)}, u32[]{:S(2)}) collective-permute-start(f32[96,128]{1,0:T(8,128)S(1)} %get-tuple-element.63), channel_id=1, source_target_pairs={{1,2},{2,1},{5,6},{6,5},{9,10},{10,9},{13,14},{14,13},{17,18},{18,... | collective-permute-start | bytes 147464 | tf_op jit(solution)/shard_map/ppermute | solution.py:440
  44.0 1.3 %collective-permute-start.14 = (f32[96,128]{1,0:T(8,128)S(1)}, f32[96,128]{1,0:T(8,128)S(1)}, u32[]{:S(2)}, u32[]{:S(2)}) collective-permute-start(f32[96,128]{1,0:T(8,128)S(1)} %get-tuple-element.58.time_own), channel_id=1, source_target_pairs={{0,1},{1,0},{2,3},{3,2},{4,5},{5,4},{6,7},{7,6},{8,9},{9,8},{10,11... | collective-permute-start | bytes 147464 | tf_op jit(solution)/shard_map/ppermute | solution.py:384
  47.0 13.3 %collective-permute-start.16 = (f32[96,1024]{1,0:T(8,128)S(1)}, f32[96,1024]{1,0:T(8,128)S(1)}, u32[]{:S(2)}, u32[]{:S(2)}) collective-permute-start(f32[96,1024]{1,0:T(8,128)S(1)} %get-tuple-element.64.surface), channel_id=1, source_target_pairs={{0,1},{1,0},{2,3},{3,2},{4,5},{5,4},{6,7},{7,6},{8,9},{9,8},{10,11... | collective-permute-start | bytes 1179656 | tf_op jit(solution)/shard_map/ppermute | solution.py:384
  47.2 4.4 %collective-permute-start.18 = (bf16[208,128]{1,0:T(8,128)(2,1)S(1)}, bf16[208,128]{1,0:T(8,128)(2,1)S(1)}, u32[]{:S(2)}, u32[]{:S(2)}) collective-permute-start(bf16[208,128]{1,0:T(8,128)(2,1)S(1)} %get-tuple-element.66.mine), channel_id=1, source_target_pairs={{0,2},{2,0},{1,3},{3,1},{4,6},{6,4},{5,7},{7,5},{8,10},{10,8},{9,1... | collective-permute-start | bytes 159752 | tf_op jit(solution)/shard_map/ppermute | solution.py:384
  48.2 4.0 %collective-permute-start.19 = (bf16[208,128]{1,0:T(8,128)(2,1)S(1)}, bf16[208,128]{1,0:T(8,128)(2,1)S(1)}, u32[]{:S(2)}, u32[]{:S(2)}) collective-permute-start(bf16[208,128]{1,0:T(8,128)(2,1)S(1)} %get-tuple-element.67), channel_id=1, source_target_pairs={{0,3},{1,2},{2,1},{3,0},{4,7},{5,6},{6,5},{7,4},{8,11},{9,10},{10,... | collective-permute-start | bytes 159752 | tf_op jit(solution)/shard_map/ppermute | solution.py:384
  48.9 3.3 %collective-permute-start.17 = (bf16[208,128]{1,0:T(8,128)(2,1)S(1)}, bf16[208,128]{1,0:T(8,128)(2,1)S(1)}, u32[]{:S(2)}, u32[]{:S(2)}) collective-permute-start(bf16[208,128]{1,0:T(8,128)(2,1)S(1)} %get-tuple-element.67), channel_id=1, source_target_pairs={{0,1},{1,0},{2,3},{3,2},{4,5},{5,4},{6,7},{7,6},{8,9},{9,8},{10,11... | collective-permute-start | bytes 159752 | tf_op jit(solution)/shard_map/ppermute | solution.py:384
  52.3 6.3 %collective-permute-start.22 = (bf16[208,128]{1,0:T(8,128)(2,1)S(1)}, bf16[208,128]{1,0:T(8,128)(2,1)S(1)}, u32[]{:S(2)}, u32[]{:S(2)}) collective-permute-start(bf16[208,128]{1,0:T(8,128)(2,1)S(1)} %shard_map.93.rest_0_), channel_id=1, source_target_pairs={{0,12},{4,8},{8,4},{12,0},{1,13},{5,9},{9,5},{13,1},{2,14},{6,10},... | collective-permute-start | bytes 159752 | tf_op jit(solution)/shard_map/ppermute | solution.py:384
  54.9 5.4 %collective-permute-start.21 = (bf16[208,128]{1,0:T(8,128)(2,1)S(1)}, bf16[208,128]{1,0:T(8,128)(2,1)S(1)}, u32[]{:S(2)}, u32[]{:S(2)}) collective-permute-start(bf16[208,128]{1,0:T(8,128)(2,1)S(1)} %shard_map.93.rest_0_), channel_id=1, source_target_pairs={{0,8},{4,12},{8,0},{12,4},{1,9},{5,13},{9,1},{13,5},{2,10},{6,14},... | collective-permute-start | bytes 159752 | tf_op jit(solution)/shard_map/ppermute | solution.py:384
  54.9 5.4 %collective-permute-start.20 = (bf16[208,128]{1,0:T(8,128)(2,1)S(1)}, bf16[208,128]{1,0:T(8,128)(2,1)S(1)}, u32[]{:S(2)}, u32[]{:S(2)}) collective-permute-start(bf16[208,128]{1,0:T(8,128)(2,1)S(1)} %shard_map.93.rest_0_), channel_id=1, source_target_pairs={{0,4},{4,0},{8,12},{12,8},{1,5},{5,1},{9,13},{13,9},{2,6},{6,2},{1... | collective-permute-start | bytes 159752 | tf_op jit(solution)/shard_map/ppermute | solution.py:384

commit v10 on v9

--- a/solution.py
+++ b/solution.py
@@ -20,7 +20,8 @@
 COLS = 16
 NORM = 8
 SPARE = 2 * 1024 * 1024
-SWATH_COPIES = 4
+SWATH_COPIES = 1
+UNROLL = 4
 
 
 def dot(a, b, contract):
@@ -47,25 +48,28 @@
         copy.wait()
 
     def owner(d, carry):
-        step = jnp.bitwise_xor(d, me)
-
-        def entry(k, carry):
-            slot = list_ref[0, d, k]
-            row = target_ref[slot]
-            far = jnp.bitwise_xor(lax.div(row, half), core)
-            place[slot] = (far * n_lon + step) * half + lax.rem(row, half)
+        first = jnp.bitwise_xor(d, me) * half
+        count = count_ref[0, d]
+
+        def entries(i, carry):
+            for k in range(UNROLL):
+                k = i * UNROLL + k
+                slot = list_ref[0, d, k]
+                row = target_ref[slot]
+                far = jnp.bitwise_xor(lax.shift_right_logical(row, half.bit_length() - 1), core)
+                place[jnp.where(k < count, slot, slots)] = far * (n_lon * half) + first + jnp.bitwise_and(row, half - 1)
             return carry
 
-        return lax.fori_loop(0, count_ref[0, d], entry, carry)
+        return lax.fori_loop(0, lax.div(count + UNROLL - 1, UNROLL), entries, carry)
 
     lax.fori_loop(0, n_lon, owner, 0)
     mask = mask_ref[...].astype(F32)
-    by_day = mask.T
+    by_day = mask.T.astype(BF16)
     for slot in range(slots):
         if slot % chunk == 0:
             copies[len(small) + slot // chunk].wait()
         at = place[slot]
-        total[at] += swath_ref[slot].astype(F32) * by_day[:, slot:slot + 1]
+        total[at] += (swath_ref[slot] * by_day[:, slot:slot + 1]).astype(F32)
         seen[pl.ds(at, 1), :days] += mask[slot:slot + 1, :]
     for copy in copies[len(small) + len(large):]:
         copy.wait()
@@ -75,7 +79,8 @@
         surface[:, row * LANES:(row + 1) * LANES] = space_ref[pl.ds(core * half + row, rank, stride=height), :]
     edge_near[...] = space_ref[pl.ds(half - core, rank, stride=height), :]
     edge_far[...] = space_ref[pl.ds(core * (height - 1), rank, stride=height), :]
-    cols[...] = columns_as_rows(border(surface[...], half), flip)[:COLS, :]
+    cols[...] = jnp.zeros(cols.shape, F32)
+    cols[:, :rank] = border(surface[...], half)
     for (side, step), out in zip(sends, outs):
         at = (side * n_lon + step) * half
         end = half * days + TAIL
@@ -96,20 +101,18 @@
     return surface[:, row * LANES:(row + 1) * LANES]
 
 
-def columns_as_rows(columns, flip):
-    rank = columns[0].shape[0]
-    lane = lax.broadcasted_iota(jnp.int32, (rank, LANES), 1)
-    block = jnp.zeros((rank, LANES), F32)
-    for at, column in enumerate(columns):
-        block = jnp.where(lane == at, column, block)
+def column_as_row(column, flip):
+    rank = column.shape[0]
     flip[...] = jnp.zeros(flip.shape, F32)
-    flip[:rank, :] = block
-    return flip[...].T
+    flip[:rank, :] = jnp.broadcast_to(column, (rank, LANES))
+    return flip[...].T[:NORM, :]
 
 
 def border(surface, half):
-    strips = [row_of(surface, row) for row in range(half)]
-    return [strip[:, :1] for strip in strips] + [strip[:, LANES - 1:] for strip in strips]
+    line = lax.broadcasted_iota(jnp.int32, (COLS, half * LANES), 0)
+    lane = lax.broadcasted_iota(jnp.int32, (COLS, half * LANES), 1)
+    pick_lane = jnp.where(line < half, line * LANES, (line - half) * LANES + LANES - 1)
+    return dot((lane == pick_lane).astype(BF16), surface.astype(BF16), (1, 1))
 
 
 def rows_as_columns(rows, rank, flip):
@@ -203,12 +206,14 @@
     rank = norm.shape[0]
     days = LANES // 2
     own = lax.broadcasted_iota(jnp.int32, grad_time.shape, 1) < days
-    last = columns_as_rows([norm] * NORM + border(fresh[...], half), flip)
+    last = column_as_row(norm, flip)
     message[:rank, :] = jnp.where(own, grad_time, pltpu.roll(grad_diag, days, 1))
-    message[rank:, :] = last[: NORM + COLS, :]
+    message[rank:rank + NORM, :] = last
+    message[rank + NORM:, :] = jnp.zeros((COLS, LANES), F32)
+    message[rank + NORM:, :rank] = border(fresh[...], half)
     for out in (crossing, outgoing):
         out[:rank, :] = jnp.where(own, pltpu.roll(grad_time, days, 1), grad_diag)
-        out[rank:rank + NORM, :] = last[:NORM, :]
+        out[rank:rank + NORM, :] = last
     first_row, last_row = fresh[:, :LANES], fresh[:, (half - 1) * LANES:]
     outgoing[rank + NORM:, :] = pick(core == 0, last_row, first_row)
     edge_far[...] = pick(core == 0, first_row, last_row)
@@ -228,7 +233,7 @@
 def post_all(sums, message, outgoing, flip):
     grad_time, grad_diag, norm = sums
     rank = norm.shape[0]
-    last = columns_as_rows([norm], flip)[:NORM, :]
+    last = column_as_row(norm, flip)
     for out, shift in ((message, 0), (outgoing, LANES // 2)):
         parts = [pltpu.roll(part, shift, 1) if shift else part for part in (grad_time, grad_diag)]
         out[: 2 * rank, :], out[2 * rank:, :] = narrow(jnp.concatenate([*parts, last], axis=0), rank)
@@ -412,7 +417,7 @@
         [pltpu.SMEM(ref.shape, jnp.int32) for ref in operands[:3]]
         + [pltpu.VMEM(ref.shape, ref.dtype) for ref in operands[3:]]
         + [
-            pltpu.SMEM((slots,), jnp.int32),
+            pltpu.SMEM((slots + 1,), jnp.int32),
             pltpu.VMEM((2 * n_lon * half, days, cells), F32),
             pltpu.VMEM((2 * n_lon * half + TAIL, LANES), F32),
             flip,

time: 62 us -> 60.5 us (0.976)
  Pallas kernels: 9.21 us -> 7.69 us
    pallas_call x9, Pallas kernels: 9.21 us -> 7.69 us  [run(): pl.pallas_call(kernel, out_shape=out_shape, in_specs=[pl.BlockSpec(memory...]
where the time goes in v10:
time: 60.5 us; the launch traced here: 60.3 us
  waiting for transfers between devices  29.4 us (49%)
  starting transfers between devices  22.4 us (37%)
  Pallas kernels  7.69 us (13%)
  between operations  0.74 us (1%)
    ppermute x21, waiting for transfers between devices, across(): lax.ppermute(value, axis, [(i, i ^ step) for i in range(lax.axis_size(axi...  29.4 us
    ppermute x21, starting transfers between devices, across(): lax.ppermute(value, axis, [(i, i ^ step) for i in range(lax.axis_size(axi...  21.1 us
    pallas_call x9, Pallas kernels, run(): pl.pallas_call(kernel, out_shape=out_shape, in_specs=[pl.BlockSpec(memory...  7.69 us
    ppermute x2, starting transfers between devices, bands(): return lax.ppermute(edge, ('lat', 'ta'), there + [(b, a) for a, b in there])  1.31 us
  transfers between devices with their start and end apart: 23, of which 11 were waited for; matrix products, arithmetic and copies ran while one was open for 0% of the time, Pallas kernels for 1%

profile of v10, /device:TPU:0, one launch (start us, length us, event | category | flops | bytes accessed | tf_op | source)
XLA Modules:
  0.0 60.3 jit_solution(17691118403140944856)
XLA Ops:
  0.6 2.8 %shard_map.86 = (bf16[528,128]{1,0:T(8,128)(2,1)S(1)}, bf16[528,128]{1,0:T(8,128)(2,1)S(1)}, bf16[528,128]{1,0:T(8,128)(2,1)S(1)}, bf16[544,128]{1,0:T(8,128)(2,...) custom-call(s32[1,4,32]{2,1,0:T(4,128)} %list_hbm.1, ...), custom_call_target="tpu_custom_call" | custom-call | flops 1000000 | bytes 1000000 | tf_op jit(solution)/shard_map/pallas_call | solution.py:375
  3.5 3.1 %collective-permute-start.1 = (bf16[528,128]{1,0:T(8,128)(2,1)S(1)}, bf16[528,128]{1,0:T(8,128)(2,1)S(1)}, u32[]{:S(2)}, u32[]{:S(2)}) collective-permute-start(bf16[528,128]{1,0:T(8,128)(2,1)S(1)} %get-tuple-element.43), channel_id=1, source_target_pairs={{0,4},{4,0},{8,12},{12,8},{1,5},{5,1},{9,13},{13,9},{2,6},{6,2},{1... | collective-permute-start | bytes 405512 | tf_op jit(solution)/shard_map/ppermute | solution.py:389
  6.6 2.6 %collective-permute-start.3 = (bf16[528,128]{1,0:T(8,128)(2,1)S(1)}, bf16[528,128]{1,0:T(8,128)(2,1)S(1)}, u32[]{:S(2)}, u32[]{:S(2)}) collective-permute-start(bf16[528,128]{1,0:T(8,128)(2,1)S(1)} %get-tuple-element.47), channel_id=1, source_target_pairs={{0,8},{4,12},{8,0},{12,4},{1,9},{5,13},{9,1},{13,5},{2,10},{6,14},... | collective-permute-start | bytes 405512 | tf_op jit(solution)/shard_map/ppermute | solution.py:389
  9.2 0.9 %collective-permute-start.5 = (bf16[544,128]{1,0:T(8,128)(2,1)S(1)}, bf16[544,128]{1,0:T(8,128)(2,1)S(1)}, u32[]{:S(2)}, u32[]{:S(2)}) collective-permute-start(bf16[544,128]{1,0:T(8,128)(2,1)S(1)} %get-tuple-element.49), channel_id=1, source_target_pairs={{0,4},{4,0},{8,12},{12,8},{1,5},{5,1},{9,13},{13,9},{2,6},{6,2},{1... | collective-permute-start | bytes 417800 | tf_op jit(solution)/shard_map/ppermute | solution.py:389
  10.1 2.1 %collective-permute-done.1.theirs = bf16[528,128]{1,0:T(8,128)(2,1)S(1)} collective-permute-done((bf16[528,128]{1,0:T(8,128)(2,1)S(1)}, bf16[528,128]{1,0:T(8,128)(2,1)S(1)}, u32[]{:S(2)}, u32[]{:S(2)}) %collective-permute-start.1) | collective-permute-done | bytes 135200 | tf_op jit(solution)/shard_map/ppermute | solution.py:389
  12.2 1.0 %collective-permute-start.2 = (bf16[528,128]{1,0:T(8,128)(2,1)S(1)}, bf16[528,128]{1,0:T(8,128)(2,1)S(1)}, u32[]{:S(2)}, u32[]{:S(2)}) collective-permute-start(bf16[528,128]{1,0:T(8,128)(2,1)S(1)} %get-tuple-element.46), channel_id=1, source_target_pairs={{0,9},{1,8},{4,13},{5,12},{8,1},{9,0},{12,5},{13,4},{2,11},{3,10},... | collective-permute-start | bytes 405512 | tf_op jit(solution)/shard_map/ppermute | solution.py:389
  13.2 6.0 %collective-permute-done.3.rest_1_ = bf16[528,128]{1,0:T(8,128)(2,1)S(1)} collective-permute-done((bf16[528,128]{1,0:T(8,128)(2,1)S(1)}, bf16[528,128]{1,0:T(8,128)(2,1)S(1)}, u32[]{:S(2)}, u32[]{:S(2)}) %collective-permute-start.3) | collective-permute-done | bytes 135200 | tf_op jit(solution)/shard_map/ppermute | solution.py:389
  19.2 0.7 %collective-permute-start.7 = (f32[96,128]{1,0:T(8,128)S(1)}, f32[96,128]{1,0:T(8,128)S(1)}, u32[]{:S(2)}, u32[]{:S(2)}) collective-permute-start(f32[96,128]{1,0:T(8,128)S(1)} %get-tuple-element.52), channel_id=1, source_target_pairs={{1,2},{2,1},{5,6},{6,5},{9,10},{10,9},{13,14},{14,13},{17,18},{18,... | collective-permute-start | bytes 147464 | tf_op jit(solution)/shard_map/ppermute | solution.py:445
  19.9 0.2 shard_map.87
  20.1 6.2 %collective-permute-done.2.rest_0_ = bf16[528,128]{1,0:T(8,128)(2,1)S(1)} collective-permute-done((bf16[528,128]{1,0:T(8,128)(2,1)S(1)}, bf16[528,128]{1,0:T(8,128)(2,1)S(1)}, u32[]{:S(2)}, u32[]{:S(2)}) %collective-permute-start.2) | collective-permute-done | bytes 135200 | tf_op jit(solution)/shard_map/ppermute | solution.py:389
  26.3 1.2 %shard_map.89 = (f32[96,1024]{1,0:T(8,128)S(1)}, f32[120,128]{1,0:T(8,128)S(1)}, f32[104,128]{1,0:T(8,128)S(1)}, f32[200,128]{1,0:T(8,128)S(1)}, f32[96,128]{1,0...) custom-call(f32[96,1024]{1,0:T(8,128)S(1)} %get-tuple-element.36.surface, ...), custom_call_target="tpu_custom_call" | custom-call | flops 1000000 | bytes 1000000 | tf_op jit(solution)/shard_map/pallas_call | solution.py:375
  27.5 0.7 %collective-permute-start.8 = (f32[200,128]{1,0:T(8,128)S(1)}, f32[200,128]{1,0:T(8,128)S(1)}, u32[]{:S(2)}, u32[]{:S(2)}) collective-permute-start(f32[200,128]{1,0:T(8,128)S(1)} %get-tuple-element.55), channel_id=1, source_target_pairs={{0,1},{1,0},{2,3},{3,2},{4,5},{5,4},{6,7},{7,6},{8,9},{9,8},{10,11... | collective-permute-start | bytes 307208 | tf_op jit(solution)/shard_map/ppermute | solution.py:389
  28.3 1.5 %collective-permute-start.9 = (f32[120,128]{1,0:T(8,128)S(1)}, f32[120,128]{1,0:T(8,128)S(1)}, u32[]{:S(2)}, u32[]{:S(2)}) collective-permute-start(f32[120,128]{1,0:T(8,128)S(1)} %get-tuple-element.54.mine), channel_id=1, source_target_pairs={{0,2},{2,0},{1,3},{3,1},{4,6},{6,4},{5,7},{7,5},{8,10},{10,8},{9,1... | collective-permute-start | bytes 184328 | tf_op jit(solution)/shard_map/ppermute | solution.py:389
  29.8 4.1 %collective-permute-done.10.both = f32[104,128]{1,0:T(8,128)S(1)} collective-permute-done((f32[104,128]{1,0:T(8,128)S(1)}, f32[104,128]{1,0:T(8,128)S(1)}, u32[]{:S(2)}, u32[]{:S(2)}) %collective-permute-start.10) | collective-permute-done | bytes 53280 | tf_op jit(solution)/shard_map/ppermute | solution.py:389
  33.9 2.6 %collective-permute-start.13 = (f32[120,128]{1,0:T(8,128)S(1)}, f32[120,128]{1,0:T(8,128)S(1)}, u32[]{:S(2)}, u32[]{:S(2)}) collective-permute-start(f32[120,128]{1,0:T(8,128)S(1)} %get-tuple-element.57.rest_0_), channel_id=1, source_target_pairs={{0,12},{4,8},{8,4},{12,0},{1,13},{5,9},{9,5},{13,1},{2,14},{6,10},... | collective-permute-start | bytes 184328 | tf_op jit(solution)/shard_map/ppermute | solution.py:389
  36.5 1.8 %collective-permute-start.11 = (f32[120,128]{1,0:T(8,128)S(1)}, f32[120,128]{1,0:T(8,128)S(1)}, u32[]{:S(2)}, u32[]{:S(2)}) collective-permute-start(f32[120,128]{1,0:T(8,128)S(1)} %get-tuple-element.57.rest_0_), channel_id=1, source_target_pairs={{0,4},{4,0},{8,12},{12,8},{1,5},{5,1},{9,13},{13,9},{2,6},{6,2},{1... | collective-permute-start | bytes 184328 | tf_op jit(solution)/shard_map/ppermute | solution.py:389
  38.3 0.7 %collective-permute-start.15 = (f32[96,128]{1,0:T(8,128)S(1)}, f32[96,128]{1,0:T(8,128)S(1)}, u32[]{:S(2)}, u32[]{:S(2)}) collective-permute-start(f32[96,128]{1,0:T(8,128)S(1)} %get-tuple-element.63), channel_id=1, source_target_pairs={{1,2},{2,1},{5,6},{6,5},{9,10},{10,9},{13,14},{14,13},{17,18},{18,... | collective-permute-start | bytes 147464 | tf_op jit(solution)/shard_map/ppermute | solution.py:445
  39.0 1.5 %collective-permute-done.13.rest_3_.cols_b = f32[120,128]{1,0:T(8,128)S(1)} collective-permute-done((f32[120,128]{1,0:T(8,128)S(1)}, f32[120,128]{1,0:T(8,128)S(1)}, u32[]{:S(2)}, u32[]{:S(2)}) %collective-permute-start.13) | collective-permute-done | bytes 61472 | tf_op jit(solution)/shard_map/ppermute | solution.py:389
  40.5 1.9 %collective-permute-done.12.rest_2_ = f32[120,128]{1,0:T(8,128)S(1)} collective-permute-done((f32[120,128]{1,0:T(8,128)S(1)}, f32[120,128]{1,0:T(8,128)S(1)}, u32[]{:S(2)}, u32[]{:S(2)}) %collective-permute-start.12) | collective-permute-done | bytes 61472 | tf_op jit(solution)/shard_map/ppermute | solution.py:389
  42.6 1.2 %collective-permute-done.14.time_other = f32[96,128]{1,0:T(8,128)S(1)} collective-permute-done((f32[96,128]{1,0:T(8,128)S(1)}, f32[96,128]{1,0:T(8,128)S(1)}, u32[]{:S(2)}, u32[]{:S(2)}) %collective-permute-start.14) | collective-permute-done | bytes 49184 | tf_op jit(solution)/shard_map/ppermute | solution.py:389
  43.8 1.7 %shard_map.92 = (f32[96,1024]{1,0:T(8,128)S(1)}, f32[96,128]{1,0:T(8,128)S(1)}, bf16[208,128]{1,0:T(8,128)(2,1)S(1)}, bf16[208,128]{1,0:T(8,128)(2,1)S(1)}) custom-call(f32[96,1024]{1,0:T(8,128)S(1)} %get-tuple-element.53.surface, f32[96,128]{1,0:T(8,128)S(1)} %get-tuple-element.58.time_own, f32[96,128]{1,0:T(8,128)S(1)} %collective-permute-done.14.time_other, ...), custom_call_target="tpu_custom_call" | custom-call | flops 1000000 | bytes 1000000 | tf_op jit(solution)/shard_map/pallas_call | solution.py:375
  45.5 0.2 collective-permute-start.16
  45.7 1.0 %collective-permute-start.18 = (bf16[208,128]{1,0:T(8,128)(2,1)S(1)}, bf16[208,128]{1,0:T(8,128)(2,1)S(1)}, u32[]{:S(2)}, u32[]{:S(2)}) collective-permute-start(bf16[208,128]{1,0:T(8,128)(2,1)S(1)} %get-tuple-element.66.mine), channel_id=1, source_target_pairs={{0,2},{2,0},{1,3},{3,1},{4,6},{6,4},{5,7},{7,5},{8,10},{10,8},{9,1... | collective-permute-start | bytes 159752 | tf_op jit(solution)/shard_map/ppermute | solution.py:389
  46.7 0.7 %collective-permute-start.19 = (bf16[208,128]{1,0:T(8,128)(2,1)S(1)}, bf16[208,128]{1,0:T(8,128)(2,1)S(1)}, u32[]{:S(2)}, u32[]{:S(2)}) collective-permute-start(bf16[208,128]{1,0:T(8,128)(2,1)S(1)} %get-tuple-element.67), channel_id=1, source_target_pairs={{0,3},{1,2},{2,1},{3,0},{4,7},{5,6},{6,5},{7,4},{8,11},{9,10},{10,... | collective-permute-start | bytes 159752 | tf_op jit(solution)/shard_map/ppermute | solution.py:389
  47.4 0.4 collective-permute-start.17
  47.9 2.2 %collective-permute-done.18.band = bf16[208,128]{1,0:T(8,128)(2,1)S(1)} collective-permute-done((bf16[208,128]{1,0:T(8,128)(2,1)S(1)}, bf16[208,128]{1,0:T(8,128)(2,1)S(1)}, u32[]{:S(2)}, u32[]{:S(2)}) %collective-permute-start.18) | collective-permute-done | bytes 53280 | tf_op jit(solution)/shard_map/ppermute | solution.py:389
  50.1 0.7 %collective-permute-done.19.both = bf16[208,128]{1,0:T(8,128)(2,1)S(1)} collective-permute-done((bf16[208,128]{1,0:T(8,128)(2,1)S(1)}, bf16[208,128]{1,0:T(8,128)(2,1)S(1)}, u32[]{:S(2)}, u32[]{:S(2)}) %collective-permute-start.19) | collective-permute-done | bytes 53280 | tf_op jit(solution)/shard_map/ppermute | solution.py:389
  50.8 2.6 %collective-permute-start.22 = (bf16[208,128]{1,0:T(8,128)(2,1)S(1)}, bf16[208,128]{1,0:T(8,128)(2,1)S(1)}, u32[]{:S(2)}, u32[]{:S(2)}) collective-permute-start(bf16[208,128]{1,0:T(8,128)(2,1)S(1)} %shard_map.93.rest_0_), channel_id=1, source_target_pairs={{0,12},{4,8},{8,4},{12,0},{1,13},{5,9},{9,5},{13,1},{2,14},{6,10},... | collective-permute-start | bytes 159752 | tf_op jit(solution)/shard_map/ppermute | solution.py:389
  53.4 1.8 %collective-permute-start.20 = (bf16[208,128]{1,0:T(8,128)(2,1)S(1)}, bf16[208,128]{1,0:T(8,128)(2,1)S(1)}, u32[]{:S(2)}, u32[]{:S(2)}) collective-permute-start(bf16[208,128]{1,0:T(8,128)(2,1)S(1)} %shard_map.93.rest_0_), channel_id=1, source_target_pairs={{0,4},{4,0},{8,12},{12,8},{1,5},{5,1},{9,13},{13,9},{2,6},{6,2},{1... | collective-permute-start | bytes 159752 | tf_op jit(solution)/shard_map/ppermute | solution.py:389
  55.2 1.9 %collective-permute-done.22.rest_3_ = bf16[208,128]{1,0:T(8,128)(2,1)S(1)} collective-permute-done((bf16[208,128]{1,0:T(8,128)(2,1)S(1)}, bf16[208,128]{1,0:T(8,128)(2,1)S(1)}, u32[]{:S(2)}, u32[]{:S(2)}) %collective-permute-start.22) | collective-permute-done | bytes 53280 | tf_op jit(solution)/shard_map/ppermute | solution.py:389
  57.1 1.7 %collective-permute-done.21.rest_2_ = bf16[208,128]{1,0:T(8,128)(2,1)S(1)} collective-permute-done((bf16[208,128]{1,0:T(8,128)(2,1)S(1)}, bf16[208,128]{1,0:T(8,128)(2,1)S(1)}, u32[]{:S(2)}, u32[]{:S(2)}) %collective-permute-start.21) | collective-permute-done | bytes 53280 | tf_op jit(solution)/shard_map/ppermute | solution.py:389
  58.8 1.5 %shard_map.94 = (f32[1536,128]{1,0:T(8,128)}, f32[64,96]{1,0:T(8,128)}) custom-call(f32[96,1024]{1,0:T(8,128)S(1)} %get-tuple-element.64.surface, f32[96,1024]{1,0:T(8,128)S(1)} %collective-permute-done.16.other, f32[96,128]{1,0:T(8,128)S(1)} %get-tuple-element.65.time_t, bf16[208,128]{1,0:T(8,128)(2,1)S(1)} %shard_map.93.rest_0_, ...), custom_call_target="tpu_custom_call" | custom-call | flops 1000000 | bytes 1000000 | tf_op jit(solution)/shard_map/pallas_call | solution.py:375
  (25 shorter events, 0.3 us)
Async XLA Ops:
  3.5 8.7 %collective-permute-start.1 = (bf16[528,128]{1,0:T(8,128)(2,1)S(1)}, bf16[528,128]{1,0:T(8,128)(2,1)S(1)}, u32[]{:S(2)}, u32[]{:S(2)}) collective-permute-start(bf16[528,128]{1,0:T(8,128)(2,1)S(1)} %get-tuple-element.43), channel_id=1, source_target_pairs={{0,4},{4,0},{8,12},{12,8},{1,5},{5,1},{9,13},{13,9},{2,6},{6,2},{1... | collective-permute-start | bytes 405512 | tf_op jit(solution)/shard_map/ppermute | solution.py:389
  6.6 12.6 %collective-permute-start.3 = (bf16[528,128]{1,0:T(8,128)(2,1)S(1)}, bf16[528,128]{1,0:T(8,128)(2,1)S(1)}, u32[]{:S(2)}, u32[]{:S(2)}) collective-permute-start(bf16[528,128]{1,0:T(8,128)(2,1)S(1)} %get-tuple-element.47), channel_id=1, source_target_pairs={{0,8},{4,12},{8,0},{12,4},{1,9},{5,13},{9,1},{13,5},{2,10},{6,14},... | collective-permute-start | bytes 405512 | tf_op jit(solution)/shard_map/ppermute | solution.py:389
  9.2 10.0 %collective-permute-start = (bf16[720,128]{1,0:T(8,128)(2,1)S(1)}, bf16[720,128]{1,0:T(8,128)(2,1)S(1)}, u32[]{:S(2)}, u32[]{:S(2)}) collective-permute-start(bf16[720,128]{1,0:T(8,128)(2,1)S(1)} %get-tuple-element.38), channel_id=1, source_target_pairs={{0,1},{1,0},{4,5},{5,4},{8,9},{9,8},{12,13},{13,12},{2,3},{3,2},{6... | collective-permute-start | bytes 552968 | tf_op jit(solution)/shard_map/ppermute | solution.py:389
  9.2 10.9 %collective-permute-start.4 = (bf16[544,128]{1,0:T(8,128)(2,1)S(1)}, bf16[544,128]{1,0:T(8,128)(2,1)S(1)}, u32[]{:S(2)}, u32[]{:S(2)}) collective-permute-start(bf16[544,128]{1,0:T(8,128)(2,1)S(1)} %get-tuple-element.48), channel_id=1, source_target_pairs={{0,12},{4,8},{8,4},{12,0},{1,13},{5,9},{9,5},{13,1},{2,14},{6,10},... | collective-permute-start | bytes 417800 | tf_op jit(solution)/shard_map/ppermute | solution.py:389
  9.2 10.9 %collective-permute-start.5 = (bf16[544,128]{1,0:T(8,128)(2,1)S(1)}, bf16[544,128]{1,0:T(8,128)(2,1)S(1)}, u32[]{:S(2)}, u32[]{:S(2)}) collective-permute-start(bf16[544,128]{1,0:T(8,128)(2,1)S(1)} %get-tuple-element.49), channel_id=1, source_target_pairs={{0,4},{4,0},{8,12},{12,8},{1,5},{5,1},{9,13},{13,9},{2,6},{6,2},{1... | collective-permute-start | bytes 417800 | tf_op jit(solution)/shard_map/ppermute | solution.py:389
  12.2 7.7 %copy-start = (f32[64,96]{1,0:T(8,128)S(1)}, f32[64,96]{1,0:T(8,128)}, u32[]{:S(2)}) copy-start(f32[64,96]{1,0:T(8,128)} %time_own.1) | copy-start | bytes 73732
  12.2 14.1 %collective-permute-start.2 = (bf16[528,128]{1,0:T(8,128)(2,1)S(1)}, bf16[528,128]{1,0:T(8,128)(2,1)S(1)}, u32[]{:S(2)}, u32[]{:S(2)}) collective-permute-start(bf16[528,128]{1,0:T(8,128)(2,1)S(1)} %get-tuple-element.46), channel_id=1, source_target_pairs={{0,9},{1,8},{4,13},{5,12},{8,1},{9,0},{12,5},{13,4},{2,11},{3,10},... | collective-permute-start | bytes 405512 | tf_op jit(solution)/shard_map/ppermute | solution.py:389
  19.2 7.2 %collective-permute-start.6 = (bf16[528,128]{1,0:T(8,128)(2,1)S(1)}, bf16[528,128]{1,0:T(8,128)(2,1)S(1)}, u32[]{:S(2)}, u32[]{:S(2)}) collective-permute-start(bf16[528,128]{1,0:T(8,128)(2,1)S(1)} %get-tuple-element.50), channel_id=1, source_target_pairs={{0,5},{1,4},{4,1},{5,0},{8,13},{9,12},{12,9},{13,8},{2,7},{3,6},{6... | collective-permute-start | bytes 405512 | tf_op jit(solution)/shard_map/ppermute | solution.py:389
  19.2 0.9 %collective-permute-start.7 = (f32[96,128]{1,0:T(8,128)S(1)}, f32[96,128]{1,0:T(8,128)S(1)}, u32[]{:S(2)}, u32[]{:S(2)}) collective-permute-start(f32[96,128]{1,0:T(8,128)S(1)} %get-tuple-element.52), channel_id=1, source_target_pairs={{1,2},{2,1},{5,6},{6,5},{9,10},{10,9},{13,14},{14,13},{17,18},{18,... | collective-permute-start | bytes 147464 | tf_op jit(solution)/shard_map/ppermute | solution.py:445
  27.5 6.3 %collective-permute-start.8 = (f32[200,128]{1,0:T(8,128)S(1)}, f32[200,128]{1,0:T(8,128)S(1)}, u32[]{:S(2)}, u32[]{:S(2)}) collective-permute-start(f32[200,128]{1,0:T(8,128)S(1)} %get-tuple-element.55), channel_id=1, source_target_pairs={{0,1},{1,0},{2,3},{3,2},{4,5},{5,4},{6,7},{7,6},{8,9},{9,8},{10,11... | collective-permute-start | bytes 307208 | tf_op jit(solution)/shard_map/ppermute | solution.py:389
  28.3 5.6 %collective-permute-start.9 = (f32[120,128]{1,0:T(8,128)S(1)}, f32[120,128]{1,0:T(8,128)S(1)}, u32[]{:S(2)}, u32[]{:S(2)}) collective-permute-start(f32[120,128]{1,0:T(8,128)S(1)} %get-tuple-element.54.mine), channel_id=1, source_target_pairs={{0,2},{2,0},{1,3},{3,1},{4,6},{6,4},{5,7},{7,5},{8,10},{10,8},{9,1... | collective-permute-start | bytes 184328 | tf_op jit(solution)/shard_map/ppermute | solution.py:389
  29.8 4.1 %collective-permute-start.10 = (f32[104,128]{1,0:T(8,128)S(1)}, f32[104,128]{1,0:T(8,128)S(1)}, u32[]{:S(2)}, u32[]{:S(2)}) collective-permute-start(f32[104,128]{1,0:T(8,128)S(1)} %get-tuple-element.56), channel_id=1, source_target_pairs={{0,3},{1,2},{2,1},{3,0},{4,7},{5,6},{6,5},{7,4},{8,11},{9,10},{10,... | collective-permute-start | bytes 159752 | tf_op jit(solution)/shard_map/ppermute | solution.py:389
  33.9 6.6 %collective-permute-start.13 = (f32[120,128]{1,0:T(8,128)S(1)}, f32[120,128]{1,0:T(8,128)S(1)}, u32[]{:S(2)}, u32[]{:S(2)}) collective-permute-start(f32[120,128]{1,0:T(8,128)S(1)} %get-tuple-element.57.rest_0_), channel_id=1, source_target_pairs={{0,12},{4,8},{8,4},{12,0},{1,13},{5,9},{9,5},{13,1},{2,14},{6,10},... | collective-permute-start | bytes 184328 | tf_op jit(solution)/shard_map/ppermute | solution.py:389
  36.5 5.9 %collective-permute-start.12 = (f32[120,128]{1,0:T(8,128)S(1)}, f32[120,128]{1,0:T(8,128)S(1)}, u32[]{:S(2)}, u32[]{:S(2)}) collective-permute-start(f32[120,128]{1,0:T(8,128)S(1)} %get-tuple-element.57.rest_0_), channel_id=1, source_target_pairs={{0,8},{4,12},{8,0},{12,4},{1,9},{5,13},{9,1},{13,5},{2,10},{6,14},... | collective-permute-start | bytes 184328 | tf_op jit(solution)/shard_map/ppermute | solution.py:389
  36.5 5.9 %collective-permute-start.11 = (f32[120,128]{1,0:T(8,128)S(1)}, f32[120,128]{1,0:T(8,128)S(1)}, u32[]{:S(2)}, u32[]{:S(2)}) collective-permute-start(f32[120,128]{1,0:T(8,128)S(1)} %get-tuple-element.57.rest_0_), channel_id=1, source_target_pairs={{0,4},{4,0},{8,12},{12,8},{1,5},{5,1},{9,13},{13,9},{2,6},{6,2},{1... | collective-permute-start | bytes 184328 | tf_op jit(solution)/shard_map/ppermute | solution.py:389
  38.3 4.2 %collective-permute-start.15 = (f32[96,128]{1,0:T(8,128)S(1)}, f32[96,128]{1,0:T(8,128)S(1)}, u32[]{:S(2)}, u32[]{:S(2)}) collective-permute-start(f32[96,128]{1,0:T(8,128)S(1)} %get-tuple-element.63), channel_id=1, source_target_pairs={{1,2},{2,1},{5,6},{6,5},{9,10},{10,9},{13,14},{14,13},{17,18},{18,... | collective-permute-start | bytes 147464 | tf_op jit(solution)/shard_map/ppermute | solution.py:445
  42.5 1.3 %collective-permute-start.14 = (f32[96,128]{1,0:T(8,128)S(1)}, f32[96,128]{1,0:T(8,128)S(1)}, u32[]{:S(2)}, u32[]{:S(2)}) collective-permute-start(f32[96,128]{1,0:T(8,128)S(1)} %get-tuple-element.58.time_own), channel_id=1, source_target_pairs={{0,1},{1,0},{2,3},{3,2},{4,5},{5,4},{6,7},{7,6},{8,9},{9,8},{10,11... | collective-permute-start | bytes 147464 | tf_op jit(solution)/shard_map/ppermute | solution.py:389
  45.5 13.3 %collective-permute-start.16 = (f32[96,1024]{1,0:T(8,128)S(1)}, f32[96,1024]{1,0:T(8,128)S(1)}, u32[]{:S(2)}, u32[]{:S(2)}) collective-permute-start(f32[96,1024]{1,0:T(8,128)S(1)} %get-tuple-element.64.surface), channel_id=1, source_target_pairs={{0,1},{1,0},{2,3},{3,2},{4,5},{5,4},{6,7},{7,6},{8,9},{9,8},{10,11... | collective-permute-start | bytes 1179656 | tf_op jit(solution)/shard_map/ppermute | solution.py:389
  45.7 4.4 %collective-permute-start.18 = (bf16[208,128]{1,0:T(8,128)(2,1)S(1)}, bf16[208,128]{1,0:T(8,128)(2,1)S(1)}, u32[]{:S(2)}, u32[]{:S(2)}) collective-permute-start(bf16[208,128]{1,0:T(8,128)(2,1)S(1)} %get-tuple-element.66.mine), channel_id=1, source_target_pairs={{0,2},{2,0},{1,3},{3,1},{4,6},{6,4},{5,7},{7,5},{8,10},{10,8},{9,1... | collective-permute-start | bytes 159752 | tf_op jit(solution)/shard_map/ppermute | solution.py:389
  46.7 4.0 %collective-permute-start.19 = (bf16[208,128]{1,0:T(8,128)(2,1)S(1)}, bf16[208,128]{1,0:T(8,128)(2,1)S(1)}, u32[]{:S(2)}, u32[]{:S(2)}) collective-permute-start(bf16[208,128]{1,0:T(8,128)(2,1)S(1)} %get-tuple-element.67), channel_id=1, source_target_pairs={{0,3},{1,2},{2,1},{3,0},{4,7},{5,6},{6,5},{7,4},{8,11},{9,10},{10,... | collective-permute-start | bytes 159752 | tf_op jit(solution)/shard_map/ppermute | solution.py:389
  47.4 3.3 %collective-permute-start.17 = (bf16[208,128]{1,0:T(8,128)(2,1)S(1)}, bf16[208,128]{1,0:T(8,128)(2,1)S(1)}, u32[]{:S(2)}, u32[]{:S(2)}) collective-permute-start(bf16[208,128]{1,0:T(8,128)(2,1)S(1)} %get-tuple-element.67), channel_id=1, source_target_pairs={{0,1},{1,0},{2,3},{3,2},{4,5},{5,4},{6,7},{7,6},{8,9},{9,8},{10,11... | collective-permute-start | bytes 159752 | tf_op jit(solution)/shard_map/ppermute | solution.py:389
  50.8 6.3 %collective-permute-start.22 = (bf16[208,128]{1,0:T(8,128)(2,1)S(1)}, bf16[208,128]{1,0:T(8,128)(2,1)S(1)}, u32[]{:S(2)}, u32[]{:S(2)}) collective-permute-start(bf16[208,128]{1,0:T(8,128)(2,1)S(1)} %shard_map.93.rest_0_), channel_id=1, source_target_pairs={{0,12},{4,8},{8,4},{12,0},{1,13},{5,9},{9,5},{13,1},{2,14},{6,10},... | collective-permute-start | bytes 159752 | tf_op jit(solution)/shard_map/ppermute | solution.py:389
  53.4 5.4 %collective-permute-start.21 = (bf16[208,128]{1,0:T(8,128)(2,1)S(1)}, bf16[208,128]{1,0:T(8,128)(2,1)S(1)}, u32[]{:S(2)}, u32[]{:S(2)}) collective-permute-start(bf16[208,128]{1,0:T(8,128)(2,1)S(1)} %shard_map.93.rest_0_), channel_id=1, source_target_pairs={{0,8},{4,12},{8,0},{12,4},{1,9},{5,13},{9,1},{13,5},{2,10},{6,14},... | collective-permute-start | bytes 159752 | tf_op jit(solution)/shard_map/ppermute | solution.py:389
  53.4 5.4 %collective-permute-start.20 = (bf16[208,128]{1,0:T(8,128)(2,1)S(1)}, bf16[208,128]{1,0:T(8,128)(2,1)S(1)}, u32[]{:S(2)}, u32[]{:S(2)}) collective-permute-start(bf16[208,128]{1,0:T(8,128)(2,1)S(1)} %shard_map.93.rest_0_), channel_id=1, source_target_pairs={{0,4},{4,0},{8,12},{12,8},{1,5},{5,1},{9,13},{13,9},{2,6},{6,2},{1... | collective-permute-start | bytes 159752 | tf_op jit(solution)/shard_map/ppermute | solution.py:389

commit v11 on v10

--- a/solution.py
+++ b/solution.py
@@ -16,6 +16,7 @@
 F32 = jnp.float32
 BF16 = jnp.bfloat16
 LANES = 128
+WIDTH = 512
 TAIL = 16
 COLS = 16
 NORM = 8
@@ -31,7 +32,7 @@
 def route_kernel(half, sends, paired, list_hbm, count_hbm, target_hbm, swath_hbm, mask_hbm, space_hbm, time_hbm, *rest):
     outs, rest = rest[: len(sends)], rest[len(sends):]
     surface, edge_near, edge_far, cols, rest = *rest[:4], rest[4:]
-    list_ref, count_ref, target_ref, swath_ref, mask_ref, space_ref, time_ref, place, total, seen, flip, arrived = rest
+    list_ref, count_ref, target_ref, swath_ref, mask_ref, space_ref, time_ref, place, total, seen, arrived = rest
     me, core = lax.axis_index("lon"), lax.axis_index("ta")
     n_lon = list_ref.shape[1]
     slots, days, cells = swath_ref.shape
@@ -101,11 +102,19 @@
     return surface[:, row * LANES:(row + 1) * LANES]
 
 
-def column_as_row(column, flip):
-    rank = column.shape[0]
-    flip[...] = jnp.zeros(flip.shape, F32)
-    flip[:rank, :] = jnp.broadcast_to(column, (rank, LANES))
-    return flip[...].T[:NORM, :]
+def diagonal(value, rank):
+    row = lax.broadcasted_iota(jnp.int32, (rank, LANES), 0)
+    lane = lax.broadcasted_iota(jnp.int32, (rank, LANES), 1)
+    return jnp.where(row == lane, value, 0.0)
+
+
+def column_as_row(column):
+    row = jnp.sum(diagonal(column, column.shape[0]), axis=0, keepdims=True)
+    return jnp.broadcast_to(row, (NORM, LANES))
+
+
+def row_as_column(row, rank):
+    return jnp.sum(diagonal(row, rank), axis=1, keepdims=True)
 
 
 def border(surface, half):
@@ -115,22 +124,16 @@
     return dot((lane == pick_lane).astype(BF16), surface.astype(BF16), (1, 1))
 
 
-def rows_as_columns(rows, rank, flip):
-    flip[...] = jnp.zeros(flip.shape, F32)
-    flip[: rows.shape[0], :] = rows
-    return flip[...].T[:rank, :]
-
-
-def smoothed(surface, half, above, below, left_cols, right_cols):
+def smoothed(surface, half, above, below, sides):
     lane = lax.broadcasted_iota(jnp.int32, above.shape, 1)
     strips = []
     for row in range(half):
         here = row_of(surface, row)
         up = above if row == 0 else row_of(surface, row - 1)
         down = below if row == half - 1 else row_of(surface, row + 1)
-        left = jnp.where(lane == 0, left_cols[:, half + row:half + row + 1], pltpu.roll(here, 1, 1))
-        right = jnp.where(lane == LANES - 1, right_cols[:, row:row + 1], pltpu.roll(here, LANES - 1, 1))
-        lap = 4.0 * here - (up + down + left + right)
+        left = jnp.where(lane == 0, 0.0, pltpu.roll(here, 1, 1))
+        right = jnp.where(lane == LANES - 1, 0.0, pltpu.roll(here, LANES - 1, 1))
+        lap = 4.0 * here - (up + down + left + right + row_of(sides, row))
         strips.append(here - (ETA_SPACE * SMOOTH) * lap)
     return strips
 
@@ -155,16 +158,20 @@
         predicted[:, at:at + 2 * LANES] = dot(time_bf, packed[:, at:at + 2 * LANES], (1, 0))
 
 
-def smooth(half, odd, surface, edge_near, edge_far, cols_a, cols_b, scale, base, flip):
+def smooth(half, odd, surface, edge_near, edge_far, cols_a, cols_b, scale, base):
     core = lax.axis_index("ta")
     rank = surface.shape[0]
     above = pick(core == 0, edge_far, edge_near)
     below = pick(core == 0, edge_near, edge_far)
-    left = rows_as_columns(pick(odd, cols_a, cols_b), rank, flip)
-    right = rows_as_columns(pick(odd, cols_b, cols_a), rank, flip)
+    cols = jnp.concatenate([pick(odd, cols_a, cols_b), pick(odd, cols_b, cols_a)], axis=0)
+    line = lax.broadcasted_iota(jnp.int32, (2 * COLS, half * LANES), 0)
+    lane = lax.broadcasted_iota(jnp.int32, (2 * COLS, half * LANES), 1)
+    from_left = (line >= half) & (line < 2 * half) & (lane == (line - half) * LANES)
+    from_right = (line >= COLS) & (line < COLS + half) & (lane == (line - COLS) * LANES + LANES - 1)
+    sides = dot(cols[:, :rank].astype(BF16), (from_left | from_right).astype(BF16), (0, 0))
     if scale is not None:
-        above, below, left, right = above * scale, below * scale, left * scale, right * scale
-    for row, strip in enumerate(smoothed(surface, half, above, below, left, right)):
+        above, below, sides = above * scale, below * scale, sides * scale
+    for row, strip in enumerate(smoothed(surface, half, above, below, sides)):
         base[:, row * LANES:(row + 1) * LANES] = strip
 
 
@@ -173,10 +180,10 @@
     time_bf = time_t.astype(BF16)
     time_twice = jnp.concatenate([time_bf, time_bf], axis=1)
     seen_bf = seen.astype(BF16)
-    width = 2 * LANES
+    width = WIDTH
     owner = lax.broadcasted_iota(jnp.int32, (TAIL, width), 0)
     lane = lax.broadcasted_iota(jnp.int32, (TAIL, width), 1)
-    grad_time = jnp.zeros((rank, width), F32)
+    grad_time = jnp.zeros((rank, 2 * LANES), F32)
     grad_diag = jnp.zeros((rank, LANES), F32)
     norm = jnp.zeros((rank, 1), F32)
     for at in range(0, half * LANES, width):
@@ -200,22 +207,21 @@
     return grad_time[:, :LANES] + grad_time[:, LANES:], grad_diag, norm
 
 
-def post_own(half, sums, fresh, message, crossing, outgoing, edge_far, flip):
+def post_own(half, sums, fresh, message, crossing, edge_near, edge_far):
     grad_time, grad_diag, norm = sums
     core = lax.axis_index("ta")
     rank = norm.shape[0]
     days = LANES // 2
     own = lax.broadcasted_iota(jnp.int32, grad_time.shape, 1) < days
-    last = column_as_row(norm, flip)
+    last = column_as_row(norm)
     message[:rank, :] = jnp.where(own, grad_time, pltpu.roll(grad_diag, days, 1))
     message[rank:rank + NORM, :] = last
     message[rank + NORM:, :] = jnp.zeros((COLS, LANES), F32)
     message[rank + NORM:, :rank] = border(fresh[...], half)
-    for out in (crossing, outgoing):
-        out[:rank, :] = jnp.where(own, pltpu.roll(grad_time, days, 1), grad_diag)
-        out[rank:rank + NORM, :] = last
+    crossing[:rank, :] = jnp.where(own, pltpu.roll(grad_time, days, 1), grad_diag)
+    crossing[rank:, :] = last
     first_row, last_row = fresh[:, :LANES], fresh[:, (half - 1) * LANES:]
-    outgoing[rank + NORM:, :] = pick(core == 0, last_row, first_row)
+    edge_near[...] = pick(core == 0, last_row, first_row)
     edge_far[...] = pick(core == 0, first_row, last_row)
 
 
@@ -230,10 +236,10 @@
     return jnp.concatenate([value[: 2 * rank, :], value[2 * rank:2 * rank + NORM, :] + value[2 * rank + NORM:, :]], axis=0)
 
 
-def post_all(sums, message, outgoing, flip):
+def post_all(sums, message, outgoing):
     grad_time, grad_diag, norm = sums
     rank = norm.shape[0]
-    last = column_as_row(norm, flip)
+    last = column_as_row(norm)
     for out, shift in ((message, 0), (outgoing, LANES // 2)):
         parts = [pltpu.roll(part, shift, 1) if shift else part for part in (grad_time, grad_diag)]
         out[: 2 * rank, :], out[2 * rank:, :] = narrow(jnp.concatenate([*parts, last], axis=0), rank)
@@ -247,8 +253,8 @@
         cols = [pieces[0, step][at:, :].astype(F32) for step in (1, 3)]
     else:
         cols, rest = [ref[...] for ref in rest[:2]], rest[2:]
-    fresh, message, crossing, outgoing, edge_far, summed, seen, flip, base = rest
-    smooth(half, swap(), surface[...], edge_near[...], edge_far_in[...], *cols, None, base, flip)
+    fresh, message, crossing, edge_out, edge_far, summed, seen, base = rest
+    smooth(half, swap(), surface[...], edge_near[...], edge_far_in[...], *cols, None, base)
     sides = [[pieces[key] for key in sorted(pieces) if key[0] == side] for side in (0, 1)]
 
     def add_up(parts, rows):
@@ -263,7 +269,7 @@
     near, far = (add_up(parts, slice(half * days, half * days + TAIL)) for parts in sides)
     seen[...] = near + pltpu.roll(far, days, 1)
     sums = gradients(half, base, predicted, packed, time_t[...], seen[...], summed, fresh)
-    post_own(half, sums, fresh, message, crossing, outgoing, edge_far, flip)
+    post_own(half, sums, fresh, message, crossing, edge_out, edge_far)
 
 
 def total_of(parts):
@@ -285,9 +291,9 @@
     norm[...] = total[rank:rank + NORM, :]
 
 
-def rescaling(counts, norm, time_new, flip):
+def rescaling(counts, norm, time_new):
     day_count, cell_count = counts
-    space_sq = rows_as_columns(norm, time_new.shape[0], flip)[:, :1]
+    space_sq = row_as_column(norm[:1, :], time_new.shape[0])
     square = time_new * time_new
     time_sq = 0.5 * jnp.sum(square + pltpu.roll(square, LANES // 2, 1), axis=1, keepdims=True)
     ratio = (time_sq / day_count + EPSILON) / (space_sq / cell_count + EPSILON)
@@ -295,21 +301,21 @@
 
 
 def second_kernel(half, counts, swap, surface, time_own, time_other, norm, summed, seen, edge_near, edge_far, cols_a, cols_b, *rest):
-    fresh, time_out, message, outgoing, flip, scaled, base, predicted, packed = rest
+    fresh, time_out, message, outgoing, scaled, base, predicted, packed = rest
     rank = surface.shape[0]
     time_new = time_own[...] + pltpu.roll(time_other[...], LANES // 2, 1)
-    scale = rescaling(counts, norm[...], time_new, flip)
+    scale = rescaling(counts, norm[...], time_new)
     time_now = time_new / scale
     time_out[...] = time_now
     scaled[...] = surface[...] * scale
     packed[...] = scaled[...].astype(BF16)
-    time_bf = time_now.T.astype(BF16)
-    for at in range(0, half * LANES, 2 * LANES):
-        predicted[:, at:at + 2 * LANES] = dot(time_bf, packed[:, at:at + 2 * LANES], (1, 0))
+    time_bf = time_now.astype(BF16)
+    for at in range(0, half * LANES, WIDTH):
+        predicted[:, at:at + WIDTH] = dot(time_bf, packed[:, at:at + WIDTH], (0, 0))
     cols = [ref[ref.shape[0] - COLS:, :] for ref in (cols_a, cols_b)]
-    smooth(half, swap(), scaled[...], edge_near[...], edge_far[...], *cols, scale, base, flip)
+    smooth(half, swap(), scaled[...], edge_near[...], edge_far[...], *cols, scale, base)
     sums = gradients(half, base, predicted, packed, time_now, seen[...], summed, fresh)
-    post_all(sums, message, outgoing, flip)
+    post_all(sums, message, outgoing)
 
 
 def last_kernel(half, counts, n_parts, surface, other, time_t, *rest):
@@ -322,7 +328,7 @@
     if parts[0].dtype == BF16:
         total = widened(total, rank)
     time_new = time_t[...] - total[:rank, :] / (total[rank:2 * rank, :] + RIDGE)
-    scale = rescaling(counts, total[2 * rank:, :], time_new, flip)
+    scale = rescaling(counts, total[2 * rank:, :], time_new)
     flip[...] = jnp.zeros(flip.shape, F32)
     flip[:rank, :] = time_new / scale
     time_out[...] = flip[...].T[: time_out.shape[0], :rank]
@@ -342,11 +348,10 @@
     total[...] = mine[...] + theirs[...]
 
 
-def own_sum_kernel(mine, core, band, both, total, beside):
+def own_sum_kernel(mine, core, band, both, total):
     rows = both.shape[0]
-    total[:rows, :] = (mine[:rows, :] + core[:rows, :]) + (band[:rows, :] + both[...])
+    total[:rows, :] = (mine[:rows, :] + core[...]) + (band[:rows, :] + both[...])
     total[rows:, :] = mine[rows:, :]
-    beside[...] = core[rows:, :]
 
 
 def all_sum_kernel(rank, mine, core, band, both, total):
@@ -420,7 +425,6 @@
             pltpu.SMEM((slots + 1,), jnp.int32),
             pltpu.VMEM((2 * n_lon * half, days, cells), F32),
             pltpu.VMEM((2 * n_lon * half + TAIL, LANES), F32),
-            flip,
             pltpu.SemaphoreType.DMA((len(operands) - 1 + SWATH_COPIES,)),
         ],
         hbm=len(operands),
@@ -460,10 +464,10 @@
     )(surface, factor_time, pieces[1, 0])
 
     fresh, edge = shape((rank, wide)), shape((rank, LANES))
-    surface, message, crossing, outgoing, edge_far, summed, seen = call(
+    surface, message, crossing, edge_near, edge_far, summed, seen = call(
         functools.partial(first_kernel, half, days, order, paired, swap),
-        [fresh, shape((own_rows + COLS, LANES)), shape((own_rows, LANES)), shape((own_rows + rank, LANES)), edge, shape((2 * days, wide)), shape((TAIL, LANES))],
-        [flip, pltpu.VMEM((rank, wide), F32)],
+        [fresh, shape((own_rows + COLS, LANES)), shape((own_rows, LANES)), edge, edge, shape((2 * days, wide)), shape((TAIL, LANES))],
+        [pltpu.VMEM((rank, wide), F32)],
     )(surface, edge_near, predicted, packed, time_t, *[pieces[key] for key in order], bands(edge_far), *(() if paired else columns(cols)))
 
     narrowed = shape((sum_rows + NORM, LANES), BF16)
@@ -485,7 +489,7 @@
     def around(mine, core, both):
         return mine, across(core, "ta", 1), across(mine, "lat", 1), across(both, ("lat", "ta"), 3)
 
-    total, edge_near = call(own_sum_kernel, [shape(message.shape), edge])(*around(message, outgoing, crossing))
+    total = call(own_sum_kernel, shape(message.shape))(*around(message, crossing, crossing))
     parts = over_lon(doubled(total, "lat", 2))
     cols = (parts[1], parts[3]) if paired else columns(message[own_rows:])
     time_own, norm = call(functools.partial(own_kernel, len(parts)), [edge, shape((NORM, LANES))])(time_t, *parts)
@@ -493,8 +497,8 @@
     surface, time_t, message, outgoing = call(
         functools.partial(second_kernel, half, counts, swap),
         [fresh, edge, narrowed, narrowed],
-        [flip, pltpu.VMEM((rank, wide), F32), pltpu.VMEM((rank, wide), F32), pltpu.VMEM((2 * days, wide), F32), pltpu.VMEM((rank, wide), BF16)],
-    )(surface, time_own, across(time_own, "ta", 1), norm, summed, seen, edge_near, bands(edge_far), *cols)
+        [pltpu.VMEM((rank, wide), F32), pltpu.VMEM((rank, wide), F32), pltpu.VMEM((2 * days, wide), F32), pltpu.VMEM((rank, wide), BF16)],
+    )(surface, time_own, across(time_own, "ta", 1), norm, summed, seen, across(edge_near, "ta", 1), bands(edge_far), *cols)
 
     other = across(surface, "ta", 1)
     total = narrowed if paired and n_lat == 2 else shape((sum_rows, LANES))

time: 60.5 us -> 59.5 us (0.983)
  Pallas kernels: 7.69 us -> 7.08 us
    pallas_call x9, Pallas kernels: 7.69 us -> 7.08 us  [run(): pl.pallas_call(kernel, out_shape=out_shape, in_specs=[pl.BlockSpec(memory...]
    ppermute x21 -> x22, waiting for transfers between devices: 29.4 us -> 28.8 us  [across(): lax.ppermute(value, axis, [(i, i ^ step) for i in range(lax.axis_size(axi...]
    ppermute x21 -> x22, starting transfers between devices: 21.1 us -> 21.3 us  [across(): lax.ppermute(value, axis, [(i, i ^ step) for i in range(lax.axis_size(axi...]
  transfers between devices with their start and end apart: 23 -> 24, of which waited for: 11 -> 11; matrix products, arithmetic and copies ran while one was open for 0% -> 0% of each run, Pallas kernels for 1% -> 1%
where the time goes in v11:
time: 59.5 us; the launch traced here: 59.3 us
  waiting for transfers between devices  28.9 us (49%)
  starting transfers between devices  22.6 us (38%)
  Pallas kernels  7.08 us (12%)
  between operations  0.74 us (1%)
    ppermute x22, waiting for transfers between devices, across(): lax.ppermute(value, axis, [(i, i ^ step) for i in range(lax.axis_size(axi...  28.8 us
    ppermute x22, starting transfers between devices, across(): lax.ppermute(value, axis, [(i, i ^ step) for i in range(lax.axis_size(axi...  21.3 us
    pallas_call x9, Pallas kernels, run(): pl.pallas_call(kernel, out_shape=out_shape, in_specs=[pl.BlockSpec(memory...  7.08 us
    ppermute x2, starting transfers between devices, bands(): return lax.ppermute(edge, ('lat', 'ta'), there + [(b, a) for a, b in there])  1.31 us
  transfers between devices with their start and end apart: 24, of which 11 were waited for; matrix products, arithmetic and copies ran while one was open for 0% of the time, Pallas kernels for 1%

profile of v11, /device:TPU:0, one launch (start us, length us, event | category | flops | bytes accessed | tf_op | source)
XLA Modules:
  0.0 59.3 jit_solution(18432642020582968477)
XLA Ops:
  0.6 2.8 %shard_map.86 = (bf16[528,128]{1,0:T(8,128)(2,1)S(1)}, bf16[528,128]{1,0:T(8,128)(2,1)S(1)}, bf16[528,128]{1,0:T(8,128)(2,1)S(1)}, bf16[544,128]{1,0:T(8,128)(2,...) custom-call(s32[1,4,32]{2,1,0:T(4,128)} %list_hbm.1, ...), custom_call_target="tpu_custom_call" | custom-call | flops 1000000 | bytes 1000000 | tf_op jit(solution)/shard_map/pallas_call | solution.py:380
  3.5 3.1 %collective-permute-start.1 = (bf16[528,128]{1,0:T(8,128)(2,1)S(1)}, bf16[528,128]{1,0:T(8,128)(2,1)S(1)}, u32[]{:S(2)}, u32[]{:S(2)}) collective-permute-start(bf16[528,128]{1,0:T(8,128)(2,1)S(1)} %get-tuple-element.41), channel_id=1, source_target_pairs={{0,4},{4,0},{8,12},{12,8},{1,5},{5,1},{9,13},{13,9},{2,6},{6,2},{1... | collective-permute-start | bytes 405512 | tf_op jit(solution)/shard_map/ppermute | solution.py:394
  6.6 2.6 %collective-permute-start.3 = (bf16[528,128]{1,0:T(8,128)(2,1)S(1)}, bf16[528,128]{1,0:T(8,128)(2,1)S(1)}, u32[]{:S(2)}, u32[]{:S(2)}) collective-permute-start(bf16[528,128]{1,0:T(8,128)(2,1)S(1)} %get-tuple-element.45), channel_id=1, source_target_pairs={{0,8},{4,12},{8,0},{12,4},{1,9},{5,13},{9,1},{13,5},{2,10},{6,14},... | collective-permute-start | bytes 405512 | tf_op jit(solution)/shard_map/ppermute | solution.py:394
  9.2 0.9 %collective-permute-start.5 = (bf16[544,128]{1,0:T(8,128)(2,1)S(1)}, bf16[544,128]{1,0:T(8,128)(2,1)S(1)}, u32[]{:S(2)}, u32[]{:S(2)}) collective-permute-start(bf16[544,128]{1,0:T(8,128)(2,1)S(1)} %get-tuple-element.47), channel_id=1, source_target_pairs={{0,4},{4,0},{8,12},{12,8},{1,5},{5,1},{9,13},{13,9},{2,6},{6,2},{1... | collective-permute-start | bytes 417800 | tf_op jit(solution)/shard_map/ppermute | solution.py:394
  10.1 2.1 %collective-permute-done.1.theirs = bf16[528,128]{1,0:T(8,128)(2,1)S(1)} collective-permute-done((bf16[528,128]{1,0:T(8,128)(2,1)S(1)}, bf16[528,128]{1,0:T(8,128)(2,1)S(1)}, u32[]{:S(2)}, u32[]{:S(2)}) %collective-permute-start.1) | collective-permute-done | bytes 135200 | tf_op jit(solution)/shard_map/ppermute | solution.py:394
  12.2 1.0 %collective-permute-start.2 = (bf16[528,128]{1,0:T(8,128)(2,1)S(1)}, bf16[528,128]{1,0:T(8,128)(2,1)S(1)}, u32[]{:S(2)}, u32[]{:S(2)}) collective-permute-start(bf16[528,128]{1,0:T(8,128)(2,1)S(1)} %get-tuple-element.44), channel_id=1, source_target_pairs={{0,9},{1,8},{4,13},{5,12},{8,1},{9,0},{12,5},{13,4},{2,11},{3,10},... | collective-permute-start | bytes 405512 | tf_op jit(solution)/shard_map/ppermute | solution.py:394
  13.2 6.0 %collective-permute-done.3.rest_1_ = bf16[528,128]{1,0:T(8,128)(2,1)S(1)} collective-permute-done((bf16[528,128]{1,0:T(8,128)(2,1)S(1)}, bf16[528,128]{1,0:T(8,128)(2,1)S(1)}, u32[]{:S(2)}, u32[]{:S(2)}) %collective-permute-start.3) | collective-permute-done | bytes 135200 | tf_op jit(solution)/shard_map/ppermute | solution.py:394
  19.2 0.7 %collective-permute-start.7 = (f32[96,128]{1,0:T(8,128)S(1)}, f32[96,128]{1,0:T(8,128)S(1)}, u32[]{:S(2)}, u32[]{:S(2)}) collective-permute-start(f32[96,128]{1,0:T(8,128)S(1)} %get-tuple-element.50), channel_id=1, source_target_pairs={{1,2},{2,1},{5,6},{6,5},{9,10},{10,9},{13,14},{14,13},{17,18},{18,... | collective-permute-start | bytes 147464 | tf_op jit(solution)/shard_map/ppermute | solution.py:449
  19.9 0.2 shard_map.87
  20.1 6.2 %collective-permute-done.2.rest_0_ = bf16[528,128]{1,0:T(8,128)(2,1)S(1)} collective-permute-done((bf16[528,128]{1,0:T(8,128)(2,1)S(1)}, bf16[528,128]{1,0:T(8,128)(2,1)S(1)}, u32[]{:S(2)}, u32[]{:S(2)}) %collective-permute-start.2) | collective-permute-done | bytes 135200 | tf_op jit(solution)/shard_map/ppermute | solution.py:394
  26.3 1.1 %shard_map.89 = (f32[96,1024]{1,0:T(8,128)S(1)}, f32[120,128]{1,0:T(8,128)S(1)}, f32[104,128]{1,0:T(8,128)S(1)}, f32[96,128]{1,0:T(8,128)S(1)}, f32[96,128]{1,0:...) custom-call(f32[96,1024]{1,0:T(8,128)S(1)} %get-tuple-element.34.surface, ...), custom_call_target="tpu_custom_call" | custom-call | flops 1000000 | bytes 1000000 | tf_op jit(solution)/shard_map/pallas_call | solution.py:380
  27.5 1.6 %collective-permute-start.9 = (f32[120,128]{1,0:T(8,128)S(1)}, f32[120,128]{1,0:T(8,128)S(1)}, u32[]{:S(2)}, u32[]{:S(2)}) collective-permute-start(f32[120,128]{1,0:T(8,128)S(1)} %get-tuple-element.52.mine), channel_id=1, source_target_pairs={{0,2},{2,0},{1,3},{3,1},{4,6},{6,4},{5,7},{7,5},{8,10},{10,8},{9,1... | collective-permute-start | bytes 184328 | tf_op jit(solution)/shard_map/ppermute | solution.py:394
  29.0 0.6 collective-permute-start.10
  29.7 3.2 %collective-permute-done.10.both = f32[104,128]{1,0:T(8,128)S(1)} collective-permute-done((f32[104,128]{1,0:T(8,128)S(1)}, f32[104,128]{1,0:T(8,128)S(1)}, u32[]{:S(2)}, u32[]{:S(2)}) %collective-permute-start.10) | collective-permute-done | bytes 53280 | tf_op jit(solution)/shard_map/ppermute | solution.py:394
  32.9 2.4 %collective-permute-start.13 = (f32[120,128]{1,0:T(8,128)S(1)}, f32[120,128]{1,0:T(8,128)S(1)}, u32[]{:S(2)}, u32[]{:S(2)}) collective-permute-start(f32[120,128]{1,0:T(8,128)S(1)} %shard_map.90.rest_0_), channel_id=1, source_target_pairs={{0,12},{4,8},{8,4},{12,0},{1,13},{5,9},{9,5},{13,1},{2,14},{6,10},... | collective-permute-start | bytes 184328 | tf_op jit(solution)/shard_map/ppermute | solution.py:394
  35.3 2.0 %collective-permute-start.11 = (f32[120,128]{1,0:T(8,128)S(1)}, f32[120,128]{1,0:T(8,128)S(1)}, u32[]{:S(2)}, u32[]{:S(2)}) collective-permute-start(f32[120,128]{1,0:T(8,128)S(1)} %shard_map.90.rest_0_), channel_id=1, source_target_pairs={{0,4},{4,0},{8,12},{12,8},{1,5},{5,1},{9,13},{13,9},{2,6},{6,2},{1... | collective-permute-start | bytes 184328 | tf_op jit(solution)/shard_map/ppermute | solution.py:394
  37.3 0.7 %collective-permute-start.16 = (f32[96,128]{1,0:T(8,128)S(1)}, f32[96,128]{1,0:T(8,128)S(1)}, u32[]{:S(2)}, u32[]{:S(2)}) collective-permute-start(f32[96,128]{1,0:T(8,128)S(1)} %get-tuple-element.59), channel_id=1, source_target_pairs={{1,2},{2,1},{5,6},{6,5},{9,10},{10,9},{13,14},{14,13},{17,18},{18,... | collective-permute-start | bytes 147464 | tf_op jit(solution)/shard_map/ppermute | solution.py:449
  38.0 1.6 %collective-permute-done.13.rest_3_.cols_b = f32[120,128]{1,0:T(8,128)S(1)} collective-permute-done((f32[120,128]{1,0:T(8,128)S(1)}, f32[120,128]{1,0:T(8,128)S(1)}, u32[]{:S(2)}, u32[]{:S(2)}) %collective-permute-start.13) | collective-permute-done | bytes 61472 | tf_op jit(solution)/shard_map/ppermute | solution.py:394
  39.6 1.9 %collective-permute-done.12.rest_2_ = f32[120,128]{1,0:T(8,128)S(1)} collective-permute-done((f32[120,128]{1,0:T(8,128)S(1)}, f32[120,128]{1,0:T(8,128)S(1)}, u32[]{:S(2)}, u32[]{:S(2)}) %collective-permute-start.12) | collective-permute-done | bytes 61472 | tf_op jit(solution)/shard_map/ppermute | solution.py:394
  41.7 1.2 %collective-permute-done.14.time_other = f32[96,128]{1,0:T(8,128)S(1)} collective-permute-done((f32[96,128]{1,0:T(8,128)S(1)}, f32[96,128]{1,0:T(8,128)S(1)}, u32[]{:S(2)}, u32[]{:S(2)}) %collective-permute-start.14) | collective-permute-done | bytes 49184 | tf_op jit(solution)/shard_map/ppermute | solution.py:394
  42.9 1.3 %shard_map.92 = (f32[96,1024]{1,0:T(8,128)S(1)}, f32[96,128]{1,0:T(8,128)S(1)}, bf16[208,128]{1,0:T(8,128)(2,1)S(1)}, bf16[208,128]{1,0:T(8,128)(2,1)S(1)}) custom-call(f32[96,1024]{1,0:T(8,128)S(1)} %get-tuple-element.51.surface, f32[96,128]{1,0:T(8,128)S(1)} %get-tuple-element.54.time_own, f32[96,128]{1,0:T(8,128)S(1)} %collective-permute-done.14.time_other, ...), custom_call_target="tpu_custom_call" | custom-call | flops 1000000 | bytes 1000000 | tf_op jit(solution)/shard_map/pallas_call | solution.py:380
  44.2 0.4 collective-permute-start.17
  44.6 1.3 %collective-permute-start.19 = (bf16[208,128]{1,0:T(8,128)(2,1)S(1)}, bf16[208,128]{1,0:T(8,128)(2,1)S(1)}, u32[]{:S(2)}, u32[]{:S(2)}) collective-permute-start(bf16[208,128]{1,0:T(8,128)(2,1)S(1)} %get-tuple-element.62.mine), channel_id=1, source_target_pairs={{0,2},{2,0},{1,3},{3,1},{4,6},{6,4},{5,7},{7,5},{8,10},{10,8},{9,1... | collective-permute-start | bytes 159752 | tf_op jit(solution)/shard_map/ppermute | solution.py:394
  45.9 0.2 collective-permute-start.20
  46.2 0.6 collective-permute-start.18
  46.7 2.0 %collective-permute-done.19.band = bf16[208,128]{1,0:T(8,128)(2,1)S(1)} collective-permute-done((bf16[208,128]{1,0:T(8,128)(2,1)S(1)}, bf16[208,128]{1,0:T(8,128)(2,1)S(1)}, u32[]{:S(2)}, u32[]{:S(2)}) %collective-permute-start.19) | collective-permute-done | bytes 53280 | tf_op jit(solution)/shard_map/ppermute | solution.py:394
  48.7 1.1 %collective-permute-done.20.both = bf16[208,128]{1,0:T(8,128)(2,1)S(1)} collective-permute-done((bf16[208,128]{1,0:T(8,128)(2,1)S(1)}, bf16[208,128]{1,0:T(8,128)(2,1)S(1)}, u32[]{:S(2)}, u32[]{:S(2)}) %collective-permute-start.20) | collective-permute-done | bytes 53280 | tf_op jit(solution)/shard_map/ppermute | solution.py:394
  49.9 2.6 %collective-permute-start.23 = (bf16[208,128]{1,0:T(8,128)(2,1)S(1)}, bf16[208,128]{1,0:T(8,128)(2,1)S(1)}, u32[]{:S(2)}, u32[]{:S(2)}) collective-permute-start(bf16[208,128]{1,0:T(8,128)(2,1)S(1)} %shard_map.93.rest_0_), channel_id=1, source_target_pairs={{0,12},{4,8},{8,4},{12,0},{1,13},{5,9},{9,5},{13,1},{2,14},{6,10},... | collective-permute-start | bytes 159752 | tf_op jit(solution)/shard_map/ppermute | solution.py:394
  52.5 1.8 %collective-permute-start.21 = (bf16[208,128]{1,0:T(8,128)(2,1)S(1)}, bf16[208,128]{1,0:T(8,128)(2,1)S(1)}, u32[]{:S(2)}, u32[]{:S(2)}) collective-permute-start(bf16[208,128]{1,0:T(8,128)(2,1)S(1)} %shard_map.93.rest_0_), channel_id=1, source_target_pairs={{0,4},{4,0},{8,12},{12,8},{1,5},{5,1},{9,13},{13,9},{2,6},{6,2},{1... | collective-permute-start | bytes 159752 | tf_op jit(solution)/shard_map/ppermute | solution.py:394
  54.3 1.9 %collective-permute-done.23.rest_3_ = bf16[208,128]{1,0:T(8,128)(2,1)S(1)} collective-permute-done((bf16[208,128]{1,0:T(8,128)(2,1)S(1)}, bf16[208,128]{1,0:T(8,128)(2,1)S(1)}, u32[]{:S(2)}, u32[]{:S(2)}) %collective-permute-start.23) | collective-permute-done | bytes 53280 | tf_op jit(solution)/shard_map/ppermute | solution.py:394
  56.2 1.7 %collective-permute-done.22.rest_2_ = bf16[208,128]{1,0:T(8,128)(2,1)S(1)} collective-permute-done((bf16[208,128]{1,0:T(8,128)(2,1)S(1)}, bf16[208,128]{1,0:T(8,128)(2,1)S(1)}, u32[]{:S(2)}, u32[]{:S(2)}) %collective-permute-start.22) | collective-permute-done | bytes 53280 | tf_op jit(solution)/shard_map/ppermute | solution.py:394
  57.9 1.4 %shard_map.94 = (f32[1536,128]{1,0:T(8,128)}, f32[64,96]{1,0:T(8,128)}) custom-call(f32[96,1024]{1,0:T(8,128)S(1)} %get-tuple-element.60.surface, f32[96,1024]{1,0:T(8,128)S(1)} %collective-permute-done.17.other, f32[96,128]{1,0:T(8,128)S(1)} %get-tuple-element.61.time_t, bf16[208,128]{1,0:T(8,128)(2,1)S(1)} %shard_map.93.rest_0_, ...), custom_call_target="tpu_custom_call" | custom-call | flops 1000000 | bytes 1000000 | tf_op jit(solution)/shard_map/pallas_call | solution.py:380
  (27 shorter events, 0.4 us)
Async XLA Ops:
  3.5 8.7 %collective-permute-start.1 = (bf16[528,128]{1,0:T(8,128)(2,1)S(1)}, bf16[528,128]{1,0:T(8,128)(2,1)S(1)}, u32[]{:S(2)}, u32[]{:S(2)}) collective-permute-start(bf16[528,128]{1,0:T(8,128)(2,1)S(1)} %get-tuple-element.41), channel_id=1, source_target_pairs={{0,4},{4,0},{8,12},{12,8},{1,5},{5,1},{9,13},{13,9},{2,6},{6,2},{1... | collective-permute-start | bytes 405512 | tf_op jit(solution)/shard_map/ppermute | solution.py:394
  6.6 12.6 %collective-permute-start.3 = (bf16[528,128]{1,0:T(8,128)(2,1)S(1)}, bf16[528,128]{1,0:T(8,128)(2,1)S(1)}, u32[]{:S(2)}, u32[]{:S(2)}) collective-permute-start(bf16[528,128]{1,0:T(8,128)(2,1)S(1)} %get-tuple-element.45), channel_id=1, source_target_pairs={{0,8},{4,12},{8,0},{12,4},{1,9},{5,13},{9,1},{13,5},{2,10},{6,14},... | collective-permute-start | bytes 405512 | tf_op jit(solution)/shard_map/ppermute | solution.py:394
  9.2 10.1 %collective-permute-start = (bf16[720,128]{1,0:T(8,128)(2,1)S(1)}, bf16[720,128]{1,0:T(8,128)(2,1)S(1)}, u32[]{:S(2)}, u32[]{:S(2)}) collective-permute-start(bf16[720,128]{1,0:T(8,128)(2,1)S(1)} %get-tuple-element.36), channel_id=1, source_target_pairs={{0,1},{1,0},{4,5},{5,4},{8,9},{9,8},{12,13},{13,12},{2,3},{3,2},{6... | collective-permute-start | bytes 552968 | tf_op jit(solution)/shard_map/ppermute | solution.py:394
  9.2 11.0 %collective-permute-start.4 = (bf16[544,128]{1,0:T(8,128)(2,1)S(1)}, bf16[544,128]{1,0:T(8,128)(2,1)S(1)}, u32[]{:S(2)}, u32[]{:S(2)}) collective-permute-start(bf16[544,128]{1,0:T(8,128)(2,1)S(1)} %get-tuple-element.46), channel_id=1, source_target_pairs={{0,12},{4,8},{8,4},{12,0},{1,13},{5,9},{9,5},{13,1},{2,14},{6,10},... | collective-permute-start | bytes 417800 | tf_op jit(solution)/shard_map/ppermute | solution.py:394
  9.2 11.0 %collective-permute-start.5 = (bf16[544,128]{1,0:T(8,128)(2,1)S(1)}, bf16[544,128]{1,0:T(8,128)(2,1)S(1)}, u32[]{:S(2)}, u32[]{:S(2)}) collective-permute-start(bf16[544,128]{1,0:T(8,128)(2,1)S(1)} %get-tuple-element.47), channel_id=1, source_target_pairs={{0,4},{4,0},{8,12},{12,8},{1,5},{5,1},{9,13},{13,9},{2,6},{6,2},{1... | collective-permute-start | bytes 417800 | tf_op jit(solution)/shard_map/ppermute | solution.py:394
  12.2 7.7 %copy-start = (f32[64,96]{1,0:T(8,128)S(1)}, f32[64,96]{1,0:T(8,128)}, u32[]{:S(2)}) copy-start(f32[64,96]{1,0:T(8,128)} %time_own.1) | copy-start | bytes 73732
  12.2 14.1 %collective-permute-start.2 = (bf16[528,128]{1,0:T(8,128)(2,1)S(1)}, bf16[528,128]{1,0:T(8,128)(2,1)S(1)}, u32[]{:S(2)}, u32[]{:S(2)}) collective-permute-start(bf16[528,128]{1,0:T(8,128)(2,1)S(1)} %get-tuple-element.44), channel_id=1, source_target_pairs={{0,9},{1,8},{4,13},{5,12},{8,1},{9,0},{12,5},{13,4},{2,11},{3,10},... | collective-permute-start | bytes 405512 | tf_op jit(solution)/shard_map/ppermute | solution.py:394
  19.2 7.1 %collective-permute-start.6 = (bf16[528,128]{1,0:T(8,128)(2,1)S(1)}, bf16[528,128]{1,0:T(8,128)(2,1)S(1)}, u32[]{:S(2)}, u32[]{:S(2)}) collective-permute-start(bf16[528,128]{1,0:T(8,128)(2,1)S(1)} %get-tuple-element.48), channel_id=1, source_target_pairs={{0,5},{1,4},{4,1},{5,0},{8,13},{9,12},{12,9},{13,8},{2,7},{3,6},{6... | collective-permute-start | bytes 405512 | tf_op jit(solution)/shard_map/ppermute | solution.py:394
  19.2 0.9 %collective-permute-start.7 = (f32[96,128]{1,0:T(8,128)S(1)}, f32[96,128]{1,0:T(8,128)S(1)}, u32[]{:S(2)}, u32[]{:S(2)}) collective-permute-start(f32[96,128]{1,0:T(8,128)S(1)} %get-tuple-element.50), channel_id=1, source_target_pairs={{1,2},{2,1},{5,6},{6,5},{9,10},{10,9},{13,14},{14,13},{17,18},{18,... | collective-permute-start | bytes 147464 | tf_op jit(solution)/shard_map/ppermute | solution.py:449
  27.5 5.4 %collective-permute-start.9 = (f32[120,128]{1,0:T(8,128)S(1)}, f32[120,128]{1,0:T(8,128)S(1)}, u32[]{:S(2)}, u32[]{:S(2)}) collective-permute-start(f32[120,128]{1,0:T(8,128)S(1)} %get-tuple-element.52.mine), channel_id=1, source_target_pairs={{0,2},{2,0},{1,3},{3,1},{4,6},{6,4},{5,7},{7,5},{8,10},{10,8},{9,1... | collective-permute-start | bytes 184328 | tf_op jit(solution)/shard_map/ppermute | solution.py:394
  29.0 3.8 %collective-permute-start.10 = (f32[104,128]{1,0:T(8,128)S(1)}, f32[104,128]{1,0:T(8,128)S(1)}, u32[]{:S(2)}, u32[]{:S(2)}) collective-permute-start(f32[104,128]{1,0:T(8,128)S(1)} %get-tuple-element.53), channel_id=1, source_target_pairs={{0,3},{1,2},{2,1},{3,0},{4,7},{5,6},{6,5},{7,4},{8,11},{9,10},{10,... | collective-permute-start | bytes 159752 | tf_op jit(solution)/shard_map/ppermute | solution.py:394
  29.6 3.3 %collective-permute-start.8 = (f32[104,128]{1,0:T(8,128)S(1)}, f32[104,128]{1,0:T(8,128)S(1)}, u32[]{:S(2)}, u32[]{:S(2)}) collective-permute-start(f32[104,128]{1,0:T(8,128)S(1)} %get-tuple-element.53), channel_id=1, source_target_pairs={{0,1},{1,0},{2,3},{3,2},{4,5},{5,4},{6,7},{7,6},{8,9},{9,8},{10,11... | collective-permute-start | bytes 159752 | tf_op jit(solution)/shard_map/ppermute | solution.py:394
  32.9 6.8 %collective-permute-start.13 = (f32[120,128]{1,0:T(8,128)S(1)}, f32[120,128]{1,0:T(8,128)S(1)}, u32[]{:S(2)}, u32[]{:S(2)}) collective-permute-start(f32[120,128]{1,0:T(8,128)S(1)} %shard_map.90.rest_0_), channel_id=1, source_target_pairs={{0,12},{4,8},{8,4},{12,0},{1,13},{5,9},{9,5},{13,1},{2,14},{6,10},... | collective-permute-start | bytes 184328 | tf_op jit(solution)/shard_map/ppermute | solution.py:394
  35.3 6.2 %collective-permute-start.12 = (f32[120,128]{1,0:T(8,128)S(1)}, f32[120,128]{1,0:T(8,128)S(1)}, u32[]{:S(2)}, u32[]{:S(2)}) collective-permute-start(f32[120,128]{1,0:T(8,128)S(1)} %shard_map.90.rest_0_), channel_id=1, source_target_pairs={{0,8},{4,12},{8,0},{12,4},{1,9},{5,13},{9,1},{13,5},{2,10},{6,14},... | collective-permute-start | bytes 184328 | tf_op jit(solution)/shard_map/ppermute | solution.py:394
  35.3 6.2 %collective-permute-start.11 = (f32[120,128]{1,0:T(8,128)S(1)}, f32[120,128]{1,0:T(8,128)S(1)}, u32[]{:S(2)}, u32[]{:S(2)}) collective-permute-start(f32[120,128]{1,0:T(8,128)S(1)} %shard_map.90.rest_0_), channel_id=1, source_target_pairs={{0,4},{4,0},{8,12},{12,8},{1,5},{5,1},{9,13},{13,9},{2,6},{6,2},{1... | collective-permute-start | bytes 184328 | tf_op jit(solution)/shard_map/ppermute | solution.py:394
  37.3 4.4 %collective-permute-start.15 = (f32[96,128]{1,0:T(8,128)S(1)}, f32[96,128]{1,0:T(8,128)S(1)}, u32[]{:S(2)}, u32[]{:S(2)}) collective-permute-start(f32[96,128]{1,0:T(8,128)S(1)} %get-tuple-element.58), channel_id=1, source_target_pairs={{0,1},{1,0},{2,3},{3,2},{4,5},{5,4},{6,7},{7,6},{8,9},{9,8},{10,11... | collective-permute-start | bytes 147464 | tf_op jit(solution)/shard_map/ppermute | solution.py:394
  37.3 4.4 %collective-permute-start.16 = (f32[96,128]{1,0:T(8,128)S(1)}, f32[96,128]{1,0:T(8,128)S(1)}, u32[]{:S(2)}, u32[]{:S(2)}) collective-permute-start(f32[96,128]{1,0:T(8,128)S(1)} %get-tuple-element.59), channel_id=1, source_target_pairs={{1,2},{2,1},{5,6},{6,5},{9,10},{10,9},{13,14},{14,13},{17,18},{18,... | collective-permute-start | bytes 147464 | tf_op jit(solution)/shard_map/ppermute | solution.py:449
  41.6 1.3 %collective-permute-start.14 = (f32[96,128]{1,0:T(8,128)S(1)}, f32[96,128]{1,0:T(8,128)S(1)}, u32[]{:S(2)}, u32[]{:S(2)}) collective-permute-start(f32[96,128]{1,0:T(8,128)S(1)} %get-tuple-element.54.time_own), channel_id=1, source_target_pairs={{0,1},{1,0},{2,3},{3,2},{4,5},{5,4},{6,7},{7,6},{8,9},{9,8},{10,11... | collective-permute-start | bytes 147464 | tf_op jit(solution)/shard_map/ppermute | solution.py:394
  44.2 13.6 %collective-permute-start.17 = (f32[96,1024]{1,0:T(8,128)S(1)}, f32[96,1024]{1,0:T(8,128)S(1)}, u32[]{:S(2)}, u32[]{:S(2)}) collective-permute-start(f32[96,1024]{1,0:T(8,128)S(1)} %get-tuple-element.60.surface), channel_id=1, source_target_pairs={{0,1},{1,0},{2,3},{3,2},{4,5},{5,4},{6,7},{7,6},{8,9},{9,8},{10,11... | collective-permute-start | bytes 1179656 | tf_op jit(solution)/shard_map/ppermute | solution.py:394
  44.6 4.1 %collective-permute-start.19 = (bf16[208,128]{1,0:T(8,128)(2,1)S(1)}, bf16[208,128]{1,0:T(8,128)(2,1)S(1)}, u32[]{:S(2)}, u32[]{:S(2)}) collective-permute-start(bf16[208,128]{1,0:T(8,128)(2,1)S(1)} %get-tuple-element.62.mine), channel_id=1, source_target_pairs={{0,2},{2,0},{1,3},{3,1},{4,6},{6,4},{5,7},{7,5},{8,10},{10,8},{9,1... | collective-permute-start | bytes 159752 | tf_op jit(solution)/shard_map/ppermute | solution.py:394
  45.9 3.9 %collective-permute-start.20 = (bf16[208,128]{1,0:T(8,128)(2,1)S(1)}, bf16[208,128]{1,0:T(8,128)(2,1)S(1)}, u32[]{:S(2)}, u32[]{:S(2)}) collective-permute-start(bf16[208,128]{1,0:T(8,128)(2,1)S(1)} %get-tuple-element.63), channel_id=1, source_target_pairs={{0,3},{1,2},{2,1},{3,0},{4,7},{5,6},{6,5},{7,4},{8,11},{9,10},{10,... | collective-permute-start | bytes 159752 | tf_op jit(solution)/shard_map/ppermute | solution.py:394
  46.2 3.7 %collective-permute-start.18 = (bf16[208,128]{1,0:T(8,128)(2,1)S(1)}, bf16[208,128]{1,0:T(8,128)(2,1)S(1)}, u32[]{:S(2)}, u32[]{:S(2)}) collective-permute-start(bf16[208,128]{1,0:T(8,128)(2,1)S(1)} %get-tuple-element.63), channel_id=1, source_target_pairs={{0,1},{1,0},{2,3},{3,2},{4,5},{5,4},{6,7},{7,6},{8,9},{9,8},{10,11... | collective-permute-start | bytes 159752 | tf_op jit(solution)/shard_map/ppermute | solution.py:394
  49.9 6.3 %collective-permute-start.23 = (bf16[208,128]{1,0:T(8,128)(2,1)S(1)}, bf16[208,128]{1,0:T(8,128)(2,1)S(1)}, u32[]{:S(2)}, u32[]{:S(2)}) collective-permute-start(bf16[208,128]{1,0:T(8,128)(2,1)S(1)} %shard_map.93.rest_0_), channel_id=1, source_target_pairs={{0,12},{4,8},{8,4},{12,0},{1,13},{5,9},{9,5},{13,1},{2,14},{6,10},... | collective-permute-start | bytes 159752 | tf_op jit(solution)/shard_map/ppermute | solution.py:394
  52.5 5.4 %collective-permute-start.22 = (bf16[208,128]{1,0:T(8,128)(2,1)S(1)}, bf16[208,128]{1,0:T(8,128)(2,1)S(1)}, u32[]{:S(2)}, u32[]{:S(2)}) collective-permute-start(bf16[208,128]{1,0:T(8,128)(2,1)S(1)} %shard_map.93.rest_0_), channel_id=1, source_target_pairs={{0,8},{4,12},{8,0},{12,4},{1,9},{5,13},{9,1},{13,5},{2,10},{6,14},... | collective-permute-start | bytes 159752 | tf_op jit(solution)/shard_map/ppermute | solution.py:394
  52.5 5.4 %collective-permute-start.21 = (bf16[208,128]{1,0:T(8,128)(2,1)S(1)}, bf16[208,128]{1,0:T(8,128)(2,1)S(1)}, u32[]{:S(2)}, u32[]{:S(2)}) collective-permute-start(bf16[208,128]{1,0:T(8,128)(2,1)S(1)} %shard_map.93.rest_0_), channel_id=1, source_target_pairs={{0,4},{4,0},{8,12},{12,8},{1,5},{5,1},{9,13},{13,9},{2,6},{6,2},{1... | collective-permute-start | bytes 159752 | tf_op jit(solution)/shard_map/ppermute | solution.py:394

commit v12 on v11

--- a/solution.py
+++ b/solution.py
@@ -40,7 +40,7 @@
     small = [(list_hbm, list_ref), (count_hbm, count_ref), (target_hbm, target_ref), (mask_hbm, mask_ref)]
     large = [(swath_hbm.at[pl.ds(at, chunk)], swath_ref.at[pl.ds(at, chunk)]) for at in range(0, slots, chunk)]
     model = [(space_hbm, space_ref), (time_hbm, time_ref)]
-    copies = [pltpu.make_async_copy(src, dst, arrived.at[i]) for i, (src, dst) in enumerate(small + large + model)]
+    copies = [pltpu.make_async_copy(src, dst, arrived.at[i]) for i, (src, dst) in enumerate(small + model + large)]
     for copy in copies:
         copy.start()
     total[...] = jnp.zeros(total.shape, F32)
@@ -64,15 +64,7 @@
         return lax.fori_loop(0, lax.div(count + UNROLL - 1, UNROLL), entries, carry)
 
     lax.fori_loop(0, n_lon, owner, 0)
-    mask = mask_ref[...].astype(F32)
-    by_day = mask.T.astype(BF16)
-    for slot in range(slots):
-        if slot % chunk == 0:
-            copies[len(small) + slot // chunk].wait()
-        at = place[slot]
-        total[at] += (swath_ref[slot] * by_day[:, slot:slot + 1]).astype(F32)
-        seen[pl.ds(at, 1), :days] += mask[slot:slot + 1, :]
-    for copy in copies[len(small) + len(large):]:
+    for copy in copies[len(small):len(small) + len(model)]:
         copy.wait()
     rank = surface.shape[0]
     height = space_ref.shape[0] // rank
@@ -82,6 +74,14 @@
     edge_far[...] = space_ref[pl.ds(core * (height - 1), rank, stride=height), :]
     cols[...] = jnp.zeros(cols.shape, F32)
     cols[:, :rank] = border(surface[...], half)
+    mask = mask_ref[...].astype(F32)
+    by_day = mask.T.astype(BF16)
+    for slot in range(slots):
+        if slot % chunk == 0:
+            copies[len(small) + len(model) + slot // chunk].wait()
+        at = place[slot]
+        total[at] += (swath_ref[slot] * by_day[:, slot:slot + 1]).astype(F32)
+        seen[pl.ds(at, 1), :days] += mask[slot:slot + 1, :]
     for (side, step), out in zip(sends, outs):
         at = (side * n_lon + step) * half
         end = half * days + TAIL
@@ -94,7 +94,7 @@
                 out[part:part + days, :] = jnp.zeros((days, LANES), BF16)
                 out[part:part + days, :rank] = value
                 left = left - value.astype(F32)
-        elif paired and side == 0 and step in (1, 3):
+        elif paired and (side, step) == (0, 3):
             out[end:, :] = cols[...].astype(BF16)
 
 
@@ -250,7 +250,8 @@
     edge_far_in, rest = rest[0], rest[1:]
     if paired:
         at = half * days + TAIL
-        cols = [pieces[0, step][at:, :].astype(F32) for step in (1, 3)]
+        cols = [ref[at:, :].astype(F32) for ref in (rest[0], pieces[0, 2])]
+        rest = rest[1:]
     else:
         cols, rest = [ref[...] for ref in rest[:2]], rest[2:]
     fresh, message, crossing, edge_out, edge_far, summed, seen, base = rest
@@ -338,7 +339,13 @@
         space_out[pl.ds((1 - core) * half + row, rank, stride=height), :] = other[:, at:at + LANES] * scale
 
 
-def merge_kernel(mine, theirs, piece_in, edge_in, out, piece_out, edge_out):
+def near_merge_kernel(mine, theirs, out):
+    rows = mine.shape[0]
+    out[:rows, :] = (mine[...].astype(F32) + theirs[:rows, :].astype(F32)).astype(BF16)
+    out[rows:, :] = theirs[rows:, :]
+
+
+def far_merge_kernel(mine, theirs, piece_in, edge_in, out, piece_out, edge_out):
     piece_out[...] = piece_in[...]
     edge_out[...] = edge_in[...]
     out[...] = (mine[...].astype(F32) + theirs[...].astype(F32)).astype(BF16)
@@ -348,10 +355,14 @@
     total[...] = mine[...] + theirs[...]
 
 
-def own_sum_kernel(mine, core, band, both, total):
-    rows = both.shape[0]
-    total[:rows, :] = (mine[:rows, :] + core[...]) + (band[:rows, :] + both[...])
-    total[rows:, :] = mine[rows:, :]
+def core_sum_kernel(mine, core, total):
+    total[...] = mine[: total.shape[0], :] + core[...]
+
+
+def band_sum_kernel(mine, band, message, total):
+    rows = mine.shape[0]
+    total[:rows, :] = mine[...] + band[...]
+    total[rows:, :] = message[rows:, :]
 
 
 def all_sum_kernel(rank, mine, core, band, both, total):
@@ -407,11 +418,11 @@
     paired = n_lon == 4
 
     distant, close = range(n_lon // 2, n_lon), range(1, n_lon // 2)
-    sends = [(1, step) for step in reversed(distant)] + [(0, step) for step in distant] + [(1, 0)]
+    sends = [(side, step) for step in reversed(distant) for side in (0, 1)] + [(1, 0)]
     sends += [(side, step) for side in (0, 1) for step in close] + [(0, 0)]
 
     def piece_rows(side, step):
-        more = 3 * days if (side, step) == (1, 0) else COLS if paired and side == 0 and step in (1, 3) else 0
+        more = 3 * days if (side, step) == (1, 0) else COLS if paired and (side, step) == (0, 3) else 0
         return half * days + TAIL + more
 
     operands = (send_list, send_count, target, swath, obs_mask, factor_space.reshape(rank * height, cells), factor_time)
@@ -437,10 +448,13 @@
         return across(piece, "lon", step) if step else piece
 
     pieces = dict(zip(sends, pieces))
+    borders = ()
     if paired:
-        passing = across(pieces.pop((1, 3)), "lon", 1)
-        outs = [shape(passing.shape, BF16), shape(passing.shape, BF16), shape(edge_far.shape)]
-        pieces[1, 2], pieces[1, 1], edge_far = call(merge_kernel, outs)(pieces[1, 2], passing, pieces[1, 1], edge_far)
+        near, far = (across(pieces.pop((side, 3)), "lon", 1) for side in (0, 1))
+        borders = (near,)
+        pieces[0, 2] = call(near_merge_kernel, shape(near.shape, BF16))(pieces[0, 2], near)
+        outs = [shape(far.shape, BF16), shape(far.shape, BF16), shape(edge_far.shape)]
+        pieces[1, 2], pieces[1, 1], edge_far = call(far_merge_kernel, outs)(pieces[1, 2], far, pieces[1, 1], edge_far)
     pieces = {key: arrived(key, piece) for key, piece in pieces.items()}
     order = list(pieces)
 
@@ -468,7 +482,7 @@
         functools.partial(first_kernel, half, days, order, paired, swap),
         [fresh, shape((own_rows + COLS, LANES)), shape((own_rows, LANES)), edge, edge, shape((2 * days, wide)), shape((TAIL, LANES))],
         [pltpu.VMEM((rank, wide), F32)],
-    )(surface, edge_near, predicted, packed, time_t, *[pieces[key] for key in order], bands(edge_far), *(() if paired else columns(cols)))
+    )(surface, edge_near, predicted, packed, time_t, *[pieces[key] for key in order], bands(edge_far), *(borders if paired else columns(cols)))
 
     narrowed = shape((sum_rows + NORM, LANES), BF16)
 
@@ -489,7 +503,8 @@
     def around(mine, core, both):
         return mine, across(core, "ta", 1), across(mine, "lat", 1), across(both, ("lat", "ta"), 3)
 
-    total = call(own_sum_kernel, shape(message.shape))(*around(message, crossing, crossing))
+    total = call(core_sum_kernel, shape(crossing.shape))(message, across(crossing, "ta", 1))
+    total = call(band_sum_kernel, shape(message.shape))(total, across(total, "lat", 1), message)
     parts = over_lon(doubled(total, "lat", 2))
     cols = (parts[1], parts[3]) if paired else columns(message[own_rows:])
     time_own, norm = call(functools.partial(own_kernel, len(parts)), [edge, shape((NORM, LANES))])(time_t, *parts)

time: 59.5 us -> 58.7 us (0.987)
  waiting for transfers between devices: 28.9 us -> 25.4 us
  starting transfers between devices: 22.6 us -> 25.5 us
    ppermute x22 -> x21, waiting for transfers between devices: 28.8 us -> 25.4 us  [across(): lax.ppermute(value, axis, [(i, i ^ step) for i in range(lax.axis_size(axi...]
    ppermute x22 -> x21, starting transfers between devices: 21.3 us -> 24.2 us  [across(): lax.ppermute(value, axis, [(i, i ^ step) for i in range(lax.axis_size(axi...]
    pallas_call x9 -> x11, Pallas kernels: 7.08 us -> 6.94 us  [run(): pl.pallas_call(kernel, out_shape=out_shape, in_specs=[pl.BlockSpec(memory...]
  transfers between devices with their start and end apart: 24 -> 23, of which waited for: 11 -> 15; matrix products, arithmetic and copies ran while one was open for 0% -> 0% of each run, Pallas kernels for 1% -> 1%
where the time goes in v12:
time: 58.7 us; the launch traced here: 58.6 us
  starting transfers between devices  25.5 us (43%)
  waiting for transfers between devices  25.4 us (43%)
  Pallas kernels  6.94 us (12%)
  between operations  0.75 us (1%)
    ppermute x21, waiting for transfers between devices, across(): lax.ppermute(value, axis, [(i, i ^ step) for i in range(lax.axis_size(axi...  25.4 us
    ppermute x21, starting transfers between devices, across(): lax.ppermute(value, axis, [(i, i ^ step) for i in range(lax.axis_size(axi...  24.2 us
    pallas_call x11, Pallas kernels, run(): pl.pallas_call(kernel, out_shape=out_shape, in_specs=[pl.BlockSpec(memory...  6.94 us
    ppermute x2, starting transfers between devices, bands(): return lax.ppermute(edge, ('lat', 'ta'), there + [(b, a) for a, b in there])  1.3 us
  transfers between devices with their start and end apart: 23, of which 15 were waited for; matrix products, arithmetic and copies ran while one was open for 0% of the time, Pallas kernels for 1%

profile of v12, /device:TPU:0, one launch (start us, length us, event | category | flops | bytes accessed | tf_op | source)
XLA Modules:
  0.0 58.6 jit_solution(3574104599698555087)
XLA Ops:
  0.6 2.7 %shard_map.86 = (bf16[544,128]{1,0:T(8,128)(2,1)S(1)}, bf16[528,128]{1,0:T(8,128)(2,1)S(1)}, bf16[528,128]{1,0:T(8,128)(2,1)S(1)}, bf16[528,128]{1,0:T(8,128)(2,...) custom-call(s32[1,4,32]{2,1,0:T(4,128)} %list_hbm.1, ...), custom_call_target="tpu_custom_call" | custom-call | flops 1000000 | bytes 1000000 | tf_op jit(solution)/shard_map/pallas_call | solution.py:391
  3.3 3.1 %collective-permute-start.1 = (bf16[544,128]{1,0:T(8,128)(2,1)S(1)}, bf16[544,128]{1,0:T(8,128)(2,1)S(1)}, u32[]{:S(2)}, u32[]{:S(2)}) collective-permute-start(bf16[544,128]{1,0:T(8,128)(2,1)S(1)} %get-tuple-element.41), channel_id=1, source_target_pairs={{0,4},{4,0},{8,12},{12,8},{1,5},{5,1},{9,13},{13,9},{2,6},{6,2},{1... | collective-permute-start | bytes 417800 | tf_op jit(solution)/shard_map/ppermute | solution.py:405
  6.5 4.4 %collective-permute-done.1.theirs.rest_7_ = bf16[544,128]{1,0:T(8,128)(2,1)S(1)} collective-permute-done((bf16[544,128]{1,0:T(8,128)(2,1)S(1)}, bf16[544,128]{1,0:T(8,128)(2,1)S(1)}, u32[]{:S(2)}, u32[]{:S(2)}) %collective-permute-start.1) | collective-permute-done | bytes 139296 | tf_op jit(solution)/shard_map/ppermute | solution.py:405
  11.0 3.1 %collective-permute-start.2 = (bf16[544,128]{1,0:T(8,128)(2,1)S(1)}, bf16[544,128]{1,0:T(8,128)(2,1)S(1)}, u32[]{:S(2)}, u32[]{:S(2)}) collective-permute-start(bf16[544,128]{1,0:T(8,128)(2,1)S(1)} %shard_map.88), channel_id=1, source_target_pairs={{0,8},{4,12},{8,0},{12,4},{1,9},{5,13},{9,1},{13,5},{2,10},{6,14},... | collective-permute-start | bytes 417800 | tf_op jit(solution)/shard_map/ppermute | solution.py:405
  14.1 1.6 %collective-permute-start.5 = (bf16[528,128]{1,0:T(8,128)(2,1)S(1)}, bf16[528,128]{1,0:T(8,128)(2,1)S(1)}, u32[]{:S(2)}, u32[]{:S(2)}) collective-permute-start(bf16[528,128]{1,0:T(8,128)(2,1)S(1)} %get-tuple-element.47), channel_id=1, source_target_pairs={{0,4},{4,0},{8,12},{12,8},{1,5},{5,1},{9,13},{13,9},{2,6},{6,2},{1... | collective-permute-start | bytes 405512 | tf_op jit(solution)/shard_map/ppermute | solution.py:405
  15.8 2.7 %collective-permute-start.6 = (bf16[528,128]{1,0:T(8,128)(2,1)S(1)}, bf16[528,128]{1,0:T(8,128)(2,1)S(1)}, u32[]{:S(2)}, u32[]{:S(2)}) collective-permute-start(bf16[528,128]{1,0:T(8,128)(2,1)S(1)} %get-tuple-element.48), channel_id=1, source_target_pairs={{0,5},{1,4},{4,1},{5,0},{8,13},{9,12},{12,9},{13,8},{2,7},{3,6},{6... | collective-permute-start | bytes 405512 | tf_op jit(solution)/shard_map/ppermute | solution.py:405
  18.5 0.7 %collective-permute-start.7 = (f32[96,128]{1,0:T(8,128)S(1)}, f32[96,128]{1,0:T(8,128)S(1)}, u32[]{:S(2)}, u32[]{:S(2)}) collective-permute-start(f32[96,128]{1,0:T(8,128)S(1)} %get-tuple-element.50), channel_id=1, source_target_pairs={{1,2},{2,1},{5,6},{6,5},{9,10},{10,9},{13,14},{14,13},{17,18},{18,... | collective-permute-start | bytes 147464 | tf_op jit(solution)/shard_map/ppermute | solution.py:463
  19.2 0.2 shard_map.87
  19.5 0.9 %collective-permute-done.5.rest_3_ = bf16[528,128]{1,0:T(8,128)(2,1)S(1)} collective-permute-done((bf16[528,128]{1,0:T(8,128)(2,1)S(1)}, bf16[528,128]{1,0:T(8,128)(2,1)S(1)}, u32[]{:S(2)}, u32[]{:S(2)}) %collective-permute-start.5) | collective-permute-done | bytes 135200 | tf_op jit(solution)/shard_map/ppermute | solution.py:405
  20.4 4.4 %collective-permute-done.4.rest_1_ = bf16[528,128]{1,0:T(8,128)(2,1)S(1)} collective-permute-done((bf16[528,128]{1,0:T(8,128)(2,1)S(1)}, bf16[528,128]{1,0:T(8,128)(2,1)S(1)}, u32[]{:S(2)}, u32[]{:S(2)}) %collective-permute-start.4) | collective-permute-done | bytes 135200 | tf_op jit(solution)/shard_map/ppermute | solution.py:405
  24.8 0.4 collective-permute-done.6.rest_4_
  25.2 1.1 %shard_map.90 = (f32[96,1024]{1,0:T(8,128)S(1)}, f32[120,128]{1,0:T(8,128)S(1)}, f32[104,128]{1,0:T(8,128)S(1)}, f32[96,128]{1,0:T(8,128)S(1)}, f32[96,128]{1,0:...) custom-call(f32[96,1024]{1,0:T(8,128)S(1)} %get-tuple-element.34.surface, ...), custom_call_target="tpu_custom_call" | custom-call | flops 1000000 | bytes 1000000 | tf_op jit(solution)/shard_map/pallas_call | solution.py:391
  26.5 1.1 %collective-permute-done.8.core = f32[104,128]{1,0:T(8,128)S(1)} collective-permute-done((f32[104,128]{1,0:T(8,128)S(1)}, f32[104,128]{1,0:T(8,128)S(1)}, u32[]{:S(2)}, u32[]{:S(2)}) %collective-permute-start.8) | collective-permute-done | bytes 53280 | tf_op jit(solution)/shard_map/ppermute | solution.py:405
  27.6 1.7 %collective-permute-start.9 = (f32[104,128]{1,0:T(8,128)S(1)}, f32[104,128]{1,0:T(8,128)S(1)}, u32[]{:S(2)}, u32[]{:S(2)}) collective-permute-start(f32[104,128]{1,0:T(8,128)S(1)} %shard_map.91.mine), channel_id=1, source_target_pairs={{0,2},{2,0},{1,3},{3,1},{4,6},{6,4},{5,7},{7,5},{8,10},{10,8},{9,1... | collective-permute-start | bytes 159752 | tf_op jit(solution)/shard_map/ppermute | solution.py:405
  29.4 2.5 %collective-permute-done.9.band = f32[104,128]{1,0:T(8,128)S(1)} collective-permute-done((f32[104,128]{1,0:T(8,128)S(1)}, f32[104,128]{1,0:T(8,128)S(1)}, u32[]{:S(2)}, u32[]{:S(2)}) %collective-permute-start.9) | collective-permute-done | bytes 53280 | tf_op jit(solution)/shard_map/ppermute | solution.py:405
  31.8 3.2 %collective-permute-start.12 = (f32[120,128]{1,0:T(8,128)S(1)}, f32[120,128]{1,0:T(8,128)S(1)}, u32[]{:S(2)}, u32[]{:S(2)}) collective-permute-start(f32[120,128]{1,0:T(8,128)S(1)} %shard_map.92.rest_0_), channel_id=1, source_target_pairs={{0,12},{4,8},{8,4},{12,0},{1,13},{5,9},{9,5},{13,1},{2,14},{6,10},... | collective-permute-start | bytes 184328 | tf_op jit(solution)/shard_map/ppermute | solution.py:405
  35.1 1.2 %collective-permute-start.10 = (f32[120,128]{1,0:T(8,128)S(1)}, f32[120,128]{1,0:T(8,128)S(1)}, u32[]{:S(2)}, u32[]{:S(2)}) collective-permute-start(f32[120,128]{1,0:T(8,128)S(1)} %shard_map.92.rest_0_), channel_id=1, source_target_pairs={{0,4},{4,0},{8,12},{12,8},{1,5},{5,1},{9,13},{13,9},{2,6},{6,2},{1... | collective-permute-start | bytes 184328 | tf_op jit(solution)/shard_map/ppermute | solution.py:405
  36.3 0.7 %collective-permute-start.15 = (f32[96,128]{1,0:T(8,128)S(1)}, f32[96,128]{1,0:T(8,128)S(1)}, u32[]{:S(2)}, u32[]{:S(2)}) collective-permute-start(f32[96,128]{1,0:T(8,128)S(1)} %get-tuple-element.59), channel_id=1, source_target_pairs={{1,2},{2,1},{5,6},{6,5},{9,10},{10,9},{13,14},{14,13},{17,18},{18,... | collective-permute-start | bytes 147464 | tf_op jit(solution)/shard_map/ppermute | solution.py:463
  37.0 1.0 %collective-permute-done.12.rest_3_.cols_b = f32[120,128]{1,0:T(8,128)S(1)} collective-permute-done((f32[120,128]{1,0:T(8,128)S(1)}, f32[120,128]{1,0:T(8,128)S(1)}, u32[]{:S(2)}, u32[]{:S(2)}) %collective-permute-start.12) | collective-permute-done | bytes 61472 | tf_op jit(solution)/shard_map/ppermute | solution.py:405
  37.9 2.3 %collective-permute-done.11.rest_2_ = f32[120,128]{1,0:T(8,128)S(1)} collective-permute-done((f32[120,128]{1,0:T(8,128)S(1)}, f32[120,128]{1,0:T(8,128)S(1)}, u32[]{:S(2)}, u32[]{:S(2)}) %collective-permute-start.11) | collective-permute-done | bytes 61472 | tf_op jit(solution)/shard_map/ppermute | solution.py:405
  40.6 1.2 %collective-permute-done.13.time_other = f32[96,128]{1,0:T(8,128)S(1)} collective-permute-done((f32[96,128]{1,0:T(8,128)S(1)}, f32[96,128]{1,0:T(8,128)S(1)}, u32[]{:S(2)}, u32[]{:S(2)}) %collective-permute-start.13) | collective-permute-done | bytes 49184 | tf_op jit(solution)/shard_map/ppermute | solution.py:405
  41.8 1.3 %shard_map.94 = (f32[96,1024]{1,0:T(8,128)S(1)}, f32[96,128]{1,0:T(8,128)S(1)}, bf16[208,128]{1,0:T(8,128)(2,1)S(1)}, bf16[208,128]{1,0:T(8,128)(2,1)S(1)}) custom-call(f32[96,1024]{1,0:T(8,128)S(1)} %get-tuple-element.51.surface, f32[96,128]{1,0:T(8,128)S(1)} %get-tuple-element.54.time_own, f32[96,128]{1,0:T(8,128)S(1)} %collective-permute-done.13.time_other, ...), custom_call_target="tpu_custom_call" | custom-call | flops 1000000 | bytes 1000000 | tf_op jit(solution)/shard_map/pallas_call | solution.py:391
  43.1 0.5 collective-permute-start.16
  43.6 1.4 %collective-permute-start.18 = (bf16[208,128]{1,0:T(8,128)(2,1)S(1)}, bf16[208,128]{1,0:T(8,128)(2,1)S(1)}, u32[]{:S(2)}, u32[]{:S(2)}) collective-permute-start(bf16[208,128]{1,0:T(8,128)(2,1)S(1)} %get-tuple-element.62.mine), channel_id=1, source_target_pairs={{0,2},{2,0},{1,3},{3,1},{4,6},{6,4},{5,7},{7,5},{8,10},{10,8},{9,1... | collective-permute-start | bytes 159752 | tf_op jit(solution)/shard_map/ppermute | solution.py:405
  45.1 0.7 %collective-permute-start.17 = (bf16[208,128]{1,0:T(8,128)(2,1)S(1)}, bf16[208,128]{1,0:T(8,128)(2,1)S(1)}, u32[]{:S(2)}, u32[]{:S(2)}) collective-permute-start(bf16[208,128]{1,0:T(8,128)(2,1)S(1)} %get-tuple-element.63), channel_id=1, source_target_pairs={{0,1},{1,0},{2,3},{3,2},{4,5},{5,4},{6,7},{7,6},{8,9},{9,8},{10,11... | collective-permute-start | bytes 159752 | tf_op jit(solution)/shard_map/ppermute | solution.py:405
  45.7 2.0 %collective-permute-done.18.band = bf16[208,128]{1,0:T(8,128)(2,1)S(1)} collective-permute-done((bf16[208,128]{1,0:T(8,128)(2,1)S(1)}, bf16[208,128]{1,0:T(8,128)(2,1)S(1)}, u32[]{:S(2)}, u32[]{:S(2)}) %collective-permute-start.18) | collective-permute-done | bytes 53280 | tf_op jit(solution)/shard_map/ppermute | solution.py:405
  47.7 1.1 %collective-permute-done.19.both = bf16[208,128]{1,0:T(8,128)(2,1)S(1)} collective-permute-done((bf16[208,128]{1,0:T(8,128)(2,1)S(1)}, bf16[208,128]{1,0:T(8,128)(2,1)S(1)}, u32[]{:S(2)}, u32[]{:S(2)}) %collective-permute-start.19) | collective-permute-done | bytes 53280 | tf_op jit(solution)/shard_map/ppermute | solution.py:405
  48.8 3.0 %collective-permute-start.22 = (bf16[208,128]{1,0:T(8,128)(2,1)S(1)}, bf16[208,128]{1,0:T(8,128)(2,1)S(1)}, u32[]{:S(2)}, u32[]{:S(2)}) collective-permute-start(bf16[208,128]{1,0:T(8,128)(2,1)S(1)} %shard_map.95.rest_0_), channel_id=1, source_target_pairs={{0,12},{4,8},{8,4},{12,0},{1,13},{5,9},{9,5},{13,1},{2,14},{6,10},... | collective-permute-start | bytes 159752 | tf_op jit(solution)/shard_map/ppermute | solution.py:405
  51.9 1.4 %collective-permute-start.20 = (bf16[208,128]{1,0:T(8,128)(2,1)S(1)}, bf16[208,128]{1,0:T(8,128)(2,1)S(1)}, u32[]{:S(2)}, u32[]{:S(2)}) collective-permute-start(bf16[208,128]{1,0:T(8,128)(2,1)S(1)} %shard_map.95.rest_0_), channel_id=1, source_target_pairs={{0,4},{4,0},{8,12},{12,8},{1,5},{5,1},{9,13},{13,9},{2,6},{6,2},{1... | collective-permute-start | bytes 159752 | tf_op jit(solution)/shard_map/ppermute | solution.py:405
  53.3 1.9 %collective-permute-done.22.rest_3_ = bf16[208,128]{1,0:T(8,128)(2,1)S(1)} collective-permute-done((bf16[208,128]{1,0:T(8,128)(2,1)S(1)}, bf16[208,128]{1,0:T(8,128)(2,1)S(1)}, u32[]{:S(2)}, u32[]{:S(2)}) %collective-permute-start.22) | collective-permute-done | bytes 53280 | tf_op jit(solution)/shard_map/ppermute | solution.py:405
  55.2 1.7 %collective-permute-done.21.rest_2_ = bf16[208,128]{1,0:T(8,128)(2,1)S(1)} collective-permute-done((bf16[208,128]{1,0:T(8,128)(2,1)S(1)}, bf16[208,128]{1,0:T(8,128)(2,1)S(1)}, u32[]{:S(2)}, u32[]{:S(2)}) %collective-permute-start.21) | collective-permute-done | bytes 53280 | tf_op jit(solution)/shard_map/ppermute | solution.py:405
  57.1 1.4 %shard_map.96 = (f32[1536,128]{1,0:T(8,128)}, f32[64,96]{1,0:T(8,128)}) custom-call(f32[96,1024]{1,0:T(8,128)S(1)} %get-tuple-element.60.surface, f32[96,1024]{1,0:T(8,128)S(1)} %collective-permute-done.16.other, f32[96,128]{1,0:T(8,128)S(1)} %get-tuple-element.61.time_t, bf16[208,128]{1,0:T(8,128)(2,1)S(1)} %shard_map.95.rest_0_, ...), custom_call_target="tpu_custom_call" | custom-call | flops 1000000 | bytes 1000000 | tf_op jit(solution)/shard_map/pallas_call | solution.py:391
  (27 shorter events, 1.1 us)
Async XLA Ops:
  3.3 7.6 %collective-permute-start.1 = (bf16[544,128]{1,0:T(8,128)(2,1)S(1)}, bf16[544,128]{1,0:T(8,128)(2,1)S(1)}, u32[]{:S(2)}, u32[]{:S(2)}) collective-permute-start(bf16[544,128]{1,0:T(8,128)(2,1)S(1)} %get-tuple-element.41), channel_id=1, source_target_pairs={{0,4},{4,0},{8,12},{12,8},{1,5},{5,1},{9,13},{13,9},{2,6},{6,2},{1... | collective-permute-start | bytes 417800 | tf_op jit(solution)/shard_map/ppermute | solution.py:405
  6.4 9.3 %collective-permute-start.3 = (bf16[528,128]{1,0:T(8,128)(2,1)S(1)}, bf16[528,128]{1,0:T(8,128)(2,1)S(1)}, u32[]{:S(2)}, u32[]{:S(2)}) collective-permute-start(bf16[528,128]{1,0:T(8,128)(2,1)S(1)} %get-tuple-element.43), channel_id=1, source_target_pairs={{0,4},{4,0},{8,12},{12,8},{1,5},{5,1},{9,13},{13,9},{2,6},{6,2},{1... | collective-permute-start | bytes 405512 | tf_op jit(solution)/shard_map/ppermute | solution.py:405
  6.5 12.1 %collective-permute-start = (bf16[720,128]{1,0:T(8,128)(2,1)S(1)}, bf16[720,128]{1,0:T(8,128)(2,1)S(1)}, u32[]{:S(2)}, u32[]{:S(2)}) collective-permute-start(bf16[720,128]{1,0:T(8,128)(2,1)S(1)} %get-tuple-element.36), channel_id=1, source_target_pairs={{0,1},{1,0},{4,5},{5,4},{8,9},{9,8},{12,13},{13,12},{2,3},{3,2},{6... | collective-permute-start | bytes 552968 | tf_op jit(solution)/shard_map/ppermute | solution.py:405
  11.0 14.3 %collective-permute-start.2 = (bf16[544,128]{1,0:T(8,128)(2,1)S(1)}, bf16[544,128]{1,0:T(8,128)(2,1)S(1)}, u32[]{:S(2)}, u32[]{:S(2)}) collective-permute-start(bf16[544,128]{1,0:T(8,128)(2,1)S(1)} %shard_map.88), channel_id=1, source_target_pairs={{0,8},{4,12},{8,0},{12,4},{1,9},{5,13},{9,1},{13,5},{2,10},{6,14},... | collective-permute-start | bytes 417800 | tf_op jit(solution)/shard_map/ppermute | solution.py:405
  14.1 6.3 %collective-permute-start.5 = (bf16[528,128]{1,0:T(8,128)(2,1)S(1)}, bf16[528,128]{1,0:T(8,128)(2,1)S(1)}, u32[]{:S(2)}, u32[]{:S(2)}) collective-permute-start(bf16[528,128]{1,0:T(8,128)(2,1)S(1)} %get-tuple-element.47), channel_id=1, source_target_pairs={{0,4},{4,0},{8,12},{12,8},{1,5},{5,1},{9,13},{13,9},{2,6},{6,2},{1... | collective-permute-start | bytes 405512 | tf_op jit(solution)/shard_map/ppermute | solution.py:405
  15.7 3.5 %copy-start = (f32[64,96]{1,0:T(8,128)S(1)}, f32[64,96]{1,0:T(8,128)}, u32[]{:S(2)}) copy-start(f32[64,96]{1,0:T(8,128)} %time_own.1) | copy-start | bytes 73732
  15.7 9.1 %collective-permute-start.4 = (bf16[528,128]{1,0:T(8,128)(2,1)S(1)}, bf16[528,128]{1,0:T(8,128)(2,1)S(1)}, u32[]{:S(2)}, u32[]{:S(2)}) collective-permute-start(bf16[528,128]{1,0:T(8,128)(2,1)S(1)} %get-tuple-element.46), channel_id=1, source_target_pairs={{0,9},{1,8},{4,13},{5,12},{8,1},{9,0},{12,5},{13,4},{2,11},{3,10},... | collective-permute-start | bytes 405512 | tf_op jit(solution)/shard_map/ppermute | solution.py:405
  15.8 9.4 %collective-permute-start.6 = (bf16[528,128]{1,0:T(8,128)(2,1)S(1)}, bf16[528,128]{1,0:T(8,128)(2,1)S(1)}, u32[]{:S(2)}, u32[]{:S(2)}) collective-permute-start(bf16[528,128]{1,0:T(8,128)(2,1)S(1)} %get-tuple-element.48), channel_id=1, source_target_pairs={{0,5},{1,4},{4,1},{5,0},{8,13},{9,12},{12,9},{13,8},{2,7},{3,6},{6... | collective-permute-start | bytes 405512 | tf_op jit(solution)/shard_map/ppermute | solution.py:405
  18.5 1.8 %collective-permute-start.7 = (f32[96,128]{1,0:T(8,128)S(1)}, f32[96,128]{1,0:T(8,128)S(1)}, u32[]{:S(2)}, u32[]{:S(2)}) collective-permute-start(f32[96,128]{1,0:T(8,128)S(1)} %get-tuple-element.50), channel_id=1, source_target_pairs={{1,2},{2,1},{5,6},{6,5},{9,10},{10,9},{13,14},{14,13},{17,18},{18,... | collective-permute-start | bytes 147464 | tf_op jit(solution)/shard_map/ppermute | solution.py:463
  26.3 1.3 %collective-permute-start.8 = (f32[104,128]{1,0:T(8,128)S(1)}, f32[104,128]{1,0:T(8,128)S(1)}, u32[]{:S(2)}, u32[]{:S(2)}) collective-permute-start(f32[104,128]{1,0:T(8,128)S(1)} %get-tuple-element.53), channel_id=1, source_target_pairs={{0,1},{1,0},{2,3},{3,2},{4,5},{5,4},{6,7},{7,6},{8,9},{9,8},{10,11... | collective-permute-start | bytes 159752 | tf_op jit(solution)/shard_map/ppermute | solution.py:405
  27.6 4.2 %collective-permute-start.9 = (f32[104,128]{1,0:T(8,128)S(1)}, f32[104,128]{1,0:T(8,128)S(1)}, u32[]{:S(2)}, u32[]{:S(2)}) collective-permute-start(f32[104,128]{1,0:T(8,128)S(1)} %shard_map.91.mine), channel_id=1, source_target_pairs={{0,2},{2,0},{1,3},{3,1},{4,6},{6,4},{5,7},{7,5},{8,10},{10,8},{9,1... | collective-permute-start | bytes 159752 | tf_op jit(solution)/shard_map/ppermute | solution.py:405
  31.8 6.1 %collective-permute-start.12 = (f32[120,128]{1,0:T(8,128)S(1)}, f32[120,128]{1,0:T(8,128)S(1)}, u32[]{:S(2)}, u32[]{:S(2)}) collective-permute-start(f32[120,128]{1,0:T(8,128)S(1)} %shard_map.92.rest_0_), channel_id=1, source_target_pairs={{0,12},{4,8},{8,4},{12,0},{1,13},{5,9},{9,5},{13,1},{2,14},{6,10},... | collective-permute-start | bytes 184328 | tf_op jit(solution)/shard_map/ppermute | solution.py:405
  35.1 5.2 %collective-permute-start.11 = (f32[120,128]{1,0:T(8,128)S(1)}, f32[120,128]{1,0:T(8,128)S(1)}, u32[]{:S(2)}, u32[]{:S(2)}) collective-permute-start(f32[120,128]{1,0:T(8,128)S(1)} %shard_map.92.rest_0_), channel_id=1, source_target_pairs={{0,8},{4,12},{8,0},{12,4},{1,9},{5,13},{9,1},{13,5},{2,10},{6,14},... | collective-permute-start | bytes 184328 | tf_op jit(solution)/shard_map/ppermute | solution.py:405
  35.1 5.3 %collective-permute-start.10 = (f32[120,128]{1,0:T(8,128)S(1)}, f32[120,128]{1,0:T(8,128)S(1)}, u32[]{:S(2)}, u32[]{:S(2)}) collective-permute-start(f32[120,128]{1,0:T(8,128)S(1)} %shard_map.92.rest_0_), channel_id=1, source_target_pairs={{0,4},{4,0},{8,12},{12,8},{1,5},{5,1},{9,13},{13,9},{2,6},{6,2},{1... | collective-permute-start | bytes 184328 | tf_op jit(solution)/shard_map/ppermute | solution.py:405
  36.3 4.3 %collective-permute-start.14 = (f32[96,128]{1,0:T(8,128)S(1)}, f32[96,128]{1,0:T(8,128)S(1)}, u32[]{:S(2)}, u32[]{:S(2)}) collective-permute-start(f32[96,128]{1,0:T(8,128)S(1)} %get-tuple-element.58), channel_id=1, source_target_pairs={{0,1},{1,0},{2,3},{3,2},{4,5},{5,4},{6,7},{7,6},{8,9},{9,8},{10,11... | collective-permute-start | bytes 147464 | tf_op jit(solution)/shard_map/ppermute | solution.py:405
  36.3 4.3 %collective-permute-start.15 = (f32[96,128]{1,0:T(8,128)S(1)}, f32[96,128]{1,0:T(8,128)S(1)}, u32[]{:S(2)}, u32[]{:S(2)}) collective-permute-start(f32[96,128]{1,0:T(8,128)S(1)} %get-tuple-element.59), channel_id=1, source_target_pairs={{1,2},{2,1},{5,6},{6,5},{9,10},{10,9},{13,14},{14,13},{17,18},{18,... | collective-permute-start | bytes 147464 | tf_op jit(solution)/shard_map/ppermute | solution.py:463
  40.5 1.3 %collective-permute-start.13 = (f32[96,128]{1,0:T(8,128)S(1)}, f32[96,128]{1,0:T(8,128)S(1)}, u32[]{:S(2)}, u32[]{:S(2)}) collective-permute-start(f32[96,128]{1,0:T(8,128)S(1)} %get-tuple-element.54.time_own), channel_id=1, source_target_pairs={{0,1},{1,0},{2,3},{3,2},{4,5},{5,4},{6,7},{7,6},{8,9},{9,8},{10,11... | collective-permute-start | bytes 147464 | tf_op jit(solution)/shard_map/ppermute | solution.py:405
  43.1 14.0 %collective-permute-start.16 = (f32[96,1024]{1,0:T(8,128)S(1)}, f32[96,1024]{1,0:T(8,128)S(1)}, u32[]{:S(2)}, u32[]{:S(2)}) collective-permute-start(f32[96,1024]{1,0:T(8,128)S(1)} %get-tuple-element.60.surface), channel_id=1, source_target_pairs={{0,1},{1,0},{2,3},{3,2},{4,5},{5,4},{6,7},{7,6},{8,9},{9,8},{10,11... | collective-permute-start | bytes 1179656 | tf_op jit(solution)/shard_map/ppermute | solution.py:405
  43.6 4.1 %collective-permute-start.18 = (bf16[208,128]{1,0:T(8,128)(2,1)S(1)}, bf16[208,128]{1,0:T(8,128)(2,1)S(1)}, u32[]{:S(2)}, u32[]{:S(2)}) collective-permute-start(bf16[208,128]{1,0:T(8,128)(2,1)S(1)} %get-tuple-element.62.mine), channel_id=1, source_target_pairs={{0,2},{2,0},{1,3},{3,1},{4,6},{6,4},{5,7},{7,5},{8,10},{10,8},{9,1... | collective-permute-start | bytes 159752 | tf_op jit(solution)/shard_map/ppermute | solution.py:405
  44.9 3.9 %collective-permute-start.19 = (bf16[208,128]{1,0:T(8,128)(2,1)S(1)}, bf16[208,128]{1,0:T(8,128)(2,1)S(1)}, u32[]{:S(2)}, u32[]{:S(2)}) collective-permute-start(bf16[208,128]{1,0:T(8,128)(2,1)S(1)} %get-tuple-element.63), channel_id=1, source_target_pairs={{0,3},{1,2},{2,1},{3,0},{4,7},{5,6},{6,5},{7,4},{8,11},{9,10},{10,... | collective-permute-start | bytes 159752 | tf_op jit(solution)/shard_map/ppermute | solution.py:405
  45.1 3.8 %collective-permute-start.17 = (bf16[208,128]{1,0:T(8,128)(2,1)S(1)}, bf16[208,128]{1,0:T(8,128)(2,1)S(1)}, u32[]{:S(2)}, u32[]{:S(2)}) collective-permute-start(bf16[208,128]{1,0:T(8,128)(2,1)S(1)} %get-tuple-element.63), channel_id=1, source_target_pairs={{0,1},{1,0},{2,3},{3,2},{4,5},{5,4},{6,7},{7,6},{8,9},{9,8},{10,11... | collective-permute-start | bytes 159752 | tf_op jit(solution)/shard_map/ppermute | solution.py:405
  48.8 6.4 %collective-permute-start.22 = (bf16[208,128]{1,0:T(8,128)(2,1)S(1)}, bf16[208,128]{1,0:T(8,128)(2,1)S(1)}, u32[]{:S(2)}, u32[]{:S(2)}) collective-permute-start(bf16[208,128]{1,0:T(8,128)(2,1)S(1)} %shard_map.95.rest_0_), channel_id=1, source_target_pairs={{0,12},{4,8},{8,4},{12,0},{1,13},{5,9},{9,5},{13,1},{2,14},{6,10},... | collective-permute-start | bytes 159752 | tf_op jit(solution)/shard_map/ppermute | solution.py:405
  51.9 5.1 %collective-permute-start.21 = (bf16[208,128]{1,0:T(8,128)(2,1)S(1)}, bf16[208,128]{1,0:T(8,128)(2,1)S(1)}, u32[]{:S(2)}, u32[]{:S(2)}) collective-permute-start(bf16[208,128]{1,0:T(8,128)(2,1)S(1)} %shard_map.95.rest_0_), channel_id=1, source_target_pairs={{0,8},{4,12},{8,0},{12,4},{1,9},{5,13},{9,1},{13,5},{2,10},{6,14},... | collective-permute-start | bytes 159752 | tf_op jit(solution)/shard_map/ppermute | solution.py:405
  51.9 5.3 %collective-permute-start.20 = (bf16[208,128]{1,0:T(8,128)(2,1)S(1)}, bf16[208,128]{1,0:T(8,128)(2,1)S(1)}, u32[]{:S(2)}, u32[]{:S(2)}) collective-permute-start(bf16[208,128]{1,0:T(8,128)(2,1)S(1)} %shard_map.95.rest_0_), channel_id=1, source_target_pairs={{0,4},{4,0},{8,12},{12,8},{1,5},{5,1},{9,13},{13,9},{2,6},{6,2},{1... | collective-permute-start | bytes 159752 | tf_op jit(solution)/shard_map/ppermute | solution.py:405

commit v13 on v12

--- a/solution.py
+++ b/solution.py
@@ -142,6 +142,10 @@
     return jnp.where(flag, a, b)
 
 
+def in_order(odd, a, b):
+    return pick(odd, a, b), pick(odd, b, a)
+
+
 def model_kernel(half, surface, time_own, piece, predicted, packed, time_t, days_all):
     rank = surface.shape[0]
     days = time_own.shape[0]
@@ -158,24 +162,26 @@
         predicted[:, at:at + 2 * LANES] = dot(time_bf, packed[:, at:at + 2 * LANES], (1, 0))
 
 
-def smooth(half, odd, surface, edge_near, edge_far, cols_a, cols_b, scale, base):
+def smooth(half, surface, edge_near, edge_far, left, right, scale, base):
     core = lax.axis_index("ta")
     rank = surface.shape[0]
+    band = lax.axis_index("lat")
+    outer = pick(core == 0, band == 0, band == lax.axis_size("lat") - 1)
+    edge_far = jnp.where(outer, 0.0, edge_far)
     above = pick(core == 0, edge_far, edge_near)
     below = pick(core == 0, edge_near, edge_far)
-    cols = jnp.concatenate([pick(odd, cols_a, cols_b), pick(odd, cols_b, cols_a)], axis=0)
-    line = lax.broadcasted_iota(jnp.int32, (2 * COLS, half * LANES), 0)
-    lane = lax.broadcasted_iota(jnp.int32, (2 * COLS, half * LANES), 1)
-    from_left = (line >= half) & (line < 2 * half) & (lane == (line - half) * LANES)
-    from_right = (line >= COLS) & (line < COLS + half) & (lane == (line - COLS) * LANES + LANES - 1)
-    sides = dot(cols[:, :rank].astype(BF16), (from_left | from_right).astype(BF16), (0, 0))
+    line = lax.broadcasted_iota(jnp.int32, (2 * half, half * LANES), 0)
+    lane = lax.broadcasted_iota(jnp.int32, (2 * half, half * LANES), 1)
+    place = jnp.where(line < half, line * LANES, (line - half) * LANES + LANES - 1)
+    cols = jnp.concatenate([left, right], axis=0)
+    sides = dot(cols[:, :rank].astype(BF16), (lane == place).astype(BF16), (0, 0))
     if scale is not None:
         above, below, sides = above * scale, below * scale, sides * scale
     for row, strip in enumerate(smoothed(surface, half, above, below, sides)):
         base[:, row * LANES:(row + 1) * LANES] = strip
 
 
-def gradients(half, base, predicted, packed, time_t, seen, summed, fresh):
+def gradients(half, base, predicted, packed, time_t, seen, near, far, fresh):
     rank = time_t.shape[0]
     time_bf = time_t.astype(BF16)
     time_twice = jnp.concatenate([time_bf, time_bf], axis=1)
@@ -190,7 +196,8 @@
         spread = (owner * LANES <= lane + at) & (lane + at < (owner + 1) * LANES)
         weight = dot(seen_bf, spread.astype(BF16), (0, 0))
         part = packed[:, at:at + width]
-        residual = weight * predicted[:, at:at + width] - summed[:, at:at + width]
+        summed = jnp.concatenate([near[:, at:at + width], far[:, at:at + width]], axis=0)
+        residual = weight * predicted[:, at:at + width] - summed
         high = residual.astype(BF16)
         low = (residual - high.astype(F32)).astype(BF16)
         both = jnp.concatenate([high, low], axis=0)
@@ -207,22 +214,46 @@
     return grad_time[:, :LANES] + grad_time[:, LANES:], grad_diag, norm
 
 
-def post_own(half, sums, fresh, message, crossing, edge_near, edge_far):
-    grad_time, grad_diag, norm = sums
-    core = lax.axis_index("ta")
-    rank = norm.shape[0]
-    days = LANES // 2
-    own = lax.broadcasted_iota(jnp.int32, grad_time.shape, 1) < days
-    last = column_as_row(norm)
-    message[:rank, :] = jnp.where(own, grad_time, pltpu.roll(grad_diag, days, 1))
-    message[rank:rank + NORM, :] = last
-    message[rank + NORM:, :] = jnp.zeros((COLS, LANES), F32)
-    message[rank + NORM:, :rank] = border(fresh[...], half)
-    crossing[:rank, :] = jnp.where(own, pltpu.roll(grad_time, days, 1), grad_diag)
-    crossing[rank:, :] = last
-    first_row, last_row = fresh[:, :LANES], fresh[:, (half - 1) * LANES:]
-    edge_near[...] = pick(core == 0, last_row, first_row)
-    edge_far[...] = pick(core == 0, first_row, last_row)
+def side_gradients(half, first, predicted, packed, time_t, seen, summed, take):
+    rank, days = time_t.shape[0], summed.shape[0]
+    below = lax.broadcasted_iota(jnp.int32, time_t.shape, 1) < days
+    moved = pltpu.roll(time_t, days, 1)
+    time_twice = (jnp.where(below, moved, time_t) if first else jnp.where(below, time_t, moved)).astype(BF16)
+    seen_bf = seen[:, :days].astype(BF16)
+    owner = lax.broadcasted_iota(jnp.int32, (TAIL, WIDTH), 0)
+    lane = lax.broadcasted_iota(jnp.int32, (TAIL, WIDTH), 1)
+    grad_time = jnp.zeros((rank, LANES), F32)
+    grad_diag = jnp.zeros((rank, LANES), F32)
+    for at in range(0, half * LANES, WIDTH):
+        spread = (owner * LANES <= lane + at) & (lane + at < (owner + 1) * LANES)
+        weight = dot(seen_bf, spread.astype(BF16), (0, 0))
+        part = packed[:, at:at + WIDTH]
+        residual = weight * predicted[first:first + days, at:at + WIDTH] - summed[:, at:at + WIDTH]
+        high = residual.astype(BF16)
+        low = (residual - high.astype(F32)).astype(BF16)
+        both = jnp.concatenate([high, low], axis=0)
+        take(at, dot(time_twice, both, (1, 0)))
+        grad_time = grad_time + dot(part, both, (1, 1))
+        wide = part.astype(F32)
+        for row in range(WIDTH // LANES):
+            strip = row_of(wide, row)
+            square = jnp.sum(strip * strip, axis=1, keepdims=True)
+            grad_diag = grad_diag + square * seen[at // LANES + row:at // LANES + row + 1, :]
+    return jnp.where(below, grad_time + pltpu.roll(grad_time, days, 1), pltpu.roll(grad_diag, days, 1))
+
+
+def add_up(parts, rows):
+    value = parts[0][rows, :].astype(F32)
+    for piece in parts[1:]:
+        value = value + piece[rows, :].astype(F32)
+    return value
+
+
+def unpack_pieces(half, parts, summed, seen):
+    days = summed.shape[0]
+    for row in range(half):
+        summed[:, row * LANES:(row + 1) * LANES] = add_up(parts, slice(row * days, (row + 1) * days))
+    seen[...] = add_up(parts, slice(half * days, half * days + TAIL))
 
 
 def narrow(value, rank):
@@ -245,32 +276,43 @@
         out[: 2 * rank, :], out[2 * rank:, :] = narrow(jnp.concatenate([*parts, last], axis=0), rank)
 
 
-def first_kernel(half, days, order, paired, swap, surface, edge_near, predicted, packed, time_t, *rest):
+def near_kernel(half, days, order, paired, swap, surface, edge_near, predicted, packed, time_t, edge_far, *rest):
     pieces, rest = dict(zip(order, rest)), rest[len(order):]
-    edge_far_in, rest = rest[0], rest[1:]
+    cols, (base, block, summed, seen) = rest[:-4], rest[-4:]
     if paired:
         at = half * days + TAIL
-        cols = [ref[at:, :].astype(F32) for ref in (rest[0], pieces[0, 2])]
-        rest = rest[1:]
-    else:
-        cols, rest = [ref[...] for ref in rest[:2]], rest[2:]
-    fresh, message, crossing, edge_out, edge_far, summed, seen, base = rest
-    smooth(half, swap(), surface[...], edge_near[...], edge_far_in[...], *cols, None, base)
-    sides = [[pieces[key] for key in sorted(pieces) if key[0] == side] for side in (0, 1)]
-
-    def add_up(parts, rows):
-        value = parts[0][rows, :].astype(F32)
-        for piece in parts[1:]:
-            value = value + piece[rows, :].astype(F32)
-        return value
-
-    for row in range(half):
-        for first, parts in zip((0, days), sides):
-            summed[first:first + days, row * LANES:(row + 1) * LANES] = add_up(parts, slice(row * days, (row + 1) * days))
-    near, far = (add_up(parts, slice(half * days, half * days + TAIL)) for parts in sides)
-    seen[...] = near + pltpu.roll(far, days, 1)
-    sums = gradients(half, base, predicted, packed, time_t[...], seen[...], summed, fresh)
-    post_own(half, sums, fresh, message, crossing, edge_out, edge_far)
+        cols = in_order(swap(), *[ref[at:, :].astype(F32) for ref in (cols[0], pieces[0, 2])])
+    left, right = (ref[...] for ref in cols)
+    smooth(half, surface[...], edge_near[...], edge_far[...], left[half:, :], right[:half, :], None, base)
+    unpack_pieces(half, [pieces[key] for key in sorted(pieces)], summed, seen)
+
+    def take(at, grad_space):
+        base[:, at:at + WIDTH] = base[:, at:at + WIDTH] - ETA_SPACE * grad_space
+
+    block[...] = side_gradients(half, 0, predicted, packed, time_t[...], seen, summed, take)
+
+
+def far_kernel(half, days, n_lon, base, predicted, packed, time_t, block, *rest):
+    parts, rest = rest[:n_lon], rest[n_lon:]
+    fresh, message, crossing, cols, edge_near, edge_far, summed, seen = rest
+    core = lax.axis_index("ta")
+    rank = block.shape[0]
+    unpack_pieces(half, parts, summed, seen)
+
+    def take(at, grad_space):
+        fresh[:, at:at + WIDTH] = base[:, at:at + WIDTH] - ETA_SPACE * grad_space
+
+    crossing[:rank, :] = side_gradients(half, days, predicted, packed, time_t[...], seen, summed, take)
+    message[:rank, :] = block[...]
+    new = fresh[...]
+    norm = column_as_row(jnp.sum(new * new, axis=1, keepdims=True))
+    message[rank:, :] = norm
+    crossing[rank:, :] = norm
+    cols[...] = jnp.zeros(cols.shape, F32)
+    cols[:, :rank] = border(new, half)
+    first_row, last_row = row_of(new, 0), row_of(new, half - 1)
+    edge_near[...] = pick(core == 0, last_row, first_row)
+    edge_far[...] = pick(core == 0, first_row, last_row)
 
 
 def total_of(parts):
@@ -279,6 +321,27 @@
         one, two, three = (part[...].astype(F32) for part in parts[1:])
         total = (total + one) + (two + three)
     return total
+
+
+def packed_norm(norm, cols, rank):
+    free = LANES - rank
+    line = lax.broadcasted_iota(jnp.int32, cols.shape, 0)
+    lane = lax.broadcasted_iota(jnp.int32, cols.shape, 1)
+    for part in range(rank // free):
+        moved = pltpu.roll(norm, rank - part * free, 1)
+        cols = jnp.where((lane >= rank) & (line == part), moved, cols)
+    return cols
+
+
+def unpacked(block, rank):
+    free = LANES - rank
+    line = lax.broadcasted_iota(jnp.int32, block.shape, 0)
+    lane = lax.broadcasted_iota(jnp.int32, block.shape, 1)
+    norm = jnp.zeros(block.shape, F32)
+    for part in range(rank // free):
+        row = jnp.where((lane >= rank) & (line == part), block, 0.0)
+        norm = norm + pltpu.roll(row, LANES - rank + part * free, 1)
+    return jnp.broadcast_to(jnp.sum(norm, axis=0, keepdims=True), block.shape)
 
 
 def own_kernel(n_parts, time_t, *rest):
@@ -289,7 +352,7 @@
     block = total[:rank, :]
     own = lax.broadcasted_iota(jnp.int32, block.shape, 1) < days
     time_own[...] = jnp.where(own, time_t[...] - block / (pltpu.roll(block, days, 1) + RIDGE), 0.0)
-    norm[...] = total[rank:rank + NORM, :]
+    norm[...] = unpacked(total[rank:, :], rank) if n_parts > 1 else total[rank:, :]
 
 
 def rescaling(counts, norm, time_new):
@@ -301,7 +364,7 @@
     return jnp.sqrt(jnp.sqrt(ratio))
 
 
-def second_kernel(half, counts, swap, surface, time_own, time_other, norm, summed, seen, edge_near, edge_far, cols_a, cols_b, *rest):
+def second_kernel(half, counts, paired, swap, surface, time_own, time_other, norm, near, far, seen_near, seen_far, edge_near, edge_far, cols_a, cols_b, *rest):
     fresh, time_out, message, outgoing, scaled, base, predicted, packed = rest
     rank = surface.shape[0]
     time_new = time_own[...] + pltpu.roll(time_other[...], LANES // 2, 1)
@@ -313,9 +376,13 @@
     time_bf = time_now.astype(BF16)
     for at in range(0, half * LANES, WIDTH):
         predicted[:, at:at + WIDTH] = dot(time_bf, packed[:, at:at + WIDTH], (0, 0))
-    cols = [ref[ref.shape[0] - COLS:, :] for ref in (cols_a, cols_b)]
-    smooth(half, swap(), scaled[...], edge_near[...], edge_far[...], *cols, scale, base)
-    sums = gradients(half, base, predicted, packed, time_now, seen[...], summed, fresh)
+    if paired:
+        left, right = in_order(swap(), cols_a[rank:, :], cols_b[rank:, :])
+    else:
+        left, right = cols_a[half:, :], cols_b[:half, :]
+    smooth(half, scaled[...], edge_near[...], edge_far[...], left, right, scale, base)
+    seen = seen_near[...] + pltpu.roll(seen_far[...], LANES // 2, 1)
+    sums = gradients(half, base, predicted, packed, time_now, seen, near, far, fresh)
     post_all(sums, message, outgoing)
 
 
@@ -359,10 +426,13 @@
     total[...] = mine[: total.shape[0], :] + core[...]
 
 
-def band_sum_kernel(mine, band, message, total):
-    rows = mine.shape[0]
-    total[:rows, :] = mine[...] + band[...]
-    total[rows:, :] = message[rows:, :]
+def band_sum_kernel(half, swap, mine, band, cols, *totals):
+    rank = mine.shape[0] - NORM
+    value = mine[...] + band[...]
+    borders = in_order(swap(), cols[:half, :], cols[half:, :])
+    for total, lines in zip(totals, borders):
+        total[:rank, :] = value[:rank, :]
+        total[rank:, :] = value[rank:, :] if len(totals) == 1 else packed_norm(value[rank:, :], lines, rank)
 
 
 def all_sum_kernel(rank, mine, core, band, both, total):
@@ -459,7 +529,7 @@
     order = list(pieces)
 
     def bands(edge):
-        there = [(2 * band + 1, 2 * band + 2) for band in range(n_lat - 1)]
+        there = [(2 * band + 1, (2 * band + 2) % (2 * n_lat)) for band in range(n_lat)]
         return lax.ppermute(edge, ("lat", "ta"), there + [(b, a) for a, b in there])
 
     def swap():
@@ -478,11 +548,16 @@
     )(surface, factor_time, pieces[1, 0])
 
     fresh, edge = shape((rank, wide)), shape((rank, LANES))
-    surface, message, crossing, edge_near, edge_far, summed, seen = call(
-        functools.partial(first_kernel, half, days, order, paired, swap),
-        [fresh, shape((own_rows + COLS, LANES)), shape((own_rows, LANES)), edge, edge, shape((2 * days, wide)), shape((TAIL, LANES))],
-        [pltpu.VMEM((rank, wide), F32)],
-    )(surface, edge_near, predicted, packed, time_t, *[pieces[key] for key in order], bands(edge_far), *(borders if paired else columns(cols)))
+    sides = [[key for key in order if key[0] == side] for side in (0, 1)]
+    side_out = [shape((days, wide)), shape((TAIL, LANES))]
+    base, block, near, seen_near = call(
+        functools.partial(near_kernel, half, days, sides[0], paired, swap),
+        [fresh, edge, *side_out],
+    )(surface, edge_near, predicted, packed, time_t, bands(edge_far), *[pieces[key] for key in sides[0]], *(borders if paired else columns(cols)))
+    surface, message, crossing, cols, edge_near, edge_far, far, seen_far = call(
+        functools.partial(far_kernel, half, days, len(sides[1])),
+        [fresh, shape((own_rows, LANES)), shape((own_rows, LANES)), shape((COLS, LANES)), edge, edge, *side_out],
+    )(base, predicted, packed, time_t, block, *[pieces[key] for key in sides[1]])
 
     narrowed = shape((sum_rows + NORM, LANES), BF16)
 
@@ -504,16 +579,22 @@
         return mine, across(core, "ta", 1), across(mine, "lat", 1), across(both, ("lat", "ta"), 3)
 
     total = call(core_sum_kernel, shape(crossing.shape))(message, across(crossing, "ta", 1))
-    total = call(band_sum_kernel, shape(message.shape))(total, across(total, "lat", 1), message)
-    parts = over_lon(doubled(total, "lat", 2))
-    cols = (parts[1], parts[3]) if paired else columns(message[own_rows:])
+    direct = paired and n_lat == 2
+    band_sum = functools.partial(band_sum_kernel, half, swap)
+    total, *again = call(band_sum, [shape(crossing.shape)] * (1 + direct))(total, across(total, "lat", 1), cols)
+    if direct:
+        parts = [total] + [across(value, "lon", step) for step, value in ((1, total), (2, again[0]), (3, again[0]))]
+        cols = parts[1], parts[3]
+    else:
+        parts = [doubled(doubled(total, "lat", 2), "lon", 1)]
+        cols = columns(cols)
     time_own, norm = call(functools.partial(own_kernel, len(parts)), [edge, shape((NORM, LANES))])(time_t, *parts)
 
     surface, time_t, message, outgoing = call(
-        functools.partial(second_kernel, half, counts, swap),
+        functools.partial(second_kernel, half, counts, direct, swap),
         [fresh, edge, narrowed, narrowed],
         [pltpu.VMEM((rank, wide), F32), pltpu.VMEM((rank, wide), F32), pltpu.VMEM((2 * days, wide), F32), pltpu.VMEM((rank, wide), BF16)],
-    )(surface, time_own, across(time_own, "ta", 1), norm, summed, seen, across(edge_near, "ta", 1), bands(edge_far), *cols)
+    )(surface, time_own, across(time_own, "ta", 1), norm, near, far, seen_near, seen_far, across(edge_near, "ta", 1), bands(edge_far), *cols)
 
     other = across(surface, "ta", 1)
     total = narrowed if paired and n_lat == 2 else shape((sum_rows, LANES))

time: 58.7 us -> 58 us (0.988)
  waiting for transfers between devices: 25.4 us -> 24.7 us
  starting transfers between devices: 25.5 us -> 24.9 us
    ppermute x21, waiting for transfers between devices: 25.4 us -> 22.5 us  [across(): lax.ppermute(value, axis, [(i, i ^ step) for i in range(lax.axis_size(axi...]
    ppermute x2, waiting for transfers between devices: 0.01 us -> 2.18 us  [bands(): return lax.ppermute(edge, ('lat', 'ta'), there + [(b, a) for a, b in there])]
    ppermute x21, starting transfers between devices: 24.2 us -> 23.3 us  [across(): lax.ppermute(value, axis, [(i, i ^ step) for i in range(lax.axis_size(axi...]
    pallas_call x11 -> x12, Pallas kernels: 6.94 us -> 7.49 us  [run(): pl.pallas_call(kernel, out_shape=out_shape, in_specs=[pl.BlockSpec(memory...]
  transfers between devices with their start and end apart: 23 -> 23, of which waited for: 15 -> 14; matrix products, arithmetic and copies ran while one was open for 0% -> 0% of each run, Pallas kernels for 1% -> 2%
where the time goes in v13:
time: 58 us; the launch traced here: 57.8 us
  starting transfers between devices  24.9 us (43%)
  waiting for transfers between devices  24.7 us (43%)
  Pallas kernels  7.49 us (13%)
  between operations  0.74 us (1%)
    ppermute x21, starting transfers between devices, across(): lax.ppermute(value, axis, [(i, i ^ step) for i in range(lax.axis_size(axi...  23.3 us
    ppermute x21, waiting for transfers between devices, across(): lax.ppermute(value, axis, [(i, i ^ step) for i in range(lax.axis_size(axi...  22.5 us
    pallas_call x12, Pallas kernels, run(): pl.pallas_call(kernel, out_shape=out_shape, in_specs=[pl.BlockSpec(memory...  7.49 us
    ppermute x2, waiting for transfers between devices, bands(): return lax.ppermute(edge, ('lat', 'ta'), there + [(b, a) for a, b in there])  2.18 us
    ppermute x2, starting transfers between devices, bands(): return lax.ppermute(edge, ('lat', 'ta'), there + [(b, a) for a, b in there])  1.6 us
  transfers between devices with their start and end apart: 23, of which 14 were waited for; matrix products, arithmetic and copies ran while one was open for 0% of the time, Pallas kernels for 2%

profile of v13, /device:TPU:0, one launch (start us, length us, event | category | flops | bytes accessed | tf_op | source)
XLA Modules:
  0.0 57.8 jit_solution(16885383863219521847)
XLA Ops:
  0.6 2.7 %shard_map.86 = (bf16[544,128]{1,0:T(8,128)(2,1)S(1)}, bf16[528,128]{1,0:T(8,128)(2,1)S(1)}, bf16[528,128]{1,0:T(8,128)(2,1)S(1)}, bf16[528,128]{1,0:T(8,128)(2,...) custom-call(s32[1,4,32]{2,1,0:T(4,128)} %list_hbm.1, ...), custom_call_target="tpu_custom_call" | custom-call | flops 1000000 | bytes 1000000 | tf_op jit(solution)/shard_map/pallas_call | solution.py:461
  3.3 3.1 %collective-permute-start.3 = (bf16[544,128]{1,0:T(8,128)(2,1)S(1)}, bf16[544,128]{1,0:T(8,128)(2,1)S(1)}, u32[]{:S(2)}, u32[]{:S(2)}) collective-permute-start(bf16[544,128]{1,0:T(8,128)(2,1)S(1)} %get-tuple-element.53), channel_id=1, source_target_pairs={{0,4},{4,0},{8,12},{12,8},{1,5},{5,1},{9,13},{13,9},{2,6},{6,2},{1... | collective-permute-start | bytes 417800 | tf_op jit(solution)/shard_map/ppermute | solution.py:475
  6.5 4.4 %collective-permute-done.3.theirs.rest_3_ = bf16[544,128]{1,0:T(8,128)(2,1)S(1)} collective-permute-done((bf16[544,128]{1,0:T(8,128)(2,1)S(1)}, bf16[544,128]{1,0:T(8,128)(2,1)S(1)}, u32[]{:S(2)}, u32[]{:S(2)}) %collective-permute-start.3) | collective-permute-done | bytes 139296 | tf_op jit(solution)/shard_map/ppermute | solution.py:475
  11.0 3.1 %collective-permute-start.4 = (bf16[544,128]{1,0:T(8,128)(2,1)S(1)}, bf16[544,128]{1,0:T(8,128)(2,1)S(1)}, u32[]{:S(2)}, u32[]{:S(2)}) collective-permute-start(bf16[544,128]{1,0:T(8,128)(2,1)S(1)} %shard_map.89), channel_id=1, source_target_pairs={{0,8},{4,12},{8,0},{12,4},{1,9},{5,13},{9,1},{13,5},{2,10},{6,14},... | collective-permute-start | bytes 417800 | tf_op jit(solution)/shard_map/ppermute | solution.py:475
  14.1 1.6 %collective-permute-start.5 = (bf16[528,128]{1,0:T(8,128)(2,1)S(1)}, bf16[528,128]{1,0:T(8,128)(2,1)S(1)}, u32[]{:S(2)}, u32[]{:S(2)}) collective-permute-start(bf16[528,128]{1,0:T(8,128)(2,1)S(1)} %get-tuple-element.54), channel_id=1, source_target_pairs={{0,4},{4,0},{8,12},{12,8},{1,5},{5,1},{9,13},{13,9},{2,6},{6,2},{1... | collective-permute-start | bytes 405512 | tf_op jit(solution)/shard_map/ppermute | solution.py:475
  15.8 2.7 %collective-permute-start.7 = (bf16[528,128]{1,0:T(8,128)(2,1)S(1)}, bf16[528,128]{1,0:T(8,128)(2,1)S(1)}, u32[]{:S(2)}, u32[]{:S(2)}) collective-permute-start(bf16[528,128]{1,0:T(8,128)(2,1)S(1)} %get-tuple-element.59), channel_id=1, source_target_pairs={{0,5},{1,4},{4,1},{5,0},{8,13},{9,12},{12,9},{13,8},{2,7},{3,6},{6... | collective-permute-start | bytes 405512 | tf_op jit(solution)/shard_map/ppermute | solution.py:475
  18.8 1.6 %collective-permute-done.5.rest_1_ = bf16[528,128]{1,0:T(8,128)(2,1)S(1)} collective-permute-done((bf16[528,128]{1,0:T(8,128)(2,1)S(1)}, bf16[528,128]{1,0:T(8,128)(2,1)S(1)}, u32[]{:S(2)}, u32[]{:S(2)}) %collective-permute-start.5) | collective-permute-done | bytes 135200 | tf_op jit(solution)/shard_map/ppermute | solution.py:475
  20.4 2.2 %collective-permute-done.2.edge_far = f32[96,128]{1,0:T(8,128)S(1)} collective-permute-done((f32[96,128]{1,0:T(8,128)S(1)}, f32[96,128]{1,0:T(8,128)S(1)}, u32[]{:S(2)}, u32[]{:S(2)}) %collective-permute-start.2) | collective-permute-done | bytes 49184 | tf_op jit(solution)/shard_map/ppermute | solution.py:533
  22.6 0.8 %shard_map.90 = (f32[96,1024]{1,0:T(8,128)S(1)}, f32[96,128]{1,0:T(8,128)S(1)}, f32[64,1024]{1,0:T(8,128)S(1)}, f32[16,128]{1,0:T(8,128)S(1)}) custom-call(f32[96,1024]{1,0:T(8,128)S(1)} %get-tuple-element.41.surface, f32[96,128]{1,0:T(8,128)S(1)} %get-tuple-element.42.edge_near, f32[128,1024]{1,0:T(8,128)S(1)} %get-tuple-element.44.predicted, ...), custom_call_target="tpu_custom_call" | custom-call | flops 1000000 | bytes 1000000 | tf_op jit(solution)/shard_map/pallas_call | solution.py:461
  23.4 1.4 %collective-permute-done.6.rest_0_ = bf16[528,128]{1,0:T(8,128)(2,1)S(1)} collective-permute-done((bf16[528,128]{1,0:T(8,128)(2,1)S(1)}, bf16[528,128]{1,0:T(8,128)(2,1)S(1)}, u32[]{:S(2)}, u32[]{:S(2)}) %collective-permute-start.6) | collective-permute-done | bytes 135200 | tf_op jit(solution)/shard_map/ppermute | solution.py:475
  24.8 0.4 collective-permute-done.7.rest_2_
  25.2 0.7 %shard_map.91 = (f32[96,1024]{1,0:T(8,128)S(1)}, f32[104,128]{1,0:T(8,128)S(1)}, f32[104,128]{1,0:T(8,128)S(1)}, f32[16,128]{1,0:T(8,128)S(1)}, f32[96,128]{1,0:...) custom-call(f32[96,1024]{1,0:T(8,128)S(1)} %get-tuple-element.56.base, ...), custom_call_target="tpu_custom_call" | custom-call | flops 1000000 | bytes 1000000 | tf_op jit(solution)/shard_map/pallas_call | solution.py:461
  26.1 1.1 %collective-permute-done.8.core = f32[104,128]{1,0:T(8,128)S(1)} collective-permute-done((f32[104,128]{1,0:T(8,128)S(1)}, f32[104,128]{1,0:T(8,128)S(1)}, u32[]{:S(2)}, u32[]{:S(2)}) %collective-permute-start.8) | collective-permute-done | bytes 53280 | tf_op jit(solution)/shard_map/ppermute | solution.py:475
  27.3 1.7 %collective-permute-start.9 = (f32[104,128]{1,0:T(8,128)S(1)}, f32[104,128]{1,0:T(8,128)S(1)}, u32[]{:S(2)}, u32[]{:S(2)}) collective-permute-start(f32[104,128]{1,0:T(8,128)S(1)} %shard_map.92.mine), channel_id=1, source_target_pairs={{0,2},{2,0},{1,3},{3,1},{4,6},{6,4},{5,7},{7,5},{8,10},{10,8},{9,1... | collective-permute-start | bytes 159752 | tf_op jit(solution)/shard_map/ppermute | solution.py:475
  29.0 2.5 %collective-permute-done.9.band = f32[104,128]{1,0:T(8,128)S(1)} collective-permute-done((f32[104,128]{1,0:T(8,128)S(1)}, f32[104,128]{1,0:T(8,128)S(1)}, u32[]{:S(2)}, u32[]{:S(2)}) %collective-permute-start.9) | collective-permute-done | bytes 53280 | tf_op jit(solution)/shard_map/ppermute | solution.py:475
  31.6 0.7 %collective-permute-start.10 = (f32[104,128]{1,0:T(8,128)S(1)}, f32[104,128]{1,0:T(8,128)S(1)}, u32[]{:S(2)}, u32[]{:S(2)}) collective-permute-start(f32[104,128]{1,0:T(8,128)S(1)} %get-tuple-element.64.rest_0_), channel_id=1, source_target_pairs={{0,4},{4,0},{8,12},{12,8},{1,5},{5,1},{9,13},{13,9},{2,6},{6,2},{1... | collective-permute-start | bytes 159752 | tf_op jit(solution)/shard_map/ppermute | solution.py:475
  32.3 2.6 %collective-permute-start.12 = (f32[104,128]{1,0:T(8,128)S(1)}, f32[104,128]{1,0:T(8,128)S(1)}, u32[]{:S(2)}, u32[]{:S(2)}) collective-permute-start(f32[104,128]{1,0:T(8,128)S(1)} %get-tuple-element.65), channel_id=1, source_target_pairs={{0,12},{4,8},{8,4},{12,0},{1,13},{5,9},{9,5},{13,1},{2,14},{6,10},... | collective-permute-start | bytes 159752 | tf_op jit(solution)/shard_map/ppermute | solution.py:475
  34.8 0.5 collective-permute-start.11
  35.3 1.6 %collective-permute-start.15 = (f32[96,128]{1,0:T(8,128)S(1)}, f32[96,128]{1,0:T(8,128)S(1)}, u32[]{:S(2)}, u32[]{:S(2)}) collective-permute-start(f32[96,128]{1,0:T(8,128)S(1)} %get-tuple-element.73), channel_id=1, source_target_pairs={{1,2},{3,0},{2,1},{0,3},{5,6},{7,4},{6,5},{4,7},{9,10},{11,8},{10,... | collective-permute-start | bytes 147464 | tf_op jit(solution)/shard_map/ppermute | solution.py:533
  36.9 1.6 %collective-permute-done.12.rest_3_.cols_b = f32[104,128]{1,0:T(8,128)S(1)} collective-permute-done((f32[104,128]{1,0:T(8,128)S(1)}, f32[104,128]{1,0:T(8,128)S(1)}, u32[]{:S(2)}, u32[]{:S(2)}) %collective-permute-start.12) | collective-permute-done | bytes 53280 | tf_op jit(solution)/shard_map/ppermute | solution.py:475
  38.5 1.4 %collective-permute-done.11.rest_2_ = f32[104,128]{1,0:T(8,128)S(1)} collective-permute-done((f32[104,128]{1,0:T(8,128)S(1)}, f32[104,128]{1,0:T(8,128)S(1)}, u32[]{:S(2)}, u32[]{:S(2)}) %collective-permute-start.11) | collective-permute-done | bytes 53280 | tf_op jit(solution)/shard_map/ppermute | solution.py:475
  40.1 1.2 %collective-permute-done.13.time_other = f32[96,128]{1,0:T(8,128)S(1)} collective-permute-done((f32[96,128]{1,0:T(8,128)S(1)}, f32[96,128]{1,0:T(8,128)S(1)}, u32[]{:S(2)}, u32[]{:S(2)}) %collective-permute-start.13) | collective-permute-done | bytes 49184 | tf_op jit(solution)/shard_map/ppermute | solution.py:475
  41.3 1.3 %shard_map.95 = (f32[96,1024]{1,0:T(8,128)S(1)}, f32[96,128]{1,0:T(8,128)S(1)}, bf16[208,128]{1,0:T(8,128)(2,1)S(1)}, bf16[208,128]{1,0:T(8,128)(2,1)S(1)}) custom-call(f32[96,1024]{1,0:T(8,128)S(1)} %get-tuple-element.60.surface, f32[96,128]{1,0:T(8,128)S(1)} %get-tuple-element.66.time_own, f32[96,128]{1,0:T(8,128)S(1)} %collective-permute-done.13.time_other, ...), custom_call_target="tpu_custom_call" | custom-call | flops 1000000 | bytes 1000000 | tf_op jit(solution)/shard_map/pallas_call | solution.py:461
  42.8 1.5 %collective-permute-start.18 = (bf16[208,128]{1,0:T(8,128)(2,1)S(1)}, bf16[208,128]{1,0:T(8,128)(2,1)S(1)}, u32[]{:S(2)}, u32[]{:S(2)}) collective-permute-start(bf16[208,128]{1,0:T(8,128)(2,1)S(1)} %get-tuple-element.76.mine), channel_id=1, source_target_pairs={{0,2},{2,0},{1,3},{3,1},{4,6},{6,4},{5,7},{7,5},{8,10},{10,8},{9,1... | collective-permute-start | bytes 159752 | tf_op jit(solution)/shard_map/ppermute | solution.py:475
  44.5 0.4 collective-permute-start.17
  44.9 2.0 %collective-permute-done.18.band = bf16[208,128]{1,0:T(8,128)(2,1)S(1)} collective-permute-done((bf16[208,128]{1,0:T(8,128)(2,1)S(1)}, bf16[208,128]{1,0:T(8,128)(2,1)S(1)}, u32[]{:S(2)}, u32[]{:S(2)}) %collective-permute-start.18) | collective-permute-done | bytes 53280 | tf_op jit(solution)/shard_map/ppermute | solution.py:475
  46.9 1.2 %collective-permute-done.19.both = bf16[208,128]{1,0:T(8,128)(2,1)S(1)} collective-permute-done((bf16[208,128]{1,0:T(8,128)(2,1)S(1)}, bf16[208,128]{1,0:T(8,128)(2,1)S(1)}, u32[]{:S(2)}, u32[]{:S(2)}) %collective-permute-start.19) | collective-permute-done | bytes 53280 | tf_op jit(solution)/shard_map/ppermute | solution.py:475
  48.2 2.6 %collective-permute-start.22 = (bf16[208,128]{1,0:T(8,128)(2,1)S(1)}, bf16[208,128]{1,0:T(8,128)(2,1)S(1)}, u32[]{:S(2)}, u32[]{:S(2)}) collective-permute-start(bf16[208,128]{1,0:T(8,128)(2,1)S(1)} %shard_map.96.rest_0_), channel_id=1, source_target_pairs={{0,12},{4,8},{8,4},{12,0},{1,13},{5,9},{9,5},{13,1},{2,14},{6,10},... | collective-permute-start | bytes 159752 | tf_op jit(solution)/shard_map/ppermute | solution.py:475
  50.8 1.8 %collective-permute-start.20 = (bf16[208,128]{1,0:T(8,128)(2,1)S(1)}, bf16[208,128]{1,0:T(8,128)(2,1)S(1)}, u32[]{:S(2)}, u32[]{:S(2)}) collective-permute-start(bf16[208,128]{1,0:T(8,128)(2,1)S(1)} %shard_map.96.rest_0_), channel_id=1, source_target_pairs={{0,4},{4,0},{8,12},{12,8},{1,5},{5,1},{9,13},{13,9},{2,6},{6,2},{1... | collective-permute-start | bytes 159752 | tf_op jit(solution)/shard_map/ppermute | solution.py:475
  52.7 1.9 %collective-permute-done.22.rest_3_ = bf16[208,128]{1,0:T(8,128)(2,1)S(1)} collective-permute-done((bf16[208,128]{1,0:T(8,128)(2,1)S(1)}, bf16[208,128]{1,0:T(8,128)(2,1)S(1)}, u32[]{:S(2)}, u32[]{:S(2)}) %collective-permute-start.22) | collective-permute-done | bytes 53280 | tf_op jit(solution)/shard_map/ppermute | solution.py:475
  54.6 1.8 %collective-permute-done.21.rest_2_ = bf16[208,128]{1,0:T(8,128)(2,1)S(1)} collective-permute-done((bf16[208,128]{1,0:T(8,128)(2,1)S(1)}, bf16[208,128]{1,0:T(8,128)(2,1)S(1)}, u32[]{:S(2)}, u32[]{:S(2)}) %collective-permute-start.21) | collective-permute-done | bytes 53280 | tf_op jit(solution)/shard_map/ppermute | solution.py:475
  56.4 1.4 %shard_map.97 = (f32[1536,128]{1,0:T(8,128)}, f32[64,96]{1,0:T(8,128)}) custom-call(f32[96,1024]{1,0:T(8,128)S(1)} %get-tuple-element.74.surface, f32[96,1024]{1,0:T(8,128)S(1)} %collective-permute-done.16.other, f32[96,128]{1,0:T(8,128)S(1)} %get-tuple-element.75.time_t, bf16[208,128]{1,0:T(8,128)(2,1)S(1)} %shard_map.96.rest_0_, ...), custom_call_target="tpu_custom_call" | custom-call | flops 1000000 | bytes 1000000 | tf_op jit(solution)/shard_map/pallas_call | solution.py:461
  (28 shorter events, 1.4 us)
Async XLA Ops:
  3.3 7.6 %collective-permute-start.3 = (bf16[544,128]{1,0:T(8,128)(2,1)S(1)}, bf16[544,128]{1,0:T(8,128)(2,1)S(1)}, u32[]{:S(2)}, u32[]{:S(2)}) collective-permute-start(bf16[544,128]{1,0:T(8,128)(2,1)S(1)} %get-tuple-element.53), channel_id=1, source_target_pairs={{0,4},{4,0},{8,12},{12,8},{1,5},{5,1},{9,13},{13,9},{2,6},{6,2},{1... | collective-permute-start | bytes 417800 | tf_op jit(solution)/shard_map/ppermute | solution.py:475
  6.4 9.3 %collective-permute-start.1 = (bf16[528,128]{1,0:T(8,128)(2,1)S(1)}, bf16[528,128]{1,0:T(8,128)(2,1)S(1)}, u32[]{:S(2)}, u32[]{:S(2)}) collective-permute-start(bf16[528,128]{1,0:T(8,128)(2,1)S(1)} %get-tuple-element.48), channel_id=1, source_target_pairs={{0,4},{4,0},{8,12},{12,8},{1,5},{5,1},{9,13},{13,9},{2,6},{6,2},{1... | collective-permute-start | bytes 405512 | tf_op jit(solution)/shard_map/ppermute | solution.py:475
  6.5 12.1 %collective-permute-start = (bf16[720,128]{1,0:T(8,128)(2,1)S(1)}, bf16[720,128]{1,0:T(8,128)(2,1)S(1)}, u32[]{:S(2)}, u32[]{:S(2)}) collective-permute-start(bf16[720,128]{1,0:T(8,128)(2,1)S(1)} %get-tuple-element.43), channel_id=1, source_target_pairs={{0,1},{1,0},{4,5},{5,4},{8,9},{9,8},{12,13},{13,12},{2,3},{3,2},{6... | collective-permute-start | bytes 552968 | tf_op jit(solution)/shard_map/ppermute | solution.py:475
  11.0 11.6 %collective-permute-start.4 = (bf16[544,128]{1,0:T(8,128)(2,1)S(1)}, bf16[544,128]{1,0:T(8,128)(2,1)S(1)}, u32[]{:S(2)}, u32[]{:S(2)}) collective-permute-start(bf16[544,128]{1,0:T(8,128)(2,1)S(1)} %shard_map.89), channel_id=1, source_target_pairs={{0,8},{4,12},{8,0},{12,4},{1,9},{5,13},{9,1},{13,5},{2,10},{6,14},... | collective-permute-start | bytes 417800 | tf_op jit(solution)/shard_map/ppermute | solution.py:475
  14.1 6.3 %collective-permute-start.5 = (bf16[528,128]{1,0:T(8,128)(2,1)S(1)}, bf16[528,128]{1,0:T(8,128)(2,1)S(1)}, u32[]{:S(2)}, u32[]{:S(2)}) collective-permute-start(bf16[528,128]{1,0:T(8,128)(2,1)S(1)} %get-tuple-element.54), channel_id=1, source_target_pairs={{0,4},{4,0},{8,12},{12,8},{1,5},{5,1},{9,13},{13,9},{2,6},{6,2},{1... | collective-permute-start | bytes 405512 | tf_op jit(solution)/shard_map/ppermute | solution.py:475
  15.7 2.9 %copy-start = (f32[64,96]{1,0:T(8,128)S(1)}, f32[64,96]{1,0:T(8,128)}, u32[]{:S(2)}) copy-start(f32[64,96]{1,0:T(8,128)} %time_own.1) | copy-start | bytes 73732
  15.7 9.1 %collective-permute-start.6 = (bf16[528,128]{1,0:T(8,128)(2,1)S(1)}, bf16[528,128]{1,0:T(8,128)(2,1)S(1)}, u32[]{:S(2)}, u32[]{:S(2)}) collective-permute-start(bf16[528,128]{1,0:T(8,128)(2,1)S(1)} %get-tuple-element.58), channel_id=1, source_target_pairs={{0,9},{1,8},{4,13},{5,12},{8,1},{9,0},{12,5},{13,4},{2,11},{3,10},... | collective-permute-start | bytes 405512 | tf_op jit(solution)/shard_map/ppermute | solution.py:475
  15.8 9.4 %collective-permute-start.7 = (bf16[528,128]{1,0:T(8,128)(2,1)S(1)}, bf16[528,128]{1,0:T(8,128)(2,1)S(1)}, u32[]{:S(2)}, u32[]{:S(2)}) collective-permute-start(bf16[528,128]{1,0:T(8,128)(2,1)S(1)} %get-tuple-element.59), channel_id=1, source_target_pairs={{0,5},{1,4},{4,1},{5,0},{8,13},{9,12},{12,9},{13,8},{2,7},{3,6},{6... | collective-permute-start | bytes 405512 | tf_op jit(solution)/shard_map/ppermute | solution.py:475
  18.6 4.0 %collective-permute-start.2 = (f32[96,128]{1,0:T(8,128)S(1)}, f32[96,128]{1,0:T(8,128)S(1)}, u32[]{:S(2)}, u32[]{:S(2)}) collective-permute-start(f32[96,128]{1,0:T(8,128)S(1)} %get-tuple-element.51), channel_id=1, source_target_pairs={{1,2},{3,0},{2,1},{0,3},{5,6},{7,4},{6,5},{4,7},{9,10},{11,8},{10,... | collective-permute-start | bytes 147464 | tf_op jit(solution)/shard_map/ppermute | solution.py:533
  26.0 1.3 %collective-permute-start.8 = (f32[104,128]{1,0:T(8,128)S(1)}, f32[104,128]{1,0:T(8,128)S(1)}, u32[]{:S(2)}, u32[]{:S(2)}) collective-permute-start(f32[104,128]{1,0:T(8,128)S(1)} %get-tuple-element.62), channel_id=1, source_target_pairs={{0,1},{1,0},{2,3},{3,2},{4,5},{5,4},{6,7},{7,6},{8,9},{9,8},{10,11... | collective-permute-start | bytes 159752 | tf_op jit(solution)/shard_map/ppermute | solution.py:475
  27.3 4.2 %collective-permute-start.9 = (f32[104,128]{1,0:T(8,128)S(1)}, f32[104,128]{1,0:T(8,128)S(1)}, u32[]{:S(2)}, u32[]{:S(2)}) collective-permute-start(f32[104,128]{1,0:T(8,128)S(1)} %shard_map.92.mine), channel_id=1, source_target_pairs={{0,2},{2,0},{1,3},{3,1},{4,6},{6,4},{5,7},{7,5},{8,10},{10,8},{9,1... | collective-permute-start | bytes 159752 | tf_op jit(solution)/shard_map/ppermute | solution.py:475
  31.6 5.4 %collective-permute-start.10 = (f32[104,128]{1,0:T(8,128)S(1)}, f32[104,128]{1,0:T(8,128)S(1)}, u32[]{:S(2)}, u32[]{:S(2)}) collective-permute-start(f32[104,128]{1,0:T(8,128)S(1)} %get-tuple-element.64.rest_0_), channel_id=1, source_target_pairs={{0,4},{4,0},{8,12},{12,8},{1,5},{5,1},{9,13},{13,9},{2,6},{6,2},{1... | collective-permute-start | bytes 159752 | tf_op jit(solution)/shard_map/ppermute | solution.py:475
  32.3 6.2 %collective-permute-start.12 = (f32[104,128]{1,0:T(8,128)S(1)}, f32[104,128]{1,0:T(8,128)S(1)}, u32[]{:S(2)}, u32[]{:S(2)}) collective-permute-start(f32[104,128]{1,0:T(8,128)S(1)} %get-tuple-element.65), channel_id=1, source_target_pairs={{0,12},{4,8},{8,4},{12,0},{1,13},{5,9},{9,5},{13,1},{2,14},{6,10},... | collective-permute-start | bytes 159752 | tf_op jit(solution)/shard_map/ppermute | solution.py:475
  34.8 5.0 %collective-permute-start.11 = (f32[104,128]{1,0:T(8,128)S(1)}, f32[104,128]{1,0:T(8,128)S(1)}, u32[]{:S(2)}, u32[]{:S(2)}) collective-permute-start(f32[104,128]{1,0:T(8,128)S(1)} %get-tuple-element.65), channel_id=1, source_target_pairs={{0,8},{4,12},{8,0},{12,4},{1,9},{5,13},{9,1},{13,5},{2,10},{6,14},... | collective-permute-start | bytes 159752 | tf_op jit(solution)/shard_map/ppermute | solution.py:475
  35.3 4.7 %collective-permute-start.14 = (f32[96,128]{1,0:T(8,128)S(1)}, f32[96,128]{1,0:T(8,128)S(1)}, u32[]{:S(2)}, u32[]{:S(2)}) collective-permute-start(f32[96,128]{1,0:T(8,128)S(1)} %get-tuple-element.72), channel_id=1, source_target_pairs={{0,1},{1,0},{2,3},{3,2},{4,5},{5,4},{6,7},{7,6},{8,9},{9,8},{10,11... | collective-permute-start | bytes 147464 | tf_op jit(solution)/shard_map/ppermute | solution.py:475
  35.3 4.7 %collective-permute-start.15 = (f32[96,128]{1,0:T(8,128)S(1)}, f32[96,128]{1,0:T(8,128)S(1)}, u32[]{:S(2)}, u32[]{:S(2)}) collective-permute-start(f32[96,128]{1,0:T(8,128)S(1)} %get-tuple-element.73), channel_id=1, source_target_pairs={{1,2},{3,0},{2,1},{0,3},{5,6},{7,4},{6,5},{4,7},{9,10},{11,8},{10,... | collective-permute-start | bytes 147464 | tf_op jit(solution)/shard_map/ppermute | solution.py:533
  40.0 1.3 %collective-permute-start.13 = (f32[96,128]{1,0:T(8,128)S(1)}, f32[96,128]{1,0:T(8,128)S(1)}, u32[]{:S(2)}, u32[]{:S(2)}) collective-permute-start(f32[96,128]{1,0:T(8,128)S(1)} %get-tuple-element.66.time_own), channel_id=1, source_target_pairs={{0,1},{1,0},{2,3},{3,2},{4,5},{5,4},{6,7},{7,6},{8,9},{9,8},{10,11... | collective-permute-start | bytes 147464 | tf_op jit(solution)/shard_map/ppermute | solution.py:475
  42.6 13.8 %collective-permute-start.16 = (f32[96,1024]{1,0:T(8,128)S(1)}, f32[96,1024]{1,0:T(8,128)S(1)}, u32[]{:S(2)}, u32[]{:S(2)}) collective-permute-start(f32[96,1024]{1,0:T(8,128)S(1)} %get-tuple-element.74.surface), channel_id=1, source_target_pairs={{0,1},{1,0},{2,3},{3,2},{4,5},{5,4},{6,7},{7,6},{8,9},{9,8},{10,11... | collective-permute-start | bytes 1179656 | tf_op jit(solution)/shard_map/ppermute | solution.py:475
  42.8 4.1 %collective-permute-start.18 = (bf16[208,128]{1,0:T(8,128)(2,1)S(1)}, bf16[208,128]{1,0:T(8,128)(2,1)S(1)}, u32[]{:S(2)}, u32[]{:S(2)}) collective-permute-start(bf16[208,128]{1,0:T(8,128)(2,1)S(1)} %get-tuple-element.76.mine), channel_id=1, source_target_pairs={{0,2},{2,0},{1,3},{3,1},{4,6},{6,4},{5,7},{7,5},{8,10},{10,8},{9,1... | collective-permute-start | bytes 159752 | tf_op jit(solution)/shard_map/ppermute | solution.py:475
  44.3 3.9 %collective-permute-start.19 = (bf16[208,128]{1,0:T(8,128)(2,1)S(1)}, bf16[208,128]{1,0:T(8,128)(2,1)S(1)}, u32[]{:S(2)}, u32[]{:S(2)}) collective-permute-start(bf16[208,128]{1,0:T(8,128)(2,1)S(1)} %get-tuple-element.77), channel_id=1, source_target_pairs={{0,3},{1,2},{2,1},{3,0},{4,7},{5,6},{6,5},{7,4},{8,11},{9,10},{10,... | collective-permute-start | bytes 159752 | tf_op jit(solution)/shard_map/ppermute | solution.py:475
  44.5 3.7 %collective-permute-start.17 = (bf16[208,128]{1,0:T(8,128)(2,1)S(1)}, bf16[208,128]{1,0:T(8,128)(2,1)S(1)}, u32[]{:S(2)}, u32[]{:S(2)}) collective-permute-start(bf16[208,128]{1,0:T(8,128)(2,1)S(1)} %get-tuple-element.77), channel_id=1, source_target_pairs={{0,1},{1,0},{2,3},{3,2},{4,5},{5,4},{6,7},{7,6},{8,9},{9,8},{10,11... | collective-permute-start | bytes 159752 | tf_op jit(solution)/shard_map/ppermute | solution.py:475
  48.2 6.4 %collective-permute-start.22 = (bf16[208,128]{1,0:T(8,128)(2,1)S(1)}, bf16[208,128]{1,0:T(8,128)(2,1)S(1)}, u32[]{:S(2)}, u32[]{:S(2)}) collective-permute-start(bf16[208,128]{1,0:T(8,128)(2,1)S(1)} %shard_map.96.rest_0_), channel_id=1, source_target_pairs={{0,12},{4,8},{8,4},{12,0},{1,13},{5,9},{9,5},{13,1},{2,14},{6,10},... | collective-permute-start | bytes 159752 | tf_op jit(solution)/shard_map/ppermute | solution.py:475
  50.8 5.6 %collective-permute-start.21 = (bf16[208,128]{1,0:T(8,128)(2,1)S(1)}, bf16[208,128]{1,0:T(8,128)(2,1)S(1)}, u32[]{:S(2)}, u32[]{:S(2)}) collective-permute-start(bf16[208,128]{1,0:T(8,128)(2,1)S(1)} %shard_map.96.rest_0_), channel_id=1, source_target_pairs={{0,8},{4,12},{8,0},{12,4},{1,9},{5,13},{9,1},{13,5},{2,10},{6,14},... | collective-permute-start | bytes 159752 | tf_op jit(solution)/shard_map/ppermute | solution.py:475
  50.8 5.5 %collective-permute-start.20 = (bf16[208,128]{1,0:T(8,128)(2,1)S(1)}, bf16[208,128]{1,0:T(8,128)(2,1)S(1)}, u32[]{:S(2)}, u32[]{:S(2)}) collective-permute-start(bf16[208,128]{1,0:T(8,128)(2,1)S(1)} %shard_map.96.rest_0_), channel_id=1, source_target_pairs={{0,4},{4,0},{8,12},{12,8},{1,5},{5,1},{9,13},{13,9},{2,6},{6,2},{1... | collective-permute-start | bytes 159752 | tf_op jit(solution)/shard_map/ppermute | solution.py:475

commit v14 on v13

--- a/solution.py
+++ b/solution.py
@@ -29,10 +29,10 @@
     return lax.dot_general(a, b, ((contract[:1], contract[1:]), ((), ())), preferred_element_type=F32)
 
 
-def route_kernel(half, sends, paired, list_hbm, count_hbm, target_hbm, swath_hbm, mask_hbm, space_hbm, time_hbm, *rest):
-    outs, rest = rest[: len(sends)], rest[len(sends):]
-    surface, edge_near, edge_far, cols, rest = *rest[:4], rest[4:]
-    list_ref, count_ref, target_ref, swath_ref, mask_ref, space_ref, time_ref, place, total, seen, arrived = rest
+def route_kernel(half, early, paired, list_hbm, count_hbm, target_hbm, swath_hbm, mask_hbm, space_hbm, time_hbm, *rest):
+    piece, total, seen, surface, space_ref, time_ref, *rest = rest
+    cols = rest.pop(-1 if paired else 0)
+    list_ref, count_ref, target_ref, swath_ref, mask_ref, place, arrived = rest
     me, core = lax.axis_index("lon"), lax.axis_index("ta")
     n_lon = list_ref.shape[1]
     slots, days, cells = swath_ref.shape
@@ -70,8 +70,6 @@
     height = space_ref.shape[0] // rank
     for row in range(half):
         surface[:, row * LANES:(row + 1) * LANES] = space_ref[pl.ds(core * half + row, rank, stride=height), :]
-    edge_near[...] = space_ref[pl.ds(half - core, rank, stride=height), :]
-    edge_far[...] = space_ref[pl.ds(core * (height - 1), rank, stride=height), :]
     cols[...] = jnp.zeros(cols.shape, F32)
     cols[:, :rank] = border(surface[...], half)
     mask = mask_ref[...].astype(F32)
@@ -82,20 +80,38 @@
         at = place[slot]
         total[at] += (swath_ref[slot] * by_day[:, slot:slot + 1]).astype(F32)
         seen[pl.ds(at, 1), :days] += mask[slot:slot + 1, :]
-    for (side, step), out in zip(sends, outs):
-        at = (side * n_lon + step) * half
-        end = half * days + TAIL
-        out[: half * days, :] = total[at:at + half].reshape(half * days, cells).astype(BF16)
-        out[half * days:end, :] = seen[at:at + TAIL, :].astype(BF16)
-        if (side, step) == (1, 0):
+    pack(half, n_lon, early, total, seen, piece)
+    end = half * days + TAIL
+    if piece.shape[0] > end:
+        piece[end:, :] = cols[...].astype(BF16)
+
+
+def pack(half, n_lon, key, total, seen, out):
+    side, step = key
+    at = (side * n_lon + step) * half
+    end = half * total.shape[1]
+    out[:end, :] = total[at:at + half].reshape(end, LANES).astype(BF16)
+    out[end:end + TAIL, :] = seen[at:at + TAIL, :].astype(BF16)
+
+
+def pack_kernel(half, n_lon, sends, total, seen, space_ref, time_ref, *rest):
+    outs, (edge_near, edge_far) = rest[: len(sends)], rest[len(sends):]
+    core = lax.axis_index("ta")
+    days = total.shape[1]
+    end = half * days + TAIL
+    rank = edge_near.shape[0]
+    height = space_ref.shape[0] // rank
+    edge_near[...] = space_ref[pl.ds(half - core, rank, stride=height), :]
+    edge_far[...] = space_ref[pl.ds(core * (height - 1), rank, stride=height), :]
+    for key, out in zip(sends, outs):
+        pack(half, n_lon, key, total, seen, out)
+        if key == (1, 0):
             left = time_ref[...]
             for part in range(end, end + 3 * days, days):
                 value = left.astype(BF16)
                 out[part:part + days, :] = jnp.zeros((days, LANES), BF16)
                 out[part:part + days, :rank] = value
                 left = left - value.astype(F32)
-        elif paired and (side, step) == (0, 3):
-            out[end:, :] = cols[...].astype(BF16)
 
 
 def row_of(surface, row):
@@ -496,20 +512,25 @@
         return half * days + TAIL + more
 
     operands = (send_list, send_count, target, swath, obs_mask, factor_space.reshape(rank * height, cells), factor_time)
-    *pieces, surface, edge_near, edge_far, cols = call(
-        functools.partial(route_kernel, half, sends, paired),
-        [shape((piece_rows(*key), cells), BF16) for key in sends]
-        + [shape((rank, wide)), shape((rank, LANES)), shape((rank, LANES)), shape((COLS, LANES))],
+    early = (0, n_lon - 1)
+    sends.remove(early)
+    first, total, seen, surface, space, time, *cols = call(
+        functools.partial(route_kernel, half, early, paired),
+        [shape((piece_rows(*early), cells), BF16), shape((2 * n_lon * half, days, cells)), shape((2 * n_lon * half + TAIL, LANES))]
+        + [shape((rank, wide))]
+        + [shape(ref.shape) for ref in operands[5:]]
+        + [shape((COLS, LANES))] * (not paired),
         [pltpu.SMEM(ref.shape, jnp.int32) for ref in operands[:3]]
-        + [pltpu.VMEM(ref.shape, ref.dtype) for ref in operands[3:]]
-        + [
-            pltpu.SMEM((slots + 1,), jnp.int32),
-            pltpu.VMEM((2 * n_lon * half, days, cells), F32),
-            pltpu.VMEM((2 * n_lon * half + TAIL, LANES), F32),
-            pltpu.SemaphoreType.DMA((len(operands) - 1 + SWATH_COPIES,)),
-        ],
+        + [pltpu.VMEM(ref.shape, ref.dtype) for ref in operands[3:5]]
+        + [pltpu.SMEM((slots + 1,), jnp.int32), pltpu.SemaphoreType.DMA((len(operands) - 1 + SWATH_COPIES,))]
+        + [pltpu.VMEM((COLS, LANES), F32)] * paired,
         hbm=len(operands),
     )(*operands)
+    *pieces, edge_near, edge_far = call(
+        functools.partial(pack_kernel, half, n_lon, sends),
+        [shape((piece_rows(*key), cells), BF16) for key in sends]
+        + [shape((rank, LANES)), shape((rank, LANES))],
+    )(total, seen, space, time)
 
     def arrived(key, piece):
         side, step = key
@@ -517,7 +538,7 @@
             return across(piece, ("lon", "ta"), 2 * step + 1)
         return across(piece, "lon", step) if step else piece
 
-    pieces = dict(zip(sends, pieces))
+    pieces = dict(zip([early, *sends], [first, *pieces]))
     borders = ()
     if paired:
         near, far = (across(pieces.pop((side, 3)), "lon", 1) for side in (0, 1))
@@ -553,7 +574,7 @@
     base, block, near, seen_near = call(
         functools.partial(near_kernel, half, days, sides[0], paired, swap),
         [fresh, edge, *side_out],
-    )(surface, edge_near, predicted, packed, time_t, bands(edge_far), *[pieces[key] for key in sides[0]], *(borders if paired else columns(cols)))
+    )(surface, edge_near, predicted, packed, time_t, bands(edge_far), *[pieces[key] for key in sides[0]], *(borders if paired else columns(*cols)))
     surface, message, crossing, cols, edge_near, edge_far, far, seen_far = call(
         functools.partial(far_kernel, half, days, len(sides[1])),
         [fresh, shape((own_rows, LANES)), shape((own_rows, LANES)), shape((COLS, LANES)), edge, edge, *side_out],

time: 58 us -> 57.4 us (0.990)
    pallas_call x12 -> x13, Pallas kernels: 7.49 us -> 7.04 us  [run(): pl.pallas_call(kernel, out_shape=out_shape, in_specs=[pl.BlockSpec(memory...]
where the time goes in v14:
time: 57.4 us; the launch traced here: 57.2 us
  starting transfers between devices  25 us (44%)
  waiting for transfers between devices  24.5 us (43%)
  Pallas kernels  7.04 us (12%)
  between operations  0.75 us (1%)
    ppermute x21, starting transfers between devices, across(): lax.ppermute(value, axis, [(i, i ^ step) for i in range(lax.axis_size(axi...  23.4 us
    ppermute x21, waiting for transfers between devices, across(): lax.ppermute(value, axis, [(i, i ^ step) for i in range(lax.axis_size(axi...  22.3 us
    pallas_call x13, Pallas kernels, run(): pl.pallas_call(kernel, out_shape=out_shape, in_specs=[pl.BlockSpec(memory...  7.04 us
    ppermute x2, waiting for transfers between devices, bands(): return lax.ppermute(edge, ('lat', 'ta'), there + [(b, a) for a, b in there])  2.2 us
    ppermute x2, starting transfers between devices, bands(): return lax.ppermute(edge, ('lat', 'ta'), there + [(b, a) for a, b in there])  1.59 us
  transfers between devices with their start and end apart: 23, of which 14 were waited for; matrix products, arithmetic and copies ran while one was open for 0% of the time, Pallas kernels for 2%

profile of v14, /device:TPU:0, one launch (start us, length us, event | category | flops | bytes accessed | tf_op | source)
XLA Modules:
  0.0 57.2 jit_solution(1630904501355047653)
XLA Ops:
  0.6 2.1 %shard_map.86 = (bf16[544,128]{1,0:T(8,128)(2,1)S(1)}, f32[64,64,128]{2,1,0:T(8,128)S(1)}, f32[80,128]{1,0:T(8,128)S(1)}, f32[96,1024]{1,0:T(8,128)S(1)}, f32[1536,128]{1,0:T(8,128)S(1)}, /*index=5*/f32[64,96]{1,0:T(8,128)S(1)}) custom-call(s32[1,4,32]{2,1,0:T(4,128)} %list_hbm.1, s32[1,4]{1,0:T(1,128)} %count_hbm.1, s32[64]{0:T(128)} %target_hbm.1, ...), custom_call_target="tpu_custom_call" | custom-call | flops 1000000 | bytes 1000000 | tf_op jit(solution)/shard_map/pallas_call | solution.py:477
  2.8 3.1 %collective-permute-start.3 = (bf16[544,128]{1,0:T(8,128)(2,1)S(1)}, bf16[544,128]{1,0:T(8,128)(2,1)S(1)}, u32[]{:S(2)}, u32[]{:S(2)}) collective-permute-start(bf16[544,128]{1,0:T(8,128)(2,1)S(1)} %get-tuple-element.61), channel_id=1, source_target_pairs={{0,4},{4,0},{8,12},{12,8},{1,5},{5,1},{9,13},{13,9},{2,6},{6,2},{1... | collective-permute-start | bytes 417800 | tf_op jit(solution)/shard_map/ppermute | solution.py:491
  6.2 4.2 %collective-permute-done.3.theirs.rest_3_ = bf16[544,128]{1,0:T(8,128)(2,1)S(1)} collective-permute-done((bf16[544,128]{1,0:T(8,128)(2,1)S(1)}, bf16[544,128]{1,0:T(8,128)(2,1)S(1)}, u32[]{:S(2)}, u32[]{:S(2)}) %collective-permute-start.3) | collective-permute-done | bytes 139296 | tf_op jit(solution)/shard_map/ppermute | solution.py:491
  10.4 3.1 %collective-permute-start.4 = (bf16[544,128]{1,0:T(8,128)(2,1)S(1)}, bf16[544,128]{1,0:T(8,128)(2,1)S(1)}, u32[]{:S(2)}, u32[]{:S(2)}) collective-permute-start(bf16[544,128]{1,0:T(8,128)(2,1)S(1)} %shard_map.90), channel_id=1, source_target_pairs={{0,8},{4,12},{8,0},{12,4},{1,9},{5,13},{9,1},{13,5},{2,10},{6,14},... | collective-permute-start | bytes 417800 | tf_op jit(solution)/shard_map/ppermute | solution.py:491
  13.5 1.6 %collective-permute-start.5 = (bf16[528,128]{1,0:T(8,128)(2,1)S(1)}, bf16[528,128]{1,0:T(8,128)(2,1)S(1)}, u32[]{:S(2)}, u32[]{:S(2)}) collective-permute-start(bf16[528,128]{1,0:T(8,128)(2,1)S(1)} %get-tuple-element.62), channel_id=1, source_target_pairs={{0,4},{4,0},{8,12},{12,8},{1,5},{5,1},{9,13},{13,9},{2,6},{6,2},{1... | collective-permute-start | bytes 405512 | tf_op jit(solution)/shard_map/ppermute | solution.py:491
  15.2 2.7 %collective-permute-start.7 = (bf16[528,128]{1,0:T(8,128)(2,1)S(1)}, bf16[528,128]{1,0:T(8,128)(2,1)S(1)}, u32[]{:S(2)}, u32[]{:S(2)}) collective-permute-start(bf16[528,128]{1,0:T(8,128)(2,1)S(1)} %get-tuple-element.67), channel_id=1, source_target_pairs={{0,5},{1,4},{4,1},{5,0},{8,13},{9,12},{12,9},{13,8},{2,7},{3,6},{6... | collective-permute-start | bytes 405512 | tf_op jit(solution)/shard_map/ppermute | solution.py:491
  18.2 1.6 %collective-permute-done.5.rest_1_ = bf16[528,128]{1,0:T(8,128)(2,1)S(1)} collective-permute-done((bf16[528,128]{1,0:T(8,128)(2,1)S(1)}, bf16[528,128]{1,0:T(8,128)(2,1)S(1)}, u32[]{:S(2)}, u32[]{:S(2)}) %collective-permute-start.5) | collective-permute-done | bytes 135200 | tf_op jit(solution)/shard_map/ppermute | solution.py:491
  19.8 2.2 %collective-permute-done.2.edge_far = f32[96,128]{1,0:T(8,128)S(1)} collective-permute-done((f32[96,128]{1,0:T(8,128)S(1)}, f32[96,128]{1,0:T(8,128)S(1)}, u32[]{:S(2)}, u32[]{:S(2)}) %collective-permute-start.2) | collective-permute-done | bytes 49184 | tf_op jit(solution)/shard_map/ppermute | solution.py:554
  22.0 0.8 %shard_map.91 = (f32[96,1024]{1,0:T(8,128)S(1)}, f32[96,128]{1,0:T(8,128)S(1)}, f32[64,1024]{1,0:T(8,128)S(1)}, f32[16,128]{1,0:T(8,128)S(1)}) custom-call(f32[96,1024]{1,0:T(8,128)S(1)} %get-tuple-element.45.surface, f32[96,128]{1,0:T(8,128)S(1)} %get-tuple-element.50.edge_near, f32[128,1024]{1,0:T(8,128)S(1)} %get-tuple-element.52.predicted, ...), custom_call_target="tpu_custom_call" | custom-call | flops 1000000 | bytes 1000000 | tf_op jit(solution)/shard_map/pallas_call | solution.py:477
  22.8 1.4 %collective-permute-done.6.rest_0_ = bf16[528,128]{1,0:T(8,128)(2,1)S(1)} collective-permute-done((bf16[528,128]{1,0:T(8,128)(2,1)S(1)}, bf16[528,128]{1,0:T(8,128)(2,1)S(1)}, u32[]{:S(2)}, u32[]{:S(2)}) %collective-permute-start.6) | collective-permute-done | bytes 135200 | tf_op jit(solution)/shard_map/ppermute | solution.py:491
  24.2 0.4 collective-permute-done.7.rest_2_
  24.7 0.7 %shard_map.92 = (f32[96,1024]{1,0:T(8,128)S(1)}, f32[104,128]{1,0:T(8,128)S(1)}, f32[104,128]{1,0:T(8,128)S(1)}, f32[16,128]{1,0:T(8,128)S(1)}, f32[96,128]{1,0:...) custom-call(f32[96,1024]{1,0:T(8,128)S(1)} %get-tuple-element.64.base, ...), custom_call_target="tpu_custom_call" | custom-call | flops 1000000 | bytes 1000000 | tf_op jit(solution)/shard_map/pallas_call | solution.py:477
  25.6 1.1 %collective-permute-done.8.core = f32[104,128]{1,0:T(8,128)S(1)} collective-permute-done((f32[104,128]{1,0:T(8,128)S(1)}, f32[104,128]{1,0:T(8,128)S(1)}, u32[]{:S(2)}, u32[]{:S(2)}) %collective-permute-start.8) | collective-permute-done | bytes 53280 | tf_op jit(solution)/shard_map/ppermute | solution.py:491
  26.7 1.8 %collective-permute-start.9 = (f32[104,128]{1,0:T(8,128)S(1)}, f32[104,128]{1,0:T(8,128)S(1)}, u32[]{:S(2)}, u32[]{:S(2)}) collective-permute-start(f32[104,128]{1,0:T(8,128)S(1)} %shard_map.93.mine), channel_id=1, source_target_pairs={{0,2},{2,0},{1,3},{3,1},{4,6},{6,4},{5,7},{7,5},{8,10},{10,8},{9,1... | collective-permute-start | bytes 159752 | tf_op jit(solution)/shard_map/ppermute | solution.py:491
  28.4 2.4 %collective-permute-done.9.band = f32[104,128]{1,0:T(8,128)S(1)} collective-permute-done((f32[104,128]{1,0:T(8,128)S(1)}, f32[104,128]{1,0:T(8,128)S(1)}, u32[]{:S(2)}, u32[]{:S(2)}) %collective-permute-start.9) | collective-permute-done | bytes 53280 | tf_op jit(solution)/shard_map/ppermute | solution.py:491
  31.0 0.7 %collective-permute-start.10 = (f32[104,128]{1,0:T(8,128)S(1)}, f32[104,128]{1,0:T(8,128)S(1)}, u32[]{:S(2)}, u32[]{:S(2)}) collective-permute-start(f32[104,128]{1,0:T(8,128)S(1)} %get-tuple-element.72.rest_0_), channel_id=1, source_target_pairs={{0,4},{4,0},{8,12},{12,8},{1,5},{5,1},{9,13},{13,9},{2,6},{6,2},{1... | collective-permute-start | bytes 159752 | tf_op jit(solution)/shard_map/ppermute | solution.py:491
  31.7 2.6 %collective-permute-start.12 = (f32[104,128]{1,0:T(8,128)S(1)}, f32[104,128]{1,0:T(8,128)S(1)}, u32[]{:S(2)}, u32[]{:S(2)}) collective-permute-start(f32[104,128]{1,0:T(8,128)S(1)} %get-tuple-element.73), channel_id=1, source_target_pairs={{0,12},{4,8},{8,4},{12,0},{1,13},{5,9},{9,5},{13,1},{2,14},{6,10},... | collective-permute-start | bytes 159752 | tf_op jit(solution)/shard_map/ppermute | solution.py:491
  34.3 0.5 collective-permute-start.11
  34.7 1.6 %collective-permute-start.15 = (f32[96,128]{1,0:T(8,128)S(1)}, f32[96,128]{1,0:T(8,128)S(1)}, u32[]{:S(2)}, u32[]{:S(2)}) collective-permute-start(f32[96,128]{1,0:T(8,128)S(1)} %get-tuple-element.81), channel_id=1, source_target_pairs={{1,2},{3,0},{2,1},{0,3},{5,6},{7,4},{6,5},{4,7},{9,10},{11,8},{10,... | collective-permute-start | bytes 147464 | tf_op jit(solution)/shard_map/ppermute | solution.py:554
  36.3 1.6 %collective-permute-done.12.rest_3_.cols_b = f32[104,128]{1,0:T(8,128)S(1)} collective-permute-done((f32[104,128]{1,0:T(8,128)S(1)}, f32[104,128]{1,0:T(8,128)S(1)}, u32[]{:S(2)}, u32[]{:S(2)}) %collective-permute-start.12) | collective-permute-done | bytes 53280 | tf_op jit(solution)/shard_map/ppermute | solution.py:491
  37.9 1.4 %collective-permute-done.11.rest_2_ = f32[104,128]{1,0:T(8,128)S(1)} collective-permute-done((f32[104,128]{1,0:T(8,128)S(1)}, f32[104,128]{1,0:T(8,128)S(1)}, u32[]{:S(2)}, u32[]{:S(2)}) %collective-permute-start.11) | collective-permute-done | bytes 53280 | tf_op jit(solution)/shard_map/ppermute | solution.py:491
  39.5 1.2 %collective-permute-done.13.time_other = f32[96,128]{1,0:T(8,128)S(1)} collective-permute-done((f32[96,128]{1,0:T(8,128)S(1)}, f32[96,128]{1,0:T(8,128)S(1)}, u32[]{:S(2)}, u32[]{:S(2)}) %collective-permute-start.13) | collective-permute-done | bytes 49184 | tf_op jit(solution)/shard_map/ppermute | solution.py:491
  40.7 1.3 %shard_map.96 = (f32[96,1024]{1,0:T(8,128)S(1)}, f32[96,128]{1,0:T(8,128)S(1)}, bf16[208,128]{1,0:T(8,128)(2,1)S(1)}, bf16[208,128]{1,0:T(8,128)(2,1)S(1)}) custom-call(f32[96,1024]{1,0:T(8,128)S(1)} %get-tuple-element.68.surface, f32[96,128]{1,0:T(8,128)S(1)} %get-tuple-element.74.time_own, f32[96,128]{1,0:T(8,128)S(1)} %collective-permute-done.13.time_other, ...), custom_call_target="tpu_custom_call" | custom-call | flops 1000000 | bytes 1000000 | tf_op jit(solution)/shard_map/pallas_call | solution.py:477
  42.2 1.5 %collective-permute-start.18 = (bf16[208,128]{1,0:T(8,128)(2,1)S(1)}, bf16[208,128]{1,0:T(8,128)(2,1)S(1)}, u32[]{:S(2)}, u32[]{:S(2)}) collective-permute-start(bf16[208,128]{1,0:T(8,128)(2,1)S(1)} %get-tuple-element.84.mine), channel_id=1, source_target_pairs={{0,2},{2,0},{1,3},{3,1},{4,6},{6,4},{5,7},{7,5},{8,10},{10,8},{9,1... | collective-permute-start | bytes 159752 | tf_op jit(solution)/shard_map/ppermute | solution.py:491
  43.9 0.4 collective-permute-start.17
  44.4 2.0 %collective-permute-done.18.band = bf16[208,128]{1,0:T(8,128)(2,1)S(1)} collective-permute-done((bf16[208,128]{1,0:T(8,128)(2,1)S(1)}, bf16[208,128]{1,0:T(8,128)(2,1)S(1)}, u32[]{:S(2)}, u32[]{:S(2)}) %collective-permute-start.18) | collective-permute-done | bytes 53280 | tf_op jit(solution)/shard_map/ppermute | solution.py:491
  46.4 1.2 %collective-permute-done.19.both = bf16[208,128]{1,0:T(8,128)(2,1)S(1)} collective-permute-done((bf16[208,128]{1,0:T(8,128)(2,1)S(1)}, bf16[208,128]{1,0:T(8,128)(2,1)S(1)}, u32[]{:S(2)}, u32[]{:S(2)}) %collective-permute-start.19) | collective-permute-done | bytes 53280 | tf_op jit(solution)/shard_map/ppermute | solution.py:491
  47.6 2.6 %collective-permute-start.22 = (bf16[208,128]{1,0:T(8,128)(2,1)S(1)}, bf16[208,128]{1,0:T(8,128)(2,1)S(1)}, u32[]{:S(2)}, u32[]{:S(2)}) collective-permute-start(bf16[208,128]{1,0:T(8,128)(2,1)S(1)} %shard_map.97.rest_0_), channel_id=1, source_target_pairs={{0,12},{4,8},{8,4},{12,0},{1,13},{5,9},{9,5},{13,1},{2,14},{6,10},... | collective-permute-start | bytes 159752 | tf_op jit(solution)/shard_map/ppermute | solution.py:491
  50.3 1.8 %collective-permute-start.20 = (bf16[208,128]{1,0:T(8,128)(2,1)S(1)}, bf16[208,128]{1,0:T(8,128)(2,1)S(1)}, u32[]{:S(2)}, u32[]{:S(2)}) collective-permute-start(bf16[208,128]{1,0:T(8,128)(2,1)S(1)} %shard_map.97.rest_0_), channel_id=1, source_target_pairs={{0,4},{4,0},{8,12},{12,8},{1,5},{5,1},{9,13},{13,9},{2,6},{6,2},{1... | collective-permute-start | bytes 159752 | tf_op jit(solution)/shard_map/ppermute | solution.py:491
  52.1 1.9 %collective-permute-done.22.rest_3_ = bf16[208,128]{1,0:T(8,128)(2,1)S(1)} collective-permute-done((bf16[208,128]{1,0:T(8,128)(2,1)S(1)}, bf16[208,128]{1,0:T(8,128)(2,1)S(1)}, u32[]{:S(2)}, u32[]{:S(2)}) %collective-permute-start.22) | collective-permute-done | bytes 53280 | tf_op jit(solution)/shard_map/ppermute | solution.py:491
  54.0 1.8 %collective-permute-done.21.rest_2_ = bf16[208,128]{1,0:T(8,128)(2,1)S(1)} collective-permute-done((bf16[208,128]{1,0:T(8,128)(2,1)S(1)}, bf16[208,128]{1,0:T(8,128)(2,1)S(1)}, u32[]{:S(2)}, u32[]{:S(2)}) %collective-permute-start.21) | collective-permute-done | bytes 53280 | tf_op jit(solution)/shard_map/ppermute | solution.py:491
  55.8 1.4 %shard_map.98 = (f32[1536,128]{1,0:T(8,128)}, f32[64,96]{1,0:T(8,128)}) custom-call(f32[96,1024]{1,0:T(8,128)S(1)} %get-tuple-element.82.surface, f32[96,1024]{1,0:T(8,128)S(1)} %collective-permute-done.16.other, f32[96,128]{1,0:T(8,128)S(1)} %get-tuple-element.83.time_t, bf16[208,128]{1,0:T(8,128)(2,1)S(1)} %shard_map.97.rest_0_, ...), custom_call_target="tpu_custom_call" | custom-call | flops 1000000 | bytes 1000000 | tf_op jit(solution)/shard_map/pallas_call | solution.py:477
  (29 shorter events, 1.6 us)
Async XLA Ops:
  2.7 15.2 %copy-start = (f32[64,96]{1,0:T(8,128)S(1)}, f32[64,96]{1,0:T(8,128)}, u32[]{:S(2)}) copy-start(f32[64,96]{1,0:T(8,128)} %time_own.1) | copy-start | bytes 73732
  2.8 7.6 %collective-permute-start.3 = (bf16[544,128]{1,0:T(8,128)(2,1)S(1)}, bf16[544,128]{1,0:T(8,128)(2,1)S(1)}, u32[]{:S(2)}, u32[]{:S(2)}) collective-permute-start(bf16[544,128]{1,0:T(8,128)(2,1)S(1)} %get-tuple-element.61), channel_id=1, source_target_pairs={{0,4},{4,0},{8,12},{12,8},{1,5},{5,1},{9,13},{13,9},{2,6},{6,2},{1... | collective-permute-start | bytes 417800 | tf_op jit(solution)/shard_map/ppermute | solution.py:491
  6.0 9.1 %collective-permute-start.1 = (bf16[528,128]{1,0:T(8,128)(2,1)S(1)}, bf16[528,128]{1,0:T(8,128)(2,1)S(1)}, u32[]{:S(2)}, u32[]{:S(2)}) collective-permute-start(bf16[528,128]{1,0:T(8,128)(2,1)S(1)} %get-tuple-element.56), channel_id=1, source_target_pairs={{0,4},{4,0},{8,12},{12,8},{1,5},{5,1},{9,13},{13,9},{2,6},{6,2},{1... | collective-permute-start | bytes 405512 | tf_op jit(solution)/shard_map/ppermute | solution.py:491
  6.1 11.9 %collective-permute-start = (bf16[720,128]{1,0:T(8,128)(2,1)S(1)}, bf16[720,128]{1,0:T(8,128)(2,1)S(1)}, u32[]{:S(2)}, u32[]{:S(2)}) collective-permute-start(bf16[720,128]{1,0:T(8,128)(2,1)S(1)} %get-tuple-element.51), channel_id=1, source_target_pairs={{0,1},{1,0},{4,5},{5,4},{8,9},{9,8},{12,13},{13,12},{2,3},{3,2},{6... | collective-permute-start | bytes 552968 | tf_op jit(solution)/shard_map/ppermute | solution.py:491
  10.4 11.6 %collective-permute-start.4 = (bf16[544,128]{1,0:T(8,128)(2,1)S(1)}, bf16[544,128]{1,0:T(8,128)(2,1)S(1)}, u32[]{:S(2)}, u32[]{:S(2)}) collective-permute-start(bf16[544,128]{1,0:T(8,128)(2,1)S(1)} %shard_map.90), channel_id=1, source_target_pairs={{0,8},{4,12},{8,0},{12,4},{1,9},{5,13},{9,1},{13,5},{2,10},{6,14},... | collective-permute-start | bytes 417800 | tf_op jit(solution)/shard_map/ppermute | solution.py:491
  13.5 6.3 %collective-permute-start.5 = (bf16[528,128]{1,0:T(8,128)(2,1)S(1)}, bf16[528,128]{1,0:T(8,128)(2,1)S(1)}, u32[]{:S(2)}, u32[]{:S(2)}) collective-permute-start(bf16[528,128]{1,0:T(8,128)(2,1)S(1)} %get-tuple-element.62), channel_id=1, source_target_pairs={{0,4},{4,0},{8,12},{12,8},{1,5},{5,1},{9,13},{13,9},{2,6},{6,2},{1... | collective-permute-start | bytes 405512 | tf_op jit(solution)/shard_map/ppermute | solution.py:491
  15.2 9.1 %collective-permute-start.6 = (bf16[528,128]{1,0:T(8,128)(2,1)S(1)}, bf16[528,128]{1,0:T(8,128)(2,1)S(1)}, u32[]{:S(2)}, u32[]{:S(2)}) collective-permute-start(bf16[528,128]{1,0:T(8,128)(2,1)S(1)} %get-tuple-element.66), channel_id=1, source_target_pairs={{0,9},{1,8},{4,13},{5,12},{8,1},{9,0},{12,5},{13,4},{2,11},{3,10},... | collective-permute-start | bytes 405512 | tf_op jit(solution)/shard_map/ppermute | solution.py:491
  15.2 9.4 %collective-permute-start.7 = (bf16[528,128]{1,0:T(8,128)(2,1)S(1)}, bf16[528,128]{1,0:T(8,128)(2,1)S(1)}, u32[]{:S(2)}, u32[]{:S(2)}) collective-permute-start(bf16[528,128]{1,0:T(8,128)(2,1)S(1)} %get-tuple-element.67), channel_id=1, source_target_pairs={{0,5},{1,4},{4,1},{5,0},{8,13},{9,12},{12,9},{13,8},{2,7},{3,6},{6... | collective-permute-start | bytes 405512 | tf_op jit(solution)/shard_map/ppermute | solution.py:491
  18.0 4.0 %collective-permute-start.2 = (f32[96,128]{1,0:T(8,128)S(1)}, f32[96,128]{1,0:T(8,128)S(1)}, u32[]{:S(2)}, u32[]{:S(2)}) collective-permute-start(f32[96,128]{1,0:T(8,128)S(1)} %get-tuple-element.59), channel_id=1, source_target_pairs={{1,2},{3,0},{2,1},{0,3},{5,6},{7,4},{6,5},{4,7},{9,10},{11,8},{10,... | collective-permute-start | bytes 147464 | tf_op jit(solution)/shard_map/ppermute | solution.py:554
  25.4 1.3 %collective-permute-start.8 = (f32[104,128]{1,0:T(8,128)S(1)}, f32[104,128]{1,0:T(8,128)S(1)}, u32[]{:S(2)}, u32[]{:S(2)}) collective-permute-start(f32[104,128]{1,0:T(8,128)S(1)} %get-tuple-element.70), channel_id=1, source_target_pairs={{0,1},{1,0},{2,3},{3,2},{4,5},{5,4},{6,7},{7,6},{8,9},{9,8},{10,11... | collective-permute-start | bytes 159752 | tf_op jit(solution)/shard_map/ppermute | solution.py:491
  26.7 4.2 %collective-permute-start.9 = (f32[104,128]{1,0:T(8,128)S(1)}, f32[104,128]{1,0:T(8,128)S(1)}, u32[]{:S(2)}, u32[]{:S(2)}) collective-permute-start(f32[104,128]{1,0:T(8,128)S(1)} %shard_map.93.mine), channel_id=1, source_target_pairs={{0,2},{2,0},{1,3},{3,1},{4,6},{6,4},{5,7},{7,5},{8,10},{10,8},{9,1... | collective-permute-start | bytes 159752 | tf_op jit(solution)/shard_map/ppermute | solution.py:491
  31.0 5.4 %collective-permute-start.10 = (f32[104,128]{1,0:T(8,128)S(1)}, f32[104,128]{1,0:T(8,128)S(1)}, u32[]{:S(2)}, u32[]{:S(2)}) collective-permute-start(f32[104,128]{1,0:T(8,128)S(1)} %get-tuple-element.72.rest_0_), channel_id=1, source_target_pairs={{0,4},{4,0},{8,12},{12,8},{1,5},{5,1},{9,13},{13,9},{2,6},{6,2},{1... | collective-permute-start | bytes 159752 | tf_op jit(solution)/shard_map/ppermute | solution.py:491
  31.7 6.2 %collective-permute-start.12 = (f32[104,128]{1,0:T(8,128)S(1)}, f32[104,128]{1,0:T(8,128)S(1)}, u32[]{:S(2)}, u32[]{:S(2)}) collective-permute-start(f32[104,128]{1,0:T(8,128)S(1)} %get-tuple-element.73), channel_id=1, source_target_pairs={{0,12},{4,8},{8,4},{12,0},{1,13},{5,9},{9,5},{13,1},{2,14},{6,10},... | collective-permute-start | bytes 159752 | tf_op jit(solution)/shard_map/ppermute | solution.py:491
  34.3 5.0 %collective-permute-start.11 = (f32[104,128]{1,0:T(8,128)S(1)}, f32[104,128]{1,0:T(8,128)S(1)}, u32[]{:S(2)}, u32[]{:S(2)}) collective-permute-start(f32[104,128]{1,0:T(8,128)S(1)} %get-tuple-element.73), channel_id=1, source_target_pairs={{0,8},{4,12},{8,0},{12,4},{1,9},{5,13},{9,1},{13,5},{2,10},{6,14},... | collective-permute-start | bytes 159752 | tf_op jit(solution)/shard_map/ppermute | solution.py:491
  34.7 4.7 %collective-permute-start.14 = (f32[96,128]{1,0:T(8,128)S(1)}, f32[96,128]{1,0:T(8,128)S(1)}, u32[]{:S(2)}, u32[]{:S(2)}) collective-permute-start(f32[96,128]{1,0:T(8,128)S(1)} %get-tuple-element.80), channel_id=1, source_target_pairs={{0,1},{1,0},{2,3},{3,2},{4,5},{5,4},{6,7},{7,6},{8,9},{9,8},{10,11... | collective-permute-start | bytes 147464 | tf_op jit(solution)/shard_map/ppermute | solution.py:491
  34.7 4.7 %collective-permute-start.15 = (f32[96,128]{1,0:T(8,128)S(1)}, f32[96,128]{1,0:T(8,128)S(1)}, u32[]{:S(2)}, u32[]{:S(2)}) collective-permute-start(f32[96,128]{1,0:T(8,128)S(1)} %get-tuple-element.81), channel_id=1, source_target_pairs={{1,2},{3,0},{2,1},{0,3},{5,6},{7,4},{6,5},{4,7},{9,10},{11,8},{10,... | collective-permute-start | bytes 147464 | tf_op jit(solution)/shard_map/ppermute | solution.py:554
  39.4 1.3 %collective-permute-start.13 = (f32[96,128]{1,0:T(8,128)S(1)}, f32[96,128]{1,0:T(8,128)S(1)}, u32[]{:S(2)}, u32[]{:S(2)}) collective-permute-start(f32[96,128]{1,0:T(8,128)S(1)} %get-tuple-element.74.time_own), channel_id=1, source_target_pairs={{0,1},{1,0},{2,3},{3,2},{4,5},{5,4},{6,7},{7,6},{8,9},{9,8},{10,11... | collective-permute-start | bytes 147464 | tf_op jit(solution)/shard_map/ppermute | solution.py:491
  42.0 13.8 %collective-permute-start.16 = (f32[96,1024]{1,0:T(8,128)S(1)}, f32[96,1024]{1,0:T(8,128)S(1)}, u32[]{:S(2)}, u32[]{:S(2)}) collective-permute-start(f32[96,1024]{1,0:T(8,128)S(1)} %get-tuple-element.82.surface), channel_id=1, source_target_pairs={{0,1},{1,0},{2,3},{3,2},{4,5},{5,4},{6,7},{7,6},{8,9},{9,8},{10,11... | collective-permute-start | bytes 1179656 | tf_op jit(solution)/shard_map/ppermute | solution.py:491
  42.2 4.1 %collective-permute-start.18 = (bf16[208,128]{1,0:T(8,128)(2,1)S(1)}, bf16[208,128]{1,0:T(8,128)(2,1)S(1)}, u32[]{:S(2)}, u32[]{:S(2)}) collective-permute-start(bf16[208,128]{1,0:T(8,128)(2,1)S(1)} %get-tuple-element.84.mine), channel_id=1, source_target_pairs={{0,2},{2,0},{1,3},{3,1},{4,6},{6,4},{5,7},{7,5},{8,10},{10,8},{9,1... | collective-permute-start | bytes 159752 | tf_op jit(solution)/shard_map/ppermute | solution.py:491
  43.7 3.9 %collective-permute-start.19 = (bf16[208,128]{1,0:T(8,128)(2,1)S(1)}, bf16[208,128]{1,0:T(8,128)(2,1)S(1)}, u32[]{:S(2)}, u32[]{:S(2)}) collective-permute-start(bf16[208,128]{1,0:T(8,128)(2,1)S(1)} %get-tuple-element.85), channel_id=1, source_target_pairs={{0,3},{1,2},{2,1},{3,0},{4,7},{5,6},{6,5},{7,4},{8,11},{9,10},{10,... | collective-permute-start | bytes 159752 | tf_op jit(solution)/shard_map/ppermute | solution.py:491
  43.9 3.7 %collective-permute-start.17 = (bf16[208,128]{1,0:T(8,128)(2,1)S(1)}, bf16[208,128]{1,0:T(8,128)(2,1)S(1)}, u32[]{:S(2)}, u32[]{:S(2)}) collective-permute-start(bf16[208,128]{1,0:T(8,128)(2,1)S(1)} %get-tuple-element.85), channel_id=1, source_target_pairs={{0,1},{1,0},{2,3},{3,2},{4,5},{5,4},{6,7},{7,6},{8,9},{9,8},{10,11... | collective-permute-start | bytes 159752 | tf_op jit(solution)/shard_map/ppermute | solution.py:491
  47.6 6.4 %collective-permute-start.22 = (bf16[208,128]{1,0:T(8,128)(2,1)S(1)}, bf16[208,128]{1,0:T(8,128)(2,1)S(1)}, u32[]{:S(2)}, u32[]{:S(2)}) collective-permute-start(bf16[208,128]{1,0:T(8,128)(2,1)S(1)} %shard_map.97.rest_0_), channel_id=1, source_target_pairs={{0,12},{4,8},{8,4},{12,0},{1,13},{5,9},{9,5},{13,1},{2,14},{6,10},... | collective-permute-start | bytes 159752 | tf_op jit(solution)/shard_map/ppermute | solution.py:491
  50.2 5.6 %collective-permute-start.21 = (bf16[208,128]{1,0:T(8,128)(2,1)S(1)}, bf16[208,128]{1,0:T(8,128)(2,1)S(1)}, u32[]{:S(2)}, u32[]{:S(2)}) collective-permute-start(bf16[208,128]{1,0:T(8,128)(2,1)S(1)} %shard_map.97.rest_0_), channel_id=1, source_target_pairs={{0,8},{4,12},{8,0},{12,4},{1,9},{5,13},{9,1},{13,5},{2,10},{6,14},... | collective-permute-start | bytes 159752 | tf_op jit(solution)/shard_map/ppermute | solution.py:491
  50.3 5.5 %collective-permute-start.20 = (bf16[208,128]{1,0:T(8,128)(2,1)S(1)}, bf16[208,128]{1,0:T(8,128)(2,1)S(1)}, u32[]{:S(2)}, u32[]{:S(2)}) collective-permute-start(bf16[208,128]{1,0:T(8,128)(2,1)S(1)} %shard_map.97.rest_0_), channel_id=1, source_target_pairs={{0,4},{4,0},{8,12},{12,8},{1,5},{5,1},{9,13},{13,9},{2,6},{6,2},{1... | collective-permute-start | bytes 159752 | tf_op jit(solution)/shard_map/ppermute | solution.py:491

commit v15 on v14

--- a/solution.py
+++ b/solution.py
@@ -91,14 +91,17 @@
     at = (side * n_lon + step) * half
     end = half * total.shape[1]
     out[:end, :] = total[at:at + half].reshape(end, LANES).astype(BF16)
-    out[end:end + TAIL, :] = seen[at:at + TAIL, :].astype(BF16)
+    if side == 0:
+        other = at + n_lon * half
+        both = jnp.concatenate([seen[at:at + half, :], seen[other:other + half, :]], axis=0)
+        out[end:end + TAIL, :] = both.astype(BF16)
 
 
 def pack_kernel(half, n_lon, sends, total, seen, space_ref, time_ref, *rest):
     outs, (edge_near, edge_far) = rest[: len(sends)], rest[len(sends):]
     core = lax.axis_index("ta")
     days = total.shape[1]
-    end = half * days + TAIL
+    end = half * days
     rank = edge_near.shape[0]
     height = space_ref.shape[0] // rank
     edge_near[...] = space_ref[pl.ds(half - core, rank, stride=height), :]
@@ -165,7 +168,7 @@
 def model_kernel(half, surface, time_own, piece, predicted, packed, time_t, days_all):
     rank = surface.shape[0]
     days = time_own.shape[0]
-    at = half * days + TAIL
+    at = half * days
     high, middle, low = (piece[first:first + days, :].astype(F32) for first in range(at, at + 3 * days, days))
     days_all[...] = jnp.zeros(days_all.shape, F32)
     days_all[:days, :rank] = time_own[...]
@@ -265,11 +268,10 @@
     return value
 
 
-def unpack_pieces(half, parts, summed, seen):
+def unpack_pieces(half, parts, summed):
     days = summed.shape[0]
     for row in range(half):
         summed[:, row * LANES:(row + 1) * LANES] = add_up(parts, slice(row * days, (row + 1) * days))
-    seen[...] = add_up(parts, slice(half * days, half * days + TAIL))
 
 
 def narrow(value, rank):
@@ -294,13 +296,16 @@
 
 def near_kernel(half, days, order, paired, swap, surface, edge_near, predicted, packed, time_t, edge_far, *rest):
     pieces, rest = dict(zip(order, rest)), rest[len(order):]
-    cols, (base, block, summed, seen) = rest[:-4], rest[-4:]
+    cols, (base, block, summed, seen, beside) = rest[:-5], rest[-5:]
     if paired:
         at = half * days + TAIL
         cols = in_order(swap(), *[ref[at:, :].astype(F32) for ref in (cols[0], pieces[0, 2])])
     left, right = (ref[...] for ref in cols)
     smooth(half, surface[...], edge_near[...], edge_far[...], left[half:, :], right[:half, :], None, base)
-    unpack_pieces(half, [pieces[key] for key in sorted(pieces)], summed, seen)
+    parts = [pieces[key] for key in sorted(pieces)]
+    unpack_pieces(half, parts, summed)
+    seen[...] = add_up(parts, slice(half * days, half * days + TAIL))
+    beside[...] = jnp.concatenate([seen[half:, :], jnp.zeros((half, LANES), F32)], axis=0)
 
     def take(at, grad_space):
         base[:, at:at + WIDTH] = base[:, at:at + WIDTH] - ETA_SPACE * grad_space
@@ -310,10 +315,10 @@
 
 def far_kernel(half, days, n_lon, base, predicted, packed, time_t, block, *rest):
     parts, rest = rest[:n_lon], rest[n_lon:]
-    fresh, message, crossing, cols, edge_near, edge_far, summed, seen = rest
+    seen, fresh, message, crossing, cols, edge_near, edge_far, summed = rest
     core = lax.axis_index("ta")
     rank = block.shape[0]
-    unpack_pieces(half, parts, summed, seen)
+    unpack_pieces(half, parts, summed)
 
     def take(at, grad_space):
         fresh[:, at:at + WIDTH] = base[:, at:at + WIDTH] - ETA_SPACE * grad_space
@@ -508,8 +513,9 @@
     sends += [(side, step) for side in (0, 1) for step in close] + [(0, 0)]
 
     def piece_rows(side, step):
-        more = 3 * days if (side, step) == (1, 0) else COLS if paired and (side, step) == (0, 3) else 0
-        return half * days + TAIL + more
+        more = TAIL if side == 0 else 0
+        more += 3 * days if (side, step) == (1, 0) else COLS if paired and (side, step) == (0, 3) else 0
+        return half * days + more
 
     operands = (send_list, send_count, target, swath, obs_mask, factor_space.reshape(rank * height, cells), factor_time)
     early = (0, n_lon - 1)
@@ -570,15 +576,17 @@
 
     fresh, edge = shape((rank, wide)), shape((rank, LANES))
     sides = [[key for key in order if key[0] == side] for side in (0, 1)]
-    side_out = [shape((days, wide)), shape((TAIL, LANES))]
-    base, block, near, seen_near = call(
+    side_out = shape((days, wide))
+    counts_out = shape((TAIL, LANES))
+    base, block, near, seen_near, beside = call(
         functools.partial(near_kernel, half, days, sides[0], paired, swap),
-        [fresh, edge, *side_out],
+        [fresh, edge, side_out, counts_out, counts_out],
     )(surface, edge_near, predicted, packed, time_t, bands(edge_far), *[pieces[key] for key in sides[0]], *(borders if paired else columns(*cols)))
-    surface, message, crossing, cols, edge_near, edge_far, far, seen_far = call(
+    seen_far = across(beside, "ta", 1)
+    surface, message, crossing, cols, edge_near, edge_far, far = call(
         functools.partial(far_kernel, half, days, len(sides[1])),
-        [fresh, shape((own_rows, LANES)), shape((own_rows, LANES)), shape((COLS, LANES)), edge, edge, *side_out],
-    )(base, predicted, packed, time_t, block, *[pieces[key] for key in sides[1]])
+        [fresh, shape((own_rows, LANES)), shape((own_rows, LANES)), shape((COLS, LANES)), edge, edge, side_out],
+    )(base, predicted, packed, time_t, block, *[pieces[key] for key in sides[1]], seen_far)
 
     narrowed = shape((sum_rows + NORM, LANES), BF16)
 

time: 57.4 us -> 57.4 us (level)
    ppermute x21 -> x22, waiting for transfers between devices: 22.3 us -> 23.2 us  [across(): lax.ppermute(value, axis, [(i, i ^ step) for i in range(lax.axis_size(axi...]
    ppermute x2, waiting for transfers between devices: 2.2 us -> 1.55 us  [bands(): return lax.ppermute(edge, ('lat', 'ta'), there + [(b, a) for a, b in there])]
    ppermute x21 -> x22, starting transfers between devices: 23.4 us -> 23 us  [across(): lax.ppermute(value, axis, [(i, i ^ step) for i in range(lax.axis_size(axi...]
  transfers between devices with their start and end apart: 23 -> 24, of which waited for: 14 -> 14; matrix products, arithmetic and copies ran while one was open for 0% -> 0% of each run, Pallas kernels for 2% -> 2%
where the time goes in v15:
time: 57.4 us; the launch traced here: 57.2 us
  starting transfers between devices  24.7 us (43%)
  waiting for transfers between devices  24.7 us (43%)
  Pallas kernels  7.02 us (12%)
  between operations  0.76 us (1%)
    ppermute x22, waiting for transfers between devices, across(): lax.ppermute(value, axis, [(i, i ^ step) for i in range(lax.axis_size(axi...  23.2 us
    ppermute x22, starting transfers between devices, across(): lax.ppermute(value, axis, [(i, i ^ step) for i in range(lax.axis_size(axi...  23 us
    pallas_call x13, Pallas kernels, run(): pl.pallas_call(kernel, out_shape=out_shape, in_specs=[pl.BlockSpec(memory...  7.02 us
    ppermute x2, starting transfers between devices, bands(): return lax.ppermute(edge, ('lat', 'ta'), there + [(b, a) for a, b in there])  1.76 us
    ppermute x2, waiting for transfers between devices, bands(): return lax.ppermute(edge, ('lat', 'ta'), there + [(b, a) for a, b in there])  1.55 us
  transfers between devices with their start and end apart: 24, of which 14 were waited for; matrix products, arithmetic and copies ran while one was open for 0% of the time, Pallas kernels for 2%

profile of v15, /device:TPU:0, one launch (start us, length us, event | category | flops | bytes accessed | tf_op | source)
XLA Modules:
  0.0 57.2 jit_solution(5139678999454796412)
XLA Ops:
  0.6 2.1 %shard_map.86 = (bf16[544,128]{1,0:T(8,128)(2,1)S(1)}, f32[64,64,128]{2,1,0:T(8,128)S(1)}, f32[80,128]{1,0:T(8,128)S(1)}, f32[96,1024]{1,0:T(8,128)S(1)}, f32[1536,128]{1,0:T(8,128)S(1)}, /*index=5*/f32[64,96]{1,0:T(8,128)S(1)}) custom-call(s32[1,4,32]{2,1,0:T(4,128)} %list_hbm.1, s32[1,4]{1,0:T(1,128)} %count_hbm.1, s32[64]{0:T(128)} %target_hbm.1, ...), custom_call_target="tpu_custom_call" | custom-call | flops 1000000 | bytes 1000000 | tf_op jit(solution)/shard_map/pallas_call | solution.py:482
  2.7 3.1 %collective-permute-start.3 = (bf16[544,128]{1,0:T(8,128)(2,1)S(1)}, bf16[544,128]{1,0:T(8,128)(2,1)S(1)}, u32[]{:S(2)}, u32[]{:S(2)}) collective-permute-start(bf16[544,128]{1,0:T(8,128)(2,1)S(1)} %get-tuple-element.61), channel_id=1, source_target_pairs={{0,4},{4,0},{8,12},{12,8},{1,5},{5,1},{9,13},{13,9},{2,6},{6,2},{1... | collective-permute-start | bytes 417800 | tf_op jit(solution)/shard_map/ppermute | solution.py:496
  6.2 4.2 %collective-permute-done.3.theirs.rest_3_ = bf16[544,128]{1,0:T(8,128)(2,1)S(1)} collective-permute-done((bf16[544,128]{1,0:T(8,128)(2,1)S(1)}, bf16[544,128]{1,0:T(8,128)(2,1)S(1)}, u32[]{:S(2)}, u32[]{:S(2)}) %collective-permute-start.3) | collective-permute-done | bytes 139296 | tf_op jit(solution)/shard_map/ppermute | solution.py:496
  10.4 3.1 %collective-permute-start.4 = (bf16[544,128]{1,0:T(8,128)(2,1)S(1)}, bf16[544,128]{1,0:T(8,128)(2,1)S(1)}, u32[]{:S(2)}, u32[]{:S(2)}) collective-permute-start(bf16[544,128]{1,0:T(8,128)(2,1)S(1)} %shard_map.90), channel_id=1, source_target_pairs={{0,8},{4,12},{8,0},{12,4},{1,9},{5,13},{9,1},{13,5},{2,10},{6,14},... | collective-permute-start | bytes 417800 | tf_op jit(solution)/shard_map/ppermute | solution.py:496
  13.5 1.6 %collective-permute-start.5 = (bf16[528,128]{1,0:T(8,128)(2,1)S(1)}, bf16[528,128]{1,0:T(8,128)(2,1)S(1)}, u32[]{:S(2)}, u32[]{:S(2)}) collective-permute-start(bf16[528,128]{1,0:T(8,128)(2,1)S(1)} %get-tuple-element.62), channel_id=1, source_target_pairs={{0,4},{4,0},{8,12},{12,8},{1,5},{5,1},{9,13},{13,9},{2,6},{6,2},{1... | collective-permute-start | bytes 405512 | tf_op jit(solution)/shard_map/ppermute | solution.py:496
  15.2 2.4 %collective-permute-start.7 = (bf16[512,128]{1,0:T(8,128)(2,1)S(1)}, bf16[512,128]{1,0:T(8,128)(2,1)S(1)}, u32[]{:S(2)}, u32[]{:S(2)}) collective-permute-start(bf16[512,128]{1,0:T(8,128)(2,1)S(1)} %get-tuple-element.67), channel_id=1, source_target_pairs={{0,5},{1,4},{4,1},{5,0},{8,13},{9,12},{12,9},{13,8},{2,7},{3,6},{6... | collective-permute-start | bytes 393224 | tf_op jit(solution)/shard_map/ppermute | solution.py:496
  17.9 2.2 %collective-permute-done.5.rest_1_ = bf16[528,128]{1,0:T(8,128)(2,1)S(1)} collective-permute-done((bf16[528,128]{1,0:T(8,128)(2,1)S(1)}, bf16[528,128]{1,0:T(8,128)(2,1)S(1)}, u32[]{:S(2)}, u32[]{:S(2)}) %collective-permute-start.5) | collective-permute-done | bytes 135200 | tf_op jit(solution)/shard_map/ppermute | solution.py:496
  20.1 1.5 %collective-permute-done.2.edge_far = f32[96,128]{1,0:T(8,128)S(1)} collective-permute-done((f32[96,128]{1,0:T(8,128)S(1)}, f32[96,128]{1,0:T(8,128)S(1)}, u32[]{:S(2)}, u32[]{:S(2)}) %collective-permute-start.2) | collective-permute-done | bytes 49184 | tf_op jit(solution)/shard_map/ppermute | solution.py:560
  21.6 0.8 %shard_map.91 = (f32[96,1024]{1,0:T(8,128)S(1)}, f32[96,128]{1,0:T(8,128)S(1)}, f32[64,1024]{1,0:T(8,128)S(1)}, f32[16,128]{1,0:T(8,128)S(1)}, f32[16,128]{1,0:T(8,128)S(1)}) custom-call(f32[96,1024]{1,0:T(8,128)S(1)} %get-tuple-element.45.surface, f32[96,128]{1,0:T(8,128)S(1)} %get-tuple-element.50.edge_near, f32[128,1024]{1,0:T(8,128)S(1)} %get-tuple-element.52.predicted, ...), custom_call_target="tpu_custom_call" | custom-call | flops 1000000 | bytes 1000000 | tf_op jit(solution)/shard_map/pallas_call | solution.py:482
  22.7 1.3 %collective-permute-done.6.rest_0_ = bf16[512,128]{1,0:T(8,128)(2,1)S(1)} collective-permute-done((bf16[512,128]{1,0:T(8,128)(2,1)S(1)}, bf16[512,128]{1,0:T(8,128)(2,1)S(1)}, u32[]{:S(2)}, u32[]{:S(2)}) %collective-permute-start.6) | collective-permute-done | bytes 131104 | tf_op jit(solution)/shard_map/ppermute | solution.py:496
  24.1 0.2 collective-permute-done.7.rest_2_
  24.3 0.7 %shard_map.92 = (f32[96,1024]{1,0:T(8,128)S(1)}, f32[104,128]{1,0:T(8,128)S(1)}, f32[104,128]{1,0:T(8,128)S(1)}, f32[16,128]{1,0:T(8,128)S(1)}, f32[96,128]{1,0:...) custom-call(f32[96,1024]{1,0:T(8,128)S(1)} %get-tuple-element.64.base, ...), custom_call_target="tpu_custom_call" | custom-call | flops 1000000 | bytes 1000000 | tf_op jit(solution)/shard_map/pallas_call | solution.py:482
  25.2 1.1 %collective-permute-done.9.core = f32[104,128]{1,0:T(8,128)S(1)} collective-permute-done((f32[104,128]{1,0:T(8,128)S(1)}, f32[104,128]{1,0:T(8,128)S(1)}, u32[]{:S(2)}, u32[]{:S(2)}) %collective-permute-start.9) | collective-permute-done | bytes 53280 | tf_op jit(solution)/shard_map/ppermute | solution.py:496
  26.3 1.7 %collective-permute-start.10 = (f32[104,128]{1,0:T(8,128)S(1)}, f32[104,128]{1,0:T(8,128)S(1)}, u32[]{:S(2)}, u32[]{:S(2)}) collective-permute-start(f32[104,128]{1,0:T(8,128)S(1)} %shard_map.93.mine), channel_id=1, source_target_pairs={{0,2},{2,0},{1,3},{3,1},{4,6},{6,4},{5,7},{7,5},{8,10},{10,8},{9,1... | collective-permute-start | bytes 159752 | tf_op jit(solution)/shard_map/ppermute | solution.py:496
  28.0 2.5 %collective-permute-done.10.band = f32[104,128]{1,0:T(8,128)S(1)} collective-permute-done((f32[104,128]{1,0:T(8,128)S(1)}, f32[104,128]{1,0:T(8,128)S(1)}, u32[]{:S(2)}, u32[]{:S(2)}) %collective-permute-start.10) | collective-permute-done | bytes 53280 | tf_op jit(solution)/shard_map/ppermute | solution.py:496
  30.6 0.9 %collective-permute-start.11 = (f32[104,128]{1,0:T(8,128)S(1)}, f32[104,128]{1,0:T(8,128)S(1)}, u32[]{:S(2)}, u32[]{:S(2)}) collective-permute-start(f32[104,128]{1,0:T(8,128)S(1)} %get-tuple-element.73.rest_0_), channel_id=1, source_target_pairs={{0,4},{4,0},{8,12},{12,8},{1,5},{5,1},{9,13},{13,9},{2,6},{6,2},{1... | collective-permute-start | bytes 159752 | tf_op jit(solution)/shard_map/ppermute | solution.py:496
  31.5 2.3 %collective-permute-start.13 = (f32[104,128]{1,0:T(8,128)S(1)}, f32[104,128]{1,0:T(8,128)S(1)}, u32[]{:S(2)}, u32[]{:S(2)}) collective-permute-start(f32[104,128]{1,0:T(8,128)S(1)} %get-tuple-element.74), channel_id=1, source_target_pairs={{0,12},{4,8},{8,4},{12,0},{1,13},{5,9},{9,5},{13,1},{2,14},{6,10},... | collective-permute-start | bytes 159752 | tf_op jit(solution)/shard_map/ppermute | solution.py:496
  33.8 0.3 collective-permute-start.12
  34.1 1.8 %collective-permute-start.16 = (f32[96,128]{1,0:T(8,128)S(1)}, f32[96,128]{1,0:T(8,128)S(1)}, u32[]{:S(2)}, u32[]{:S(2)}) collective-permute-start(f32[96,128]{1,0:T(8,128)S(1)} %get-tuple-element.81), channel_id=1, source_target_pairs={{1,2},{3,0},{2,1},{0,3},{5,6},{7,4},{6,5},{4,7},{9,10},{11,8},{10,... | collective-permute-start | bytes 147464 | tf_op jit(solution)/shard_map/ppermute | solution.py:560
  35.9 1.7 %collective-permute-done.13.rest_3_.cols_b = f32[104,128]{1,0:T(8,128)S(1)} collective-permute-done((f32[104,128]{1,0:T(8,128)S(1)}, f32[104,128]{1,0:T(8,128)S(1)}, u32[]{:S(2)}, u32[]{:S(2)}) %collective-permute-start.13) | collective-permute-done | bytes 53280 | tf_op jit(solution)/shard_map/ppermute | solution.py:496
  37.6 1.8 %collective-permute-done.12.rest_2_ = f32[104,128]{1,0:T(8,128)S(1)} collective-permute-done((f32[104,128]{1,0:T(8,128)S(1)}, f32[104,128]{1,0:T(8,128)S(1)}, u32[]{:S(2)}, u32[]{:S(2)}) %collective-permute-start.12) | collective-permute-done | bytes 53280 | tf_op jit(solution)/shard_map/ppermute | solution.py:496
  39.6 1.2 %collective-permute-done.14.time_other = f32[96,128]{1,0:T(8,128)S(1)} collective-permute-done((f32[96,128]{1,0:T(8,128)S(1)}, f32[96,128]{1,0:T(8,128)S(1)}, u32[]{:S(2)}, u32[]{:S(2)}) %collective-permute-start.14) | collective-permute-done | bytes 49184 | tf_op jit(solution)/shard_map/ppermute | solution.py:496
  40.8 1.3 %shard_map.96 = (f32[96,1024]{1,0:T(8,128)S(1)}, f32[96,128]{1,0:T(8,128)S(1)}, bf16[208,128]{1,0:T(8,128)(2,1)S(1)}, bf16[208,128]{1,0:T(8,128)(2,1)S(1)}) custom-call(f32[96,1024]{1,0:T(8,128)S(1)} %get-tuple-element.69.surface, f32[96,128]{1,0:T(8,128)S(1)} %get-tuple-element.75.time_own, f32[96,128]{1,0:T(8,128)S(1)} %collective-permute-done.14.time_other, ...), custom_call_target="tpu_custom_call" | custom-call | flops 1000000 | bytes 1000000 | tf_op jit(solution)/shard_map/pallas_call | solution.py:482
  42.3 1.5 %collective-permute-start.19 = (bf16[208,128]{1,0:T(8,128)(2,1)S(1)}, bf16[208,128]{1,0:T(8,128)(2,1)S(1)}, u32[]{:S(2)}, u32[]{:S(2)}) collective-permute-start(bf16[208,128]{1,0:T(8,128)(2,1)S(1)} %get-tuple-element.84.mine), channel_id=1, source_target_pairs={{0,2},{2,0},{1,3},{3,1},{4,6},{6,4},{5,7},{7,5},{8,10},{10,8},{9,1... | collective-permute-start | bytes 159752 | tf_op jit(solution)/shard_map/ppermute | solution.py:496
  44.0 0.4 collective-permute-start.18
  44.5 2.0 %collective-permute-done.19.band = bf16[208,128]{1,0:T(8,128)(2,1)S(1)} collective-permute-done((bf16[208,128]{1,0:T(8,128)(2,1)S(1)}, bf16[208,128]{1,0:T(8,128)(2,1)S(1)}, u32[]{:S(2)}, u32[]{:S(2)}) %collective-permute-start.19) | collective-permute-done | bytes 53280 | tf_op jit(solution)/shard_map/ppermute | solution.py:496
  46.5 1.3 %collective-permute-done.20.both = bf16[208,128]{1,0:T(8,128)(2,1)S(1)} collective-permute-done((bf16[208,128]{1,0:T(8,128)(2,1)S(1)}, bf16[208,128]{1,0:T(8,128)(2,1)S(1)}, u32[]{:S(2)}, u32[]{:S(2)}) %collective-permute-start.20) | collective-permute-done | bytes 53280 | tf_op jit(solution)/shard_map/ppermute | solution.py:496
  47.8 2.2 %collective-permute-start.23 = (bf16[208,128]{1,0:T(8,128)(2,1)S(1)}, bf16[208,128]{1,0:T(8,128)(2,1)S(1)}, u32[]{:S(2)}, u32[]{:S(2)}) collective-permute-start(bf16[208,128]{1,0:T(8,128)(2,1)S(1)} %shard_map.97.rest_0_), channel_id=1, source_target_pairs={{0,12},{4,8},{8,4},{12,0},{1,13},{5,9},{9,5},{13,1},{2,14},{6,10},... | collective-permute-start | bytes 159752 | tf_op jit(solution)/shard_map/ppermute | solution.py:496
  49.9 2.3 %collective-permute-start.21 = (bf16[208,128]{1,0:T(8,128)(2,1)S(1)}, bf16[208,128]{1,0:T(8,128)(2,1)S(1)}, u32[]{:S(2)}, u32[]{:S(2)}) collective-permute-start(bf16[208,128]{1,0:T(8,128)(2,1)S(1)} %shard_map.97.rest_0_), channel_id=1, source_target_pairs={{0,4},{4,0},{8,12},{12,8},{1,5},{5,1},{9,13},{13,9},{2,6},{6,2},{1... | collective-permute-start | bytes 159752 | tf_op jit(solution)/shard_map/ppermute | solution.py:496
  52.2 1.9 %collective-permute-done.23.rest_3_ = bf16[208,128]{1,0:T(8,128)(2,1)S(1)} collective-permute-done((bf16[208,128]{1,0:T(8,128)(2,1)S(1)}, bf16[208,128]{1,0:T(8,128)(2,1)S(1)}, u32[]{:S(2)}, u32[]{:S(2)}) %collective-permute-start.23) | collective-permute-done | bytes 53280 | tf_op jit(solution)/shard_map/ppermute | solution.py:496
  54.2 1.6 %collective-permute-done.22.rest_2_ = bf16[208,128]{1,0:T(8,128)(2,1)S(1)} collective-permute-done((bf16[208,128]{1,0:T(8,128)(2,1)S(1)}, bf16[208,128]{1,0:T(8,128)(2,1)S(1)}, u32[]{:S(2)}, u32[]{:S(2)}) %collective-permute-start.22) | collective-permute-done | bytes 53280 | tf_op jit(solution)/shard_map/ppermute | solution.py:496
  55.8 1.4 %shard_map.98 = (f32[1536,128]{1,0:T(8,128)}, f32[64,96]{1,0:T(8,128)}) custom-call(f32[96,1024]{1,0:T(8,128)S(1)} %get-tuple-element.82.surface, f32[96,1024]{1,0:T(8,128)S(1)} %collective-permute-done.17.other, f32[96,128]{1,0:T(8,128)S(1)} %get-tuple-element.83.time_t, bf16[208,128]{1,0:T(8,128)(2,1)S(1)} %shard_map.97.rest_0_, ...), custom_call_target="tpu_custom_call" | custom-call | flops 1000000 | bytes 1000000 | tf_op jit(solution)/shard_map/pallas_call | solution.py:482
  (31 shorter events, 1.8 us)
Async XLA Ops:
  2.7 14.9 %copy-start = (f32[64,96]{1,0:T(8,128)S(1)}, f32[64,96]{1,0:T(8,128)}, u32[]{:S(2)}) copy-start(f32[64,96]{1,0:T(8,128)} %time_own.1) | copy-start | bytes 73732
  2.7 7.6 %collective-permute-start.3 = (bf16[544,128]{1,0:T(8,128)(2,1)S(1)}, bf16[544,128]{1,0:T(8,128)(2,1)S(1)}, u32[]{:S(2)}, u32[]{:S(2)}) collective-permute-start(bf16[544,128]{1,0:T(8,128)(2,1)S(1)} %get-tuple-element.61), channel_id=1, source_target_pairs={{0,4},{4,0},{8,12},{12,8},{1,5},{5,1},{9,13},{13,9},{2,6},{6,2},{1... | collective-permute-start | bytes 417800 | tf_op jit(solution)/shard_map/ppermute | solution.py:496
  6.0 9.1 %collective-permute-start.1 = (bf16[512,128]{1,0:T(8,128)(2,1)S(1)}, bf16[512,128]{1,0:T(8,128)(2,1)S(1)}, u32[]{:S(2)}, u32[]{:S(2)}) collective-permute-start(bf16[512,128]{1,0:T(8,128)(2,1)S(1)} %get-tuple-element.56), channel_id=1, source_target_pairs={{0,4},{4,0},{8,12},{12,8},{1,5},{5,1},{9,13},{13,9},{2,6},{6,2},{1... | collective-permute-start | bytes 393224 | tf_op jit(solution)/shard_map/ppermute | solution.py:496
  6.1 11.6 %collective-permute-start = (bf16[704,128]{1,0:T(8,128)(2,1)S(1)}, bf16[704,128]{1,0:T(8,128)(2,1)S(1)}, u32[]{:S(2)}, u32[]{:S(2)}) collective-permute-start(bf16[704,128]{1,0:T(8,128)(2,1)S(1)} %get-tuple-element.51), channel_id=1, source_target_pairs={{0,1},{1,0},{4,5},{5,4},{8,9},{9,8},{12,13},{13,12},{2,3},{3,2},{6... | collective-permute-start | bytes 540680 | tf_op jit(solution)/shard_map/ppermute | solution.py:496
  10.4 11.3 %collective-permute-start.4 = (bf16[544,128]{1,0:T(8,128)(2,1)S(1)}, bf16[544,128]{1,0:T(8,128)(2,1)S(1)}, u32[]{:S(2)}, u32[]{:S(2)}) collective-permute-start(bf16[544,128]{1,0:T(8,128)(2,1)S(1)} %shard_map.90), channel_id=1, source_target_pairs={{0,8},{4,12},{8,0},{12,4},{1,9},{5,13},{9,1},{13,5},{2,10},{6,14},... | collective-permute-start | bytes 417800 | tf_op jit(solution)/shard_map/ppermute | solution.py:496
  13.5 6.6 %collective-permute-start.5 = (bf16[528,128]{1,0:T(8,128)(2,1)S(1)}, bf16[528,128]{1,0:T(8,128)(2,1)S(1)}, u32[]{:S(2)}, u32[]{:S(2)}) collective-permute-start(bf16[528,128]{1,0:T(8,128)(2,1)S(1)} %get-tuple-element.62), channel_id=1, source_target_pairs={{0,4},{4,0},{8,12},{12,8},{1,5},{5,1},{9,13},{13,9},{2,6},{6,2},{1... | collective-permute-start | bytes 405512 | tf_op jit(solution)/shard_map/ppermute | solution.py:496
  15.1 8.9 %collective-permute-start.6 = (bf16[512,128]{1,0:T(8,128)(2,1)S(1)}, bf16[512,128]{1,0:T(8,128)(2,1)S(1)}, u32[]{:S(2)}, u32[]{:S(2)}) collective-permute-start(bf16[512,128]{1,0:T(8,128)(2,1)S(1)} %get-tuple-element.66), channel_id=1, source_target_pairs={{0,9},{1,8},{4,13},{5,12},{8,1},{9,0},{12,5},{13,4},{2,11},{3,10},... | collective-permute-start | bytes 393224 | tf_op jit(solution)/shard_map/ppermute | solution.py:496
  15.2 9.1 %collective-permute-start.7 = (bf16[512,128]{1,0:T(8,128)(2,1)S(1)}, bf16[512,128]{1,0:T(8,128)(2,1)S(1)}, u32[]{:S(2)}, u32[]{:S(2)}) collective-permute-start(bf16[512,128]{1,0:T(8,128)(2,1)S(1)} %get-tuple-element.67), channel_id=1, source_target_pairs={{0,5},{1,4},{4,1},{5,0},{8,13},{9,12},{12,9},{13,8},{2,7},{3,6},{6... | collective-permute-start | bytes 393224 | tf_op jit(solution)/shard_map/ppermute | solution.py:496
  17.6 4.0 %collective-permute-start.2 = (f32[96,128]{1,0:T(8,128)S(1)}, f32[96,128]{1,0:T(8,128)S(1)}, u32[]{:S(2)}, u32[]{:S(2)}) collective-permute-start(f32[96,128]{1,0:T(8,128)S(1)} %get-tuple-element.59), channel_id=1, source_target_pairs={{1,2},{3,0},{2,1},{0,3},{5,6},{7,4},{6,5},{4,7},{9,10},{11,8},{10,... | collective-permute-start | bytes 147464 | tf_op jit(solution)/shard_map/ppermute | solution.py:560
  22.5 1.8 %collective-permute-start.8 = (f32[16,128]{1,0:T(8,128)S(1)}, f32[16,128]{1,0:T(8,128)S(1)}, u32[]{:S(2)}, u32[]{:S(2)}) collective-permute-start(f32[16,128]{1,0:T(8,128)S(1)} %get-tuple-element.68), channel_id=1, source_target_pairs={{0,1},{1,0},{2,3},{3,2},{4,5},{5,4},{6,7},{7,6},{8,9},{9,8},{10,11... | collective-permute-start | bytes 24584 | tf_op jit(solution)/shard_map/ppermute | solution.py:496
  25.0 1.3 %collective-permute-start.9 = (f32[104,128]{1,0:T(8,128)S(1)}, f32[104,128]{1,0:T(8,128)S(1)}, u32[]{:S(2)}, u32[]{:S(2)}) collective-permute-start(f32[104,128]{1,0:T(8,128)S(1)} %get-tuple-element.71), channel_id=1, source_target_pairs={{0,1},{1,0},{2,3},{3,2},{4,5},{5,4},{6,7},{7,6},{8,9},{9,8},{10,11... | collective-permute-start | bytes 159752 | tf_op jit(solution)/shard_map/ppermute | solution.py:496
  26.3 4.2 %collective-permute-start.10 = (f32[104,128]{1,0:T(8,128)S(1)}, f32[104,128]{1,0:T(8,128)S(1)}, u32[]{:S(2)}, u32[]{:S(2)}) collective-permute-start(f32[104,128]{1,0:T(8,128)S(1)} %shard_map.93.mine), channel_id=1, source_target_pairs={{0,2},{2,0},{1,3},{3,1},{4,6},{6,4},{5,7},{7,5},{8,10},{10,8},{9,1... | collective-permute-start | bytes 159752 | tf_op jit(solution)/shard_map/ppermute | solution.py:496
  30.6 5.3 %collective-permute-start.11 = (f32[104,128]{1,0:T(8,128)S(1)}, f32[104,128]{1,0:T(8,128)S(1)}, u32[]{:S(2)}, u32[]{:S(2)}) collective-permute-start(f32[104,128]{1,0:T(8,128)S(1)} %get-tuple-element.73.rest_0_), channel_id=1, source_target_pairs={{0,4},{4,0},{8,12},{12,8},{1,5},{5,1},{9,13},{13,9},{2,6},{6,2},{1... | collective-permute-start | bytes 159752 | tf_op jit(solution)/shard_map/ppermute | solution.py:496
  31.5 6.1 %collective-permute-start.13 = (f32[104,128]{1,0:T(8,128)S(1)}, f32[104,128]{1,0:T(8,128)S(1)}, u32[]{:S(2)}, u32[]{:S(2)}) collective-permute-start(f32[104,128]{1,0:T(8,128)S(1)} %get-tuple-element.74), channel_id=1, source_target_pairs={{0,12},{4,8},{8,4},{12,0},{1,13},{5,9},{9,5},{13,1},{2,14},{6,10},... | collective-permute-start | bytes 159752 | tf_op jit(solution)/shard_map/ppermute | solution.py:496
  33.8 5.6 %collective-permute-start.12 = (f32[104,128]{1,0:T(8,128)S(1)}, f32[104,128]{1,0:T(8,128)S(1)}, u32[]{:S(2)}, u32[]{:S(2)}) collective-permute-start(f32[104,128]{1,0:T(8,128)S(1)} %get-tuple-element.74), channel_id=1, source_target_pairs={{0,8},{4,12},{8,0},{12,4},{1,9},{5,13},{9,1},{13,5},{2,10},{6,14},... | collective-permute-start | bytes 159752 | tf_op jit(solution)/shard_map/ppermute | solution.py:496
  34.1 5.5 %collective-permute-start.15 = (f32[96,128]{1,0:T(8,128)S(1)}, f32[96,128]{1,0:T(8,128)S(1)}, u32[]{:S(2)}, u32[]{:S(2)}) collective-permute-start(f32[96,128]{1,0:T(8,128)S(1)} %get-tuple-element.80), channel_id=1, source_target_pairs={{0,1},{1,0},{2,3},{3,2},{4,5},{5,4},{6,7},{7,6},{8,9},{9,8},{10,11... | collective-permute-start | bytes 147464 | tf_op jit(solution)/shard_map/ppermute | solution.py:496
  34.1 5.5 %collective-permute-start.16 = (f32[96,128]{1,0:T(8,128)S(1)}, f32[96,128]{1,0:T(8,128)S(1)}, u32[]{:S(2)}, u32[]{:S(2)}) collective-permute-start(f32[96,128]{1,0:T(8,128)S(1)} %get-tuple-element.81), channel_id=1, source_target_pairs={{1,2},{3,0},{2,1},{0,3},{5,6},{7,4},{6,5},{4,7},{9,10},{11,8},{10,... | collective-permute-start | bytes 147464 | tf_op jit(solution)/shard_map/ppermute | solution.py:560
  39.5 1.3 %collective-permute-start.14 = (f32[96,128]{1,0:T(8,128)S(1)}, f32[96,128]{1,0:T(8,128)S(1)}, u32[]{:S(2)}, u32[]{:S(2)}) collective-permute-start(f32[96,128]{1,0:T(8,128)S(1)} %get-tuple-element.75.time_own), channel_id=1, source_target_pairs={{0,1},{1,0},{2,3},{3,2},{4,5},{5,4},{6,7},{7,6},{8,9},{9,8},{10,11... | collective-permute-start | bytes 147464 | tf_op jit(solution)/shard_map/ppermute | solution.py:496
  42.1 13.7 %collective-permute-start.17 = (f32[96,1024]{1,0:T(8,128)S(1)}, f32[96,1024]{1,0:T(8,128)S(1)}, u32[]{:S(2)}, u32[]{:S(2)}) collective-permute-start(f32[96,1024]{1,0:T(8,128)S(1)} %get-tuple-element.82.surface), channel_id=1, source_target_pairs={{0,1},{1,0},{2,3},{3,2},{4,5},{5,4},{6,7},{7,6},{8,9},{9,8},{10,11... | collective-permute-start | bytes 1179656 | tf_op jit(solution)/shard_map/ppermute | solution.py:496
  42.3 4.1 %collective-permute-start.19 = (bf16[208,128]{1,0:T(8,128)(2,1)S(1)}, bf16[208,128]{1,0:T(8,128)(2,1)S(1)}, u32[]{:S(2)}, u32[]{:S(2)}) collective-permute-start(bf16[208,128]{1,0:T(8,128)(2,1)S(1)} %get-tuple-element.84.mine), channel_id=1, source_target_pairs={{0,2},{2,0},{1,3},{3,1},{4,6},{6,4},{5,7},{7,5},{8,10},{10,8},{9,1... | collective-permute-start | bytes 159752 | tf_op jit(solution)/shard_map/ppermute | solution.py:496
  43.9 3.9 %collective-permute-start.20 = (bf16[208,128]{1,0:T(8,128)(2,1)S(1)}, bf16[208,128]{1,0:T(8,128)(2,1)S(1)}, u32[]{:S(2)}, u32[]{:S(2)}) collective-permute-start(bf16[208,128]{1,0:T(8,128)(2,1)S(1)} %get-tuple-element.85), channel_id=1, source_target_pairs={{0,3},{1,2},{2,1},{3,0},{4,7},{5,6},{6,5},{7,4},{8,11},{9,10},{10,... | collective-permute-start | bytes 159752 | tf_op jit(solution)/shard_map/ppermute | solution.py:496
  44.0 3.7 %collective-permute-start.18 = (bf16[208,128]{1,0:T(8,128)(2,1)S(1)}, bf16[208,128]{1,0:T(8,128)(2,1)S(1)}, u32[]{:S(2)}, u32[]{:S(2)}) collective-permute-start(bf16[208,128]{1,0:T(8,128)(2,1)S(1)} %get-tuple-element.85), channel_id=1, source_target_pairs={{0,1},{1,0},{2,3},{3,2},{4,5},{5,4},{6,7},{7,6},{8,9},{9,8},{10,11... | collective-permute-start | bytes 159752 | tf_op jit(solution)/shard_map/ppermute | solution.py:496
  47.8 6.4 %collective-permute-start.23 = (bf16[208,128]{1,0:T(8,128)(2,1)S(1)}, bf16[208,128]{1,0:T(8,128)(2,1)S(1)}, u32[]{:S(2)}, u32[]{:S(2)}) collective-permute-start(bf16[208,128]{1,0:T(8,128)(2,1)S(1)} %shard_map.97.rest_0_), channel_id=1, source_target_pairs={{0,12},{4,8},{8,4},{12,0},{1,13},{5,9},{9,5},{13,1},{2,14},{6,10},... | collective-permute-start | bytes 159752 | tf_op jit(solution)/shard_map/ppermute | solution.py:496
  49.9 5.8 %collective-permute-start.22 = (bf16[208,128]{1,0:T(8,128)(2,1)S(1)}, bf16[208,128]{1,0:T(8,128)(2,1)S(1)}, u32[]{:S(2)}, u32[]{:S(2)}) collective-permute-start(bf16[208,128]{1,0:T(8,128)(2,1)S(1)} %shard_map.97.rest_0_), channel_id=1, source_target_pairs={{0,8},{4,12},{8,0},{12,4},{1,9},{5,13},{9,1},{13,5},{2,10},{6,14},... | collective-permute-start | bytes 159752 | tf_op jit(solution)/shard_map/ppermute | solution.py:496
  49.9 5.8 %collective-permute-start.21 = (bf16[208,128]{1,0:T(8,128)(2,1)S(1)}, bf16[208,128]{1,0:T(8,128)(2,1)S(1)}, u32[]{:S(2)}, u32[]{:S(2)}) collective-permute-start(bf16[208,128]{1,0:T(8,128)(2,1)S(1)} %shard_map.97.rest_0_), channel_id=1, source_target_pairs={{0,4},{4,0},{8,12},{12,8},{1,5},{5,1},{9,13},{13,9},{2,6},{6,2},{1... | collective-permute-start | bytes 159752 | tf_op jit(solution)/shard_map/ppermute | solution.py:496

commit v16 on v15

--- a/solution.py
+++ b/solution.py
@@ -239,22 +239,22 @@
     moved = pltpu.roll(time_t, days, 1)
     time_twice = (jnp.where(below, moved, time_t) if first else jnp.where(below, time_t, moved)).astype(BF16)
     seen_bf = seen[:, :days].astype(BF16)
-    owner = lax.broadcasted_iota(jnp.int32, (TAIL, WIDTH), 0)
-    lane = lax.broadcasted_iota(jnp.int32, (TAIL, WIDTH), 1)
+    owner = lax.broadcasted_iota(jnp.int32, (TAIL, 2 * WIDTH), 0)
+    lane = lax.broadcasted_iota(jnp.int32, (TAIL, 2 * WIDTH), 1)
     grad_time = jnp.zeros((rank, LANES), F32)
     grad_diag = jnp.zeros((rank, LANES), F32)
-    for at in range(0, half * LANES, WIDTH):
+    for at in range(0, half * LANES, 2 * WIDTH):
         spread = (owner * LANES <= lane + at) & (lane + at < (owner + 1) * LANES)
         weight = dot(seen_bf, spread.astype(BF16), (0, 0))
-        part = packed[:, at:at + WIDTH]
-        residual = weight * predicted[first:first + days, at:at + WIDTH] - summed[:, at:at + WIDTH]
+        part = packed[:, at:at + 2 * WIDTH]
+        residual = weight * predicted[first:first + days, at:at + 2 * WIDTH] - summed[:, at:at + 2 * WIDTH]
         high = residual.astype(BF16)
         low = (residual - high.astype(F32)).astype(BF16)
         both = jnp.concatenate([high, low], axis=0)
         take(at, dot(time_twice, both, (1, 0)))
         grad_time = grad_time + dot(part, both, (1, 1))
         wide = part.astype(F32)
-        for row in range(WIDTH // LANES):
+        for row in range(2 * WIDTH // LANES):
             strip = row_of(wide, row)
             square = jnp.sum(strip * strip, axis=1, keepdims=True)
             grad_diag = grad_diag + square * seen[at // LANES + row:at // LANES + row + 1, :]
@@ -308,7 +308,7 @@
     beside[...] = jnp.concatenate([seen[half:, :], jnp.zeros((half, LANES), F32)], axis=0)
 
     def take(at, grad_space):
-        base[:, at:at + WIDTH] = base[:, at:at + WIDTH] - ETA_SPACE * grad_space
+        base[:, at:at + 2 * WIDTH] = base[:, at:at + 2 * WIDTH] - ETA_SPACE * grad_space
 
     block[...] = side_gradients(half, 0, predicted, packed, time_t[...], seen, summed, take)
 
@@ -321,7 +321,7 @@
     unpack_pieces(half, parts, summed)
 
     def take(at, grad_space):
-        fresh[:, at:at + WIDTH] = base[:, at:at + WIDTH] - ETA_SPACE * grad_space
+        fresh[:, at:at + 2 * WIDTH] = base[:, at:at + 2 * WIDTH] - ETA_SPACE * grad_space
 
     crossing[:rank, :] = side_gradients(half, days, predicted, packed, time_t[...], seen, summed, take)
     message[:rank, :] = block[...]

time: 57.4 us -> 57.1 us (level)
  no operation moved by 1% of the time
where the time goes in v16:
time: 57.1 us; the launch traced here: 56.9 us
  starting transfers between devices  24.9 us (44%)
  waiting for transfers between devices  24.4 us (43%)
  Pallas kernels  6.81 us (12%)
  between operations  0.76 us (1%)
    ppermute x22, starting transfers between devices, across(): lax.ppermute(value, axis, [(i, i ^ step) for i in range(lax.axis_size(axi...  23.3 us
    ppermute x22, waiting for transfers between devices, across(): lax.ppermute(value, axis, [(i, i ^ step) for i in range(lax.axis_size(axi...  22.8 us
    pallas_call x13, Pallas kernels, run(): pl.pallas_call(kernel, out_shape=out_shape, in_specs=[pl.BlockSpec(memory...  6.81 us
    ppermute x2, starting transfers between devices, bands(): return lax.ppermute(edge, ('lat', 'ta'), there + [(b, a) for a, b in there])  1.62 us
    ppermute x2, waiting for transfers between devices, bands(): return lax.ppermute(edge, ('lat', 'ta'), there + [(b, a) for a, b in there])  1.6 us
  transfers between devices with their start and end apart: 24, of which 14 were waited for; matrix products, arithmetic and copies ran while one was open for 0% of the time, Pallas kernels for 2%

profile of v16, /device:TPU:0, one launch (start us, length us, event | category | flops | bytes accessed | tf_op | source)
XLA Modules:
  0.0 56.9 jit_solution(11831507543104344975)
XLA Ops:
  0.6 2.1 %shard_map.86 = (bf16[544,128]{1,0:T(8,128)(2,1)S(1)}, f32[64,64,128]{2,1,0:T(8,128)S(1)}, f32[80,128]{1,0:T(8,128)S(1)}, f32[96,1024]{1,0:T(8,128)S(1)}, f32[1536,128]{1,0:T(8,128)S(1)}, /*index=5*/f32[64,96]{1,0:T(8,128)S(1)}) custom-call(s32[1,4,32]{2,1,0:T(4,128)} %list_hbm.1, s32[1,4]{1,0:T(1,128)} %count_hbm.1, s32[64]{0:T(128)} %target_hbm.1, ...), custom_call_target="tpu_custom_call" | custom-call | flops 1000000 | bytes 1000000 | tf_op jit(solution)/shard_map/pallas_call | solution.py:482
  2.8 3.1 %collective-permute-start.3 = (bf16[544,128]{1,0:T(8,128)(2,1)S(1)}, bf16[544,128]{1,0:T(8,128)(2,1)S(1)}, u32[]{:S(2)}, u32[]{:S(2)}) collective-permute-start(bf16[544,128]{1,0:T(8,128)(2,1)S(1)} %get-tuple-element.61), channel_id=1, source_target_pairs={{0,4},{4,0},{8,12},{12,8},{1,5},{5,1},{9,13},{13,9},{2,6},{6,2},{1... | collective-permute-start | bytes 417800 | tf_op jit(solution)/shard_map/ppermute | solution.py:496
  6.2 4.2 %collective-permute-done.3.theirs.rest_3_ = bf16[544,128]{1,0:T(8,128)(2,1)S(1)} collective-permute-done((bf16[544,128]{1,0:T(8,128)(2,1)S(1)}, bf16[544,128]{1,0:T(8,128)(2,1)S(1)}, u32[]{:S(2)}, u32[]{:S(2)}) %collective-permute-start.3) | collective-permute-done | bytes 139296 | tf_op jit(solution)/shard_map/ppermute | solution.py:496
  10.4 3.1 %collective-permute-start.4 = (bf16[544,128]{1,0:T(8,128)(2,1)S(1)}, bf16[544,128]{1,0:T(8,128)(2,1)S(1)}, u32[]{:S(2)}, u32[]{:S(2)}) collective-permute-start(bf16[544,128]{1,0:T(8,128)(2,1)S(1)} %shard_map.90), channel_id=1, source_target_pairs={{0,8},{4,12},{8,0},{12,4},{1,9},{5,13},{9,1},{13,5},{2,10},{6,14},... | collective-permute-start | bytes 417800 | tf_op jit(solution)/shard_map/ppermute | solution.py:496
  13.5 1.6 %collective-permute-start.5 = (bf16[528,128]{1,0:T(8,128)(2,1)S(1)}, bf16[528,128]{1,0:T(8,128)(2,1)S(1)}, u32[]{:S(2)}, u32[]{:S(2)}) collective-permute-start(bf16[528,128]{1,0:T(8,128)(2,1)S(1)} %get-tuple-element.62), channel_id=1, source_target_pairs={{0,4},{4,0},{8,12},{12,8},{1,5},{5,1},{9,13},{13,9},{2,6},{6,2},{1... | collective-permute-start | bytes 405512 | tf_op jit(solution)/shard_map/ppermute | solution.py:496
  15.2 2.4 %collective-permute-start.7 = (bf16[512,128]{1,0:T(8,128)(2,1)S(1)}, bf16[512,128]{1,0:T(8,128)(2,1)S(1)}, u32[]{:S(2)}, u32[]{:S(2)}) collective-permute-start(bf16[512,128]{1,0:T(8,128)(2,1)S(1)} %get-tuple-element.67), channel_id=1, source_target_pairs={{0,5},{1,4},{4,1},{5,0},{8,13},{9,12},{12,9},{13,8},{2,7},{3,6},{6... | collective-permute-start | bytes 393224 | tf_op jit(solution)/shard_map/ppermute | solution.py:496
  17.9 2.2 %collective-permute-done.5.rest_1_ = bf16[528,128]{1,0:T(8,128)(2,1)S(1)} collective-permute-done((bf16[528,128]{1,0:T(8,128)(2,1)S(1)}, bf16[528,128]{1,0:T(8,128)(2,1)S(1)}, u32[]{:S(2)}, u32[]{:S(2)}) %collective-permute-start.5) | collective-permute-done | bytes 135200 | tf_op jit(solution)/shard_map/ppermute | solution.py:496
  20.1 1.6 %collective-permute-done.2.edge_far = f32[96,128]{1,0:T(8,128)S(1)} collective-permute-done((f32[96,128]{1,0:T(8,128)S(1)}, f32[96,128]{1,0:T(8,128)S(1)}, u32[]{:S(2)}, u32[]{:S(2)}) %collective-permute-start.2) | collective-permute-done | bytes 49184 | tf_op jit(solution)/shard_map/ppermute | solution.py:560
  21.7 0.7 %shard_map.91 = (f32[96,1024]{1,0:T(8,128)S(1)}, f32[96,128]{1,0:T(8,128)S(1)}, f32[64,1024]{1,0:T(8,128)S(1)}, f32[16,128]{1,0:T(8,128)S(1)}, f32[16,128]{1,0:T(8,128)S(1)}) custom-call(f32[96,1024]{1,0:T(8,128)S(1)} %get-tuple-element.45.surface, f32[96,128]{1,0:T(8,128)S(1)} %get-tuple-element.50.edge_near, f32[128,1024]{1,0:T(8,128)S(1)} %get-tuple-element.52.predicted, ...), custom_call_target="tpu_custom_call" | custom-call | flops 1000000 | bytes 1000000 | tf_op jit(solution)/shard_map/pallas_call | solution.py:482
  22.6 1.4 %collective-permute-done.6.rest_0_ = bf16[512,128]{1,0:T(8,128)(2,1)S(1)} collective-permute-done((bf16[512,128]{1,0:T(8,128)(2,1)S(1)}, bf16[512,128]{1,0:T(8,128)(2,1)S(1)}, u32[]{:S(2)}, u32[]{:S(2)}) %collective-permute-start.6) | collective-permute-done | bytes 131104 | tf_op jit(solution)/shard_map/ppermute | solution.py:496
  24.1 0.3 collective-permute-done.7.rest_2_
  24.3 0.6 %shard_map.92 = (f32[96,1024]{1,0:T(8,128)S(1)}, f32[104,128]{1,0:T(8,128)S(1)}, f32[104,128]{1,0:T(8,128)S(1)}, f32[16,128]{1,0:T(8,128)S(1)}, f32[96,128]{1,0:...) custom-call(f32[96,1024]{1,0:T(8,128)S(1)} %get-tuple-element.64.base, ...), custom_call_target="tpu_custom_call" | custom-call | flops 1000000 | bytes 1000000 | tf_op jit(solution)/shard_map/pallas_call | solution.py:482
  25.1 1.1 %collective-permute-done.9.core = f32[104,128]{1,0:T(8,128)S(1)} collective-permute-done((f32[104,128]{1,0:T(8,128)S(1)}, f32[104,128]{1,0:T(8,128)S(1)}, u32[]{:S(2)}, u32[]{:S(2)}) %collective-permute-start.9) | collective-permute-done | bytes 53280 | tf_op jit(solution)/shard_map/ppermute | solution.py:496
  26.2 1.7 %collective-permute-start.10 = (f32[104,128]{1,0:T(8,128)S(1)}, f32[104,128]{1,0:T(8,128)S(1)}, u32[]{:S(2)}, u32[]{:S(2)}) collective-permute-start(f32[104,128]{1,0:T(8,128)S(1)} %shard_map.93.mine), channel_id=1, source_target_pairs={{0,2},{2,0},{1,3},{3,1},{4,6},{6,4},{5,7},{7,5},{8,10},{10,8},{9,1... | collective-permute-start | bytes 159752 | tf_op jit(solution)/shard_map/ppermute | solution.py:496
  28.0 2.5 %collective-permute-done.10.band = f32[104,128]{1,0:T(8,128)S(1)} collective-permute-done((f32[104,128]{1,0:T(8,128)S(1)}, f32[104,128]{1,0:T(8,128)S(1)}, u32[]{:S(2)}, u32[]{:S(2)}) %collective-permute-start.10) | collective-permute-done | bytes 53280 | tf_op jit(solution)/shard_map/ppermute | solution.py:496
  30.5 0.9 %collective-permute-start.11 = (f32[104,128]{1,0:T(8,128)S(1)}, f32[104,128]{1,0:T(8,128)S(1)}, u32[]{:S(2)}, u32[]{:S(2)}) collective-permute-start(f32[104,128]{1,0:T(8,128)S(1)} %get-tuple-element.73.rest_0_), channel_id=1, source_target_pairs={{0,4},{4,0},{8,12},{12,8},{1,5},{5,1},{9,13},{13,9},{2,6},{6,2},{1... | collective-permute-start | bytes 159752 | tf_op jit(solution)/shard_map/ppermute | solution.py:496
  31.4 2.5 %collective-permute-start.13 = (f32[104,128]{1,0:T(8,128)S(1)}, f32[104,128]{1,0:T(8,128)S(1)}, u32[]{:S(2)}, u32[]{:S(2)}) collective-permute-start(f32[104,128]{1,0:T(8,128)S(1)} %get-tuple-element.74), channel_id=1, source_target_pairs={{0,12},{4,8},{8,4},{12,0},{1,13},{5,9},{9,5},{13,1},{2,14},{6,10},... | collective-permute-start | bytes 159752 | tf_op jit(solution)/shard_map/ppermute | solution.py:496
  33.9 0.5 collective-permute-start.12
  34.4 1.6 %collective-permute-start.16 = (f32[96,128]{1,0:T(8,128)S(1)}, f32[96,128]{1,0:T(8,128)S(1)}, u32[]{:S(2)}, u32[]{:S(2)}) collective-permute-start(f32[96,128]{1,0:T(8,128)S(1)} %get-tuple-element.81), channel_id=1, source_target_pairs={{1,2},{3,0},{2,1},{0,3},{5,6},{7,4},{6,5},{4,7},{9,10},{11,8},{10,... | collective-permute-start | bytes 147464 | tf_op jit(solution)/shard_map/ppermute | solution.py:560
  36.0 1.5 %collective-permute-done.13.rest_3_.cols_b = f32[104,128]{1,0:T(8,128)S(1)} collective-permute-done((f32[104,128]{1,0:T(8,128)S(1)}, f32[104,128]{1,0:T(8,128)S(1)}, u32[]{:S(2)}, u32[]{:S(2)}) %collective-permute-start.13) | collective-permute-done | bytes 53280 | tf_op jit(solution)/shard_map/ppermute | solution.py:496
  37.5 1.4 %collective-permute-done.12.rest_2_ = f32[104,128]{1,0:T(8,128)S(1)} collective-permute-done((f32[104,128]{1,0:T(8,128)S(1)}, f32[104,128]{1,0:T(8,128)S(1)}, u32[]{:S(2)}, u32[]{:S(2)}) %collective-permute-start.12) | collective-permute-done | bytes 53280 | tf_op jit(solution)/shard_map/ppermute | solution.py:496
  39.1 1.2 %collective-permute-done.14.time_other = f32[96,128]{1,0:T(8,128)S(1)} collective-permute-done((f32[96,128]{1,0:T(8,128)S(1)}, f32[96,128]{1,0:T(8,128)S(1)}, u32[]{:S(2)}, u32[]{:S(2)}) %collective-permute-start.14) | collective-permute-done | bytes 49184 | tf_op jit(solution)/shard_map/ppermute | solution.py:496
  40.3 1.3 %shard_map.96 = (f32[96,1024]{1,0:T(8,128)S(1)}, f32[96,128]{1,0:T(8,128)S(1)}, bf16[208,128]{1,0:T(8,128)(2,1)S(1)}, bf16[208,128]{1,0:T(8,128)(2,1)S(1)}) custom-call(f32[96,1024]{1,0:T(8,128)S(1)} %get-tuple-element.69.surface, f32[96,128]{1,0:T(8,128)S(1)} %get-tuple-element.75.time_own, f32[96,128]{1,0:T(8,128)S(1)} %collective-permute-done.14.time_other, ...), custom_call_target="tpu_custom_call" | custom-call | flops 1000000 | bytes 1000000 | tf_op jit(solution)/shard_map/pallas_call | solution.py:482
  41.8 1.5 %collective-permute-start.19 = (bf16[208,128]{1,0:T(8,128)(2,1)S(1)}, bf16[208,128]{1,0:T(8,128)(2,1)S(1)}, u32[]{:S(2)}, u32[]{:S(2)}) collective-permute-start(bf16[208,128]{1,0:T(8,128)(2,1)S(1)} %get-tuple-element.84.mine), channel_id=1, source_target_pairs={{0,2},{2,0},{1,3},{3,1},{4,6},{6,4},{5,7},{7,5},{8,10},{10,8},{9,1... | collective-permute-start | bytes 159752 | tf_op jit(solution)/shard_map/ppermute | solution.py:496
  43.5 0.4 collective-permute-start.18
  44.0 2.0 %collective-permute-done.19.band = bf16[208,128]{1,0:T(8,128)(2,1)S(1)} collective-permute-done((bf16[208,128]{1,0:T(8,128)(2,1)S(1)}, bf16[208,128]{1,0:T(8,128)(2,1)S(1)}, u32[]{:S(2)}, u32[]{:S(2)}) %collective-permute-start.19) | collective-permute-done | bytes 53280 | tf_op jit(solution)/shard_map/ppermute | solution.py:496
  46.0 1.2 %collective-permute-done.20.both = bf16[208,128]{1,0:T(8,128)(2,1)S(1)} collective-permute-done((bf16[208,128]{1,0:T(8,128)(2,1)S(1)}, bf16[208,128]{1,0:T(8,128)(2,1)S(1)}, u32[]{:S(2)}, u32[]{:S(2)}) %collective-permute-start.20) | collective-permute-done | bytes 53280 | tf_op jit(solution)/shard_map/ppermute | solution.py:496
  47.2 2.6 %collective-permute-start.23 = (bf16[208,128]{1,0:T(8,128)(2,1)S(1)}, bf16[208,128]{1,0:T(8,128)(2,1)S(1)}, u32[]{:S(2)}, u32[]{:S(2)}) collective-permute-start(bf16[208,128]{1,0:T(8,128)(2,1)S(1)} %shard_map.97.rest_0_), channel_id=1, source_target_pairs={{0,12},{4,8},{8,4},{12,0},{1,13},{5,9},{9,5},{13,1},{2,14},{6,10},... | collective-permute-start | bytes 159752 | tf_op jit(solution)/shard_map/ppermute | solution.py:496
  49.9 1.8 %collective-permute-start.21 = (bf16[208,128]{1,0:T(8,128)(2,1)S(1)}, bf16[208,128]{1,0:T(8,128)(2,1)S(1)}, u32[]{:S(2)}, u32[]{:S(2)}) collective-permute-start(bf16[208,128]{1,0:T(8,128)(2,1)S(1)} %shard_map.97.rest_0_), channel_id=1, source_target_pairs={{0,4},{4,0},{8,12},{12,8},{1,5},{5,1},{9,13},{13,9},{2,6},{6,2},{1... | collective-permute-start | bytes 159752 | tf_op jit(solution)/shard_map/ppermute | solution.py:496
  51.7 1.9 %collective-permute-done.23.rest_3_ = bf16[208,128]{1,0:T(8,128)(2,1)S(1)} collective-permute-done((bf16[208,128]{1,0:T(8,128)(2,1)S(1)}, bf16[208,128]{1,0:T(8,128)(2,1)S(1)}, u32[]{:S(2)}, u32[]{:S(2)}) %collective-permute-start.23) | collective-permute-done | bytes 53280 | tf_op jit(solution)/shard_map/ppermute | solution.py:496
  53.6 1.8 %collective-permute-done.22.rest_2_ = bf16[208,128]{1,0:T(8,128)(2,1)S(1)} collective-permute-done((bf16[208,128]{1,0:T(8,128)(2,1)S(1)}, bf16[208,128]{1,0:T(8,128)(2,1)S(1)}, u32[]{:S(2)}, u32[]{:S(2)}) %collective-permute-start.22) | collective-permute-done | bytes 53280 | tf_op jit(solution)/shard_map/ppermute | solution.py:496
  55.4 1.4 %shard_map.98 = (f32[1536,128]{1,0:T(8,128)}, f32[64,96]{1,0:T(8,128)}) custom-call(f32[96,1024]{1,0:T(8,128)S(1)} %get-tuple-element.82.surface, f32[96,1024]{1,0:T(8,128)S(1)} %collective-permute-done.17.other, f32[96,128]{1,0:T(8,128)S(1)} %get-tuple-element.83.time_t, bf16[208,128]{1,0:T(8,128)(2,1)S(1)} %shard_map.97.rest_0_, ...), custom_call_target="tpu_custom_call" | custom-call | flops 1000000 | bytes 1000000 | tf_op jit(solution)/shard_map/pallas_call | solution.py:482
  (31 shorter events, 1.9 us)
Async XLA Ops:
  2.7 14.9 %copy-start = (f32[64,96]{1,0:T(8,128)S(1)}, f32[64,96]{1,0:T(8,128)}, u32[]{:S(2)}) copy-start(f32[64,96]{1,0:T(8,128)} %time_own.1) | copy-start | bytes 73732
  2.8 7.6 %collective-permute-start.3 = (bf16[544,128]{1,0:T(8,128)(2,1)S(1)}, bf16[544,128]{1,0:T(8,128)(2,1)S(1)}, u32[]{:S(2)}, u32[]{:S(2)}) collective-permute-start(bf16[544,128]{1,0:T(8,128)(2,1)S(1)} %get-tuple-element.61), channel_id=1, source_target_pairs={{0,4},{4,0},{8,12},{12,8},{1,5},{5,1},{9,13},{13,9},{2,6},{6,2},{1... | collective-permute-start | bytes 417800 | tf_op jit(solution)/shard_map/ppermute | solution.py:496
  6.0 9.1 %collective-permute-start.1 = (bf16[512,128]{1,0:T(8,128)(2,1)S(1)}, bf16[512,128]{1,0:T(8,128)(2,1)S(1)}, u32[]{:S(2)}, u32[]{:S(2)}) collective-permute-start(bf16[512,128]{1,0:T(8,128)(2,1)S(1)} %get-tuple-element.56), channel_id=1, source_target_pairs={{0,4},{4,0},{8,12},{12,8},{1,5},{5,1},{9,13},{13,9},{2,6},{6,2},{1... | collective-permute-start | bytes 393224 | tf_op jit(solution)/shard_map/ppermute | solution.py:496
  6.1 11.6 %collective-permute-start = (bf16[704,128]{1,0:T(8,128)(2,1)S(1)}, bf16[704,128]{1,0:T(8,128)(2,1)S(1)}, u32[]{:S(2)}, u32[]{:S(2)}) collective-permute-start(bf16[704,128]{1,0:T(8,128)(2,1)S(1)} %get-tuple-element.51), channel_id=1, source_target_pairs={{0,1},{1,0},{4,5},{5,4},{8,9},{9,8},{12,13},{13,12},{2,3},{3,2},{6... | collective-permute-start | bytes 540680 | tf_op jit(solution)/shard_map/ppermute | solution.py:496
  10.4 11.3 %collective-permute-start.4 = (bf16[544,128]{1,0:T(8,128)(2,1)S(1)}, bf16[544,128]{1,0:T(8,128)(2,1)S(1)}, u32[]{:S(2)}, u32[]{:S(2)}) collective-permute-start(bf16[544,128]{1,0:T(8,128)(2,1)S(1)} %shard_map.90), channel_id=1, source_target_pairs={{0,8},{4,12},{8,0},{12,4},{1,9},{5,13},{9,1},{13,5},{2,10},{6,14},... | collective-permute-start | bytes 417800 | tf_op jit(solution)/shard_map/ppermute | solution.py:496
  13.5 6.5 %collective-permute-start.5 = (bf16[528,128]{1,0:T(8,128)(2,1)S(1)}, bf16[528,128]{1,0:T(8,128)(2,1)S(1)}, u32[]{:S(2)}, u32[]{:S(2)}) collective-permute-start(bf16[528,128]{1,0:T(8,128)(2,1)S(1)} %get-tuple-element.62), channel_id=1, source_target_pairs={{0,4},{4,0},{8,12},{12,8},{1,5},{5,1},{9,13},{13,9},{2,6},{6,2},{1... | collective-permute-start | bytes 405512 | tf_op jit(solution)/shard_map/ppermute | solution.py:496
  15.1 8.9 %collective-permute-start.6 = (bf16[512,128]{1,0:T(8,128)(2,1)S(1)}, bf16[512,128]{1,0:T(8,128)(2,1)S(1)}, u32[]{:S(2)}, u32[]{:S(2)}) collective-permute-start(bf16[512,128]{1,0:T(8,128)(2,1)S(1)} %get-tuple-element.66), channel_id=1, source_target_pairs={{0,9},{1,8},{4,13},{5,12},{8,1},{9,0},{12,5},{13,4},{2,11},{3,10},... | collective-permute-start | bytes 393224 | tf_op jit(solution)/shard_map/ppermute | solution.py:496
  15.2 9.1 %collective-permute-start.7 = (bf16[512,128]{1,0:T(8,128)(2,1)S(1)}, bf16[512,128]{1,0:T(8,128)(2,1)S(1)}, u32[]{:S(2)}, u32[]{:S(2)}) collective-permute-start(bf16[512,128]{1,0:T(8,128)(2,1)S(1)} %get-tuple-element.67), channel_id=1, source_target_pairs={{0,5},{1,4},{4,1},{5,0},{8,13},{9,12},{12,9},{13,8},{2,7},{3,6},{6... | collective-permute-start | bytes 393224 | tf_op jit(solution)/shard_map/ppermute | solution.py:496
  17.7 4.0 %collective-permute-start.2 = (f32[96,128]{1,0:T(8,128)S(1)}, f32[96,128]{1,0:T(8,128)S(1)}, u32[]{:S(2)}, u32[]{:S(2)}) collective-permute-start(f32[96,128]{1,0:T(8,128)S(1)} %get-tuple-element.59), channel_id=1, source_target_pairs={{1,2},{3,0},{2,1},{0,3},{5,6},{7,4},{6,5},{4,7},{9,10},{11,8},{10,... | collective-permute-start | bytes 147464 | tf_op jit(solution)/shard_map/ppermute | solution.py:560
  22.4 1.9 %collective-permute-start.8 = (f32[16,128]{1,0:T(8,128)S(1)}, f32[16,128]{1,0:T(8,128)S(1)}, u32[]{:S(2)}, u32[]{:S(2)}) collective-permute-start(f32[16,128]{1,0:T(8,128)S(1)} %get-tuple-element.68), channel_id=1, source_target_pairs={{0,1},{1,0},{2,3},{3,2},{4,5},{5,4},{6,7},{7,6},{8,9},{9,8},{10,11... | collective-permute-start | bytes 24584 | tf_op jit(solution)/shard_map/ppermute | solution.py:496
  24.9 1.3 %collective-permute-start.9 = (f32[104,128]{1,0:T(8,128)S(1)}, f32[104,128]{1,0:T(8,128)S(1)}, u32[]{:S(2)}, u32[]{:S(2)}) collective-permute-start(f32[104,128]{1,0:T(8,128)S(1)} %get-tuple-element.71), channel_id=1, source_target_pairs={{0,1},{1,0},{2,3},{3,2},{4,5},{5,4},{6,7},{7,6},{8,9},{9,8},{10,11... | collective-permute-start | bytes 159752 | tf_op jit(solution)/shard_map/ppermute | solution.py:496
  26.2 4.2 %collective-permute-start.10 = (f32[104,128]{1,0:T(8,128)S(1)}, f32[104,128]{1,0:T(8,128)S(1)}, u32[]{:S(2)}, u32[]{:S(2)}) collective-permute-start(f32[104,128]{1,0:T(8,128)S(1)} %shard_map.93.mine), channel_id=1, source_target_pairs={{0,2},{2,0},{1,3},{3,1},{4,6},{6,4},{5,7},{7,5},{8,10},{10,8},{9,1... | collective-permute-start | bytes 159752 | tf_op jit(solution)/shard_map/ppermute | solution.py:496
  30.5 5.5 %collective-permute-start.11 = (f32[104,128]{1,0:T(8,128)S(1)}, f32[104,128]{1,0:T(8,128)S(1)}, u32[]{:S(2)}, u32[]{:S(2)}) collective-permute-start(f32[104,128]{1,0:T(8,128)S(1)} %get-tuple-element.73.rest_0_), channel_id=1, source_target_pairs={{0,4},{4,0},{8,12},{12,8},{1,5},{5,1},{9,13},{13,9},{2,6},{6,2},{1... | collective-permute-start | bytes 159752 | tf_op jit(solution)/shard_map/ppermute | solution.py:496
  31.4 6.1 %collective-permute-start.13 = (f32[104,128]{1,0:T(8,128)S(1)}, f32[104,128]{1,0:T(8,128)S(1)}, u32[]{:S(2)}, u32[]{:S(2)}) collective-permute-start(f32[104,128]{1,0:T(8,128)S(1)} %get-tuple-element.74), channel_id=1, source_target_pairs={{0,12},{4,8},{8,4},{12,0},{1,13},{5,9},{9,5},{13,1},{2,14},{6,10},... | collective-permute-start | bytes 159752 | tf_op jit(solution)/shard_map/ppermute | solution.py:496
  33.9 5.0 %collective-permute-start.12 = (f32[104,128]{1,0:T(8,128)S(1)}, f32[104,128]{1,0:T(8,128)S(1)}, u32[]{:S(2)}, u32[]{:S(2)}) collective-permute-start(f32[104,128]{1,0:T(8,128)S(1)} %get-tuple-element.74), channel_id=1, source_target_pairs={{0,8},{4,12},{8,0},{12,4},{1,9},{5,13},{9,1},{13,5},{2,10},{6,14},... | collective-permute-start | bytes 159752 | tf_op jit(solution)/shard_map/ppermute | solution.py:496
  34.4 4.7 %collective-permute-start.15 = (f32[96,128]{1,0:T(8,128)S(1)}, f32[96,128]{1,0:T(8,128)S(1)}, u32[]{:S(2)}, u32[]{:S(2)}) collective-permute-start(f32[96,128]{1,0:T(8,128)S(1)} %get-tuple-element.80), channel_id=1, source_target_pairs={{0,1},{1,0},{2,3},{3,2},{4,5},{5,4},{6,7},{7,6},{8,9},{9,8},{10,11... | collective-permute-start | bytes 147464 | tf_op jit(solution)/shard_map/ppermute | solution.py:496
  34.4 4.7 %collective-permute-start.16 = (f32[96,128]{1,0:T(8,128)S(1)}, f32[96,128]{1,0:T(8,128)S(1)}, u32[]{:S(2)}, u32[]{:S(2)}) collective-permute-start(f32[96,128]{1,0:T(8,128)S(1)} %get-tuple-element.81), channel_id=1, source_target_pairs={{1,2},{3,0},{2,1},{0,3},{5,6},{7,4},{6,5},{4,7},{9,10},{11,8},{10,... | collective-permute-start | bytes 147464 | tf_op jit(solution)/shard_map/ppermute | solution.py:560
  39.0 1.3 %collective-permute-start.14 = (f32[96,128]{1,0:T(8,128)S(1)}, f32[96,128]{1,0:T(8,128)S(1)}, u32[]{:S(2)}, u32[]{:S(2)}) collective-permute-start(f32[96,128]{1,0:T(8,128)S(1)} %get-tuple-element.75.time_own), channel_id=1, source_target_pairs={{0,1},{1,0},{2,3},{3,2},{4,5},{5,4},{6,7},{7,6},{8,9},{9,8},{10,11... | collective-permute-start | bytes 147464 | tf_op jit(solution)/shard_map/ppermute | solution.py:496
  41.6 13.8 %collective-permute-start.17 = (f32[96,1024]{1,0:T(8,128)S(1)}, f32[96,1024]{1,0:T(8,128)S(1)}, u32[]{:S(2)}, u32[]{:S(2)}) collective-permute-start(f32[96,1024]{1,0:T(8,128)S(1)} %get-tuple-element.82.surface), channel_id=1, source_target_pairs={{0,1},{1,0},{2,3},{3,2},{4,5},{5,4},{6,7},{7,6},{8,9},{9,8},{10,11... | collective-permute-start | bytes 1179656 | tf_op jit(solution)/shard_map/ppermute | solution.py:496
  41.8 4.1 %collective-permute-start.19 = (bf16[208,128]{1,0:T(8,128)(2,1)S(1)}, bf16[208,128]{1,0:T(8,128)(2,1)S(1)}, u32[]{:S(2)}, u32[]{:S(2)}) collective-permute-start(bf16[208,128]{1,0:T(8,128)(2,1)S(1)} %get-tuple-element.84.mine), channel_id=1, source_target_pairs={{0,2},{2,0},{1,3},{3,1},{4,6},{6,4},{5,7},{7,5},{8,10},{10,8},{9,1... | collective-permute-start | bytes 159752 | tf_op jit(solution)/shard_map/ppermute | solution.py:496
  43.3 3.9 %collective-permute-start.20 = (bf16[208,128]{1,0:T(8,128)(2,1)S(1)}, bf16[208,128]{1,0:T(8,128)(2,1)S(1)}, u32[]{:S(2)}, u32[]{:S(2)}) collective-permute-start(bf16[208,128]{1,0:T(8,128)(2,1)S(1)} %get-tuple-element.85), channel_id=1, source_target_pairs={{0,3},{1,2},{2,1},{3,0},{4,7},{5,6},{6,5},{7,4},{8,11},{9,10},{10,... | collective-permute-start | bytes 159752 | tf_op jit(solution)/shard_map/ppermute | solution.py:496
  43.5 3.7 %collective-permute-start.18 = (bf16[208,128]{1,0:T(8,128)(2,1)S(1)}, bf16[208,128]{1,0:T(8,128)(2,1)S(1)}, u32[]{:S(2)}, u32[]{:S(2)}) collective-permute-start(bf16[208,128]{1,0:T(8,128)(2,1)S(1)} %get-tuple-element.85), channel_id=1, source_target_pairs={{0,1},{1,0},{2,3},{3,2},{4,5},{5,4},{6,7},{7,6},{8,9},{9,8},{10,11... | collective-permute-start | bytes 159752 | tf_op jit(solution)/shard_map/ppermute | solution.py:496
  47.2 6.4 %collective-permute-start.23 = (bf16[208,128]{1,0:T(8,128)(2,1)S(1)}, bf16[208,128]{1,0:T(8,128)(2,1)S(1)}, u32[]{:S(2)}, u32[]{:S(2)}) collective-permute-start(bf16[208,128]{1,0:T(8,128)(2,1)S(1)} %shard_map.97.rest_0_), channel_id=1, source_target_pairs={{0,12},{4,8},{8,4},{12,0},{1,13},{5,9},{9,5},{13,1},{2,14},{6,10},... | collective-permute-start | bytes 159752 | tf_op jit(solution)/shard_map/ppermute | solution.py:496
  49.8 5.6 %collective-permute-start.22 = (bf16[208,128]{1,0:T(8,128)(2,1)S(1)}, bf16[208,128]{1,0:T(8,128)(2,1)S(1)}, u32[]{:S(2)}, u32[]{:S(2)}) collective-permute-start(bf16[208,128]{1,0:T(8,128)(2,1)S(1)} %shard_map.97.rest_0_), channel_id=1, source_target_pairs={{0,8},{4,12},{8,0},{12,4},{1,9},{5,13},{9,1},{13,5},{2,10},{6,14},... | collective-permute-start | bytes 159752 | tf_op jit(solution)/shard_map/ppermute | solution.py:496
  49.9 5.5 %collective-permute-start.21 = (bf16[208,128]{1,0:T(8,128)(2,1)S(1)}, bf16[208,128]{1,0:T(8,128)(2,1)S(1)}, u32[]{:S(2)}, u32[]{:S(2)}) collective-permute-start(bf16[208,128]{1,0:T(8,128)(2,1)S(1)} %shard_map.97.rest_0_), channel_id=1, source_target_pairs={{0,4},{4,0},{8,12},{12,8},{1,5},{5,1},{9,13},{13,9},{2,6},{6,2},{1... | collective-permute-start | bytes 159752 | tf_op jit(solution)/shard_map/ppermute | solution.py:496

commit v17 on v16

--- a/solution.py
+++ b/solution.py
@@ -30,7 +30,7 @@
 
 
 def route_kernel(half, early, paired, list_hbm, count_hbm, target_hbm, swath_hbm, mask_hbm, space_hbm, time_hbm, *rest):
-    piece, total, seen, surface, space_ref, time_ref, *rest = rest
+    piece, second, total, seen, surface, space_ref, time_ref, *rest = rest
     cols = rest.pop(-1 if paired else 0)
     list_ref, count_ref, target_ref, swath_ref, mask_ref, place, arrived = rest
     me, core = lax.axis_index("lon"), lax.axis_index("ta")
@@ -81,6 +81,7 @@
         total[at] += (swath_ref[slot] * by_day[:, slot:slot + 1]).astype(F32)
         seen[pl.ds(at, 1), :days] += mask[slot:slot + 1, :]
     pack(half, n_lon, early, total, seen, piece)
+    pack(half, n_lon, (1, early[1]), total, seen, second)
     end = half * days + TAIL
     if piece.shape[0] > end:
         piece[end:, :] = cols[...].astype(BF16)
@@ -520,9 +521,10 @@
     operands = (send_list, send_count, target, swath, obs_mask, factor_space.reshape(rank * height, cells), factor_time)
     early = (0, n_lon - 1)
     sends.remove(early)
-    first, total, seen, surface, space, time, *cols = call(
+    sends.remove((1, n_lon - 1))
+    first, second, total, seen, surface, space, time, *cols = call(
         functools.partial(route_kernel, half, early, paired),
-        [shape((piece_rows(*early), cells), BF16), shape((2 * n_lon * half, days, cells)), shape((2 * n_lon * half + TAIL, LANES))]
+        [shape((piece_rows(*early), cells), BF16), shape((piece_rows(1, n_lon - 1), cells), BF16), shape((2 * n_lon * half, days, cells)), shape((2 * n_lon * half + TAIL, LANES))]
         + [shape((rank, wide))]
         + [shape(ref.shape) for ref in operands[5:]]
         + [shape((COLS, LANES))] * (not paired),
@@ -544,7 +546,7 @@
             return across(piece, ("lon", "ta"), 2 * step + 1)
         return across(piece, "lon", step) if step else piece
 
-    pieces = dict(zip([early, *sends], [first, *pieces]))
+    pieces = dict(zip([early, (1, n_lon - 1), *sends], [first, second, *pieces]))
     borders = ()
     if paired:
         near, far = (across(pieces.pop((side, 3)), "lon", 1) for side in (0, 1))

time: 57.1 us -> 57.1 us (level)
  no operation moved by 1% of the time
where the time goes in v17:
time: 57.1 us; the launch traced here: 56.9 us
  starting transfers between devices  24.9 us (44%)
  waiting for transfers between devices  24.4 us (43%)
  Pallas kernels  6.84 us (12%)
  between operations  0.76 us (1%)
    ppermute x22, starting transfers between devices, across(): lax.ppermute(value, axis, [(i, i ^ step) for i in range(lax.axis_size(axi...  23.3 us
    ppermute x22, waiting for transfers between devices, across(): lax.ppermute(value, axis, [(i, i ^ step) for i in range(lax.axis_size(axi...  22.8 us
    pallas_call x13, Pallas kernels, run(): pl.pallas_call(kernel, out_shape=out_shape, in_specs=[pl.BlockSpec(memory...  6.84 us
    ppermute x2, starting transfers between devices, bands(): return lax.ppermute(edge, ('lat', 'ta'), there + [(b, a) for a, b in there])  1.61 us
    ppermute x2, waiting for transfers between devices, bands(): return lax.ppermute(edge, ('lat', 'ta'), there + [(b, a) for a, b in there])  1.56 us
  transfers between devices with their start and end apart: 24, of which 14 were waited for; matrix products, arithmetic and copies ran while one was open for 0% of the time, Pallas kernels for 2%

profile of v17, /device:TPU:0, one launch (start us, length us, event | category | flops | bytes accessed | tf_op | source)
XLA Modules:
  0.0 56.9 jit_solution(5655204226105961892)
XLA Ops:
  0.6 2.1 %shard_map.86 = (bf16[544,128]{1,0:T(8,128)(2,1)S(1)}, bf16[512,128]{1,0:T(8,128)(2,1)S(1)}, f32[64,64,128]{2,1,0:T(8,128)S(1)}, f32[80,128]{1,0:T(8,128)S(1)}, ...) custom-call(s32[1,4,32]{2,1,0:T(4,128)} %list_hbm.1, s32[1,4]{1,0:T(1,128)} %count_hbm.1, ...), custom_call_target="tpu_custom_call" | custom-call | flops 1000000 | bytes 1000000 | tf_op jit(solution)/shard_map/pallas_call | solution.py:483
  2.8 3.1 %collective-permute-start.3 = (bf16[544,128]{1,0:T(8,128)(2,1)S(1)}, bf16[544,128]{1,0:T(8,128)(2,1)S(1)}, u32[]{:S(2)}, u32[]{:S(2)}) collective-permute-start(bf16[544,128]{1,0:T(8,128)(2,1)S(1)} %get-tuple-element.61), channel_id=1, source_target_pairs={{0,4},{4,0},{8,12},{12,8},{1,5},{5,1},{9,13},{13,9},{2,6},{6,2},{1... | collective-permute-start | bytes 417800 | tf_op jit(solution)/shard_map/ppermute | solution.py:497
  6.2 4.2 %collective-permute-done.3.theirs.rest_3_ = bf16[544,128]{1,0:T(8,128)(2,1)S(1)} collective-permute-done((bf16[544,128]{1,0:T(8,128)(2,1)S(1)}, bf16[544,128]{1,0:T(8,128)(2,1)S(1)}, u32[]{:S(2)}, u32[]{:S(2)}) %collective-permute-start.3) | collective-permute-done | bytes 139296 | tf_op jit(solution)/shard_map/ppermute | solution.py:497
  10.4 3.1 %collective-permute-start.4 = (bf16[544,128]{1,0:T(8,128)(2,1)S(1)}, bf16[544,128]{1,0:T(8,128)(2,1)S(1)}, u32[]{:S(2)}, u32[]{:S(2)}) collective-permute-start(bf16[544,128]{1,0:T(8,128)(2,1)S(1)} %shard_map.90), channel_id=1, source_target_pairs={{0,8},{4,12},{8,0},{12,4},{1,9},{5,13},{9,1},{13,5},{2,10},{6,14},... | collective-permute-start | bytes 417800 | tf_op jit(solution)/shard_map/ppermute | solution.py:497
  13.5 1.6 %collective-permute-start.5 = (bf16[528,128]{1,0:T(8,128)(2,1)S(1)}, bf16[528,128]{1,0:T(8,128)(2,1)S(1)}, u32[]{:S(2)}, u32[]{:S(2)}) collective-permute-start(bf16[528,128]{1,0:T(8,128)(2,1)S(1)} %get-tuple-element.62), channel_id=1, source_target_pairs={{0,4},{4,0},{8,12},{12,8},{1,5},{5,1},{9,13},{13,9},{2,6},{6,2},{1... | collective-permute-start | bytes 405512 | tf_op jit(solution)/shard_map/ppermute | solution.py:497
  15.2 2.4 %collective-permute-start.7 = (bf16[512,128]{1,0:T(8,128)(2,1)S(1)}, bf16[512,128]{1,0:T(8,128)(2,1)S(1)}, u32[]{:S(2)}, u32[]{:S(2)}) collective-permute-start(bf16[512,128]{1,0:T(8,128)(2,1)S(1)} %get-tuple-element.67), channel_id=1, source_target_pairs={{0,5},{1,4},{4,1},{5,0},{8,13},{9,12},{12,9},{13,8},{2,7},{3,6},{6... | collective-permute-start | bytes 393224 | tf_op jit(solution)/shard_map/ppermute | solution.py:497
  17.9 2.2 %collective-permute-done.5.rest_1_ = bf16[528,128]{1,0:T(8,128)(2,1)S(1)} collective-permute-done((bf16[528,128]{1,0:T(8,128)(2,1)S(1)}, bf16[528,128]{1,0:T(8,128)(2,1)S(1)}, u32[]{:S(2)}, u32[]{:S(2)}) %collective-permute-start.5) | collective-permute-done | bytes 135200 | tf_op jit(solution)/shard_map/ppermute | solution.py:497
  20.1 1.6 %collective-permute-done.2.edge_far = f32[96,128]{1,0:T(8,128)S(1)} collective-permute-done((f32[96,128]{1,0:T(8,128)S(1)}, f32[96,128]{1,0:T(8,128)S(1)}, u32[]{:S(2)}, u32[]{:S(2)}) %collective-permute-start.2) | collective-permute-done | bytes 49184 | tf_op jit(solution)/shard_map/ppermute | solution.py:562
  21.6 0.7 %shard_map.91 = (f32[96,1024]{1,0:T(8,128)S(1)}, f32[96,128]{1,0:T(8,128)S(1)}, f32[64,1024]{1,0:T(8,128)S(1)}, f32[16,128]{1,0:T(8,128)S(1)}, f32[16,128]{1,0:T(8,128)S(1)}) custom-call(f32[96,1024]{1,0:T(8,128)S(1)} %get-tuple-element.45.surface, f32[96,128]{1,0:T(8,128)S(1)} %get-tuple-element.50.edge_near, f32[128,1024]{1,0:T(8,128)S(1)} %get-tuple-element.52.predicted, ...), custom_call_target="tpu_custom_call" | custom-call | flops 1000000 | bytes 1000000 | tf_op jit(solution)/shard_map/pallas_call | solution.py:483
  22.6 1.4 %collective-permute-done.6.rest_0_ = bf16[512,128]{1,0:T(8,128)(2,1)S(1)} collective-permute-done((bf16[512,128]{1,0:T(8,128)(2,1)S(1)}, bf16[512,128]{1,0:T(8,128)(2,1)S(1)}, u32[]{:S(2)}, u32[]{:S(2)}) %collective-permute-start.6) | collective-permute-done | bytes 131104 | tf_op jit(solution)/shard_map/ppermute | solution.py:497
  24.1 0.2 collective-permute-done.7.rest_2_
  24.3 0.6 %shard_map.92 = (f32[96,1024]{1,0:T(8,128)S(1)}, f32[104,128]{1,0:T(8,128)S(1)}, f32[104,128]{1,0:T(8,128)S(1)}, f32[16,128]{1,0:T(8,128)S(1)}, f32[96,128]{1,0:...) custom-call(f32[96,1024]{1,0:T(8,128)S(1)} %get-tuple-element.64.base, ...), custom_call_target="tpu_custom_call" | custom-call | flops 1000000 | bytes 1000000 | tf_op jit(solution)/shard_map/pallas_call | solution.py:483
  25.1 1.1 %collective-permute-done.9.core = f32[104,128]{1,0:T(8,128)S(1)} collective-permute-done((f32[104,128]{1,0:T(8,128)S(1)}, f32[104,128]{1,0:T(8,128)S(1)}, u32[]{:S(2)}, u32[]{:S(2)}) %collective-permute-start.9) | collective-permute-done | bytes 53280 | tf_op jit(solution)/shard_map/ppermute | solution.py:497
  26.3 1.7 %collective-permute-start.10 = (f32[104,128]{1,0:T(8,128)S(1)}, f32[104,128]{1,0:T(8,128)S(1)}, u32[]{:S(2)}, u32[]{:S(2)}) collective-permute-start(f32[104,128]{1,0:T(8,128)S(1)} %shard_map.93.mine), channel_id=1, source_target_pairs={{0,2},{2,0},{1,3},{3,1},{4,6},{6,4},{5,7},{7,5},{8,10},{10,8},{9,1... | collective-permute-start | bytes 159752 | tf_op jit(solution)/shard_map/ppermute | solution.py:497
  28.0 2.5 %collective-permute-done.10.band = f32[104,128]{1,0:T(8,128)S(1)} collective-permute-done((f32[104,128]{1,0:T(8,128)S(1)}, f32[104,128]{1,0:T(8,128)S(1)}, u32[]{:S(2)}, u32[]{:S(2)}) %collective-permute-start.10) | collective-permute-done | bytes 53280 | tf_op jit(solution)/shard_map/ppermute | solution.py:497
  30.5 0.9 %collective-permute-start.11 = (f32[104,128]{1,0:T(8,128)S(1)}, f32[104,128]{1,0:T(8,128)S(1)}, u32[]{:S(2)}, u32[]{:S(2)}) collective-permute-start(f32[104,128]{1,0:T(8,128)S(1)} %get-tuple-element.73.rest_0_), channel_id=1, source_target_pairs={{0,4},{4,0},{8,12},{12,8},{1,5},{5,1},{9,13},{13,9},{2,6},{6,2},{1... | collective-permute-start | bytes 159752 | tf_op jit(solution)/shard_map/ppermute | solution.py:497
  31.4 2.5 %collective-permute-start.13 = (f32[104,128]{1,0:T(8,128)S(1)}, f32[104,128]{1,0:T(8,128)S(1)}, u32[]{:S(2)}, u32[]{:S(2)}) collective-permute-start(f32[104,128]{1,0:T(8,128)S(1)} %get-tuple-element.74), channel_id=1, source_target_pairs={{0,12},{4,8},{8,4},{12,0},{1,13},{5,9},{9,5},{13,1},{2,14},{6,10},... | collective-permute-start | bytes 159752 | tf_op jit(solution)/shard_map/ppermute | solution.py:497
  33.9 0.5 collective-permute-start.12
  34.4 1.6 %collective-permute-start.16 = (f32[96,128]{1,0:T(8,128)S(1)}, f32[96,128]{1,0:T(8,128)S(1)}, u32[]{:S(2)}, u32[]{:S(2)}) collective-permute-start(f32[96,128]{1,0:T(8,128)S(1)} %get-tuple-element.81), channel_id=1, source_target_pairs={{1,2},{3,0},{2,1},{0,3},{5,6},{7,4},{6,5},{4,7},{9,10},{11,8},{10,... | collective-permute-start | bytes 147464 | tf_op jit(solution)/shard_map/ppermute | solution.py:562
  36.0 1.5 %collective-permute-done.13.rest_3_.cols_b = f32[104,128]{1,0:T(8,128)S(1)} collective-permute-done((f32[104,128]{1,0:T(8,128)S(1)}, f32[104,128]{1,0:T(8,128)S(1)}, u32[]{:S(2)}, u32[]{:S(2)}) %collective-permute-start.13) | collective-permute-done | bytes 53280 | tf_op jit(solution)/shard_map/ppermute | solution.py:497
  37.5 1.4 %collective-permute-done.12.rest_2_ = f32[104,128]{1,0:T(8,128)S(1)} collective-permute-done((f32[104,128]{1,0:T(8,128)S(1)}, f32[104,128]{1,0:T(8,128)S(1)}, u32[]{:S(2)}, u32[]{:S(2)}) %collective-permute-start.12) | collective-permute-done | bytes 53280 | tf_op jit(solution)/shard_map/ppermute | solution.py:497
  39.1 1.2 %collective-permute-done.14.time_other = f32[96,128]{1,0:T(8,128)S(1)} collective-permute-done((f32[96,128]{1,0:T(8,128)S(1)}, f32[96,128]{1,0:T(8,128)S(1)}, u32[]{:S(2)}, u32[]{:S(2)}) %collective-permute-start.14) | collective-permute-done | bytes 49184 | tf_op jit(solution)/shard_map/ppermute | solution.py:497
  40.3 1.3 %shard_map.96 = (f32[96,1024]{1,0:T(8,128)S(1)}, f32[96,128]{1,0:T(8,128)S(1)}, bf16[208,128]{1,0:T(8,128)(2,1)S(1)}, bf16[208,128]{1,0:T(8,128)(2,1)S(1)}) custom-call(f32[96,1024]{1,0:T(8,128)S(1)} %get-tuple-element.69.surface, f32[96,128]{1,0:T(8,128)S(1)} %get-tuple-element.75.time_own, f32[96,128]{1,0:T(8,128)S(1)} %collective-permute-done.14.time_other, ...), custom_call_target="tpu_custom_call" | custom-call | flops 1000000 | bytes 1000000 | tf_op jit(solution)/shard_map/pallas_call | solution.py:483
  41.9 1.5 %collective-permute-start.19 = (bf16[208,128]{1,0:T(8,128)(2,1)S(1)}, bf16[208,128]{1,0:T(8,128)(2,1)S(1)}, u32[]{:S(2)}, u32[]{:S(2)}) collective-permute-start(bf16[208,128]{1,0:T(8,128)(2,1)S(1)} %get-tuple-element.84.mine), channel_id=1, source_target_pairs={{0,2},{2,0},{1,3},{3,1},{4,6},{6,4},{5,7},{7,5},{8,10},{10,8},{9,1... | collective-permute-start | bytes 159752 | tf_op jit(solution)/shard_map/ppermute | solution.py:497
  43.6 0.4 collective-permute-start.18
  44.0 2.0 %collective-permute-done.19.band = bf16[208,128]{1,0:T(8,128)(2,1)S(1)} collective-permute-done((bf16[208,128]{1,0:T(8,128)(2,1)S(1)}, bf16[208,128]{1,0:T(8,128)(2,1)S(1)}, u32[]{:S(2)}, u32[]{:S(2)}) %collective-permute-start.19) | collective-permute-done | bytes 53280 | tf_op jit(solution)/shard_map/ppermute | solution.py:497
  46.0 1.2 %collective-permute-done.20.both = bf16[208,128]{1,0:T(8,128)(2,1)S(1)} collective-permute-done((bf16[208,128]{1,0:T(8,128)(2,1)S(1)}, bf16[208,128]{1,0:T(8,128)(2,1)S(1)}, u32[]{:S(2)}, u32[]{:S(2)}) %collective-permute-start.20) | collective-permute-done | bytes 53280 | tf_op jit(solution)/shard_map/ppermute | solution.py:497
  47.3 2.6 %collective-permute-start.23 = (bf16[208,128]{1,0:T(8,128)(2,1)S(1)}, bf16[208,128]{1,0:T(8,128)(2,1)S(1)}, u32[]{:S(2)}, u32[]{:S(2)}) collective-permute-start(bf16[208,128]{1,0:T(8,128)(2,1)S(1)} %shard_map.97.rest_0_), channel_id=1, source_target_pairs={{0,12},{4,8},{8,4},{12,0},{1,13},{5,9},{9,5},{13,1},{2,14},{6,10},... | collective-permute-start | bytes 159752 | tf_op jit(solution)/shard_map/ppermute | solution.py:497
  49.9 1.8 %collective-permute-start.21 = (bf16[208,128]{1,0:T(8,128)(2,1)S(1)}, bf16[208,128]{1,0:T(8,128)(2,1)S(1)}, u32[]{:S(2)}, u32[]{:S(2)}) collective-permute-start(bf16[208,128]{1,0:T(8,128)(2,1)S(1)} %shard_map.97.rest_0_), channel_id=1, source_target_pairs={{0,4},{4,0},{8,12},{12,8},{1,5},{5,1},{9,13},{13,9},{2,6},{6,2},{1... | collective-permute-start | bytes 159752 | tf_op jit(solution)/shard_map/ppermute | solution.py:497
  51.7 1.9 %collective-permute-done.23.rest_3_ = bf16[208,128]{1,0:T(8,128)(2,1)S(1)} collective-permute-done((bf16[208,128]{1,0:T(8,128)(2,1)S(1)}, bf16[208,128]{1,0:T(8,128)(2,1)S(1)}, u32[]{:S(2)}, u32[]{:S(2)}) %collective-permute-start.23) | collective-permute-done | bytes 53280 | tf_op jit(solution)/shard_map/ppermute | solution.py:497
  53.7 1.8 %collective-permute-done.22.rest_2_ = bf16[208,128]{1,0:T(8,128)(2,1)S(1)} collective-permute-done((bf16[208,128]{1,0:T(8,128)(2,1)S(1)}, bf16[208,128]{1,0:T(8,128)(2,1)S(1)}, u32[]{:S(2)}, u32[]{:S(2)}) %collective-permute-start.22) | collective-permute-done | bytes 53280 | tf_op jit(solution)/shard_map/ppermute | solution.py:497
  55.5 1.4 %shard_map.98 = (f32[1536,128]{1,0:T(8,128)}, f32[64,96]{1,0:T(8,128)}) custom-call(f32[96,1024]{1,0:T(8,128)S(1)} %get-tuple-element.82.surface, f32[96,1024]{1,0:T(8,128)S(1)} %collective-permute-done.17.other, f32[96,128]{1,0:T(8,128)S(1)} %get-tuple-element.83.time_t, bf16[208,128]{1,0:T(8,128)(2,1)S(1)} %shard_map.97.rest_0_, ...), custom_call_target="tpu_custom_call" | custom-call | flops 1000000 | bytes 1000000 | tf_op jit(solution)/shard_map/pallas_call | solution.py:483
  (31 shorter events, 1.9 us)
Async XLA Ops:
  2.7 14.9 %copy-start = (f32[64,96]{1,0:T(8,128)S(1)}, f32[64,96]{1,0:T(8,128)}, u32[]{:S(2)}) copy-start(f32[64,96]{1,0:T(8,128)} %time_own.1) | copy-start | bytes 73732
  2.8 7.6 %collective-permute-start.3 = (bf16[544,128]{1,0:T(8,128)(2,1)S(1)}, bf16[544,128]{1,0:T(8,128)(2,1)S(1)}, u32[]{:S(2)}, u32[]{:S(2)}) collective-permute-start(bf16[544,128]{1,0:T(8,128)(2,1)S(1)} %get-tuple-element.61), channel_id=1, source_target_pairs={{0,4},{4,0},{8,12},{12,8},{1,5},{5,1},{9,13},{13,9},{2,6},{6,2},{1... | collective-permute-start | bytes 417800 | tf_op jit(solution)/shard_map/ppermute | solution.py:497
  5.8 9.3 %collective-permute-start.1 = (bf16[512,128]{1,0:T(8,128)(2,1)S(1)}, bf16[512,128]{1,0:T(8,128)(2,1)S(1)}, u32[]{:S(2)}, u32[]{:S(2)}) collective-permute-start(bf16[512,128]{1,0:T(8,128)(2,1)S(1)} %get-tuple-element.56), channel_id=1, source_target_pairs={{0,4},{4,0},{8,12},{12,8},{1,5},{5,1},{9,13},{13,9},{2,6},{6,2},{1... | collective-permute-start | bytes 393224 | tf_op jit(solution)/shard_map/ppermute | solution.py:497
  6.1 11.6 %collective-permute-start = (bf16[704,128]{1,0:T(8,128)(2,1)S(1)}, bf16[704,128]{1,0:T(8,128)(2,1)S(1)}, u32[]{:S(2)}, u32[]{:S(2)}) collective-permute-start(bf16[704,128]{1,0:T(8,128)(2,1)S(1)} %get-tuple-element.51), channel_id=1, source_target_pairs={{0,1},{1,0},{4,5},{5,4},{8,9},{9,8},{12,13},{13,12},{2,3},{3,2},{6... | collective-permute-start | bytes 540680 | tf_op jit(solution)/shard_map/ppermute | solution.py:497
  10.4 11.3 %collective-permute-start.4 = (bf16[544,128]{1,0:T(8,128)(2,1)S(1)}, bf16[544,128]{1,0:T(8,128)(2,1)S(1)}, u32[]{:S(2)}, u32[]{:S(2)}) collective-permute-start(bf16[544,128]{1,0:T(8,128)(2,1)S(1)} %shard_map.90), channel_id=1, source_target_pairs={{0,8},{4,12},{8,0},{12,4},{1,9},{5,13},{9,1},{13,5},{2,10},{6,14},... | collective-permute-start | bytes 417800 | tf_op jit(solution)/shard_map/ppermute | solution.py:497
  13.5 6.6 %collective-permute-start.5 = (bf16[528,128]{1,0:T(8,128)(2,1)S(1)}, bf16[528,128]{1,0:T(8,128)(2,1)S(1)}, u32[]{:S(2)}, u32[]{:S(2)}) collective-permute-start(bf16[528,128]{1,0:T(8,128)(2,1)S(1)} %get-tuple-element.62), channel_id=1, source_target_pairs={{0,4},{4,0},{8,12},{12,8},{1,5},{5,1},{9,13},{13,9},{2,6},{6,2},{1... | collective-permute-start | bytes 405512 | tf_op jit(solution)/shard_map/ppermute | solution.py:497
  15.2 8.9 %collective-permute-start.6 = (bf16[512,128]{1,0:T(8,128)(2,1)S(1)}, bf16[512,128]{1,0:T(8,128)(2,1)S(1)}, u32[]{:S(2)}, u32[]{:S(2)}) collective-permute-start(bf16[512,128]{1,0:T(8,128)(2,1)S(1)} %get-tuple-element.66), channel_id=1, source_target_pairs={{0,9},{1,8},{4,13},{5,12},{8,1},{9,0},{12,5},{13,4},{2,11},{3,10},... | collective-permute-start | bytes 393224 | tf_op jit(solution)/shard_map/ppermute | solution.py:497
  15.2 9.1 %collective-permute-start.7 = (bf16[512,128]{1,0:T(8,128)(2,1)S(1)}, bf16[512,128]{1,0:T(8,128)(2,1)S(1)}, u32[]{:S(2)}, u32[]{:S(2)}) collective-permute-start(bf16[512,128]{1,0:T(8,128)(2,1)S(1)} %get-tuple-element.67), channel_id=1, source_target_pairs={{0,5},{1,4},{4,1},{5,0},{8,13},{9,12},{12,9},{13,8},{2,7},{3,6},{6... | collective-permute-start | bytes 393224 | tf_op jit(solution)/shard_map/ppermute | solution.py:497
  17.7 4.0 %collective-permute-start.2 = (f32[96,128]{1,0:T(8,128)S(1)}, f32[96,128]{1,0:T(8,128)S(1)}, u32[]{:S(2)}, u32[]{:S(2)}) collective-permute-start(f32[96,128]{1,0:T(8,128)S(1)} %get-tuple-element.59), channel_id=1, source_target_pairs={{1,2},{3,0},{2,1},{0,3},{5,6},{7,4},{6,5},{4,7},{9,10},{11,8},{10,... | collective-permute-start | bytes 147464 | tf_op jit(solution)/shard_map/ppermute | solution.py:562
  22.4 1.9 %collective-permute-start.8 = (f32[16,128]{1,0:T(8,128)S(1)}, f32[16,128]{1,0:T(8,128)S(1)}, u32[]{:S(2)}, u32[]{:S(2)}) collective-permute-start(f32[16,128]{1,0:T(8,128)S(1)} %get-tuple-element.68), channel_id=1, source_target_pairs={{0,1},{1,0},{2,3},{3,2},{4,5},{5,4},{6,7},{7,6},{8,9},{9,8},{10,11... | collective-permute-start | bytes 24584 | tf_op jit(solution)/shard_map/ppermute | solution.py:497
  24.9 1.3 %collective-permute-start.9 = (f32[104,128]{1,0:T(8,128)S(1)}, f32[104,128]{1,0:T(8,128)S(1)}, u32[]{:S(2)}, u32[]{:S(2)}) collective-permute-start(f32[104,128]{1,0:T(8,128)S(1)} %get-tuple-element.71), channel_id=1, source_target_pairs={{0,1},{1,0},{2,3},{3,2},{4,5},{5,4},{6,7},{7,6},{8,9},{9,8},{10,11... | collective-permute-start | bytes 159752 | tf_op jit(solution)/shard_map/ppermute | solution.py:497
  26.3 4.2 %collective-permute-start.10 = (f32[104,128]{1,0:T(8,128)S(1)}, f32[104,128]{1,0:T(8,128)S(1)}, u32[]{:S(2)}, u32[]{:S(2)}) collective-permute-start(f32[104,128]{1,0:T(8,128)S(1)} %shard_map.93.mine), channel_id=1, source_target_pairs={{0,2},{2,0},{1,3},{3,1},{4,6},{6,4},{5,7},{7,5},{8,10},{10,8},{9,1... | collective-permute-start | bytes 159752 | tf_op jit(solution)/shard_map/ppermute | solution.py:497
  30.5 5.5 %collective-permute-start.11 = (f32[104,128]{1,0:T(8,128)S(1)}, f32[104,128]{1,0:T(8,128)S(1)}, u32[]{:S(2)}, u32[]{:S(2)}) collective-permute-start(f32[104,128]{1,0:T(8,128)S(1)} %get-tuple-element.73.rest_0_), channel_id=1, source_target_pairs={{0,4},{4,0},{8,12},{12,8},{1,5},{5,1},{9,13},{13,9},{2,6},{6,2},{1... | collective-permute-start | bytes 159752 | tf_op jit(solution)/shard_map/ppermute | solution.py:497
  31.4 6.1 %collective-permute-start.13 = (f32[104,128]{1,0:T(8,128)S(1)}, f32[104,128]{1,0:T(8,128)S(1)}, u32[]{:S(2)}, u32[]{:S(2)}) collective-permute-start(f32[104,128]{1,0:T(8,128)S(1)} %get-tuple-element.74), channel_id=1, source_target_pairs={{0,12},{4,8},{8,4},{12,0},{1,13},{5,9},{9,5},{13,1},{2,14},{6,10},... | collective-permute-start | bytes 159752 | tf_op jit(solution)/shard_map/ppermute | solution.py:497
  33.9 5.0 %collective-permute-start.12 = (f32[104,128]{1,0:T(8,128)S(1)}, f32[104,128]{1,0:T(8,128)S(1)}, u32[]{:S(2)}, u32[]{:S(2)}) collective-permute-start(f32[104,128]{1,0:T(8,128)S(1)} %get-tuple-element.74), channel_id=1, source_target_pairs={{0,8},{4,12},{8,0},{12,4},{1,9},{5,13},{9,1},{13,5},{2,10},{6,14},... | collective-permute-start | bytes 159752 | tf_op jit(solution)/shard_map/ppermute | solution.py:497
  34.4 4.7 %collective-permute-start.15 = (f32[96,128]{1,0:T(8,128)S(1)}, f32[96,128]{1,0:T(8,128)S(1)}, u32[]{:S(2)}, u32[]{:S(2)}) collective-permute-start(f32[96,128]{1,0:T(8,128)S(1)} %get-tuple-element.80), channel_id=1, source_target_pairs={{0,1},{1,0},{2,3},{3,2},{4,5},{5,4},{6,7},{7,6},{8,9},{9,8},{10,11... | collective-permute-start | bytes 147464 | tf_op jit(solution)/shard_map/ppermute | solution.py:497
  34.4 4.7 %collective-permute-start.16 = (f32[96,128]{1,0:T(8,128)S(1)}, f32[96,128]{1,0:T(8,128)S(1)}, u32[]{:S(2)}, u32[]{:S(2)}) collective-permute-start(f32[96,128]{1,0:T(8,128)S(1)} %get-tuple-element.81), channel_id=1, source_target_pairs={{1,2},{3,0},{2,1},{0,3},{5,6},{7,4},{6,5},{4,7},{9,10},{11,8},{10,... | collective-permute-start | bytes 147464 | tf_op jit(solution)/shard_map/ppermute | solution.py:562
  39.0 1.3 %collective-permute-start.14 = (f32[96,128]{1,0:T(8,128)S(1)}, f32[96,128]{1,0:T(8,128)S(1)}, u32[]{:S(2)}, u32[]{:S(2)}) collective-permute-start(f32[96,128]{1,0:T(8,128)S(1)} %get-tuple-element.75.time_own), channel_id=1, source_target_pairs={{0,1},{1,0},{2,3},{3,2},{4,5},{5,4},{6,7},{7,6},{8,9},{9,8},{10,11... | collective-permute-start | bytes 147464 | tf_op jit(solution)/shard_map/ppermute | solution.py:497
  41.6 13.8 %collective-permute-start.17 = (f32[96,1024]{1,0:T(8,128)S(1)}, f32[96,1024]{1,0:T(8,128)S(1)}, u32[]{:S(2)}, u32[]{:S(2)}) collective-permute-start(f32[96,1024]{1,0:T(8,128)S(1)} %get-tuple-element.82.surface), channel_id=1, source_target_pairs={{0,1},{1,0},{2,3},{3,2},{4,5},{5,4},{6,7},{7,6},{8,9},{9,8},{10,11... | collective-permute-start | bytes 1179656 | tf_op jit(solution)/shard_map/ppermute | solution.py:497
  41.9 4.1 %collective-permute-start.19 = (bf16[208,128]{1,0:T(8,128)(2,1)S(1)}, bf16[208,128]{1,0:T(8,128)(2,1)S(1)}, u32[]{:S(2)}, u32[]{:S(2)}) collective-permute-start(bf16[208,128]{1,0:T(8,128)(2,1)S(1)} %get-tuple-element.84.mine), channel_id=1, source_target_pairs={{0,2},{2,0},{1,3},{3,1},{4,6},{6,4},{5,7},{7,5},{8,10},{10,8},{9,1... | collective-permute-start | bytes 159752 | tf_op jit(solution)/shard_map/ppermute | solution.py:497
  43.4 3.9 %collective-permute-start.20 = (bf16[208,128]{1,0:T(8,128)(2,1)S(1)}, bf16[208,128]{1,0:T(8,128)(2,1)S(1)}, u32[]{:S(2)}, u32[]{:S(2)}) collective-permute-start(bf16[208,128]{1,0:T(8,128)(2,1)S(1)} %get-tuple-element.85), channel_id=1, source_target_pairs={{0,3},{1,2},{2,1},{3,0},{4,7},{5,6},{6,5},{7,4},{8,11},{9,10},{10,... | collective-permute-start | bytes 159752 | tf_op jit(solution)/shard_map/ppermute | solution.py:497
  43.6 3.7 %collective-permute-start.18 = (bf16[208,128]{1,0:T(8,128)(2,1)S(1)}, bf16[208,128]{1,0:T(8,128)(2,1)S(1)}, u32[]{:S(2)}, u32[]{:S(2)}) collective-permute-start(bf16[208,128]{1,0:T(8,128)(2,1)S(1)} %get-tuple-element.85), channel_id=1, source_target_pairs={{0,1},{1,0},{2,3},{3,2},{4,5},{5,4},{6,7},{7,6},{8,9},{9,8},{10,11... | collective-permute-start | bytes 159752 | tf_op jit(solution)/shard_map/ppermute | solution.py:497
  47.3 6.4 %collective-permute-start.23 = (bf16[208,128]{1,0:T(8,128)(2,1)S(1)}, bf16[208,128]{1,0:T(8,128)(2,1)S(1)}, u32[]{:S(2)}, u32[]{:S(2)}) collective-permute-start(bf16[208,128]{1,0:T(8,128)(2,1)S(1)} %shard_map.97.rest_0_), channel_id=1, source_target_pairs={{0,12},{4,8},{8,4},{12,0},{1,13},{5,9},{9,5},{13,1},{2,14},{6,10},... | collective-permute-start | bytes 159752 | tf_op jit(solution)/shard_map/ppermute | solution.py:497
  49.9 5.6 %collective-permute-start.22 = (bf16[208,128]{1,0:T(8,128)(2,1)S(1)}, bf16[208,128]{1,0:T(8,128)(2,1)S(1)}, u32[]{:S(2)}, u32[]{:S(2)}) collective-permute-start(bf16[208,128]{1,0:T(8,128)(2,1)S(1)} %shard_map.97.rest_0_), channel_id=1, source_target_pairs={{0,8},{4,12},{8,0},{12,4},{1,9},{5,13},{9,1},{13,5},{2,10},{6,14},... | collective-permute-start | bytes 159752 | tf_op jit(solution)/shard_map/ppermute | solution.py:497
  49.9 5.5 %collective-permute-start.21 = (bf16[208,128]{1,0:T(8,128)(2,1)S(1)}, bf16[208,128]{1,0:T(8,128)(2,1)S(1)}, u32[]{:S(2)}, u32[]{:S(2)}) collective-permute-start(bf16[208,128]{1,0:T(8,128)(2,1)S(1)} %shard_map.97.rest_0_), channel_id=1, source_target_pairs={{0,4},{4,0},{8,12},{12,8},{1,5},{5,1},{9,13},{13,9},{2,6},{6,2},{1... | collective-permute-start | bytes 159752 | tf_op jit(solution)/shard_map/ppermute | solution.py:497
